TPU v7x, 32 devices: a whole 2x2x4 slice. The times are simulated.
32 devices in a mesh: dp: 8 (over z, core), seq: 4 (over y, x).
Axes of the slice: x: 2, y: 2, z: 4, core: 2. Of those that a mesh axis runs over, the one named last changes fastest.
Arguments:
- layer_input: bfloat16 [2, 8, 1024, 1024], P(None, 'dp', 'seq'), may hold values from -6 to 6
- memory: bfloat16 [2, 8, 512, 1024], P(None, 'dp', 'seq'), may hold values from -6 to 6
- target_lengths: int32 [2, 8], P(None, 'dp'), may hold values from 512 to 1024, as said below
- memory_lengths: int32 [2, 8], P(None, 'dp'), may hold values from 256 to 512, as said below
- buckets: int32 [1024], replicated, may hold values from 0 to 31, as said below
- norm_self: bfloat16 [1024], P('dp'), may hold values from 0.25 to 1.75
- self_q: bfloat16 [1024, 1024], P('dp'), may hold values from -0.046875 to 0.046875
- self_k: bfloat16 [1024, 512], P('dp'), may hold values from -0.1875 to 0.1875
- self_v: bfloat16 [1024, 512], P('dp'), may hold values from -0.1875 to 0.1875
- self_out: bfloat16 [1024, 1024], P('dp'), may hold values from -0.75 to 0.75
- rel_bias: bfloat16 [32, 16], P('dp', 'seq'), may hold values from -4 to 4
- norm_cross: bfloat16 [1024], P('dp'), may hold values from 0.25 to 1.75
- cross_q: bfloat16 [1024, 1024], P('dp'), may hold values from -0.046875 to 0.046875
- cross_k: bfloat16 [1024, 512], P('dp'), may hold values from -0.1875 to 0.1875
- cross_v: bfloat16 [1024, 512], P('dp'), may hold values from -0.1875 to 0.1875
- cross_out: bfloat16 [1024, 1024], P('dp'), may hold values from -0.75 to 0.75
- norm_ff: bfloat16 [1024], P('dp'), may hold values from 0.25 to 1.75
- ff_gate: bfloat16 [1024, 2816], P('dp'), may hold values from -0.1875 to 0.1875
- ff_up: bfloat16 [1024, 2816], P('dp'), may hold values from -0.1875 to 0.1875
- ff_down: bfloat16 [2816, 1024], P('dp'), may hold values from -0.21875 to 0.21875
- cotangent: bfloat16 [2, 8, 1024, 1024], P(None, 'dp', 'seq'), may hold values from -6 to 6
Outputs:
- output: bfloat16 [2, 8, 1024, 1024], P(None, 'dp', 'seq')
- input_grad: float32 [2, 8, 1024, 1024], P(None, 'dp', 'seq')
- memory_grad: float32 [2, 8, 512, 1024], P(None, 'dp', 'seq')
- norm_self_grad: float32 [1024], P(('dp', 'seq'))
- self_q_grad: float32 [1024, 1024], P(('dp', 'seq'))
- self_k_grad: float32 [1024, 512], P(('dp', 'seq'))
- self_v_grad: float32 [1024, 512], P(('dp', 'seq'))
- self_out_grad: float32 [1024, 1024], P(('dp', 'seq'))
- rel_bias_grad: float32 [32, 16], P('dp', 'seq')
- norm_cross_grad: float32 [1024], P(('dp', 'seq'))
- cross_q_grad: float32 [1024, 1024], P(('dp', 'seq'))
- cross_k_grad: float32 [1024, 512], P(('dp', 'seq'))
- cross_v_grad: float32 [1024, 512], P(('dp', 'seq'))
- cross_out_grad: float32 [1024, 1024], P(('dp', 'seq'))
- norm_ff_grad: float32 [1024], P(('dp', 'seq'))
- ff_gate_grad: float32 [1024, 2816], P(('dp', 'seq'))
- ff_up_grad: float32 [1024, 2816], P(('dp', 'seq'))
- ff_down_grad: float32 [2816, 1024], P(('dp', 'seq'))
Inputs may be any that keep to these rules, and one draw needn't show every extreme that they name: `target_lengths`: in every row one of the 2 micro-batches has all 1024 positions valid. `memory_lengths`: in every row one of the 2 micro-batches has all 512 positions valid. `buckets`: 0 at distance 0, never falling, rising by at most one from one distance to the next.
All inputs are finite; a program needn't handle non-finite values.
Results may differ from a plain program's by a relative error of at most 0.028.
The roundings to bfloat16 on the way count: a program that leaves them out, or rounds other values in their place, can miss the bound.
Values may be sent and summed in bfloat16 or wider, within the bound.
A program may use at most 512 MiB of HBM per device.

v0:
```python
import jax
import jax.numpy as jnp
from jax import lax
from jax.sharding import PartitionSpec as P

HEADS = 16
HEAD_DIM = 64
BUCKETS = 32
KV_HEADS = 8
TGT = 1024
MEM = 512


EPS = 1e-06
NEG = -1e30
HIGH = lax.Precision.HIGHEST


def shortened(shard):
    return jax.tree.map(lambda a: a.astype(jnp.bfloat16) if a.dtype == jnp.float32 else a, shard)


def rms_norm(value, gain):
    return value * lax.rsqrt(jnp.mean(value * value, axis=-1, keepdims=True) + EPS) * gain


def gated(gate, upward):
    return jax.nn.gelu(gate, approximate=True) * upward


def project(left, right):
    return jnp.dot(left, right, preferred_element_type=jnp.float32)


def project_back(grad, weight):
    return lax.dot_general(
        grad, weight, (((1,), (1,)), ((), ())), preferred_element_type=jnp.float32
    )


def weight_grad(left, right):
    return lax.dot_general(
        left, right, (((0,), (0,)), ((), ())), preferred_element_type=jnp.float32
    )


def split_heads(values, group):
    return values.reshape(values.shape[:2] + (-1, group, HEAD_DIM))


def split_shared(values):
    return values.reshape(values.shape[:2] + (-1, HEAD_DIM))


def causal_masks(table, length, group):

    def masks(start, block):
        stop = start + block
        rows = start + jnp.arange(block, dtype=jnp.int32)
        columns = jnp.arange(stop, dtype=jnp.int32)
        distance = rows[:, None] - columns[None, :]
        keep = (distance >= 0) & (columns[None, :] < length)
        extra = jnp.take(table, jnp.maximum(distance, 0), axis=1)
        return (extra.reshape((-1, group, block, stop)), keep, stop)

    return masks


def memory_masks(length, width):

    def masks(start, block):
        keep = jnp.broadcast_to(
            jnp.arange(width, dtype=jnp.int32)[None, :] < length, (block, width)
        )
        return (None, keep, width)

    return masks


def diagonal_sums(grads, block, stop):
    leading = grads.shape[:2]
    flipped = jnp.pad(grads[..., ::-1], ((0, 0), (0, 0), (0, 0), (0, block)))
    skewed = flipped.reshape(leading + (block * (stop + block),))[..., : block * (stop + block - 1)]
    skewed = skewed.reshape(leading + (block, stop + block - 1))
    return jnp.sum(skewed, axis=2)[..., block - 1 :]


def attend_forward(queries, keys, values, masks):
    block = min(512, queries.shape[0])
    outputs = []
    totals = []
    for index in range(queries.shape[0] // block):
        start = index * block
        extra, keep, stop = masks(start, block)
        rows = queries[start : start + block]
        scores = jnp.einsum("rkgd,skd->kgrs", rows, keys[:stop], preferred_element_type=jnp.float32)
        if extra is not None:
            scores = scores + extra
        scores = jnp.where(keep, scores, NEG)
        peak = jnp.max(scores, axis=-1, keepdims=True)
        weights = jnp.where(keep, jnp.exp(scores - peak), 0.0)
        total = jnp.sum(weights, axis=-1, keepdims=True)
        probs = (weights / total).astype(jnp.bfloat16)
        mixed = jnp.einsum(
            "kgrs,skd->rkgd", probs, values[:stop], preferred_element_type=jnp.float32
        )
        outputs.append(mixed.astype(jnp.bfloat16))
        totals.append(peak + jnp.log(total))
    return (jnp.concatenate(outputs, 0), jnp.concatenate(totals, 2))


def attend_backward(queries, keys, values, sums, grads, masks):
    block = min(512, queries.shape[0])
    key_grads = jnp.zeros(keys.shape, jnp.float32)
    value_grads = jnp.zeros(values.shape, jnp.float32)
    diagonal = jnp.zeros(sums.shape[:3], jnp.float32)
    query_grads = []
    for index in range(queries.shape[0] // block):
        start = index * block
        extra, keep, stop = masks(start, block)
        rows = queries[start : start + block]
        grad_rows = grads[start : start + block]
        scores = jnp.einsum("rkgd,skd->kgrs", rows, keys[:stop], preferred_element_type=jnp.float32)
        if extra is not None:
            scores = scores + extra
        scores = jnp.where(keep, scores, NEG)
        probs = jnp.where(keep, jnp.exp(scores - sums[:, :, start : start + block]), 0.0)
        value_grads = value_grads.at[:stop].add(
            jnp.einsum(
                "kgrs,rkgd->skd",
                probs.astype(jnp.bfloat16),
                grad_rows,
                preferred_element_type=jnp.float32,
            )
        )
        dprobs = jnp.einsum(
            "rkgd,skd->kgrs", grad_rows, values[:stop], preferred_element_type=jnp.float32
        )
        delta = jnp.sum(probs * dprobs, axis=-1, keepdims=True)
        dscores = (probs * (dprobs - delta)).astype(jnp.bfloat16)
        query_grads.append(
            jnp.einsum(
                "kgrs,skd->rkgd", dscores, keys[:stop], preferred_element_type=jnp.float32
            ).astype(jnp.bfloat16)
        )
        key_grads = key_grads.at[:stop].add(
            jnp.einsum("kgrs,rkgd->skd", dscores, rows, preferred_element_type=jnp.float32)
        )
        if extra is not None:
            diagonal = diagonal.at[:, :, :stop].add(
                diagonal_sums(dscores.astype(jnp.float32), block, stop)
            )
    return (
        jnp.concatenate(query_grads, 0),
        key_grads.astype(jnp.bfloat16),
        value_grads.astype(jnp.bfloat16),
        diagonal,
    )


def self_forward(queries, keys, values, length, table):
    return attend_forward(queries, keys, values, causal_masks(table, length, queries.shape[2]))


def self_backward(queries, keys, values, sums, grads, length, table):
    return attend_backward(
        queries, keys, values, sums, grads, causal_masks(table, length, queries.shape[2])
    )


def cross_forward(queries, keys, values, length):
    return attend_forward(queries, keys, values, memory_masks(length, keys.shape[0]))


def cross_backward(queries, keys, values, sums, grads, length):
    return attend_backward(queries, keys, values, sums, grads, memory_masks(length, keys.shape[0]))


def to_tokens(values):
    return lax.all_to_all(shortened(values), "seq", split_axis=1, concat_axis=2, tiled=True).astype(
        values.dtype
    )


def to_heads(grads):
    return lax.all_to_all(grads, "seq", split_axis=2, concat_axis=1, tiled=True)


def per_device(
    layer_input,
    memory,
    target_lengths,
    memory_lengths,
    buckets,
    norm_self,
    self_q,
    self_k,
    self_v,
    self_out,
    rel_bias,
    norm_cross,
    cross_q,
    cross_k,
    cross_v,
    cross_out,
    norm_ff,
    ff_gate,
    ff_up,
    ff_down,
    cotangent,
):
    micro_count, batch_rows, local_tokens, model_width = layer_input.shape
    memory_tokens = memory.shape[2]
    group = HEADS // KV_HEADS
    replicas = lax.axis_size("dp")
    shards = (
        norm_self,
        self_q,
        self_k,
        self_v,
        self_out,
        rel_bias,
        norm_cross,
        cross_q,
        cross_k,
        cross_v,
        cross_out,
        norm_ff,
        ff_gate,
        ff_up,
        ff_down,
    )
    totals = [
        jnp.zeros((piece.shape[0] * replicas,) + piece.shape[1:], jnp.float32) for piece in shards
    ]
    onehot = (buckets[:, None] == jnp.arange(BUCKETS, dtype=jnp.int32)[None, :]).astype(jnp.float32)
    places = lax.axis_index("seq") * local_tokens + jnp.arange(local_tokens, dtype=jnp.int32)
    diagonal = jnp.zeros((rel_bias.shape[1] // group, group, TGT), jnp.float32)
    outputs = []
    input_grads = []
    memory_grads = []
    for micro_step in range(micro_count):
        gathered = (
            lax.all_gather(norm_self, "dp", axis=0, tiled=True),
            lax.all_gather(self_q, "dp", axis=0, tiled=True),
            lax.all_gather(self_k, "dp", axis=0, tiled=True),
            lax.all_gather(self_v, "dp", axis=0, tiled=True),
            lax.all_gather(self_out, "dp", axis=0, tiled=True),
            lax.all_gather(rel_bias, "dp", axis=0, tiled=True),
            lax.all_gather(norm_cross, "dp", axis=0, tiled=True),
            lax.all_gather(cross_q, "dp", axis=0, tiled=True),
            lax.all_gather(cross_k, "dp", axis=0, tiled=True),
            lax.all_gather(cross_v, "dp", axis=0, tiled=True),
            lax.all_gather(cross_out, "dp", axis=0, tiled=True),
            lax.all_gather(norm_ff, "dp", axis=0, tiled=True),
            lax.all_gather(ff_gate, "dp", axis=0, tiled=True),
            lax.all_gather(ff_up, "dp", axis=0, tiled=True),
            lax.all_gather(ff_down, "dp", axis=0, tiled=True),
        )
        (
            gain_self,
            query_self,
            key_self,
            value_self,
            output_self,
            bias_whole,
            gain_cross,
            query_cross,
            key_cross,
            value_cross,
            output_cross,
            gain_ff,
            gate_weight,
            up_weight,
            down_weight,
        ) = gathered
        gain_self = gain_self.astype(jnp.float32)
        gain_cross = gain_cross.astype(jnp.float32)
        gain_ff = gain_ff.astype(jnp.float32)
        table = lax.dot_general(
            bias_whole.astype(jnp.float32), onehot, (((0,), (1,)), ((), ())), precision=HIGH
        )
        lengths = target_lengths[micro_step]
        spans = memory_lengths[micro_step]
        valid = (places[None, :] < lengths[:, None]).astype(jnp.float32).reshape(-1, 1)
        hidden = layer_input[micro_step].reshape(-1, model_width).astype(jnp.float32)
        normed_self = rms_norm(hidden, gain_self).astype(jnp.bfloat16)
        queries = (
            project(normed_self, query_self)
            .astype(jnp.bfloat16)
            .reshape(batch_rows, local_tokens, -1)
        )
        keys = (
            project(normed_self, key_self)
            .astype(jnp.bfloat16)
            .reshape(batch_rows, local_tokens, -1)
        )
        values = (
            project(normed_self, value_self)
            .astype(jnp.bfloat16)
            .reshape(batch_rows, local_tokens, -1)
        )
        encoded = memory[micro_step].reshape(-1, model_width)
        memory_keys = (
            project(encoded, key_cross).astype(jnp.bfloat16).reshape(batch_rows, memory_tokens, -1)
        )
        memory_values = (
            project(encoded, value_cross)
            .astype(jnp.bfloat16)
            .reshape(batch_rows, memory_tokens, -1)
        )
        head_queries, head_keys, head_values, far_keys, far_values = (
            lax.all_to_all(queries, "seq", split_axis=2, concat_axis=1, tiled=True),
            lax.all_to_all(keys, "seq", split_axis=2, concat_axis=1, tiled=True),
            lax.all_to_all(values, "seq", split_axis=2, concat_axis=1, tiled=True),
            lax.all_to_all(memory_keys, "seq", split_axis=2, concat_axis=1, tiled=True),
            lax.all_to_all(memory_values, "seq", split_axis=2, concat_axis=1, tiled=True),
        )
        self_queries = split_heads(head_queries, group)
        self_keys = split_shared(head_keys)
        self_values = split_shared(head_values)
        far_keys = split_shared(far_keys)
        far_values = split_shared(far_values)
        attended, self_sums = jax.vmap(self_forward, in_axes=(0, 0, 0, 0, None))(
            self_queries, self_keys, self_values, lengths, table
        )
        context = to_tokens(attended.reshape(batch_rows, TGT, -1)).reshape(
            batch_rows * local_tokens, -1
        )
        first = hidden + project(context, output_self)
        normed_cross = rms_norm(first, gain_cross).astype(jnp.bfloat16)
        cross_queries = (
            project(normed_cross, query_cross)
            .astype(jnp.bfloat16)
            .reshape(batch_rows, local_tokens, -1)
        )
        cross_heads = split_heads(
            lax.all_to_all(cross_queries, "seq", split_axis=2, concat_axis=1, tiled=True), group
        )
        cross_attended, cross_sums = jax.vmap(cross_forward)(
            cross_heads, far_keys, far_values, spans
        )
        cross_context = to_tokens(cross_attended.reshape(batch_rows, TGT, -1)).reshape(
            batch_rows * local_tokens, -1
        )
        second = first + project(cross_context, output_cross)
        normed_ff = rms_norm(second, gain_ff).astype(jnp.bfloat16)
        gate = project(normed_ff, gate_weight)
        upward = project(normed_ff, up_weight)
        middle = gated(gate, upward).astype(jnp.bfloat16)
        third = second + project(middle, down_weight)
        outputs.append(
            (third * valid).astype(jnp.bfloat16).reshape(batch_rows, local_tokens, model_width)
        )
        upstream = cotangent[micro_step].reshape(-1, model_width).astype(jnp.float32) * valid
        down_grad = upstream.astype(jnp.bfloat16)
        totals[14] = totals[14] + weight_grad(middle, down_grad)
        _, pullback = jax.vjp(gated, gate, upward)
        gate_grad, upward_grad = pullback(project_back(down_grad, down_weight))
        gate_grad = gate_grad.astype(jnp.bfloat16)
        upward_grad = upward_grad.astype(jnp.bfloat16)
        totals[12] = totals[12] + weight_grad(normed_ff, gate_grad)
        totals[13] = totals[13] + weight_grad(normed_ff, upward_grad)
        _, pullback = jax.vjp(rms_norm, second, gain_ff)
        second_grad, gain_grad = pullback(
            project_back(gate_grad, gate_weight) + project_back(upward_grad, up_weight)
        )
        totals[11] = totals[11] + gain_grad
        second_grad = second_grad + upstream
        cross_grad = second_grad.astype(jnp.bfloat16)
        totals[10] = totals[10] + weight_grad(cross_context, cross_grad)
        context_grad = (
            project_back(cross_grad, output_cross)
            .astype(jnp.bfloat16)
            .reshape(batch_rows, local_tokens, -1)
        )
        cross_query_grad, far_key_grad, far_value_grad, _ = jax.vmap(cross_backward)(
            cross_heads,
            far_keys,
            far_values,
            cross_sums,
            split_heads(to_heads(context_grad), group),
            spans,
        )
        query_back, key_back, value_back = (
            lax.all_to_all(
                shortened(cross_query_grad.reshape(batch_rows, TGT, -1)),
                "seq",
                split_axis=1,
                concat_axis=2,
                tiled=True,
            ),
            lax.all_to_all(
                shortened(far_key_grad.reshape(batch_rows, MEM, -1)),
                "seq",
                split_axis=1,
                concat_axis=2,
                tiled=True,
            ),
            lax.all_to_all(
                shortened(far_value_grad.reshape(batch_rows, MEM, -1)),
                "seq",
                split_axis=1,
                concat_axis=2,
                tiled=True,
            ),
        )
        query_back = query_back.reshape(batch_rows * local_tokens, -1)
        key_back = key_back.reshape(batch_rows * memory_tokens, -1)
        value_back = value_back.reshape(batch_rows * memory_tokens, -1)
        totals[7] = totals[7] + weight_grad(normed_cross, query_back)
        totals[8] = totals[8] + weight_grad(encoded, key_back)
        totals[9] = totals[9] + weight_grad(encoded, value_back)
        memory_grads.append(
            (project_back(key_back, key_cross) + project_back(value_back, value_cross)).reshape(
                batch_rows, memory_tokens, model_width
            )
        )
        _, pullback = jax.vjp(rms_norm, first, gain_cross)
        first_grad, gain_grad = pullback(project_back(query_back, query_cross))
        totals[6] = totals[6] + gain_grad
        first_grad = first_grad + second_grad
        self_grad = first_grad.astype(jnp.bfloat16)
        totals[4] = totals[4] + weight_grad(context, self_grad)
        context_grad = (
            project_back(self_grad, output_self)
            .astype(jnp.bfloat16)
            .reshape(batch_rows, local_tokens, -1)
        )
        query_grad, key_grad, value_grad, bias_grad = jax.vmap(
            self_backward, in_axes=(0, 0, 0, 0, 0, 0, None)
        )(
            self_queries,
            self_keys,
            self_values,
            self_sums,
            split_heads(to_heads(context_grad), group),
            lengths,
            table,
        )
        diagonal = diagonal + jnp.sum(bias_grad, axis=0)
        query_back, key_back, value_back = (
            lax.all_to_all(
                shortened(query_grad.reshape(batch_rows, TGT, -1)),
                "seq",
                split_axis=1,
                concat_axis=2,
                tiled=True,
            ),
            lax.all_to_all(
                shortened(key_grad.reshape(batch_rows, TGT, -1)),
                "seq",
                split_axis=1,
                concat_axis=2,
                tiled=True,
            ),
            lax.all_to_all(
                shortened(value_grad.reshape(batch_rows, TGT, -1)),
                "seq",
                split_axis=1,
                concat_axis=2,
                tiled=True,
            ),
        )
        query_back = query_back.reshape(batch_rows * local_tokens, -1)
        key_back = key_back.reshape(batch_rows * local_tokens, -1)
        value_back = value_back.reshape(batch_rows * local_tokens, -1)
        totals[1] = totals[1] + weight_grad(normed_self, query_back)
        totals[2] = totals[2] + weight_grad(normed_self, key_back)
        totals[3] = totals[3] + weight_grad(normed_self, value_back)
        _, pullback = jax.vjp(rms_norm, hidden, gain_self)
        hidden_grad, gain_grad = pullback(
            project_back(query_back, query_self)
            + project_back(key_back, key_self)
            + project_back(value_back, value_self)
        )
        totals[0] = totals[0] + gain_grad
        input_grads.append(
            (hidden_grad + first_grad).reshape(batch_rows, local_tokens, model_width)
        )
    totals[5] = lax.dot_general(
        onehot, diagonal.reshape(-1, TGT), (((0,), (1,)), ((), ())), precision=HIGH
    )
    reduced = (
        lax.psum_scatter(totals[0], ("dp", "seq"), scatter_dimension=0, tiled=True),
        lax.psum_scatter(totals[1], ("dp", "seq"), scatter_dimension=0, tiled=True),
        lax.psum_scatter(totals[2], ("dp", "seq"), scatter_dimension=0, tiled=True),
        lax.psum_scatter(totals[3], ("dp", "seq"), scatter_dimension=0, tiled=True),
        lax.psum_scatter(totals[4], ("dp", "seq"), scatter_dimension=0, tiled=True),
        lax.psum_scatter(totals[6], ("dp", "seq"), scatter_dimension=0, tiled=True),
        lax.psum_scatter(totals[7], ("dp", "seq"), scatter_dimension=0, tiled=True),
        lax.psum_scatter(totals[8], ("dp", "seq"), scatter_dimension=0, tiled=True),
        lax.psum_scatter(totals[9], ("dp", "seq"), scatter_dimension=0, tiled=True),
        lax.psum_scatter(totals[10], ("dp", "seq"), scatter_dimension=0, tiled=True),
        lax.psum_scatter(totals[11], ("dp", "seq"), scatter_dimension=0, tiled=True),
        lax.psum_scatter(totals[12], ("dp", "seq"), scatter_dimension=0, tiled=True),
        lax.psum_scatter(totals[13], ("dp", "seq"), scatter_dimension=0, tiled=True),
        lax.psum_scatter(totals[14], ("dp", "seq"), scatter_dimension=0, tiled=True),
    )
    bias_share = lax.psum_scatter(totals[5], "dp", scatter_dimension=0, tiled=True)
    return (
        jnp.stack(outputs),
        jnp.stack(input_grads),
        jnp.stack(memory_grads),
        reduced[0],
        reduced[1],
        reduced[2],
        reduced[3],
        reduced[4],
        bias_share,
        reduced[5],
        reduced[6],
        reduced[7],
        reduced[8],
        reduced[9],
        reduced[10],
        reduced[11],
        reduced[12],
        reduced[13],
    )


def solution(mesh):
    placed = (
        P(None, "dp", "seq", None),
        P(None, "dp", "seq", None),
        P(None, "dp"),
        P(None, "dp"),
        P(),
        P("dp"),
        P("dp", None),
        P("dp", None),
        P("dp", None),
        P("dp", None),
        P("dp", "seq"),
        P("dp"),
        P("dp", None),
        P("dp", None),
        P("dp", None),
        P("dp", None),
        P("dp"),
        P("dp", None),
        P("dp", None),
        P("dp", None),
        P(None, "dp", "seq", None),
    )
    return jax.shard_map(
        per_device,
        mesh=mesh,
        in_specs=placed,
        out_specs=(
            P(None, "dp", "seq", None),
            P(None, "dp", "seq", None),
            P(None, "dp", "seq", None),
            P(("dp", "seq")),
            P(("dp", "seq"), None),
            P(("dp", "seq"), None),
            P(("dp", "seq"), None),
            P(("dp", "seq"), None),
            P("dp", "seq"),
            P(("dp", "seq")),
            P(("dp", "seq"), None),
            P(("dp", "seq"), None),
            P(("dp", "seq"), None),
            P(("dp", "seq"), None),
            P(("dp", "seq")),
            P(("dp", "seq"), None),
            P(("dp", "seq"), None),
            P(("dp", "seq"), None),
        ),
        check_vma=False,
    )
```

profile of v0, /device:TPU:0, one launch (start us, length us, event | category | flops | bytes accessed | tf_op | source)
XLA Modules:
  0.0 5273.5 jit_solution(3347054849078159239)
XLA Ops:
  20.9 13.5 all-gather.1
  36.0 1730.6 %gather_fusion.1 = f32[524288,4]{1,0:T(8,128)} fusion(f32[4,1024]{0,1:T(8,128)S(1)} %copy.390, s32[524288]{0:T(1024)S(1)} %broadcast_clamp_fusion), kind=kCustom, calls=%fused_computation.1.clone | custom fusion | bytes 18874368 | tf_op jit(solution)/shard_map/vmap(jit(_take))/gather | solution.py:63
  1766.6 141.8 %copy.398 = f32[512,1024,4]{0,1,2:T(8,128)} copy(f32[512,1024,4]{2,1,0:T(8,128)} %bitcast.33) | data formatting | bytes 16777216 | tf_op jit(solution)/shard_map/vmap(jit(_take))/gather | solution.py:63
  1913.4 8.7 all-gather
  1922.5 865.7 %gather_fusion = f32[262144,4]{1,0:T(8,128)} fusion(f32[4,1024]{0,1:T(8,128)S(1)} %copy.390, s32[262144]{0:T(1024)S(1)} %broadcast_clamp_fusion.1), kind=kCustom, calls=%fused_computation.clone | custom fusion | bytes 9437184 | tf_op jit(solution)/shard_map/vmap(jit(_take))/gather | solution.py:63
  2788.2 71.7 %copy.391 = f32[512,512,4]{0,1,2:T(8,128)} copy(f32[512,512,4]{2,1,0:T(8,128)} %bitcast.22) | data formatting | bytes 8388608 | tf_op jit(solution)/shard_map/vmap(jit(_take))/gather | solution.py:63
  2864.3 8.1 broadcast_select_fusion
  2953.2 14.2 all-to-all-start
  2983.8 10.0 all-gather.2
  2998.7 8.8 all-gather.3
  3216.9 6.1 fusion.499
  3222.9 5.8 fusion.500
  3228.8 9.3 multiply_convert_fusion.1
  3254.8 7.9 multiply_convert_fusion
  3578.8 5.7 fusion.204
  3669.3 5.6 reduce.93
  3707.1 6.0 convolution_add_fusion.2
  3716.5 5.9 convolution_add_fusion.1
  3726.9 6.0 convolution_add_fusion
  3748.5 61.2 %rev.15 = f32[1,2,2,512,1024]{3,4,2,1,0:T(8,128)} reverse(bf16[1,2,2,512,1024]{3,4,2,1,0:T(8,128)(2,1)} %copy-done.6), dimensions={4} | reverse | bytes 12582912 | tf_op jit(solution)/shard_map/vmap()/rev | solution.py:82
  3809.7 60.8 %rev.13 = f32[1,2,2,512,1024]{3,4,2,1,0:T(8,128)} reverse(bf16[1,2,2,512,1024]{3,4,2,1,0:T(8,128)(2,1)} %copy-done.7), dimensions={4} | reverse | bytes 12582912 | tf_op jit(solution)/shard_map/vmap()/rev | solution.py:82
  3870.5 21.0 rev.14
  3891.5 30.9 rev.12
  3922.4 8.7 copy.598
  3931.1 9.8 pad.77.clone
  3940.9 21.6 reshape.2103
  3962.5 9.9 slice.688
  3972.4 26.1 reshape.2104
  4003.9 8.8 copy.596
  4012.6 9.8 pad.75.clone
  4022.4 22.1 reshape.2099
  4044.5 10.0 slice.684
  4054.5 26.0 reshape.2100
  4091.1 6.7 pad.76.clone
  4097.9 11.6 reshape.2101
  4109.4 7.3 slice.686
  4116.7 14.9 reshape.2102
  4141.0 6.8 pad.74.clone
  4147.8 11.6 reshape.2097
  4159.4 7.3 slice.682
  4166.7 14.9 reshape.2098
  4186.6 26.8 all-reduce.11
  4219.3 37.3 all-reduce.14
  4262.2 105.8 %reduce-scatter.24.cloned.1.call-done = f32[32,1024]{1,0:T(8,128)} async-done(((f32[1024,1024]{1,0:T(8,128)}), f32[32,1024]{1,0:T(8,128)}) %reduce-scatter.24.cloned.1.call-update) | async-done | bytes 131088 | tf_op jit(solution)/shard_map/reduce_scatter | solution.py:491
  4367.9 143.5 %reduce-scatter.16.cloned.1.call-done = f32[32,1024]{1,0:T(8,128)} async-done(((f32[1024,1024]{1,0:T(8,128)}), f32[32,1024]{1,0:T(8,128)}) %reduce-scatter.16.cloned.1.call-update) | async-done | bytes 131088 | tf_op jit(solution)/shard_map/reduce_scatter | solution.py:486
  4511.5 249.1 %reduce-scatter.28.cloned.1.call-done = f32[32,2816]{1,0:T(8,128)} async-done(((f32[1024,2816]{1,0:T(8,128)}), f32[32,2816]{1,0:T(8,128)}) %reduce-scatter.28.cloned.1.call-update) | async-done | bytes 360464 | tf_op jit(solution)/shard_map/reduce_scatter | solution.py:496
  4760.6 252.8 %reduce-scatter.30.cloned.1.call-done = f32[32,2816]{1,0:T(8,128)} async-done(((f32[1024,2816]{1,0:T(8,128)}), f32[32,2816]{1,0:T(8,128)}) %reduce-scatter.30.cloned.1.call-update) | async-done | bytes 360464 | tf_op jit(solution)/shard_map/reduce_scatter | solution.py:497
  5013.4 252.8 %reduce-scatter.32.cloned.1.call-done = f32[88,1024]{1,0:T(8,128)} async-done(((f32[2816,1024]{1,0:T(8,128)}), f32[88,1024]{1,0:T(8,128)}) %reduce-scatter.32.cloned.1.call-update) | async-done | bytes 360464 | tf_op jit(solution)/shard_map/reduce_scatter | solution.py:498
  (1003 shorter events, 846.6 us)
Async XLA Ops:
  7.2 2867.9 %all-gather.26.cloned.1.call-start = ((), (), s32[]{:S(2)}) async-start(), calls=%async_computation.48 | async-start | bytes 1179648 | tf_op jit(solution)/shard_map/all_gather | solution.py:252
  8.0 2875.1 %all-gather.24.cloned.1.call-start = ((), (), s32[]{:S(2)}) async-start(), calls=%async_computation.47 | async-start | bytes 1179648 | tf_op jit(solution)/shard_map/all_gather | solution.py:253
  8.7 2906.0 %all-gather.18.cloned.1.call-start = ((), (), s32[]{:S(2)}) async-start(), calls=%async_computation.44 | async-start | bytes 1179648 | tf_op jit(solution)/shard_map/all_gather | solution.py:246
  9.4 2916.2 %all-gather.16.cloned.1.call-start = ((), (), s32[]{:S(2)}) async-start(), calls=%async_computation.43 | async-start | bytes 1179648 | tf_op jit(solution)/shard_map/all_gather | solution.py:247
  10.0 2957.4 %all-gather.20.cloned.1.call-start = ((), (), s32[]{:S(2)}) async-start(), calls=%async_computation.45 | async-start | bytes 2359296 | tf_op jit(solution)/shard_map/all_gather | solution.py:245
  10.6 3098.6 %all-gather.22.cloned.1.call-start = ((), (), s32[]{:S(2)}) async-start(), calls=%async_computation.46 | async-start | bytes 2359296 | tf_op jit(solution)/shard_map/all_gather | solution.py:248
  11.2 3100.7 %all-gather.28.cloned.1.call-start = ((), (), s32[]{:S(2)}) async-start(), calls=%async_computation.49 | async-start | bytes 2359296 | tf_op jit(solution)/shard_map/all_gather | solution.py:251
  11.9 3199.2 %all-gather.30.cloned.1.call-start = ((), (), s32[]{:S(2)}) async-start(), calls=%async_computation.50 | async-start | bytes 2359296 | tf_op jit(solution)/shard_map/all_gather | solution.py:254
  12.7 3204.2 %all-gather.32.cloned.1.call-start = ((), (), s32[]{:S(2)}) async-start(), calls=%async_computation.51 | async-start | bytes 6488064 | tf_op jit(solution)/shard_map/all_gather | solution.py:256
  13.4 3209.5 %all-gather.34.cloned.1.call-start = ((), (), s32[]{:S(2)}) async-start(), calls=%async_computation.52 | async-start | bytes 6488064 | tf_op jit(solution)/shard_map/all_gather | solution.py:257
  14.0 3214.8 %all-gather.36.cloned.1.call-start = ((), (), s32[]{:S(2)}) async-start(), calls=%async_computation.53 | async-start | bytes 6488064 | tf_op jit(solution)/shard_map/all_gather | solution.py:258
  2890.1 11.4 all-to-all-start.12
  2910.7 10.8 all-to-all-start.4
  2921.5 12.5 all-to-all-start.9
  2953.2 26.5 all-to-all-start
  2979.7 56.9 %all-to-all-start.10 = ((bf16[4,2,32768]{2,1,0:T(2,128)(2,1)}), bf16[4,2,32768]{2,1,0:T(2,128)(2,1)}, u32[]{:S(2)}, u32[]{:S(2)}) async-start(bf16[4,2,32768]{2,1,0:T(2,128)(2,1)} %reshape.2213), calls=%async_computation.10 | async-start | bytes 1048576 | tf_op jit(solution)/shard_map/all_to_all | solution.py:313
  3036.6 34.1 all-to-all-start.2
  3070.7 29.6 all-to-all-start.11
  3100.4 23.8 all-to-all-start.3
  3124.2 17.6 all-to-all-start.14
  3141.9 24.6 all-to-all-start.6
  3167.3 24.4 all-to-all-start.15
  3191.7 11.5 all-to-all-start.7
  3281.6 15.5 all-to-all-start.22
  3297.1 16.7 all-to-all-start.16
  3342.2 22.6 all-to-all-start.30
  3364.8 17.4 all-to-all-start.28
  3382.2 24.9 all-to-all-start.31
  3386.4 875.7 %reduce-scatter.34.cloned.1.call-start = ((), (), s32[]{:S(2)}) async-start(), calls=%async_computation.63 | async-start | bytes 2162688
  3407.1 13.4 all-to-all-start.29
  3421.1 20.3 all-to-all-start.23
  3441.5 16.8 all-to-all-start.17
  3480.5 18.9 all-to-all-start.24
  3484.7 777.4 %reduce-scatter.36.cloned.1.call-start = ((), (), s32[]{:S(2)}) async-start(), calls=%async_computation.64 | async-start | bytes 2162688
  3499.4 25.5 all-to-all-start.18
  3524.8 30.7 all-to-all-start.26
  3559.7 702.4 %reduce-scatter.18.cloned.1.call-start = ((), (), s32[]{:S(2)}) async-start(), calls=%async_computation.55 | async-start | bytes 2162688 | tf_op jit(solution)/shard_map/reduce_scatter | solution.py:487
  3590.5 15.6 all-to-all-start.27
  3610.2 651.9 %reduce-scatter.20.cloned.1.call-start = ((), (), s32[]{:S(2)}) async-start(), calls=%async_computation.56 | async-start | bytes 2162688 | tf_op jit(solution)/shard_map/reduce_scatter | solution.py:488
  3619.4 642.7 %reduce-scatter.26.cloned.1.call-start = ((), (), s32[]{:S(2)}) async-start(), calls=%async_computation.59 | async-start | bytes 4325376 | tf_op jit(solution)/shard_map/reduce_scatter | solution.py:494
  3625.7 636.5 %reduce-scatter.22.cloned.1.call-start = ((), (), s32[]{:S(2)}) async-start(), calls=%async_computation.57 | async-start | bytes 4325376 | tf_op jit(solution)/shard_map/reduce_scatter | solution.py:489
  3632.7 735.2 %reduce-scatter.24.cloned.1.call-start = ((), (), s32[]{:S(2)}) async-start(), calls=%async_computation.58 | async-start | bytes 4325376 | tf_op jit(solution)/shard_map/reduce_scatter | solution.py:491
  3656.7 20.2 all-to-all-start.25
  3676.9 13.3 all-to-all-start.19
  3681.0 830.4 %reduce-scatter.16.cloned.1.call-start = ((), (), s32[]{:S(2)}) async-start(), calls=%async_computation.54 | async-start | bytes 4325376 | tf_op jit(solution)/shard_map/reduce_scatter | solution.py:486
  3702.8 1057.7 %reduce-scatter.28.cloned.1.call-start = ((), (), s32[]{:S(2)}) async-start(), calls=%async_computation.60 | async-start | bytes 11894784 | tf_op jit(solution)/shard_map/reduce_scatter | solution.py:496
  3713.0 1300.3 %reduce-scatter.30.cloned.1.call-start = ((), (), s32[]{:S(2)}) async-start(), calls=%async_computation.61 | async-start | bytes 11894784 | tf_op jit(solution)/shard_map/reduce_scatter | solution.py:497
  3722.4 1543.8 %reduce-scatter.32.cloned.1.call-start = ((), (), s32[]{:S(2)}) async-start(), calls=%async_computation.62 | async-start | bytes 11894784 | tf_op jit(solution)/shard_map/reduce_scatter | solution.py:498
  (236 other events, 6170.7 us)
Sparse Core Ops, SparseCore 0:
  9.7 24.8 all-gather.25
  36.1 21.7 all-gather.23
  59.5 21.7 all-gather.17
  82.7 21.7 all-gather.15
  105.9 28.7 all-gather.19
  136.2 28.5 all-gather.21
  166.4 28.5 all-gather.27
  196.6 28.5 all-gather.29
  226.9 59.9 all-gather.31
  288.3 59.0 all-gather.33
  349.1 59.0 all-gather.35
  3397.5 137.7 reduce-scatter.33
  3538.2 133.5 reduce-scatter.35
  3674.5 133.1 reduce-scatter.17
  3810.4 133.3 reduce-scatter.19
  3946.5 137.3 reduce-scatter.25
  4086.7 139.4 reduce-scatter.21
  4228.9 139.0 reduce-scatter.23
  4370.8 140.6 reduce-scatter.15
  4514.2 246.3 reduce-scatter.27
  4763.5 249.8 reduce-scatter.29
  5016.2 249.8 reduce-scatter.31
where the time goes:
time: 5310 us; the launch traced here: 5270 us
  local copies, waits for them, and re-layouts  3490 us (66%)
  waiting for transfers between devices  1020 us (19%)
  matrix products  294 us (6%)
  other arithmetic  199 us (4%)
  starting transfers between devices  147 us (3%)
  blocking collectives  105 us (2%)
    gather x4, local copies, waits for them, and re-layouts, masks(): extra = jnp.take(table, jnp.maximum(distance, 0), axis=1)  2810 us
    reduce_scatter x1, waiting for transfers between devices, per_device(): lax.psum_scatter(totals[14], ('dp', 'seq'), scatter_dimension=0, tiled=True)  253 us
    reduce_scatter x1, waiting for transfers between devices, per_device(): lax.psum_scatter(totals[13], ('dp', 'seq'), scatter_dimension=0, tiled=True)  253 us
    reduce_scatter x1, waiting for transfers between devices, per_device(): lax.psum_scatter(totals[12], ('dp', 'seq'), scatter_dimension=0, tiled=True)  249 us
    unnamed x570, local copies, waits for them, and re-layouts  190 us
    rev x4, local copies, waits for them, and re-layouts, diagonal_sums(): flipped = jnp.pad(grads[..., ::-1], ((0, 0), (0, 0), (0, 0), (0, block)))  174 us
    reduce_scatter x1, waiting for transfers between devices, per_device(): lax.psum_scatter(totals[1], ('dp', 'seq'), scatter_dimension=0, tiled=True)  144 us
    unnamed x36, other arithmetic  109 us
  transfers between devices with their start and end apart: 54, of which 11 were waited for; matrix products, arithmetic and copies ran while one was open for 74% of the time, Pallas kernels for 0%

commit v1 on v0

--- a/solution.py
+++ b/solution.py
@@ -1,6 +1,10 @@
+import functools
+
 import jax
 import jax.numpy as jnp
 from jax import lax
+from jax.experimental import pallas as pl
+from jax.experimental.pallas import tpu as pltpu
 from jax.sharding import PartitionSpec as P
 
 HEADS = 16
@@ -9,6 +13,7 @@
 KV_HEADS = 8
 TGT = 1024
 MEM = 512
+QB = 256
 
 
 EPS = 1e-06
@@ -520,6 +525,595 @@
     )
 
 
+def row_pieces(full):
+    blocks = full.reshape(full.shape[0], -1, QB)
+    return jnp.concatenate([blocks[:, 1:], blocks[:, :-1]], axis=2)
+
+
+def seed_rows(vectors):
+    return jnp.stack([jnp.roll(vectors, r, axis=-1) for r in range(8)], axis=-2)
+
+
+def spread(seed):
+    rows = 8
+    tile = seed
+    while rows < QB:
+        tile = jnp.concatenate([tile, pltpu.roll(tile, rows, 1)], axis=0)
+        rows *= 2
+    return tile[:, :QB]
+
+
+def fold(tile):
+    width = 2 * QB
+    tile = jnp.concatenate([tile, jnp.zeros_like(tile)], axis=1)
+    rows = QB
+    while rows > 8:
+        rows //= 2
+        tile = tile[:rows] + pltpu.roll(tile[rows:], width - rows, 1)
+    return tile
+
+
+def nt(left, right):
+    return lax.dot_general(left, right, (((1,), (1,)), ((), ())), preferred_element_type=jnp.float32)
+
+
+def tn(left, right):
+    return lax.dot_general(left, right, (((0,), (0,)), ((), ())), preferred_element_type=jnp.float32)
+
+
+def nn(left, right):
+    return lax.dot_general(left, right, (((1,), (0,)), ((), ())), preferred_element_type=jnp.float32)
+
+
+def forward_kernel(causal, q_ref, k_ref, v_ref, keep_ref, *rest):
+    if causal:
+        seed_ref, o_ref, lse_ref, bias = rest
+    else:
+        o_ref, lse_ref = rest
+    span = k_ref.shape[0]
+    for kv in range(2):
+        lanes = slice(kv * HEAD_DIM, (kv + 1) * HEAD_DIM)
+        keys = k_ref[:, lanes]
+        values = v_ref[:, lanes]
+        if causal:
+            for member in range(2):
+                for offset in range(4):
+                    bias[member * QB : (member + 1) * QB, (3 - offset) * QB : (4 - offset) * QB] = spread(
+                        seed_ref[2 * kv + member, offset]
+                    )
+        for block in range(q_ref.shape[0] // QB):
+            stop = (block + 1) * QB if causal else span
+            rows = slice(block * QB, (block + 1) * QB)
+            both = q_ref[rows, 2 * kv * HEAD_DIM : 2 * (kv + 1) * HEAD_DIM]
+            query = jnp.concatenate([both[:, :HEAD_DIM], both[:, HEAD_DIM:]], axis=0)
+            scores = nt(query, keys[:stop]) + keep_ref[:, :stop]
+            if causal:
+                scores = scores + bias[:, (3 - block) * QB : (3 - block) * QB + stop]
+            peak = jnp.max(scores, axis=1, keepdims=True)
+            weights = jnp.exp(scores - peak)
+            total = jnp.sum(weights, axis=1, keepdims=True)
+            mixed = nn(weights.astype(jnp.bfloat16), values[:stop]) / total
+            o_ref[rows, 2 * kv * HEAD_DIM : 2 * (kv + 1) * HEAD_DIM] = jnp.concatenate(
+                [mixed[:QB], mixed[QB:]], axis=1
+            ).astype(jnp.bfloat16)
+            sums = jnp.broadcast_to(peak + jnp.log(total), (2 * QB, 128)).T
+            lse_ref[2 * kv : 2 * kv + 1, rows] = sums[:1, :QB]
+            lse_ref[2 * kv + 1 : 2 * kv + 2, rows] = sums[:1, QB:]
+
+
+def backward_kernel(causal, q_ref, k_ref, v_ref, o_ref, do_ref, lse_ref, keep_ref, *rest):
+    if causal:
+        seed_ref, dq_ref, dk_ref, dv_ref, diag_ref, bias, sums, dk_sum, dv_sum = rest
+    else:
+        dq_ref, dk_ref, dv_ref, dk_sum, dv_sum = rest
+    span = k_ref.shape[0]
+    blocks = q_ref.shape[0] // QB
+    for kv in range(2):
+        lanes = slice(kv * HEAD_DIM, (kv + 1) * HEAD_DIM)
+        dk_sum[...] = jnp.zeros_like(dk_sum)
+        dv_sum[...] = jnp.zeros_like(dv_sum)
+        if causal:
+            for member in range(2):
+                for offset in range(4):
+                    bias[offset, :, member * QB : (member + 1) * QB] = spread(
+                        seed_ref[2 * kv + member, offset]
+                    )
+            sums[...] = jnp.zeros_like(sums)
+        for block in range(blocks):
+            rows = slice(block * QB, (block + 1) * QB)
+            both = slice(2 * kv * HEAD_DIM, 2 * (kv + 1) * HEAD_DIM)
+            pair = q_ref[rows, both]
+            query = jnp.concatenate([pair[:, :HEAD_DIM], pair[:, HEAD_DIM:]], axis=0)
+            upstream = do_ref[rows, both]
+            grads = jnp.concatenate([upstream[:, :HEAD_DIM], upstream[:, HEAD_DIM:]], axis=0)
+            inner = (upstream.astype(jnp.float32) * o_ref[rows, both].astype(jnp.float32)).T
+            delta = jnp.concatenate(
+                [
+                    jnp.sum(inner[:HEAD_DIM], axis=0, keepdims=True),
+                    jnp.sum(inner[HEAD_DIM:], axis=0, keepdims=True),
+                ],
+                axis=1,
+            )
+            level = jnp.concatenate(
+                [lse_ref[2 * kv : 2 * kv + 1, rows], lse_ref[2 * kv + 1 : 2 * kv + 2, rows]], axis=1
+            )
+            dq = jnp.zeros((2 * QB, HEAD_DIM), jnp.float32)
+            for part in range(block + 1 if causal else span // QB):
+                columns = slice(part * QB, (part + 1) * QB)
+                keys = k_ref[columns, lanes]
+                values = v_ref[columns, lanes]
+                scores = nt(keys, query) + keep_ref[columns]
+                if causal:
+                    scores = scores + bias[block - part]
+                probs = jnp.exp(scores - level)
+                dscores = probs * (nt(values, grads) - delta)
+                if causal:
+                    sums[block - part] += dscores
+                dscores = dscores.astype(jnp.bfloat16)
+                dv_sum[columns] += nn(probs.astype(jnp.bfloat16), grads)
+                dk_sum[columns] += nn(dscores, query)
+                dq += tn(dscores, keys)
+            dq_ref[rows, both] = jnp.concatenate([dq[:QB], dq[QB:]], axis=1).astype(jnp.bfloat16)
+        dk_ref[:, lanes] = dk_sum[...].astype(jnp.bfloat16)
+        dv_ref[:, lanes] = dv_sum[...].astype(jnp.bfloat16)
+        if causal:
+            for member in range(2):
+                for offset in range(4):
+                    diag_ref[2 * kv + member, offset] = fold(
+                        sums[offset, :, member * QB : (member + 1) * QB]
+                    )
+
+
+PARAMS = pltpu.CompilerParams(vmem_limit_bytes=56 * 2**20)
+
+
+def attention_forward(queries, kv, keep, seeds=None):
+    tokens, width = queries.shape
+    span = kv.shape[0]
+    heads = width // HEAD_DIM
+    causal = seeds is not None
+    in_specs = [
+        pl.BlockSpec((tokens, 256), lambda i: (0, i)),
+        pl.BlockSpec((span, 128), lambda i: (0, i)),
+        pl.BlockSpec((span, 128), lambda i: (0, i + 2)),
+        pl.BlockSpec((1, span), lambda i: (0, 0)),
+    ]
+    operands = [queries, kv, kv, keep.reshape(1, span)]
+    scratch = []
+    if causal:
+        in_specs.append(pl.BlockSpec((4, 4, 8, 512), lambda i: (i, 0, 0, 0)))
+        operands.append(seeds)
+        scratch.append(pltpu.VMEM((2 * QB, 4 * QB), jnp.float32))
+    work = heads * tokens * span // (2 if causal else 1)
+    context, sums = pl.pallas_call(
+        functools.partial(forward_kernel, causal),
+        grid=(heads // 4,),
+        in_specs=in_specs,
+        out_specs=[
+            pl.BlockSpec((tokens, 256), lambda i: (0, i)),
+            pl.BlockSpec((None, 4, tokens), lambda i: (i, 0, 0)),
+        ],
+        out_shape=[
+            jax.ShapeDtypeStruct((tokens, width), jnp.bfloat16),
+            jax.ShapeDtypeStruct((heads // 4, 4, tokens), jnp.float32),
+        ],
+        scratch_shapes=scratch,
+        compiler_params=PARAMS,
+        cost_estimate=pl.CostEstimate(
+            flops=work * 4 * 4 * HEAD_DIM, bytes_accessed=4 * 2**20, transcendentals=work
+        ),
+    )(*operands)
+    return context, sums
+
+
+def attention_backward(queries, kv, context, grads, sums, keep, seeds=None):
+    tokens, width = queries.shape
+    span = kv.shape[0]
+    heads = width // HEAD_DIM
+    causal = seeds is not None
+    wide = pl.BlockSpec((tokens, 256), lambda i: (0, i))
+    narrow = pl.BlockSpec((span, 128), lambda i: (0, i))
+    in_specs = [
+        wide,
+        narrow,
+        pl.BlockSpec((span, 128), lambda i: (0, i + 2)),
+        wide,
+        wide,
+        pl.BlockSpec((None, 4, tokens), lambda i: (i, 0, 0)),
+        pl.BlockSpec((span, 1), lambda i: (0, 0)),
+    ]
+    operands = [queries, kv, kv, context, grads, sums, keep.reshape(span, 1)]
+    out_specs = [wide, narrow, narrow]
+    out_shape = [
+        jax.ShapeDtypeStruct((tokens, width), jnp.bfloat16),
+        jax.ShapeDtypeStruct((span, width // 2), jnp.bfloat16),
+        jax.ShapeDtypeStruct((span, width // 2), jnp.bfloat16),
+    ]
+    scratch = []
+    if causal:
+        quad = pl.BlockSpec((4, 4, 8, 512), lambda i: (i, 0, 0, 0))
+        in_specs.append(quad)
+        operands.append(seeds)
+        out_specs.append(quad)
+        out_shape.append(jax.ShapeDtypeStruct((heads, 4, 8, 512), jnp.float32))
+        scratch = [pltpu.VMEM((4, QB, 2 * QB), jnp.float32), pltpu.VMEM((4, QB, 2 * QB), jnp.float32)]
+    scratch += [pltpu.VMEM((span, HEAD_DIM), jnp.float32), pltpu.VMEM((span, HEAD_DIM), jnp.float32)]
+    work = heads * tokens * span // (2 if causal else 1)
+    return pl.pallas_call(
+        functools.partial(backward_kernel, causal),
+        grid=(heads // 4,),
+        in_specs=in_specs,
+        out_specs=out_specs,
+        out_shape=out_shape,
+        scratch_shapes=scratch,
+        compiler_params=PARAMS,
+        cost_estimate=pl.CostEstimate(
+            flops=work * 10 * 4 * HEAD_DIM, bytes_accessed=8 * 2**20, transcendentals=work
+        ),
+    )(*operands)
+
+
+def inverse_rms(value):
+    return lax.rsqrt(jnp.mean(value * value, axis=-1, keepdims=True) + EPS)
+
+
+def rms_back(value, gain, upstream):
+    inverse = inverse_rms(value)
+    scaled = upstream * gain
+    mean = jnp.mean(value * scaled, axis=-1, keepdims=True)
+    return inverse * scaled - value * (inverse * inverse * inverse) * mean, upstream * value * inverse
+
+
+def pick(array, index, axis=0):
+    return lax.dynamic_index_in_dim(array, index, axis, keepdims=False)
+
+
+class Plane:
+    def __init__(self, dp, seq):
+        self.depth = dp // 2
+        self.seq = seq
+        place = lax.axis_index("dp")
+        self.z, self.core = place // 2, place % 2
+        self.corner = lax.axis_index("seq")
+        self.y, self.x = self.corner // 2, self.corner % 2
+
+    def move(self, array, where):
+        pairs = []
+        for z in range(self.depth):
+            for core in range(2):
+                for y in range(2):
+                    for x in range(2):
+                        z2, core2, y2, x2 = where(z, core, y, x)
+                        source = (z * 2 + core) * self.seq + y * 2 + x
+                        target = (z2 * 2 + core2) * self.seq + y2 * 2 + x2
+                        pairs.append((source, target))
+        return lax.ppermute(array, ("dp", "seq"), pairs)
+
+    def swap_core(self, array):
+        return self.move(array, lambda z, c, y, x: (z, 1 - c, y, x))
+
+    def swap_x(self, array):
+        return self.move(array, lambda z, c, y, x: (z, c, y, 1 - x))
+
+    def swap_y(self, array):
+        return self.move(array, lambda z, c, y, x: (z, c, 1 - y, x))
+
+    def shift_z(self, array, step):
+        return self.move(array, lambda z, c, y, x: ((z + step) % self.depth, c, y, x))
+
+    def collect(self, parcel):
+        received = []
+        for up in range(2):
+            for across in range(2):
+                piece = parcel.reshape((4,) + parcel.shape[2:])
+                piece = pick(piece, (self.x ^ across) * 2 + (self.y ^ up))
+                received.append(
+                    self.move(piece, lambda z, c, y, x, up=up, across=across: (z, y ^ up, x ^ across, c))
+                )
+        mine = jnp.stack(received)
+        both = jnp.concatenate([mine, self.swap_core(mine)])
+        pieces = []
+        for block in range(4):
+            for half in range(2):
+                index = 2 * (half ^ (block >> 1)) + (self.y ^ (block & 1))
+                pieces.append(pick(both, index + jnp.where(half == self.core, 0, 4)))
+        return jnp.stack(pieces).reshape((4, 2) + parcel.shape[2:])
+
+    def deliver(self, pieces):
+        received = []
+        for up in range(2):
+            for across in range(2):
+                piece = pick(pieces, 2 * (self.core ^ up) + (self.y ^ across))
+                received.append(
+                    self.move(piece, lambda z, k, Y, X, up=up, across=across: (z, X, k ^ up, Y ^ across))
+                )
+        stacked = jnp.stack(received)
+        homes = []
+        for micro in range(2):
+            for half in range(2):
+                homes.append(pick(stacked, 2 * (self.y ^ half) + (self.x ^ micro)))
+        return jnp.stack(homes).reshape((2, 2) + pieces.shape[1:])
+
+    def gather(self, shard):
+        quarter = pick(shard, self.corner, 2)
+        others = jnp.stack([self.shift_z(quarter, step) for step in range(1, self.depth)])
+        beside = self.swap_x(others)
+        below = self.swap_y(others)
+        middle = shard.shape[0]
+        near = self.swap_y(beside[..., : shard.shape[3] // 2, :])
+        far = self.swap_x(below[..., shard.shape[3] // 2 :, :])
+        diagonal = jnp.concatenate([near, far], axis=-2)
+        pieces = jnp.stack([others, beside, below, diagonal])
+        wholes = []
+        for matrix in range(middle):
+            blocks = []
+            for z in range(self.depth):
+                step = (self.z - z + self.depth) % self.depth
+                for part in range(4):
+                    away = pick(pick(pieces[:, :, matrix], self.corner ^ part), jnp.maximum(step - 1, 0))
+                    blocks.append(jnp.where(step == 0, shard[matrix, :, part], away))
+            whole = jnp.stack(blocks).reshape((self.depth, 4) + shard.shape[1:2] + shard.shape[3:])
+            whole = jnp.swapaxes(whole, 1, 2)
+            wholes.append(whole.reshape(-1, shard.shape[-1]))
+        return wholes
+
+    def scatter(self, wholes, lanes):
+        shape = (self.depth, lanes, 2, 2, wholes[0].shape[0] // (self.depth * lanes * 4), wholes[0].shape[1])
+        grads = jnp.stack([whole.reshape(shape) for whole in wholes])
+        half = self.depth // 2
+        low, high = grads[:, :half], grads[:, half:]
+        wide = lambda a: a.astype(jnp.float32)
+        low_got = self.swap_x(pick(low, 1 - self.x, 4))
+        high_got = self.swap_y(pick(high, 1 - self.y, 3))
+        low = (wide(pick(low, self.x, 4)) + wide(low_got)).astype(jnp.bfloat16)
+        high = (wide(pick(high, self.y, 3)) + wide(high_got)).astype(jnp.bfloat16)
+        low_got = self.swap_y(pick(low, 1 - self.y, 3))
+        high_got = self.swap_x(pick(high, 1 - self.x, 3))
+        low = (wide(pick(low, self.y, 3)) + wide(low_got)).astype(jnp.bfloat16)
+        high = (wide(pick(high, self.x, 3)) + wide(high_got)).astype(jnp.bfloat16)
+        column = jnp.concatenate([low, high], axis=1)
+        total = wide(pick(column, self.z, 1))
+        for step in range(1, self.depth):
+            total = total + wide(self.shift_z(pick(column, (self.z + step) % self.depth, 1), step))
+        return total
+
+
+def parity_columns(weight, core):
+    rows, columns = weight.shape
+    return pick(weight.reshape(rows, 4, 2, columns // 8), core, 2).reshape(rows, columns // 2)
+
+
+def per_chip(
+    layer_input,
+    memory,
+    target_lengths,
+    memory_lengths,
+    buckets,
+    norm_self,
+    self_q,
+    self_k,
+    self_v,
+    self_out,
+    rel_bias,
+    norm_cross,
+    cross_q,
+    cross_k,
+    cross_v,
+    cross_out,
+    norm_ff,
+    ff_gate,
+    ff_up,
+    ff_down,
+    cotangent,
+):
+    bf16, f32 = jnp.bfloat16, jnp.float32
+    plane = Plane(lax.axis_size("dp"), lax.axis_size("seq"))
+    core = plane.core
+    width = layer_input.shape[3]
+    local = layer_input.shape[2]
+    near = memory.shape[2]
+
+    small = jnp.concatenate(
+        [norm_self, norm_cross, norm_ff, rel_bias.reshape(-1), jnp.zeros((112,), bf16)]
+    )
+    small = lax.all_gather(small, ("dp", "seq"), axis=0, tiled=False)
+    small = small.reshape(-1, 4, 512).astype(f32)
+    shard = norm_self.shape[0]
+    gain_self, gain_cross, gain_ff = (
+        small[:, 0, i * shard : (i + 1) * shard].reshape(-1) for i in range(3)
+    )
+    bias = small[:, :, 3 * shard : 3 * shard + 16].reshape(-1, 4, 4, 4)
+    bias = jnp.swapaxes(bias, 1, 2).reshape(BUCKETS, HEADS)
+    bias = pick(bias.reshape(BUCKETS, 4, 2, 2), core, 2).reshape(BUCKETS, -1)
+    onehot = (buckets[:, None] == jnp.arange(BUCKETS, dtype=jnp.int32)[None, :]).astype(f32)
+    table = lax.dot_general(bias, onehot, (((0,), (1,)), ((), ())), precision=HIGH)
+    full = jnp.concatenate([jnp.full((table.shape[0], QB), NEG, f32), table], axis=1)
+    vectors = row_pieces(full)
+    seeds_back = seed_rows(vectors)
+    seeds_fore = seed_rows(jnp.roll(vectors[..., ::-1], 1, axis=-1))
+
+    parcel = jnp.concatenate(
+        [
+            layer_input.reshape(2, 2, local // 2, width),
+            cotangent.reshape(2, 2, local // 2, width),
+            memory.reshape(2, 2, near // 2, width),
+        ],
+        axis=2,
+    )
+    everything = plane.collect(parcel)
+    inputs = everything[:, :, : local // 2].reshape(-1, width)
+    upstream = everything[:, :, local // 2 : local].reshape(-1, width)
+    encoded = everything[:, :, local:].reshape(-1, width)
+    both = jnp.concatenate([target_lengths, memory_lengths]).reshape(2, 2, 1)
+    others = plane.swap_core(both.astype(f32)).astype(jnp.int32)
+    both = jnp.where(plane.x == core, both, others)[:, :, 0]
+    mine = pick(both, plane.y, 1)
+    length, span = mine[0], mine[1]
+    tokens = inputs.shape[0]
+    positions = jnp.arange(tokens, dtype=jnp.int32)
+    valid = (positions < length).astype(f32)[:, None]
+    keep_self = jnp.where(positions < length, 0.0, NEG).astype(f32)
+    keep_cross = jnp.where(jnp.arange(encoded.shape[0], dtype=jnp.int32) < span, 0.0, NEG).astype(f32)
+
+    def column_shards(matrices):
+        packed = [
+            jnp.stack([jnp.concatenate([parity_columns(w, side) for w in group], axis=1) for group in matrices])
+            for side in range(2)
+        ]
+        packed = jnp.stack(packed)
+        got = plane.swap_core(pick(packed, 1 - core))
+        own = pick(packed, core)
+        ordered = jnp.stack([jnp.where(core == 0, own, got), jnp.where(core == 0, got, own)], axis=1)
+        return ordered.reshape(ordered.shape[:2] + (4, -1) + ordered.shape[3:])
+
+    def row_shards(matrices):
+        packed = jnp.stack(matrices)[:, None]
+        return packed.reshape(packed.shape[:2] + (4, -1) + packed.shape[3:])
+
+    w_q, w_kv, w_ckv, w_cq = plane.gather(
+        column_shards([[self_q], [self_k, self_v], [cross_k, cross_v], [cross_q]])
+    )
+    w_out, w_cout = plane.gather(row_shards([self_out, cross_out]))
+    w_gate, w_up = plane.gather(column_shards([[ff_gate], [ff_up]]))
+    (w_down,) = plane.gather(row_shards([ff_down]))
+
+    def share(partial):
+        partial = partial.astype(bf16)
+        return partial.astype(f32) + plane.swap_core(partial).astype(f32)
+
+    def share_half(partial):
+        partial = partial.astype(bf16).reshape(4, 2, -1, partial.shape[-1])
+        got = plane.swap_core(pick(partial, 1 - core, 1))
+        return pick(partial, core, 1).astype(f32) + got.astype(f32)
+
+    def own_half(value):
+        return pick(value.reshape(4, 2, -1, value.shape[-1]), core, 1)
+
+    hidden = inputs.astype(f32)
+    normed_self = (hidden * inverse_rms(hidden) * gain_self).astype(bf16)
+    queries = project(normed_self, w_q).astype(bf16)
+    kv = project(normed_self, w_kv).astype(bf16)
+    far_kv = project(encoded, w_ckv).astype(bf16)
+    context, self_sums = attention_forward(queries, kv, keep_self, seeds_fore)
+    first = hidden + share(project(context, w_out))
+    normed_cross = (first * inverse_rms(first) * gain_cross).astype(bf16)
+    cross_queries = project(normed_cross, w_cq).astype(bf16)
+    cross_context, cross_sums = attention_forward(cross_queries, far_kv, keep_cross)
+    second = first + share(project(cross_context, w_cout))
+    normed_ff = (second * inverse_rms(second) * gain_ff).astype(bf16)
+    gate = project(normed_ff, w_gate)
+    upward = project(normed_ff, w_up)
+    middle = gated(gate, upward).astype(bf16)
+    third = own_half(second) + share_half(project(middle, w_down))
+    output = plane.deliver((third * own_half(valid)).astype(bf16))
+
+    top = upstream.astype(f32) * valid
+    top_low = top.astype(bf16)
+    _, pullback = jax.vjp(gated, gate, upward)
+    gate_grad, upward_grad = pullback(project_back(top_low, w_down))
+    gate_grad = gate_grad.astype(bf16)
+    upward_grad = upward_grad.astype(bf16)
+    g_down = weight_grad(middle, top_low).astype(bf16)
+    g_gate = weight_grad(normed_ff, gate_grad).astype(bf16)
+    g_up = weight_grad(normed_ff, upward_grad).astype(bf16)
+    r_down = plane.scatter([g_down], 1)
+    r_ff = plane.scatter([g_gate, g_up], 2)
+    change, gain_ff_terms = rms_back(
+        second, gain_ff, share(project_back(gate_grad, w_gate) + project_back(upward_grad, w_up))
+    )
+    second_grad = top + change
+    cross_grad = second_grad.astype(bf16)
+    g_cout = weight_grad(cross_context, cross_grad).astype(bf16)
+    cross_up = project_back(cross_grad, w_cout).astype(bf16)
+    dqc, dkc, dvc = attention_backward(
+        cross_queries, far_kv, cross_context, cross_up, cross_sums, keep_cross
+    )
+    dkvc = jnp.concatenate([dkc, dvc], axis=1)
+    g_cq = weight_grad(normed_cross, dqc).astype(bf16)
+    g_ckv = weight_grad(encoded, dkvc).astype(bf16)
+    memory_grad = plane.deliver(share_half(project_back(dkvc, w_ckv)).astype(bf16))
+    change, gain_cross_terms = rms_back(first, gain_cross, share(project_back(dqc, w_cq)))
+    first_grad = second_grad + change
+    self_grad = first_grad.astype(bf16)
+    g_out = weight_grad(context, self_grad).astype(bf16)
+    self_up = project_back(self_grad, w_out).astype(bf16)
+    dq, dk, dv, diagonal = attention_backward(
+        queries, kv, context, self_up, self_sums, keep_self, seeds_back
+    )
+    dkv = jnp.concatenate([dk, dv], axis=1)
+    g_q = weight_grad(normed_self, dq).astype(bf16)
+    g_kv = weight_grad(normed_self, dkv).astype(bf16)
+    r_rows = plane.scatter([g_out, g_cout], 1)
+    r_columns = plane.scatter([g_q, g_kv, g_ckv, g_cq], 2)
+    change, gain_self_terms = rms_back(
+        own_half(hidden), gain_self, share_half(project_back(dq, w_q) + project_back(dkv, w_kv))
+    )
+    input_grad = plane.deliver((own_half(first_grad) + change).astype(bf16)).astype(f32)
+
+    terms = [
+        jnp.sum(own_half(gain_ff_terms), axis=(0, 1)),
+        jnp.sum(own_half(gain_cross_terms), axis=(0, 1)),
+        jnp.sum(gain_self_terms, axis=(0, 1)),
+    ]
+    diagonal = sum(jnp.roll(diagonal[:, :, r], -r, axis=-1) for r in range(8))
+    blocks = jnp.zeros((diagonal.shape[0], 5, QB), f32)
+    blocks = blocks.at[:, 1:].add(diagonal[:, :, :QB]).at[:, :4].add(diagonal[:, :, QB:])
+    distances = blocks[:, 1:].reshape(-1, tokens)
+    bias_terms = lax.dot_general(onehot, distances, (((0,), (1,)), ((), ())), precision=HIGH)
+    bias_terms = bias_terms.reshape(BUCKETS, 4, 1, 2)
+    bias_terms = jnp.concatenate(
+        [jnp.where(core == 0, bias_terms, 0.0), jnp.where(core == 1, bias_terms, 0.0)], axis=2
+    ).reshape(-1)
+    packed = lax.psum(jnp.concatenate(terms + [bias_terms]), ("dp", "seq"))
+    mine = lax.axis_index("dp") * 4 + plane.corner
+    piece = width // (plane.depth * 8)
+    n_ff, n_cross, n_self = (
+        lax.dynamic_slice_in_dim(packed, i * width + mine * piece, piece) for i in range(3)
+    )
+    bias_grad = packed[3 * width :].reshape(BUCKETS, HEADS)
+    bias_grad = lax.dynamic_slice(
+        bias_grad, (lax.axis_index("dp") * rel_bias.shape[0], plane.corner * rel_bias.shape[1]), rel_bias.shape
+    )
+
+    def columns_home(sums):
+        got = plane.swap_core(pick(sums, 1 - core, 1).astype(bf16)).astype(f32)
+        own = pick(sums, core, 1)
+        return jnp.where(core == 0, own, got), jnp.where(core == 0, got, own)
+
+    def merge(even, odd):
+        rows = even.shape[0]
+        return jnp.stack([even.reshape(rows, 4, -1), odd.reshape(rows, 4, -1)], axis=2).reshape(rows, -1)
+
+    even, odd = columns_home(r_columns)
+    quarter = even.shape[-1] // 2
+    d_q = merge(even[0], odd[0])
+    d_k, d_v = (merge(even[1][:, s], odd[1][:, s]) for s in (slice(0, quarter), slice(quarter, None)))
+    d_ck, d_cv = (merge(even[2][:, s], odd[2][:, s]) for s in (slice(0, quarter), slice(quarter, None)))
+    d_cq = merge(even[3], odd[3])
+    even, odd = columns_home(r_ff)
+    d_gate, d_up = merge(even[0], odd[0]), merge(even[1], odd[1])
+    return (
+        output.reshape(layer_input.shape),
+        input_grad.reshape(layer_input.shape),
+        memory_grad.astype(f32).reshape(memory.shape),
+        n_self,
+        d_q,
+        d_k,
+        d_v,
+        r_rows[0, 0],
+        bias_grad,
+        n_cross,
+        d_cq,
+        d_ck,
+        d_cv,
+        r_rows[1, 0],
+        n_ff,
+        d_gate,
+        d_up,
+        r_down[0, 0],
+    )
+
+
 def solution(mesh):
     placed = (
         P(None, "dp", "seq", None),
@@ -544,8 +1138,9 @@
         P("dp", None),
         P(None, "dp", "seq", None),
     )
+    chips = mesh.shape["seq"] == 4 and mesh.shape["dp"] == HEADS // 2
     return jax.shard_map(
-        per_device,
+        per_chip if chips else per_device,
         mesh=mesh,
         in_specs=placed,
         out_specs=(

time: 5310 us -> 876 us (0.16)
  local copies, waits for them, and re-layouts: 3490 us -> 95.3 us
  waiting for transfers between devices: 1020 us -> 199 us
  matrix products: 294 us -> 91.2 us
  other arithmetic: 199 us -> 116 us
  Pallas kernels: 0 us -> 69.5 us
    gather x4 -> x0, local copies, waits for them, and re-layouts: 2810 us -> none  [masks(): extra = jnp.take(table, jnp.maximum(distance, 0), axis=1)]
    reduce_scatter x9 -> x0, waiting for transfers between devices: 1000 us -> none  [the longest x1 253 us: per_device(): lax.psum_scatter(totals[14], ('dp', 'seq'), scatter_dimension=0, tiled=True)]
    ppermute x0 -> x85, waiting for transfers between devices: none -> 199 us  [move(): return lax.ppermute(array, ('dp', 'seq'), pairs)]
    reshape x52 -> x19, local copies, waits for them, and re-layouts: 206 us -> 13.3 us  [the longest x8 9.07 us: merge(): jnp.stack([even.reshape(rows, 4, -1), odd.reshape(rows, 4, -1)], axis=2)]
    rev x4 -> x0, local copies, waits for them, and re-layouts: 174 us -> none  [diagonal_sums(): flipped = jnp.pad(grads[..., ::-1], ((0, 0), (0, 0), (0, 0), (0, block)))]
    ppermute x0 -> x85, starting transfers between devices: none -> 174 us  [move(): return lax.ppermute(array, ('dp', 'seq'), pairs)]
    unnamed x570 -> x237, local copies, waits for them, and re-layouts: 190 us -> 28.4 us
    all_to_all x32 -> x0, starting transfers between devices: 146 us -> none  [the longest x2 18.4 us: per_device(): lax.all_to_all(values, 'seq', split_axis=2, concat_axis=1, tiled=True)]
  transfers between devices with their start and end apart: 54 -> 85, of which waited for: 11 -> 29; matrix products, arithmetic and copies ran while one was open for 74% -> 24% of each run, Pallas kernels for 0% -> 2%
where the time goes in v1:
time: 876 us; the launch traced here: 863 us
  waiting for transfers between devices  199 us (23%)
  starting transfers between devices  174 us (20%)
  other arithmetic  116 us (13%)
  blocking collectives  114 us (13%)
  local copies, waits for them, and re-layouts  95.3 us (11%)
  matrix products  91.2 us (10%)
  Pallas kernels  69.5 us (8%)
    ppermute x85, waiting for transfers between devices, move(): return lax.ppermute(array, ('dp', 'seq'), pairs)  199 us
    ppermute x85, starting transfers between devices, move(): return lax.ppermute(array, ('dp', 'seq'), pairs)  174 us
    all_gather x1, blocking collectives, per_chip(): small = lax.all_gather(small, ('dp', 'seq'), axis=0, tiled=False)  65.6 us
    psum x1, blocking collectives, per_chip(): packed = lax.psum(jnp.concatenate(terms + [bias_terms]), ('dp', 'seq'))  48 us
    pallas_call x2, Pallas kernels, attention_backward(): pl.pallas_call(functools.partial(backward_kernel, causal), grid=(heads //...  40.8 us
    dot_general x9, matrix products, project_back(): lax.dot_general(grad, weight, (((1,), (1,)), ((), ())), preferred_element...  35.4 us
    unnamed x117, other arithmetic  31.1 us
    dot_general x9, matrix products, project(): return jnp.dot(left, right, preferred_element_type=jnp.float32)  29.8 us
  transfers between devices with their start and end apart: 85, of which 29 were waited for; matrix products, arithmetic and copies ran while one was open for 24% of the time, Pallas kernels for 2%

profile of v1, /device:TPU:0, one launch (start us, length us, event | category | flops | bytes accessed | tf_op | source)
XLA Modules:
  0.0 862.6 jit_solution(240848125800413355)
XLA Ops:
  2.3 3.0 collective-permute-start.14
  17.1 65.6 %all-gather.1 = bf16[32,1,512]{2,1,0:T(2,128)(2,1)S(1)} all-gather(bf16[1,1,512]{2,1,0:T(2,128)(2,1)S(1)} %reshape.3882), channel_id=2, replica_groups=mesh['dp'=8,'seq'=4] {'dp','seq'}, dimensions={0}, use_global_device_ids=true | all-gather | bytes 33792 | tf_op jit(solution)/shard_map/all_gather | solution.py:919
  146.7 3.8 collective-permute-start.33
  159.6 17.3 %collective-permute-done.17 = bf16[3,2,1,32,1024]{4,3,1,0,2:T(8,128)(2,1)S(1)} collective-permute-done((bf16[3,2,1,32,1024]{4,3,1,0,2:T(8,128)(2,1)S(1)}, bf16[3,2,1,32,1024]{4,3,1,0,2:T(8,128)(2,1)S(1)}, u32[]{:S(2)}, u32[]{:S(2)}) %collective-permute-start.17) | collective-permute-done | bytes 393248 | tf_op jit(solution)/shard_map/ppermute | solution.py:790
  183.5 12.7 %collective-permute-done.3 = bf16[320,1024]{1,0:T(8,128)(2,1)S(1)} collective-permute-done((bf16[320,1024]{1,0:T(8,128)(2,1)S(1)}, bf16[320,1024]{1,0:T(8,128)(2,1)S(1)}, u32[]{:S(2)}, u32[]{:S(2)}) %collective-permute-start.3) | collective-permute-done | bytes 655392 | tf_op jit(solution)/shard_map/ppermute | solution.py:790
  196.7 9.5 %collective-permute-done.19 = bf16[3,2,1,16,1024]{4,3,1,0,2:T(8,128)(2,1)S(1)} collective-permute-done((bf16[3,2,1,16,1024]{4,3,1,0,2:T(8,128)(2,1)S(1)}, bf16[3,2,1,16,1024]{4,3,1,0,2:T(8,128)(2,1)S(1)}, u32[]{:S(2)}, u32[]{:S(2)}) %collective-permute-start.19) | collective-permute-done | bytes 196640 | tf_op jit(solution)/shard_map/ppermute | solution.py:790
  217.8 9.2 %collective-permute-start.24 = (bf16[2,2,32,1408]{3,2,1,0:T(8,128)(2,1)S(1)}, bf16[2,2,32,1408]{3,2,1,0:T(8,128)(2,1)S(1)}, u32[]{:S(2)}, u32[]{:S(2)}) collective-permute-start(bf16[2,2,32,1408]{3,2,1,0:T(8,128)(2,1)S(1)} %copy_bitcast_fusion.12), channel_id=1, source_target_pairs={{0,8},{1,9},{2,10},{3,11},{4,12},{5,13},{6,14},{7,15},{8,16},{9,17... | collective-permute-start | bytes 1081352 | tf_op jit(solution)/shard_map/ppermute | solution.py:790
  227.1 12.0 %collective-permute-done.7 = bf16[4,2,32,512]{3,2,1,0:T(8,128)(2,1)S(1)} collective-permute-done((bf16[4,2,32,512]{3,2,1,0:T(8,128)(2,1)S(1)}, bf16[4,2,32,512]{3,2,1,0:T(8,128)(2,1)S(1)}, u32[]{:S(2)}, u32[]{:S(2)}) %collective-permute-start.7) | collective-permute-done | bytes 262176 | tf_op jit(solution)/shard_map/ppermute | solution.py:790
  239.1 4.3 collective-permute-start.26
  245.4 14.3 %collective-permute-done.9 = bf16[3,4,2,32,512]{4,3,2,1,0:T(8,128)(2,1)S(1)} collective-permute-done((bf16[3,4,2,32,512]{4,3,2,1,0:T(8,128)(2,1)S(1)}, bf16[3,4,2,32,512]{4,3,2,1,0:T(8,128)(2,1)S(1)}, u32[]{:S(2)}, u32[]{:S(2)}) %collective-permute-start.9) | collective-permute-done | bytes 786464 | tf_op jit(solution)/shard_map/ppermute | solution.py:790
  273.3 18.1 %collective-permute-done.27 = bf16[3,2,2,32,1408]{4,3,2,1,0:T(8,128)(2,1)S(1)} collective-permute-done((bf16[3,2,2,32,1408]{4,3,2,1,0:T(8,128)(2,1)S(1)}, bf16[3,2,2,32,1408]{4,3,2,1,0:T(8,128)(2,1)S(1)}, u32[]{:S(2)}, u32[]{:S(2)}) %collective-permute-start.27) | collective-permute-done | bytes 1081376 | tf_op jit(solution)/shard_map/ppermute | solution.py:790
  294.6 8.9 %collective-permute-done.29 = bf16[3,2,2,16,1408]{4,3,2,1,0:T(8,128)(2,1)S(1)} collective-permute-done((bf16[3,2,2,16,1408]{4,3,2,1,0:T(8,128)(2,1)S(1)}, bf16[3,2,2,16,1408]{4,3,2,1,0:T(8,128)(2,1)S(1)}, u32[]{:S(2)}, u32[]{:S(2)}) %collective-permute-start.29) | collective-permute-done | bytes 540704 | tf_op jit(solution)/shard_map/ppermute | solution.py:790
  323.0 17.9 %shard_map.340 = (bf16[1024,512]{1,0:T(8,128)(2,1)}, f32[2,4,1024]{2,1,0:T(4,128)}) custom-call(bf16[1024,512]{1,0:T(8,128)(2,1)} %convolution_convert_fusion.16.q_ref, bf16[1024,512]{1,0:T(8,128)(2,1)} %convolution_convert_fusion.15.k_ref.v_ref, bf16[1024,512]{1,0:T(8,128)(2,1)} %convolution_convert_fusion.15.k_ref.v_ref, ...), custom_call_target="tpu_custom_call" | custom-call | flops 4294967296 | bytes 4194304 | tf_op jit(solution)/shard_map/pallas_call | solution.py:688
  359.4 10.8 %shard_map.341 = (bf16[1024,512]{1,0:T(8,128)(2,1)}, f32[2,4,1024]{2,1,0:T(4,128)}) custom-call(bf16[1024,512]{1,0:T(8,128)(2,1)} %convolution_convert_fusion.14.q_ref, bf16[512,512]{1,0:T(8,128)(2,1)} %convolution_convert_fusion.19.k_ref.v_ref, bf16[512,512]{1,0:T(8,128)(2,1)} %convolution_convert_fusion.19.k_ref.v_ref, f32[1,512]{1,0:T(1,128)} %compare_select_fusion.1.keep_ref), custom_call_target="tpu_custom_call" | custom-call | flops 4294967296 | bytes 4194304 | tf_op jit(solution)/shard_map/pallas_call | solution.py:688
  381.0 5.2 fusion.386
  386.2 5.2 fusion.385
  391.4 13.5 %multiply_convert_fusion = (bf16[1024,1408]{1,0:T(8,128)(2,1)}, bf16[1024,1408]{1,0:T(8,128)(2,1)}, bf16[1024,1408]{1,0:T(8,128)(2,1)}) fusion(f32[1024,1408]{1,0:T(8,128)} %fusion.385, f32[1024,1408]{1,0:T(8,128)} %fusion.386, bf16[1024,1024]{1,0:T(8,128)(2,1)S(1)} %bitcast.1907, bf16[1408,1024]{1,0:T(8,128)(2,1)} %bitcast.2013), kind=kOutput, calls=%fused_computation.11 | convolution fusion | flops 2990276608 | bytes 25165824 | tf_op jit(solution)/shard_map/dot_general | solution.py:41
  404.9 7.0 fusion.387
  411.9 3.7 convolution_convert_fusion.1
  415.7 5.7 add_convert_fusion.1
  421.5 5.6 convolution_convert_fusion.4
  427.7 3.7 convolution_convert_fusion.2
  438.0 33.4 %collective-permute-start.41 = (bf16[128,1024]{1,0:T(8,128)(2,1)S(1)}, bf16[128,1024]{1,0:T(8,128)(2,1)S(1)}, u32[]{:S(2)}, u32[]{:S(2)}) collective-permute-start(bf16[128,1024]{1,0:T(8,128)(2,1)S(1)} %get-tuple-element.151), channel_id=1, source_target_pairs={{0,2},{1,6},{2,3},{3,7},{4,0},{5,4},{6,1},{7,5},{8,10},{9,14},{10,... | collective-permute-start | bytes 786440 | tf_op jit(solution)/shard_map/ppermute | solution.py:790
  476.8 4.7 collective-permute-done.42
  488.8 4.6 multiply_multiply_fusion.4
  493.5 7.2 convolution_convert_fusion
  508.6 15.8 %shard_map.342 = (bf16[1024,512]{1,0:T(8,128)(2,1)}, bf16[512,256]{1,0:T(8,128)(2,1)}, bf16[512,256]{1,0:T(8,128)(2,1)}) custom-call(bf16[1024,512]{1,0:T(8,128)(2,1)} %convolution_convert_fusion.14.q_ref, bf16[512,512]{1,0:T(8,128)(2,1)} %convolution_convert_fusion.19.k_ref.v_ref, bf16[512,512]{1,0:T(8,128)(2,1)} %convolution_convert_fusion.19.k_ref.v_ref, ...), custom_call_target="tpu_custom_call" | custom-call | flops 10737418240 | bytes 8388608 | tf_op jit(solution)/shard_map/pallas_call | solution.py:742
  525.4 3.8 convolution_convert_fusion.9
  536.2 11.5 %collective-permute-start.74 = (bf16[2,2,32,1408]{3,2,1,0:T(8,128)(2,1)S(1)}, bf16[2,2,32,1408]{3,2,1,0:T(8,128)(2,1)S(1)}, u32[]{:S(2)}, u32[]{:S(2)}) collective-permute-start(bf16[2,2,32,1408]{3,2,1,0:T(8,128)(2,1)S(1)} %get-tuple-element.111), channel_id=1, source_target_pairs={{0,8},{1,9},{2,10},{3,11},{4,12},{5,13},{6,14},{7,15},{8,16},{9,17... | collective-permute-start | bytes 1081352 | tf_op jit(solution)/shard_map/ppermute | solution.py:790
  548.3 3.2 collective-permute-start.76
  552.9 3.8 collective-permute-done.74
  556.7 13.0 %collective-permute-done.75 = bf16[2,2,32,1408]{3,2,1,0:T(8,128)(2,1)S(1)} collective-permute-done((bf16[2,2,32,1408]{3,2,1,0:T(8,128)(2,1)S(1)}, bf16[2,2,32,1408]{3,2,1,0:T(8,128)(2,1)S(1)}, u32[]{:S(2)}, u32[]{:S(2)}) %collective-permute-start.75) | collective-permute-done | bytes 360480 | tf_op jit(solution)/shard_map/ppermute | solution.py:790
  590.5 3.5 collective-permute-start.54
  599.3 5.8 collective-permute-done.81
  606.4 8.5 collective-permute-start.82
  614.9 3.4 collective-permute-start.83
  619.5 3.8 collective-permute-done.82
  623.3 6.0 collective-permute-done.83
  633.0 4.6 multiply_multiply_fusion.3
  641.4 25.0 %shard_map.343 = (bf16[1024,512]{1,0:T(8,128)(2,1)}, bf16[1024,256]{1,0:T(8,128)(2,1)}, bf16[1024,256]{1,0:T(8,128)(2,1)}, f32[8,4,8,512]{3,2,1,0:T(8,128)}) custom-call(bf16[1024,512]{1,0:T(8,128)(2,1)} %convolution_convert_fusion.16.q_ref, bf16[1024,512]{1,0:T(8,128)(2,1)} %convolution_convert_fusion.15.k_ref.v_ref, ...), custom_call_target="tpu_custom_call" | custom-call | flops 10737418240 | bytes 8388608 | tf_op jit(solution)/shard_map/pallas_call | solution.py:742
  683.4 29.8 %collective-permute-done.65 = bf16[2,2,1,2,32,1024]{5,4,0,1,3,2:T(8,128)(2,1)S(1)} collective-permute-done((bf16[2,2,1,2,32,1024]{5,4,0,1,3,2:T(8,128)(2,1)S(1)}, bf16[2,2,1,2,32,1024]{5,4,0,1,3,2:T(8,128)(2,1)S(1)}, u32[]{:S(2)}, u32[]{:S(2)}) %collective-permute-start.65) | collective-permute-done | bytes 524320 | tf_op jit(solution)/shard_map/ppermute | solution.py:790
  728.1 4.5 collective-permute-start.67
  757.1 8.0 collective-permute-done.55
  765.1 3.0 collective-permute-start.49
  768.6 12.3 %collective-permute-start.56 = (bf16[4,2,2,32,512]{4,3,2,1,0:T(8,128)(2,1)S(1)}, bf16[4,2,2,32,512]{4,3,2,1,0:T(8,128)(2,1)S(1)}, u32[]{:S(2)}, u32[]{:S(2)}) collective-permute-start(bf16[4,2,2,32,512]{4,3,2,1,0:T(8,128)(2,1)S(1)} %dynamic-slice_bitcast_fusion.10), channel_id=1, source_target_pairs={{0,2},{1,3},{2,0},{3,1},{4,6},{5,7},{6,4},{7,5},{8,10},{9,11},{10,... | collective-permute-start | bytes 1572872 | tf_op jit(solution)/shard_map/ppermute | solution.py:790
  780.9 48.0 %psum.7 = f32[3584]{0:T(1024)S(1)} all-reduce(f32[3584]{0:T(1024)S(1)} %pad_maximum_fusion.30), channel_id=1, replica_groups=mesh['dp'=8,'seq'=4] {'dp','seq'}, use_global_device_ids=true, to_apply=%region_10.11 | all-reduce | flops 3584 | bytes 28672 | tf_op jit(solution)/shard_map/psum | solution.py:1067
  839.1 5.4 collective-permute-done.59
  844.5 9.3 %collective-permute-done.60 = bf16[4,2,32,512]{3,2,1,0:T(8,128)(2,1)S(1)} collective-permute-done((bf16[4,2,32,512]{3,2,1,0:T(8,128)(2,1)S(1)}, bf16[4,2,32,512]{3,2,1,0:T(8,128)(2,1)S(1)}, u32[]{:S(2)}, u32[]{:S(2)}) %collective-permute-start.60) | collective-permute-done | bytes 262176 | tf_op jit(solution)/shard_map/ppermute | solution.py:790
  (808 shorter events, 319.2 us)
Async XLA Ops:
  2.3 144.4 %collective-permute-start.14 = (bf16[2,1,32,1024]{3,2,0,1:T(8,128)(2,1)}, bf16[2,1,32,1024]{3,2,0,1:T(8,128)(2,1)}, u32[]{:S(2)}, u32[]{:S(2)}) collective-permute-start(bf16[2,1,32,1024]{3,2,0,1:T(8,128)(2,1)} %fusion.113), channel_id=1, source_target_pairs={{0,8},{1,9},{2,10},{3,11},{4,12},{5,13},{6,14},{7,15},{8,16},{9,17... | collective-permute-start | bytes 393224 | tf_op jit(solution)/shard_map/ppermute | solution.py:790
  5.3 141.4 %collective-permute-start.15 = (bf16[2,1,32,1024]{3,2,0,1:T(8,128)(2,1)}, bf16[2,1,32,1024]{3,2,0,1:T(8,128)(2,1)}, u32[]{:S(2)}, u32[]{:S(2)}) collective-permute-start(bf16[2,1,32,1024]{3,2,0,1:T(8,128)(2,1)} %fusion.113), channel_id=1, source_target_pairs={{0,16},{1,17},{2,18},{3,19},{4,20},{5,21},{6,22},{7,23},{8,24},{9,... | collective-permute-start | bytes 393224 | tf_op jit(solution)/shard_map/ppermute | solution.py:790
  7.9 142.6 %collective-permute-start.16 = (bf16[2,1,32,1024]{3,2,0,1:T(8,128)(2,1)}, bf16[2,1,32,1024]{3,2,0,1:T(8,128)(2,1)}, u32[]{:S(2)}, u32[]{:S(2)}) collective-permute-start(bf16[2,1,32,1024]{3,2,0,1:T(8,128)(2,1)} %fusion.113), channel_id=1, source_target_pairs={{0,24},{1,25},{2,26},{3,27},{4,28},{5,29},{6,30},{7,31},{8,0},{9,1... | collective-permute-start | bytes 393224 | tf_op jit(solution)/shard_map/ppermute | solution.py:790
  15.6 142.8 %collective-permute-start.5 = (bf16[4,128,512]{2,1,0:T(8,128)(2,1)}, bf16[4,128,512]{2,1,0:T(8,128)(2,1)}, u32[]{:S(2)}, u32[]{:S(2)}) collective-permute-start(bf16[4,128,512]{2,1,0:T(8,128)(2,1)} %bitcast.40), channel_id=1, source_target_pairs={{0,4},{1,5},{2,6},{3,7},{4,0},{5,1},{6,2},{7,3},{8,12},{9,13},{10,... | collective-permute-start | bytes 1572872 | tf_op jit(solution)/shard_map/ppermute | solution.py:790
  16.4 121.7 %collective-permute-start.13 = (f32[2,2,1]{1,0,2:T(2,128)}, f32[2,2,1]{1,0,2:T(2,128)}, u32[]{:S(2)}, u32[]{:S(2)}) collective-permute-start(f32[2,2,1]{1,0,2:T(2,128)} %convert_element_type.606), channel_id=1, source_target_pairs={{0,4},{1,5},{2,6},{3,7},{4,0},{5,1},{6,2},{7,3},{8,12},{9,13},{10,... | collective-permute-start | bytes 56 | tf_op jit(solution)/shard_map/ppermute | solution.py:790
  150.5 28.5 %collective-permute-start = (bf16[320,1024]{1,0:T(8,128)(2,1)}, bf16[320,1024]{1,0:T(8,128)(2,1)S(1)}, u32[]{:S(2)}, u32[]{:S(2)}) collective-permute-start(bf16[320,1024]{1,0:T(8,128)(2,1)} %get-tuple-element.100), channel_id=1, source_target_pairs={{0,0},{1,2},{2,4},{3,6},{4,1},{5,3},{6,5},{7,7},{8,8},{9,10},{10,1... | collective-permute-start | bytes 1966088 | tf_op jit(solution)/shard_map/ppermute | solution.py:790
  154.6 26.7 %collective-permute-start.1 = (bf16[320,1024]{1,0:T(8,128)(2,1)}, bf16[320,1024]{1,0:T(8,128)(2,1)S(1)}, u32[]{:S(2)}, u32[]{:S(2)}) collective-permute-start(bf16[320,1024]{1,0:T(8,128)(2,1)} %get-tuple-element.99), channel_id=1, source_target_pairs={{0,2},{1,0},{2,6},{3,4},{4,3},{5,1},{6,7},{7,5},{8,10},{9,8},{10,1... | collective-permute-start | bytes 1966088 | tf_op jit(solution)/shard_map/ppermute | solution.py:790
  155.7 21.2 %collective-permute-start.17 = (bf16[3,2,1,32,1024]{4,3,1,0,2:T(8,128)(2,1)S(1)}, bf16[3,2,1,32,1024]{4,3,1,0,2:T(8,128)(2,1)S(1)}, u32[]{:S(2)}, u32[]{:S(2)}) collective-permute-start(bf16[3,2,1,32,1024]{4,3,1,0,2:T(8,128)(2,1)S(1)} %get-tuple-element.222), channel_id=1, source_target_pairs={{0,1},{1,0},{2,3},{3,2},{4,5},{5,4},{6,7},{7,6},{8,9},{9,8},{10,11... | collective-permute-start | bytes 1179656 | tf_op jit(solution)/shard_map/ppermute | solution.py:790
  156.7 20.3 %collective-permute-start.18 = (bf16[3,2,1,32,1024]{4,3,1,0,2:T(8,128)(2,1)S(1)}, bf16[3,2,1,32,1024]{4,3,1,0,2:T(8,128)(2,1)S(1)}, u32[]{:S(2)}, u32[]{:S(2)}) collective-permute-start(bf16[3,2,1,32,1024]{4,3,1,0,2:T(8,128)(2,1)S(1)} %get-tuple-element.222), channel_id=1, source_target_pairs={{0,2},{1,3},{2,0},{3,1},{4,6},{5,7},{6,4},{7,5},{8,10},{9,11},{10,... | collective-permute-start | bytes 1179656 | tf_op jit(solution)/shard_map/ppermute | solution.py:790
  158.4 24.2 %collective-permute-start.2 = (bf16[320,1024]{1,0:T(8,128)(2,1)S(1)}, bf16[320,1024]{1,0:T(8,128)(2,1)S(1)}, u32[]{:S(2)}, u32[]{:S(2)}) collective-permute-start(bf16[320,1024]{1,0:T(8,128)(2,1)S(1)} %get-tuple-element.98), channel_id=1, source_target_pairs={{0,4},{1,6},{2,0},{3,2},{4,5},{5,7},{6,1},{7,3},{8,12},{9,14},{10,... | collective-permute-start | bytes 1966088 | tf_op jit(solution)/shard_map/ppermute | solution.py:790
  177.0 38.8 %collective-permute-start.23 = (bf16[2,128,1408]{2,1,0:T(8,128)(2,1)S(1)}, bf16[2,128,1408]{2,1,0:T(8,128)(2,1)S(1)}, u32[]{:S(2)}, u32[]{:S(2)}) collective-permute-start(bf16[2,128,1408]{2,1,0:T(8,128)(2,1)S(1)} %bitcast.1948), channel_id=1, source_target_pairs={{0,4},{1,5},{2,6},{3,7},{4,0},{5,1},{6,2},{7,3},{8,12},{9,13},{10,... | collective-permute-start | bytes 2162696 | tf_op jit(solution)/shard_map/ppermute | solution.py:790
  179.0 31.6 %collective-permute-start.34 = (bf16[3,1,1,88,1024]{4,3,0,2,1:T(8,128)(2,1)S(1)}, bf16[3,1,1,88,1024]{4,3,0,2,1:T(8,128)(2,1)S(1)}, u32[]{:S(2)}, u32[]{:S(2)}) collective-permute-start(bf16[3,1,1,88,1024]{4,3,0,2,1:T(8,128)(2,1)S(1)} %get-tuple-element.203), channel_id=1, source_target_pairs={{0,1},{1,0},{2,3},{3,2},{4,5},{5,4},{6,7},{7,6},{8,9},{9,8},{10,11... | collective-permute-start | bytes 1622024 | tf_op jit(solution)/shard_map/ppermute | solution.py:790
  181.2 32.3 %collective-permute-start.35 = (bf16[3,1,1,88,1024]{4,3,0,2,1:T(8,128)(2,1)S(1)}, bf16[3,1,1,88,1024]{4,3,0,2,1:T(8,128)(2,1)S(1)}, u32[]{:S(2)}, u32[]{:S(2)}) collective-permute-start(bf16[3,1,1,88,1024]{4,3,0,2,1:T(8,128)(2,1)S(1)} %get-tuple-element.203), channel_id=1, source_target_pairs={{0,2},{1,3},{2,0},{3,1},{4,6},{5,7},{6,4},{7,5},{8,10},{9,11},{10,... | collective-permute-start | bytes 1622024 | tf_op jit(solution)/shard_map/ppermute | solution.py:790
  182.7 23.5 %collective-permute-start.19 = (bf16[3,2,1,16,1024]{4,3,1,0,2:T(8,128)(2,1)S(1)}, bf16[3,2,1,16,1024]{4,3,1,0,2:T(8,128)(2,1)S(1)}, u32[]{:S(2)}, u32[]{:S(2)}) collective-permute-start(bf16[3,2,1,16,1024]{4,3,1,0,2:T(8,128)(2,1)S(1)} %slice.1059), channel_id=1, source_target_pairs={{0,2},{1,3},{2,0},{3,1},{4,6},{5,7},{6,4},{7,5},{8,10},{9,11},{10,... | collective-permute-start | bytes 589832 | tf_op jit(solution)/shard_map/ppermute | solution.py:790
  207.1 31.9 %collective-permute-start.7 = (bf16[4,2,32,512]{3,2,1,0:T(8,128)(2,1)S(1)}, bf16[4,2,32,512]{3,2,1,0:T(8,128)(2,1)S(1)}, u32[]{:S(2)}, u32[]{:S(2)}) collective-permute-start(bf16[4,2,32,512]{3,2,1,0:T(8,128)(2,1)S(1)} %copy_bitcast_fusion.13), channel_id=1, source_target_pairs={{0,16},{1,17},{2,18},{3,19},{4,20},{5,21},{6,22},{7,23},{8,24},{9,... | collective-permute-start | bytes 786440 | tf_op jit(solution)/shard_map/ppermute | solution.py:790
  210.6 28.4 %collective-permute-start.8 = (bf16[4,2,32,512]{3,2,1,0:T(8,128)(2,1)S(1)}, bf16[4,2,32,512]{3,2,1,0:T(8,128)(2,1)S(1)}, u32[]{:S(2)}, u32[]{:S(2)}) collective-permute-start(bf16[4,2,32,512]{3,2,1,0:T(8,128)(2,1)S(1)} %copy_bitcast_fusion.13), channel_id=1, source_target_pairs={{0,24},{1,25},{2,26},{3,27},{4,28},{5,29},{6,30},{7,31},{8,0},{9,1... | collective-permute-start | bytes 786440 | tf_op jit(solution)/shard_map/ppermute | solution.py:790
  213.5 30.0 %collective-permute-start.36 = (bf16[3,1,1,44,1024]{4,3,0,2,1:T(8,128)(2,1)S(1)}, bf16[3,1,1,44,1024]{4,3,0,2,1:T(8,128)(2,1)S(1)}, u32[]{:S(2)}, u32[]{:S(2)}) collective-permute-start(bf16[3,1,1,44,1024]{4,3,0,2,1:T(8,128)(2,1)S(1)} %slice.1108), channel_id=1, source_target_pairs={{0,2},{1,3},{2,0},{3,1},{4,6},{5,7},{6,4},{7,5},{8,10},{9,11},{10,... | collective-permute-start | bytes 811016 | tf_op jit(solution)/shard_map/ppermute | solution.py:790
  215.8 27.8 %collective-permute-start.37 = (bf16[3,1,1,44,1024]{4,3,0,2,1:T(8,128)(2,1)S(1)}, bf16[3,1,1,44,1024]{4,3,0,2,1:T(8,128)(2,1)S(1)}, u32[]{:S(2)}, u32[]{:S(2)}) collective-permute-start(bf16[3,1,1,44,1024]{4,3,0,2,1:T(8,128)(2,1)S(1)} %slice.1109), channel_id=1, source_target_pairs={{0,1},{1,0},{2,3},{3,2},{4,5},{5,4},{6,7},{7,6},{8,9},{9,8},{10,11... | collective-permute-start | bytes 811016 | tf_op jit(solution)/shard_map/ppermute | solution.py:790
  217.8 44.6 %collective-permute-start.24 = (bf16[2,2,32,1408]{3,2,1,0:T(8,128)(2,1)S(1)}, bf16[2,2,32,1408]{3,2,1,0:T(8,128)(2,1)S(1)}, u32[]{:S(2)}, u32[]{:S(2)}) collective-permute-start(bf16[2,2,32,1408]{3,2,1,0:T(8,128)(2,1)S(1)} %copy_bitcast_fusion.12), channel_id=1, source_target_pairs={{0,8},{1,9},{2,10},{3,11},{4,12},{5,13},{6,14},{7,15},{8,16},{9,17... | collective-permute-start | bytes 1081352 | tf_op jit(solution)/shard_map/ppermute | solution.py:790
  239.1 23.4 %collective-permute-start.25 = (bf16[2,2,32,1408]{3,2,1,0:T(8,128)(2,1)S(1)}, bf16[2,2,32,1408]{3,2,1,0:T(8,128)(2,1)S(1)}, u32[]{:S(2)}, u32[]{:S(2)}) collective-permute-start(bf16[2,2,32,1408]{3,2,1,0:T(8,128)(2,1)S(1)} %copy_bitcast_fusion.12), channel_id=1, source_target_pairs={{0,16},{1,17},{2,18},{3,19},{4,20},{5,21},{6,22},{7,23},{8,24},{9,... | collective-permute-start | bytes 1081352 | tf_op jit(solution)/shard_map/ppermute | solution.py:790
  239.1 23.4 %collective-permute-start.26 = (bf16[2,2,32,1408]{3,2,1,0:T(8,128)(2,1)S(1)}, bf16[2,2,32,1408]{3,2,1,0:T(8,128)(2,1)S(1)}, u32[]{:S(2)}, u32[]{:S(2)}) collective-permute-start(bf16[2,2,32,1408]{3,2,1,0:T(8,128)(2,1)S(1)} %copy_bitcast_fusion.12), channel_id=1, source_target_pairs={{0,24},{1,25},{2,26},{3,27},{4,28},{5,29},{6,30},{7,31},{8,0},{9,1... | collective-permute-start | bytes 1081352 | tf_op jit(solution)/shard_map/ppermute | solution.py:790
  262.4 52.3 %collective-permute-start.4 = (bf16[4,320,1024]{2,1,0:T(8,128)(2,1)S(1)}, bf16[4,320,1024]{2,1,0:T(8,128)(2,1)S(1)}, u32[]{:S(2)}, u32[]{:S(2)}) collective-permute-start(bf16[4,320,1024]{2,1,0:T(8,128)(2,1)S(1)} %pad_maximum_fusion.4), channel_id=1, source_target_pairs={{0,4},{1,5},{2,6},{3,7},{4,0},{5,1},{6,2},{7,3},{8,12},{9,13},{10,... | collective-permute-start | bytes 7864328 | tf_op jit(solution)/shard_map/ppermute | solution.py:790
  262.6 28.7 %collective-permute-start.27 = (bf16[3,2,2,32,1408]{4,3,2,1,0:T(8,128)(2,1)S(1)}, bf16[3,2,2,32,1408]{4,3,2,1,0:T(8,128)(2,1)S(1)}, u32[]{:S(2)}, u32[]{:S(2)}) collective-permute-start(bf16[3,2,2,32,1408]{4,3,2,1,0:T(8,128)(2,1)S(1)} %get-tuple-element.131), channel_id=1, source_target_pairs={{0,1},{1,0},{2,3},{3,2},{4,5},{5,4},{6,7},{7,6},{8,9},{9,8},{10,11... | collective-permute-start | bytes 3244040 | tf_op jit(solution)/shard_map/ppermute | solution.py:790
  264.6 28.5 %collective-permute-start.28 = (bf16[3,2,2,32,1408]{4,3,2,1,0:T(8,128)(2,1)S(1)}, bf16[3,2,2,32,1408]{4,3,2,1,0:T(8,128)(2,1)S(1)}, u32[]{:S(2)}, u32[]{:S(2)}) collective-permute-start(bf16[3,2,2,32,1408]{4,3,2,1,0:T(8,128)(2,1)S(1)} %get-tuple-element.131), channel_id=1, source_target_pairs={{0,2},{1,3},{2,0},{3,1},{4,6},{5,7},{6,4},{7,5},{8,10},{9,11},{10,... | collective-permute-start | bytes 3244040 | tf_op jit(solution)/shard_map/ppermute | solution.py:790
  421.4 66.5 %collective-permute-start.43 = (bf16[1024,1024]{1,0:T(8,128)(2,1)S(1)}, bf16[1024,1024]{1,0:T(8,128)(2,1)S(1)}, u32[]{:S(2)}, u32[]{:S(2)}) collective-permute-start(bf16[1024,1024]{1,0:T(8,128)(2,1)S(1)} %add_convert_fusion.1), channel_id=1, source_target_pairs={{0,4},{1,5},{2,6},{3,7},{4,0},{5,1},{6,2},{7,3},{8,12},{9,13},{10,... | collective-permute-start | bytes 6291464 | tf_op jit(solution)/shard_map/ppermute | solution.py:790
  431.6 51.0 %collective-permute-start.72 = (bf16[2,2,2,2,32,1408]{5,4,3,2,1,0:T(8,128)(2,1)S(1)}, bf16[2,2,2,2,32,1408]{5,4,3,2,1,0:T(8,128)(2,1)S(1)}, u32[]{:S(2)}, u32[]{:S(2)}) collective-permute-start(bf16[2,2,2,2,32,1408]{5,4,3,2,1,0:T(8,128)(2,1)S(1)} %fusion.33), channel_id=1, source_target_pairs={{0,2},{1,3},{2,0},{3,1},{4,6},{5,7},{6,4},{7,5},{8,10},{9,11},{10,... | collective-permute-start | bytes 4325384 | tf_op jit(solution)/shard_map/ppermute | solution.py:790
  433.9 37.5 %collective-permute-start.40 = (bf16[128,1024]{1,0:T(8,128)(2,1)S(1)}, bf16[128,1024]{1,0:T(8,128)(2,1)S(1)}, u32[]{:S(2)}, u32[]{:S(2)}) collective-permute-start(bf16[128,1024]{1,0:T(8,128)(2,1)S(1)} %get-tuple-element.152), channel_id=1, source_target_pairs={{0,1},{1,5},{2,0},{3,4},{4,3},{5,7},{6,2},{7,6},{8,9},{9,13},{10,8... | collective-permute-start | bytes 786440 | tf_op jit(solution)/shard_map/ppermute | solution.py:790
  437.2 47.7 %collective-permute-start.70 = (bf16[2,2,2,2,32,1408]{5,4,2,1,0,3:T(8,128)(2,1)S(1)}, bf16[2,2,2,2,32,1408]{5,4,2,1,0,3:T(8,128)(2,1)S(1)}, u32[]{:S(2)}, u32[]{:S(2)}) collective-permute-start(bf16[2,2,2,2,32,1408]{5,4,2,1,0,3:T(8,128)(2,1)S(1)} %bitcast.1915), channel_id=1, source_target_pairs={{0,1},{1,0},{2,3},{3,2},{4,5},{5,4},{6,7},{7,6},{8,9},{9,8},{10,11... | collective-permute-start | bytes 4325384 | tf_op jit(solution)/shard_map/ppermute | solution.py:790
  438.0 38.8 %collective-permute-start.41 = (bf16[128,1024]{1,0:T(8,128)(2,1)S(1)}, bf16[128,1024]{1,0:T(8,128)(2,1)S(1)}, u32[]{:S(2)}, u32[]{:S(2)}) collective-permute-start(bf16[128,1024]{1,0:T(8,128)(2,1)S(1)} %get-tuple-element.151), channel_id=1, source_target_pairs={{0,2},{1,6},{2,3},{3,7},{4,0},{5,4},{6,1},{7,5},{8,10},{9,14},{10,... | collective-permute-start | bytes 786440 | tf_op jit(solution)/shard_map/ppermute | solution.py:790
  484.0 49.0 %collective-permute-start.73 = (bf16[2,2,2,32,1408]{4,3,2,1,0:T(8,128)(2,1)}, bf16[2,2,2,32,1408]{4,3,2,1,0:T(8,128)(2,1)}, u32[]{:S(2)}, u32[]{:S(2)}) collective-permute-start(bf16[2,2,2,32,1408]{4,3,2,1,0:T(8,128)(2,1)} %dynamic-slice_bitcast_fusion.3), channel_id=1, source_target_pairs={{0,1},{1,0},{2,3},{3,2},{4,5},{5,4},{6,7},{7,6},{8,9},{9,8},{10,11... | collective-permute-start | bytes 2162696 | tf_op jit(solution)/shard_map/ppermute | solution.py:790
  486.2 48.1 %collective-permute-start.71 = (bf16[2,2,2,32,1408]{4,3,2,1,0:T(8,128)(2,1)}, bf16[2,2,2,32,1408]{4,3,2,1,0:T(8,128)(2,1)}, u32[]{:S(2)}, u32[]{:S(2)}) collective-permute-start(bf16[2,2,2,32,1408]{4,3,2,1,0:T(8,128)(2,1)} %dynamic-slice_bitcast_fusion.4), channel_id=1, source_target_pairs={{0,2},{1,3},{2,0},{3,1},{4,6},{5,7},{6,4},{7,5},{8,10},{9,11},{10,... | collective-permute-start | bytes 2162696 | tf_op jit(solution)/shard_map/ppermute | solution.py:790
  503.0 85.0 %collective-permute-start.80 = (bf16[1,2,1,2,88,1024]{5,4,1,3,2,0:T(8,128)(2,1)}, bf16[1,2,1,2,88,1024]{5,4,1,3,2,0:T(8,128)(2,1)}, u32[]{:S(2)}, u32[]{:S(2)}) collective-permute-start(bf16[1,2,1,2,88,1024]{5,4,1,3,2,0:T(8,128)(2,1)} %bitcast.1656), channel_id=1, source_target_pairs={{0,2},{1,3},{2,0},{3,1},{4,6},{5,7},{6,4},{7,5},{8,10},{9,11},{10,... | collective-permute-start | bytes 2162696 | tf_op jit(solution)/shard_map/ppermute | solution.py:790
  505.3 88.7 %collective-permute-start.78 = (bf16[1,2,1,2,88,1024]{5,4,1,3,2,0:T(8,128)(2,1)}, bf16[1,2,1,2,88,1024]{5,4,1,3,2,0:T(8,128)(2,1)}, u32[]{:S(2)}, u32[]{:S(2)}) collective-permute-start(bf16[1,2,1,2,88,1024]{5,4,1,3,2,0:T(8,128)(2,1)} %bitcast.1657), channel_id=1, source_target_pairs={{0,1},{1,0},{2,3},{3,2},{4,5},{5,4},{6,7},{7,6},{8,9},{9,8},{10,11... | collective-permute-start | bytes 2162696 | tf_op jit(solution)/shard_map/ppermute | solution.py:790
  536.2 20.5 %collective-permute-start.74 = (bf16[2,2,32,1408]{3,2,1,0:T(8,128)(2,1)S(1)}, bf16[2,2,32,1408]{3,2,1,0:T(8,128)(2,1)S(1)}, u32[]{:S(2)}, u32[]{:S(2)}) collective-permute-start(bf16[2,2,32,1408]{3,2,1,0:T(8,128)(2,1)S(1)} %get-tuple-element.111), channel_id=1, source_target_pairs={{0,8},{1,9},{2,10},{3,11},{4,12},{5,13},{6,14},{7,15},{8,16},{9,17... | collective-permute-start | bytes 1081352 | tf_op jit(solution)/shard_map/ppermute | solution.py:790
  547.7 22.0 %collective-permute-start.75 = (bf16[2,2,32,1408]{3,2,1,0:T(8,128)(2,1)S(1)}, bf16[2,2,32,1408]{3,2,1,0:T(8,128)(2,1)S(1)}, u32[]{:S(2)}, u32[]{:S(2)}) collective-permute-start(bf16[2,2,32,1408]{3,2,1,0:T(8,128)(2,1)S(1)} %get-tuple-element.112), channel_id=1, source_target_pairs={{0,16},{1,17},{2,18},{3,19},{4,20},{5,21},{6,22},{7,23},{8,24},{9,... | collective-permute-start | bytes 1081352 | tf_op jit(solution)/shard_map/ppermute | solution.py:790
  548.3 21.4 %collective-permute-start.76 = (bf16[2,2,32,1408]{3,2,1,0:T(8,128)(2,1)S(1)}, bf16[2,2,32,1408]{3,2,1,0:T(8,128)(2,1)S(1)}, u32[]{:S(2)}, u32[]{:S(2)}) collective-permute-start(bf16[2,2,32,1408]{3,2,1,0:T(8,128)(2,1)S(1)} %get-tuple-element.113), channel_id=1, source_target_pairs={{0,24},{1,25},{2,26},{3,27},{4,28},{5,29},{6,30},{7,31},{8,0},{9,1... | collective-permute-start | bytes 1081352 | tf_op jit(solution)/shard_map/ppermute | solution.py:790
  556.7 73.5 %collective-permute-start.44 = (bf16[1024,1024]{1,0:T(8,128)(2,1)S(1)}, bf16[1024,1024]{1,0:T(8,128)(2,1)}, u32[]{:S(2)}, u32[]{:S(2)}) collective-permute-start(bf16[1024,1024]{1,0:T(8,128)(2,1)S(1)} %convolution_convert_fusion.3), channel_id=1, source_target_pairs={{0,4},{1,5},{2,6},{3,7},{4,0},{5,1},{6,2},{7,3},{8,12},{9,13},{10,... | collective-permute-start | bytes 6291464 | tf_op jit(solution)/shard_map/ppermute | solution.py:790
  574.8 21.0 %collective-permute-start.52 = (bf16[64,1024]{1,0:T(8,128)(2,1)}, bf16[64,1024]{1,0:T(8,128)(2,1)}, u32[]{:S(2)}, u32[]{:S(2)}) collective-permute-start(bf16[64,1024]{1,0:T(8,128)(2,1)} %get-tuple-element.220), channel_id=1, source_target_pairs={{0,1},{1,5},{2,0},{3,4},{4,3},{5,7},{6,2},{7,6},{8,9},{9,13},{10,8... | collective-permute-start | bytes 393224 | tf_op jit(solution)/shard_map/ppermute | solution.py:790
  676.8 66.5 %collective-permute-start.57 = (bf16[4,2,2,2,32,512]{5,4,3,2,1,0:T(8,128)(2,1)}, bf16[4,2,2,2,32,512]{5,4,3,2,1,0:T(8,128)(2,1)}, u32[]{:S(2)}, u32[]{:S(2)}) collective-permute-start(bf16[4,2,2,2,32,512]{5,4,3,2,1,0:T(8,128)(2,1)} %dynamic-slice_bitcast_fusion), channel_id=1, source_target_pairs={{0,2},{1,3},{2,0},{3,1},{4,6},{5,7},{6,4},{7,5},{8,10},{9,11},{10,... | collective-permute-start | bytes 3145736 | tf_op jit(solution)/shard_map/ppermute | solution.py:790
  678.4 34.8 %collective-permute-start.65 = (bf16[2,2,1,2,32,1024]{5,4,0,1,3,2:T(8,128)(2,1)S(1)}, bf16[2,2,1,2,32,1024]{5,4,0,1,3,2:T(8,128)(2,1)S(1)}, u32[]{:S(2)}, u32[]{:S(2)}) collective-permute-start(bf16[2,2,1,2,32,1024]{5,4,0,1,3,2:T(8,128)(2,1)S(1)} %bitcast.1951), channel_id=1, source_target_pairs={{0,2},{1,3},{2,0},{3,1},{4,6},{5,7},{6,4},{7,5},{8,10},{9,11},{10,... | collective-permute-start | bytes 1572872 | tf_op jit(solution)/shard_map/ppermute | solution.py:790
  679.0 37.4 %collective-permute-start.63 = (bf16[2,2,1,2,32,1024]{5,4,0,1,3,2:T(8,128)(2,1)S(1)}, bf16[2,2,1,2,32,1024]{5,4,0,1,3,2:T(8,128)(2,1)S(1)}, u32[]{:S(2)}, u32[]{:S(2)}) collective-permute-start(bf16[2,2,1,2,32,1024]{5,4,0,1,3,2:T(8,128)(2,1)S(1)} %bitcast.1950), channel_id=1, source_target_pairs={{0,1},{1,0},{2,3},{3,2},{4,5},{5,4},{6,7},{7,6},{8,9},{9,8},{10,11... | collective-permute-start | bytes 1572872 | tf_op jit(solution)/shard_map/ppermute | solution.py:790
  723.2 23.9 %collective-permute-start.45 = (bf16[4,128,1024]{2,1,0:T(8,128)(2,1)}, bf16[4,128,1024]{2,1,0:T(8,128)(2,1)}, u32[]{:S(2)}, u32[]{:S(2)}) collective-permute-start(bf16[4,128,1024]{2,1,0:T(8,128)(2,1)} %dynamic-slice_bitcast_fusion.1), channel_id=1, source_target_pairs={{0,4},{1,5},{2,6},{3,7},{4,0},{5,1},{6,2},{7,3},{8,12},{9,13},{10,... | collective-permute-start | bytes 3145736 | tf_op jit(solution)/shard_map/ppermute | solution.py:790
  738.9 26.2 %collective-permute-start.55 = (bf16[4,2,2,2,32,512]{5,4,2,1,0,3:T(8,128)(2,1)S(1)}, bf16[4,2,2,2,32,512]{5,4,2,1,0,3:T(8,128)(2,1)S(1)}, u32[]{:S(2)}, u32[]{:S(2)}) collective-permute-start(bf16[4,2,2,2,32,512]{5,4,2,1,0,3:T(8,128)(2,1)S(1)} %bitcast.1937), channel_id=1, source_target_pairs={{0,1},{1,0},{2,3},{3,2},{4,5},{5,4},{6,7},{7,6},{8,9},{9,8},{10,11... | collective-permute-start | bytes 3145736 | tf_op jit(solution)/shard_map/ppermute | solution.py:790
  746.8 84.8 %collective-permute-start.58 = (bf16[4,2,2,32,512]{4,3,2,1,0:T(8,128)(2,1)}, bf16[4,2,2,32,512]{4,3,2,1,0:T(8,128)(2,1)}, u32[]{:S(2)}, u32[]{:S(2)}) collective-permute-start(bf16[4,2,2,32,512]{4,3,2,1,0:T(8,128)(2,1)} %dynamic-slice_bitcast_fusion.9), channel_id=1, source_target_pairs={{0,1},{1,0},{2,3},{3,2},{4,5},{5,4},{6,7},{7,6},{8,9},{9,8},{10,11... | collective-permute-start | bytes 1572872 | tf_op jit(solution)/shard_map/ppermute | solution.py:790
  752.8 77.4 %collective-permute-start.47 = (bf16[128,1024]{1,0:T(8,128)(2,1)}, bf16[128,1024]{1,0:T(8,128)(2,1)}, u32[]{:S(2)}, u32[]{:S(2)}) collective-permute-start(bf16[128,1024]{1,0:T(8,128)(2,1)} %get-tuple-element.144), channel_id=1, source_target_pairs={{0,1},{1,5},{2,0},{3,4},{4,3},{5,7},{6,2},{7,6},{8,9},{9,13},{10,8... | collective-permute-start | bytes 786440 | tf_op jit(solution)/shard_map/ppermute | solution.py:790
  755.6 74.6 %collective-permute-start.48 = (bf16[128,1024]{1,0:T(8,128)(2,1)}, bf16[128,1024]{1,0:T(8,128)(2,1)}, u32[]{:S(2)}, u32[]{:S(2)}) collective-permute-start(bf16[128,1024]{1,0:T(8,128)(2,1)} %get-tuple-element.143), channel_id=1, source_target_pairs={{0,2},{1,6},{2,3},{3,7},{4,0},{5,4},{6,1},{7,5},{8,10},{9,14},{10,... | collective-permute-start | bytes 786440 | tf_op jit(solution)/shard_map/ppermute | solution.py:790
  765.1 65.1 %collective-permute-start.49 = (bf16[128,1024]{1,0:T(8,128)(2,1)S(1)}, bf16[128,1024]{1,0:T(8,128)(2,1)}, u32[]{:S(2)}, u32[]{:S(2)}) collective-permute-start(bf16[128,1024]{1,0:T(8,128)(2,1)S(1)} %get-tuple-element.142), channel_id=1, source_target_pairs={{0,3},{1,7},{2,2},{3,6},{4,1},{5,5},{6,0},{7,4},{8,11},{9,15},{10,... | collective-permute-start | bytes 786440 | tf_op jit(solution)/shard_map/ppermute | solution.py:790
  768.6 64.3 %collective-permute-start.56 = (bf16[4,2,2,32,512]{4,3,2,1,0:T(8,128)(2,1)S(1)}, bf16[4,2,2,32,512]{4,3,2,1,0:T(8,128)(2,1)S(1)}, u32[]{:S(2)}, u32[]{:S(2)}) collective-permute-start(bf16[4,2,2,32,512]{4,3,2,1,0:T(8,128)(2,1)S(1)} %dynamic-slice_bitcast_fusion.10), channel_id=1, source_target_pairs={{0,2},{1,3},{2,0},{3,1},{4,6},{5,7},{6,4},{7,5},{8,10},{9,11},{10,... | collective-permute-start | bytes 1572872 | tf_op jit(solution)/shard_map/ppermute | solution.py:790
  (131 other events, 2643.8 us)

commit v2 on v1

--- a/solution.py
+++ b/solution.py
@@ -768,119 +768,565 @@
     return lax.dynamic_index_in_dim(array, index, axis, keepdims=False)
 
 
-class Plane:
-    def __init__(self, dp, seq):
-        self.depth = dp // 2
-        self.seq = seq
+MESH = pl.DeviceIdType.MESH
+
+
+class Spot:
+    def __init__(self, depth):
+        self.depth = depth
         place = lax.axis_index("dp")
+        self.corner = lax.axis_index("seq")
         self.z, self.core = place // 2, place % 2
-        self.corner = lax.axis_index("seq")
         self.y, self.x = self.corner // 2, self.corner % 2
 
-    def move(self, array, where):
-        pairs = []
-        for z in range(self.depth):
-            for core in range(2):
-                for y in range(2):
-                    for x in range(2):
-                        z2, core2, y2, x2 = where(z, core, y, x)
-                        source = (z * 2 + core) * self.seq + y * 2 + x
-                        target = (z2 * 2 + core2) * self.seq + y2 * 2 + x2
-                        pairs.append((source, target))
-        return lax.ppermute(array, ("dp", "seq"), pairs)
-
-    def swap_core(self, array):
-        return self.move(array, lambda z, c, y, x: (z, 1 - c, y, x))
-
-    def swap_x(self, array):
-        return self.move(array, lambda z, c, y, x: (z, c, y, 1 - x))
-
-    def swap_y(self, array):
-        return self.move(array, lambda z, c, y, x: (z, c, 1 - y, x))
-
-    def shift_z(self, array, step):
-        return self.move(array, lambda z, c, y, x: ((z + step) % self.depth, c, y, x))
-
-    def collect(self, parcel):
-        received = []
-        for up in range(2):
-            for across in range(2):
-                piece = parcel.reshape((4,) + parcel.shape[2:])
-                piece = pick(piece, (self.x ^ across) * 2 + (self.y ^ up))
-                received.append(
-                    self.move(piece, lambda z, c, y, x, up=up, across=across: (z, y ^ up, x ^ across, c))
-                )
-        mine = jnp.stack(received)
-        both = jnp.concatenate([mine, self.swap_core(mine)])
-        pieces = []
-        for block in range(4):
-            for half in range(2):
-                index = 2 * (half ^ (block >> 1)) + (self.y ^ (block & 1))
-                pieces.append(pick(both, index + jnp.where(half == self.core, 0, 4)))
-        return jnp.stack(pieces).reshape((4, 2) + parcel.shape[2:])
-
-    def deliver(self, pieces):
-        received = []
-        for up in range(2):
-            for across in range(2):
-                piece = pick(pieces, 2 * (self.core ^ up) + (self.y ^ across))
-                received.append(
-                    self.move(piece, lambda z, k, Y, X, up=up, across=across: (z, X, k ^ up, Y ^ across))
-                )
-        stacked = jnp.stack(received)
-        homes = []
-        for micro in range(2):
-            for half in range(2):
-                homes.append(pick(stacked, 2 * (self.y ^ half) + (self.x ^ micro)))
-        return jnp.stack(homes).reshape((2, 2) + pieces.shape[1:])
-
-    def gather(self, shard):
-        quarter = pick(shard, self.corner, 2)
-        others = jnp.stack([self.shift_z(quarter, step) for step in range(1, self.depth)])
-        beside = self.swap_x(others)
-        below = self.swap_y(others)
-        middle = shard.shape[0]
-        near = self.swap_y(beside[..., : shard.shape[3] // 2, :])
-        far = self.swap_x(below[..., shard.shape[3] // 2 :, :])
-        diagonal = jnp.concatenate([near, far], axis=-2)
-        pieces = jnp.stack([others, beside, below, diagonal])
-        wholes = []
-        for matrix in range(middle):
-            blocks = []
-            for z in range(self.depth):
-                step = (self.z - z + self.depth) % self.depth
-                for part in range(4):
-                    away = pick(pick(pieces[:, :, matrix], self.corner ^ part), jnp.maximum(step - 1, 0))
-                    blocks.append(jnp.where(step == 0, shard[matrix, :, part], away))
-            whole = jnp.stack(blocks).reshape((self.depth, 4) + shard.shape[1:2] + shard.shape[3:])
-            whole = jnp.swapaxes(whole, 1, 2)
-            wholes.append(whole.reshape(-1, shard.shape[-1]))
-        return wholes
-
-    def scatter(self, wholes, lanes):
-        shape = (self.depth, lanes, 2, 2, wholes[0].shape[0] // (self.depth * lanes * 4), wholes[0].shape[1])
-        grads = jnp.stack([whole.reshape(shape) for whole in wholes])
-        half = self.depth // 2
-        low, high = grads[:, :half], grads[:, half:]
-        wide = lambda a: a.astype(jnp.float32)
-        low_got = self.swap_x(pick(low, 1 - self.x, 4))
-        high_got = self.swap_y(pick(high, 1 - self.y, 3))
-        low = (wide(pick(low, self.x, 4)) + wide(low_got)).astype(jnp.bfloat16)
-        high = (wide(pick(high, self.y, 3)) + wide(high_got)).astype(jnp.bfloat16)
-        low_got = self.swap_y(pick(low, 1 - self.y, 3))
-        high_got = self.swap_x(pick(high, 1 - self.x, 3))
-        low = (wide(pick(low, self.y, 3)) + wide(low_got)).astype(jnp.bfloat16)
-        high = (wide(pick(high, self.x, 3)) + wide(high_got)).astype(jnp.bfloat16)
-        column = jnp.concatenate([low, high], axis=1)
-        total = wide(pick(column, self.z, 1))
+    def at(self, z=None, core=None, y=None, x=None):
+        z = self.z if z is None else z
+        core = self.core if core is None else core
+        y = self.y if y is None else y
+        x = self.x if x is None else x
+        return (z * 2 + core, y * 2 + x)
+
+    def beside(self):
+        return self.at(x=1 - self.x)
+
+    def below(self):
+        return self.at(y=1 - self.y)
+
+    def sibling(self):
+        return self.at(core=1 - self.core)
+
+    def greet(self):
+        barrier = pltpu.get_barrier_semaphore()
+        others = [
+            self.at(None, self.core ^ (i >> 2), self.y ^ (i >> 1 & 1), self.x ^ (i & 1)) for i in range(1, 8)
+        ]
         for step in range(1, self.depth):
-            total = total + wide(self.shift_z(pick(column, (self.z + step) % self.depth, 1), step))
-        return total
-
-
-def parity_columns(weight, core):
+            for flip in range(2):
+                others.append(self.at((self.z + step) % self.depth, self.core ^ flip))
+        for other in others:
+            pl.semaphore_signal(barrier, inc=1, device_id=other, device_id_type=MESH)
+        pl.semaphore_wait(barrier, len(others))
+
+
+class Wires:
+    def __init__(self, sends, arrivals, moves):
+        self.sends, self.arrivals, self.moves = sends, arrivals, moves
+        self.count = 0
+        self.moved = 0
+        self.open = []
+
+    def take(self, number):
+        first = self.count
+        self.count += number
+        return first
+
+    def send(self, source, target, device, index, landing=None):
+        landing = index if landing is None else landing
+        copy = pltpu.make_async_remote_copy(
+            src_ref=source,
+            dst_ref=target,
+            send_sem=self.sends.at[index],
+            recv_sem=self.arrivals.at[landing],
+            device_id=device,
+            device_id_type=MESH,
+        )
+        copy.start()
+        self.open.append(copy)
+        return copy
+
+    def arrive(self, target, device, index):
+        pltpu.make_async_remote_copy(
+            src_ref=target,
+            dst_ref=target,
+            send_sem=self.sends.at[0],
+            recv_sem=self.arrivals.at[index],
+            device_id=device,
+            device_id_type=MESH,
+        ).wait_recv()
+
+    def move(self, source, target):
+        copy = pltpu.make_async_copy(source, target, self.moves.at[self.moved])
+        self.moved += 1
+        copy.start()
+        return copy
+
+    def close(self):
+        for copy in self.open:
+            copy.wait_send()
+        self.open = []
+
+
+def collect_tokens(spot, wires, parcel, whole):
+    away = wires.take(4)
+    over = wires.take(4)
+    local = wires.moved
+    wires.moved += 1
+    for index in range(4):
+        half, micro = spot.y ^ (index >> 1), spot.x ^ (index & 1)
+        home = (half == spot.core) & (micro == spot.y) & (spot.core == spot.x)
+        source = parcel.at[micro, half]
+        target = whole.at[spot.corner, half]
+        copy = pltpu.make_async_remote_copy(
+            src_ref=source,
+            dst_ref=target,
+            send_sem=wires.sends.at[away + index],
+            recv_sem=wires.arrivals.at[away + index],
+            device_id=spot.at(core=half, y=micro, x=spot.core),
+            device_id_type=MESH,
+        )
+        here = pltpu.make_async_copy(source, target, wires.moves.at[local])
+
+        @pl.when(jnp.logical_not(home))
+        def _():
+            copy.start()
+
+        @pl.when(home)
+        def _():
+            here.start()
+
+    yield
+    for index in range(4):
+        block = 2 * (spot.core ^ (index >> 1)) + (spot.y ^ (index & 1))
+        home = (spot.x == spot.core) & (block == spot.corner)
+        piece = whole.at[block, spot.core]
+        here = pltpu.make_async_copy(piece, piece, wires.moves.at[local])
+        landed = pltpu.make_async_remote_copy(
+            src_ref=piece,
+            dst_ref=piece,
+            send_sem=wires.sends.at[away + index],
+            recv_sem=wires.arrivals.at[away + index],
+            device_id=spot.sibling(),
+            device_id_type=MESH,
+        )
+
+        @pl.when(jnp.logical_not(home))
+        def _():
+            landed.wait_recv()
+
+        @pl.when(home)
+        def _():
+            here.wait()
+
+        wires.send(piece, piece, spot.sibling(), over + index)
+    yield
+    for index in range(4):
+        block = 2 * ((1 - spot.core) ^ (index >> 1)) + (spot.y ^ (index & 1))
+        wires.arrive(whole.at[block, 1 - spot.core], spot.sibling(), over + index)
+    for index in range(4):
+        half, micro = spot.y ^ (index >> 1), spot.x ^ (index & 1)
+        home = (half == spot.core) & (micro == spot.y) & (spot.core == spot.x)
+        source = parcel.at[micro, half]
+
+        @pl.when(jnp.logical_not(home))
+        def _():
+            pltpu.make_async_remote_copy(
+                src_ref=source,
+                dst_ref=source,
+                send_sem=wires.sends.at[away + index],
+                recv_sem=wires.arrivals.at[away + index],
+                device_id=spot.sibling(),
+                device_id_type=MESH,
+            ).wait_send()
+
+    yield
+
+
+def deliver_tokens(spot, wires, pieces, homes):
+    away = wires.take(4)
+    local = wires.moved
+    wires.moved += 1
+
+    def parts():
+        for index in range(4):
+            block = 2 * (spot.core ^ (index >> 1)) + (spot.y ^ (index & 1))
+            home = (spot.x == spot.core) & (block == spot.corner)
+            source = pieces.at[block]
+            target = homes.at[spot.y, spot.core]
+            remote = pltpu.make_async_remote_copy(
+                src_ref=source,
+                dst_ref=target,
+                send_sem=wires.sends.at[away + index],
+                recv_sem=wires.arrivals.at[away + index],
+                device_id=spot.at(core=spot.x, y=block // 2, x=block % 2),
+                device_id_type=MESH,
+            )
+            yield home, remote, pltpu.make_async_copy(source, target, wires.moves.at[local])
+
+    for home, remote, here in parts():
+        pl.when(jnp.logical_not(home))(remote.start)
+        pl.when(home)(here.start)
+    yield
+    for index in range(4):
+        half, micro = spot.y ^ (index >> 1), spot.x ^ (index & 1)
+        home = (half == spot.core) & (micro == spot.y) & (spot.core == spot.x)
+        piece = homes.at[micro, half]
+        landed = pltpu.make_async_remote_copy(
+            src_ref=piece,
+            dst_ref=piece,
+            send_sem=wires.sends.at[away + index],
+            recv_sem=wires.arrivals.at[away + index],
+            device_id=spot.sibling(),
+            device_id_type=MESH,
+        )
+        here = pltpu.make_async_copy(piece, piece, wires.moves.at[local])
+        pl.when(jnp.logical_not(home))(landed.wait_recv)
+        pl.when(home)(here.wait)
+    for home, remote, here in parts():
+        pl.when(jnp.logical_not(home))(remote.wait_send)
+    yield
+
+
+def gather_small(spot, wires, block, whole):
+    own = wires.move(block, whole.at[spot.z, spot.core, spot.corner])
+    first = wires.take(spot.depth + 3)
+    for step in range(1, spot.depth):
+        target = whole.at[spot.z, spot.core, spot.corner]
+        wires.send(block, target, spot.at(z=(spot.z + step) % spot.depth), first + step)
+    yield
+    own.wait()
+    for step in range(1, spot.depth):
+        z = (spot.z - step + spot.depth) % spot.depth
+        wires.arrive(whole.at[z, spot.core, spot.corner], spot.sibling(), first + step)
+    column = whole.at[:, spot.core, spot.corner]
+    wires.send(column, column, spot.beside(), first)
+    wires.send(column, column, spot.below(), first + spot.depth)
+    wires.send(column, column, spot.at(y=1 - spot.y, x=1 - spot.x), first + spot.depth + 1)
+    yield
+    for flip, index in ((1, first), (2, first + spot.depth), (3, first + spot.depth + 1)):
+        wires.arrive(whole.at[:, spot.core, spot.corner ^ flip], spot.sibling(), index)
+    plane = whole.at[:, spot.core]
+    wires.send(plane, plane, spot.sibling(), first + spot.depth + 2)
+    yield
+    wires.arrive(whole.at[:, 1 - spot.core], spot.sibling(), first + spot.depth + 2)
+    yield
+
+
+def gather_columns(spot, wires, pack, whole):
+    depth, me = spot.depth, spot.corner
+    ahead = wires.take(2 * depth)
+    flat = wires.take(4 * depth)
+    own = wires.move(pack.at[spot.core], whole.at[spot.z, spot.core])
+    for step in range(1, depth):
+        for flip in range(2):
+            wires.send(
+                pack.at[spot.core ^ flip, me],
+                whole.at[spot.z, spot.core, me],
+                spot.at((spot.z + step) % depth, spot.core ^ flip),
+                ahead + 2 * step + flip,
+            )
+    wires.send(pack.at[1 - spot.core], whole.at[spot.z, spot.core], spot.sibling(), ahead)
+    yield
+    for step in range(1, depth):
+        z = (spot.z - step + depth) % depth
+        for flip in range(2):
+            wires.arrive(whole.at[z, spot.core ^ flip, me], spot.sibling(), ahead + 2 * step + flip)
+        quarter = whole.at[z, :, me]
+        wires.send(quarter, quarter, spot.beside(), flat + 4 * step)
+        wires.send(quarter, quarter, spot.below(), flat + 4 * step + 1)
+    yield
+    for step in range(1, depth):
+        z = (spot.z - step + depth) % depth
+        wires.arrive(whole.at[z, :, me ^ 1], spot.sibling(), flat + 4 * step)
+        piece = whole.at[z, 0, me ^ 1]
+        wires.send(piece, piece, spot.below(), flat + 4 * step + 2)
+        wires.arrive(whole.at[z, :, me ^ 2], spot.sibling(), flat + 4 * step + 1)
+        piece = whole.at[z, 1, me ^ 2]
+        wires.send(piece, piece, spot.beside(), flat + 4 * step + 3)
+    yield
+    own.wait()
+    wires.arrive(whole.at[spot.z, 1 - spot.core], spot.sibling(), ahead)
+    for step in range(1, depth):
+        z = (spot.z - step + depth) % depth
+        wires.arrive(whole.at[z, 0, me ^ 3], spot.sibling(), flat + 4 * step + 2)
+        wires.arrive(whole.at[z, 1, me ^ 3], spot.sibling(), flat + 4 * step + 3)
+    yield
+
+
+def gather_rows(spot, wires, pack, whole):
+    depth, me = spot.depth, spot.corner
+    ahead = wires.take(depth)
+    flat = wires.take(4 * depth)
+    middle = pack.shape[-1] // 2
+
+    def part(z, corner, side):
+        if pack.shape[0] == 2:
+            return whole.at[side, z, corner]
+        return whole.at[0, z, corner, :, pl.ds(side * middle, middle)]
+
+    own = wires.move(pack, whole.at[:, spot.z])
+    for step in range(1, depth):
+        wires.send(
+            pack.at[:, me], whole.at[:, spot.z, me], spot.at((spot.z + step) % depth), ahead + step
+        )
+    yield
+    for step in range(1, depth):
+        z = (spot.z - step + depth) % depth
+        quarter = whole.at[:, z, me]
+        wires.arrive(quarter, spot.sibling(), ahead + step)
+        wires.send(quarter, quarter, spot.beside(), flat + 4 * step)
+        wires.send(quarter, quarter, spot.below(), flat + 4 * step + 1)
+    yield
+    for step in range(1, depth):
+        z = (spot.z - step + depth) % depth
+        wires.arrive(whole.at[:, z, me ^ 1], spot.sibling(), flat + 4 * step)
+        piece = part(z, me ^ 1, 0)
+        wires.send(piece, piece, spot.below(), flat + 4 * step + 2)
+        wires.arrive(whole.at[:, z, me ^ 2], spot.sibling(), flat + 4 * step + 1)
+        piece = part(z, me ^ 2, 1)
+        wires.send(piece, piece, spot.beside(), flat + 4 * step + 3)
+    yield
+    own.wait()
+    for step in range(1, depth):
+        z = (spot.z - step + depth) % depth
+        wires.arrive(part(z, me ^ 3, 0), spot.sibling(), flat + 4 * step + 2)
+        wires.arrive(part(z, me ^ 3, 1), spot.sibling(), flat + 4 * step + 3)
+    yield
+
+
+def add_into(target, other, places):
+    for place in places:
+        target[place] = (
+            target[place].astype(jnp.float32) + other[place].astype(jnp.float32)
+        ).astype(jnp.bfloat16)
+
+
+def scatter_buffers(depth, lanes, rows, width):
+    half = depth // 2
+    return [
+        pltpu.VMEM((half, lanes, 2, rows, width), jnp.bfloat16),
+        pltpu.VMEM((half, lanes, 2, rows, width), jnp.bfloat16),
+        pltpu.VMEM((half, lanes, 2, rows, width), jnp.bfloat16),
+        pltpu.VMEM((half, lanes, 2, rows, width), jnp.bfloat16),
+        pltpu.VMEM((half, lanes, rows, width), jnp.bfloat16),
+        pltpu.VMEM((half, lanes, rows, width), jnp.bfloat16),
+        pltpu.VMEM((depth, lanes, rows, width), jnp.bfloat16),
+        pltpu.VMEM((depth, lanes, rows, width), jnp.bfloat16),
+        pltpu.VMEM((rows, width), jnp.bfloat16),
+    ]
+
+
+def scatter_sums(spot, wires, grads, buffers, total, got):
+    depth, half = spot.depth, spot.depth // 2
+    lanes = grads.shape[1]
+    low, high, low_in, high_in, low_last, high_last, column, column_in, passing = buffers
+    first = wires.take(4)
+    away = wires.take(depth)
+    mine = [
+        wires.move(grads.at[pl.ds(0, half), :, :, spot.x], low),
+        wires.move(grads.at[pl.ds(half, half), :, spot.y], high),
+    ]
+    wires.send(grads.at[pl.ds(0, half), :, :, 1 - spot.x], low_in, spot.beside(), first)
+    wires.send(grads.at[pl.ds(half, half), :, 1 - spot.y], high_in, spot.below(), first + 1)
+    yield
+    for copy in mine:
+        copy.wait()
+    wires.arrive(low_in, spot.beside(), first)
+    add_into(low, low_in, [(z, a, s) for z in range(half) for a in range(lanes) for s in range(2)])
+    wires.send(low.at[:, :, 1 - spot.y], low_last, spot.below(), first + 2)
+    wires.arrive(high_in, spot.below(), first + 1)
+    add_into(high, high_in, [(z, a, s) for z in range(half) for a in range(lanes) for s in range(2)])
+    wires.send(high.at[:, :, 1 - spot.x], high_last, spot.beside(), first + 3)
+    yield
+    wires.arrive(low_last, spot.below(), first + 2)
+    wires.arrive(high_last, spot.beside(), first + 3)
+    for z in range(half):
+        for a in range(lanes):
+            column[z, a] = (
+                low[z, a, spot.y].astype(jnp.float32) + low_last[z, a].astype(jnp.float32)
+            ).astype(jnp.bfloat16)
+            column[half + z, a] = (
+                high[z, a, spot.x].astype(jnp.float32) + high_last[z, a].astype(jnp.float32)
+            ).astype(jnp.bfloat16)
+    for step in range(1, depth):
+        z = (spot.z + step) % depth
+        wires.send(column.at[z], column_in.at[step], spot.at(z), away + step)
+    yield
+    for step in range(1, depth):
+        wires.arrive(column_in.at[step], spot.sibling(), away + step)
+
+    def added(lane):
+        result = column[spot.z, lane].astype(jnp.float32)
+        for step in range(1, depth):
+            result = result + column_in[step, lane].astype(jnp.float32)
+        return result
+
+    if lanes == 1:
+        total[...] = added(0)
+    else:
+        passing[...] = added(1 - spot.core).astype(jnp.bfloat16)
+        wires.send(passing, got, spot.sibling(), away)
+        total[...] = added(spot.core)
+    yield
+    if lanes == 2:
+        wires.arrive(got, spot.sibling(), away)
+    yield
+
+
+def total_small(spot, wires, terms, work, total):
+    first = wires.take(3 + spot.depth)
+    work[0] = terms[...]
+    wires.send(work.at[0], work.at[1], spot.sibling(), first)
+    yield
+    wires.arrive(work.at[1], spot.sibling(), first)
+    work[2] = work[0] + work[1]
+    wires.send(work.at[2], work.at[3], spot.beside(), first + 1)
+    yield
+    wires.arrive(work.at[3], spot.sibling(), first + 1)
+    work[4] = work[2] + work[3]
+    wires.send(work.at[4], work.at[5], spot.below(), first + 2)
+    yield
+    wires.arrive(work.at[5], spot.sibling(), first + 2)
+    work[6] = work[4] + work[5]
+    for step in range(1, spot.depth):
+        target = work.at[6 + step]
+        wires.send(work.at[6], target, spot.at((spot.z + step) % spot.depth), first + 2 + step)
+    yield
+    result = work[6]
+    for step in range(1, spot.depth):
+        wires.arrive(work.at[6 + step], spot.sibling(), first + 2 + step)
+        result = result + work[6 + step]
+    total[...] = result
+    yield
+
+
+def staggered(programs):
+    live = list(enumerate(programs))
+    step = 0
+    while live:
+        rest = []
+        for start, program in reversed(live):
+            if step < start or next(program, False) is not False:
+                rest.append((start, program))
+        live = rest[::-1]
+        step += 1
+
+
+def wire_scratch(number, moves):
+    return [
+        pltpu.SemaphoreType.DMA((number,)),
+        pltpu.SemaphoreType.DMA((number,)),
+        pltpu.SemaphoreType.DMA((moves,)),
+    ]
+
+
+def front_kernel(depth, x, t, m, s, p1, p2, p3, p4, p5, wx, wt, wm, ws, w1, w2, w3, w4, w5, *sems):
+    spot = Spot(depth)
+    wires = Wires(*sems)
+    spot.greet()
+    staggered(
+        [
+            collect_tokens(spot, wires, x, wx),
+            gather_columns(spot, wires, p1, w1),
+            gather_small(spot, wires, s, ws),
+            collect_tokens(spot, wires, m, wm),
+            gather_columns(spot, wires, p2, w2),
+            gather_rows(spot, wires, p3, w3),
+            gather_columns(spot, wires, p4, w4),
+            gather_rows(spot, wires, p5, w5),
+            collect_tokens(spot, wires, t, wt),
+        ]
+    )
+    wires.close()
+
+
+def front(depth, x, t, m, small, p1, p2, p3, p4, p5):
+    bf16 = jnp.bfloat16
+
+    def whole_columns(pack):
+        return jax.ShapeDtypeStruct((depth, 2) + pack.shape[1:], bf16)
+
+    def whole_rows(pack):
+        return jax.ShapeDtypeStruct((pack.shape[0], depth) + pack.shape[1:], bf16)
+
+    def whole_tokens(parcel):
+        return jax.ShapeDtypeStruct((4, 2) + parcel.shape[2:], bf16)
+
+    hbm = pl.BlockSpec(memory_space=pl.ANY)
+    return pl.pallas_call(
+        functools.partial(front_kernel, depth),
+        in_specs=[hbm] * 9,
+        out_specs=[hbm] * 9,
+        out_shape=[
+            whole_tokens(x),
+            whole_tokens(t),
+            whole_tokens(m),
+            jax.ShapeDtypeStruct((depth, 2, 4, 8, 128), jnp.float32),
+            whole_columns(p1),
+            whole_columns(p2),
+            whole_rows(p3),
+            whole_columns(p4),
+            whole_rows(p5),
+        ],
+        scratch_shapes=wire_scratch(24 + 8 * depth + 22 * depth, 12),
+        compiler_params=pltpu.CompilerParams(
+            collective_id=0, has_side_effects=True, vmem_limit_bytes=16 * 2**20
+        ),
+        cost_estimate=pl.CostEstimate(flops=0, bytes_accessed=256 * 2**20, transcendentals=0),
+    )(x, t, m, small, p1, p2, p3, p4, p5)
+
+
+def reduce_kernel(depth, lanes, tokens, small, *refs):
+    spot = Spot(depth)
+    refs = list(refs)
+    take = lambda n: [refs.pop(0) for _ in range(n)]
+    grads = take(len(lanes))
+    pieces = take(tokens)
+    terms = take(1 if small else 0)
+    totals = take(len(lanes))
+    gots = [take(1)[0] if count == 2 else None for count in lanes]
+    homes = take(tokens)
+    sums = take(1 if small else 0)
+    buffers = [take(9) for _ in lanes]
+    work = take(1 if small else 0)
+    wires = Wires(*refs)
+    spot.greet()
+    programs = [deliver_tokens(spot, wires, *pair) for pair in zip(pieces, homes)]
+    if small:
+        programs.append(total_small(spot, wires, terms[0], work[0], sums[0]))
+    programs += [
+        scatter_sums(spot, wires, grad, scratch, total, got)
+        for grad, scratch, total, got in zip(grads, buffers, totals, gots)
+    ]
+    staggered(programs)
+    wires.close()
+
+
+def reduce_over_chips(depth, identity, grads, pieces=(), terms=None):
+    lanes = tuple(g.shape[1] for g in grads)
+    hbm = pl.BlockSpec(memory_space=pl.ANY)
+    vmem = pl.BlockSpec(memory_space=pltpu.VMEM)
+    extra = 0 if terms is None else 1
+    out_shape = [jax.ShapeDtypeStruct(g.shape[4:], jnp.float32) for g in grads]
+    out_shape += [jax.ShapeDtypeStruct(g.shape[4:], jnp.bfloat16) for g in grads if g.shape[1] == 2]
+    out_shape += [jax.ShapeDtypeStruct((2, 2) + p.shape[1:], p.dtype) for p in pieces]
+    out_shape += [jax.ShapeDtypeStruct((32, 128), jnp.float32)] * extra
+    out_specs = [vmem] * (len(grads) + sum(n == 2 for n in lanes)) + [hbm] * len(pieces) + [vmem] * extra
+    scratch = []
+    for grad in grads:
+        scratch += scatter_buffers(depth, grad.shape[1], *grad.shape[4:])
+    scratch += [pltpu.VMEM((6 + depth, 32, 128), jnp.float32)] * extra
+    number = len(grads) * (4 + depth) + 4 * len(pieces) + extra * (3 + depth)
+    results = pl.pallas_call(
+        functools.partial(reduce_kernel, depth, lanes, len(pieces), extra == 1),
+        in_specs=[hbm] * (len(grads) + len(pieces)) + [vmem] * extra,
+        out_specs=out_specs,
+        out_shape=out_shape,
+        scratch_shapes=scratch + wire_scratch(number, 2 * len(grads) + len(pieces) + 1),
+        compiler_params=pltpu.CompilerParams(
+            collective_id=identity, has_side_effects=True, vmem_limit_bytes=56 * 2**20
+        ),
+        cost_estimate=pl.CostEstimate(flops=0, bytes_accessed=256 * 2**20, transcendentals=0),
+    )(*grads, *pieces, *(() if terms is None else (terms,)))
+    results = list(results)
+    totals = [results.pop(0) for _ in grads]
+    gots = [results.pop(0) if n == 2 else None for n in lanes]
+    homes = [results.pop(0) for _ in pieces]
+    return totals, gots, homes, results[0] if extra else None
+
+
+def parity_columns(weight):
     rows, columns = weight.shape
-    return pick(weight.reshape(rows, 4, 2, columns // 8), core, 2).reshape(rows, columns // 2)
+    return jnp.moveaxis(weight.reshape(rows, 4, 2, columns // 8), 2, 0).reshape(2, rows, columns // 2)
 
 
 def per_chip(
@@ -907,24 +1353,53 @@
     cotangent,
 ):
     bf16, f32 = jnp.bfloat16, jnp.float32
-    plane = Plane(lax.axis_size("dp"), lax.axis_size("seq"))
-    core = plane.core
+    depth = lax.axis_size("dp") // 2
+    spot = Spot(depth)
+    core = spot.core
     width = layer_input.shape[3]
     local = layer_input.shape[2]
     near = memory.shape[2]
+    shard = norm_self.shape[0]
+
+    def column_pack(weights):
+        pack = jnp.concatenate([parity_columns(w) for w in weights], axis=2)
+        return pack.reshape(2, 4, -1, pack.shape[2])
 
     small = jnp.concatenate(
-        [norm_self, norm_cross, norm_ff, rel_bias.reshape(-1), jnp.zeros((112,), bf16)]
-    )
-    small = lax.all_gather(small, ("dp", "seq"), axis=0, tiled=False)
-    small = small.reshape(-1, 4, 512).astype(f32)
-    shard = norm_self.shape[0]
+        [norm_self, norm_cross, norm_ff, rel_bias.reshape(-1)]
+    ).astype(f32)
+    lengths = jnp.concatenate([target_lengths, memory_lengths]).reshape(-1).astype(f32)
+    small = jnp.concatenate([small, lengths, jnp.zeros((1024 - small.size - 4,), f32)]).reshape(8, 128)
+    inputs, upstream, encoded, small, w_qkv, w_cross, w_outs, w_gu, w_down = front(
+        depth,
+        layer_input.reshape(2, 2, local // 2, width),
+        cotangent.reshape(2, 2, local // 2, width),
+        memory.reshape(2, 2, near // 2, width),
+        small,
+        column_pack([self_q, self_k, self_v]),
+        column_pack([cross_k, cross_v, cross_q]),
+        jnp.stack([self_out, cross_out]).reshape(2, 4, -1, width),
+        column_pack([ff_gate, ff_up]),
+        ff_down.reshape(1, 4, -1, width),
+    )
+    inputs, upstream, encoded = (a.reshape(-1, width) for a in (inputs, upstream, encoded))
+    w_qkv, w_cross, w_gu, w_down = (a.reshape(-1, a.shape[-1]) for a in (w_qkv, w_cross, w_gu, w_down))
+    w_out, w_cout = w_outs[0].reshape(-1, width), w_outs[1].reshape(-1, width)
+    inner = self_q.shape[1] // 2
+    w_ckv, w_cq = w_cross[:, :inner], w_cross[:, inner:]
+    hidden_width = w_gu.shape[1] // 2
+    w_gate, w_up = w_gu[:, :hidden_width], w_gu[:, hidden_width:]
+    small = small.reshape(2 * depth, 4, 1024)
     gain_self, gain_cross, gain_ff = (
         small[:, 0, i * shard : (i + 1) * shard].reshape(-1) for i in range(3)
     )
     bias = small[:, :, 3 * shard : 3 * shard + 16].reshape(-1, 4, 4, 4)
     bias = jnp.swapaxes(bias, 1, 2).reshape(BUCKETS, HEADS)
     bias = pick(bias.reshape(BUCKETS, 4, 2, 2), core, 2).reshape(BUCKETS, -1)
+    lengths = pick(small[:, 0], 2 * spot.z + spot.x)[3 * shard + 16 : 3 * shard + 20]
+    lengths = pick(lengths.reshape(2, 2), spot.y, 1).astype(jnp.int32)
+    length, span = lengths[0], lengths[1]
+
     onehot = (buckets[:, None] == jnp.arange(BUCKETS, dtype=jnp.int32)[None, :]).astype(f32)
     table = lax.dot_general(bias, onehot, (((0,), (1,)), ((), ())), precision=HIGH)
     full = jnp.concatenate([jnp.full((table.shape[0], QB), NEG, f32), table], axis=1)
@@ -932,67 +1407,38 @@
     seeds_back = seed_rows(vectors)
     seeds_fore = seed_rows(jnp.roll(vectors[..., ::-1], 1, axis=-1))
 
-    parcel = jnp.concatenate(
-        [
-            layer_input.reshape(2, 2, local // 2, width),
-            cotangent.reshape(2, 2, local // 2, width),
-            memory.reshape(2, 2, near // 2, width),
-        ],
-        axis=2,
-    )
-    everything = plane.collect(parcel)
-    inputs = everything[:, :, : local // 2].reshape(-1, width)
-    upstream = everything[:, :, local // 2 : local].reshape(-1, width)
-    encoded = everything[:, :, local:].reshape(-1, width)
-    both = jnp.concatenate([target_lengths, memory_lengths]).reshape(2, 2, 1)
-    others = plane.swap_core(both.astype(f32)).astype(jnp.int32)
-    both = jnp.where(plane.x == core, both, others)[:, :, 0]
-    mine = pick(both, plane.y, 1)
-    length, span = mine[0], mine[1]
     tokens = inputs.shape[0]
     positions = jnp.arange(tokens, dtype=jnp.int32)
     valid = (positions < length).astype(f32)[:, None]
     keep_self = jnp.where(positions < length, 0.0, NEG).astype(f32)
     keep_cross = jnp.where(jnp.arange(encoded.shape[0], dtype=jnp.int32) < span, 0.0, NEG).astype(f32)
 
-    def column_shards(matrices):
-        packed = [
-            jnp.stack([jnp.concatenate([parity_columns(w, side) for w in group], axis=1) for group in matrices])
-            for side in range(2)
+    def swap_core(array):
+        pairs = [
+            (place * 4 + corner, (place ^ 1) * 4 + corner) for place in range(2 * depth) for corner in range(4)
         ]
-        packed = jnp.stack(packed)
-        got = plane.swap_core(pick(packed, 1 - core))
-        own = pick(packed, core)
-        ordered = jnp.stack([jnp.where(core == 0, own, got), jnp.where(core == 0, got, own)], axis=1)
-        return ordered.reshape(ordered.shape[:2] + (4, -1) + ordered.shape[3:])
-
-    def row_shards(matrices):
-        packed = jnp.stack(matrices)[:, None]
-        return packed.reshape(packed.shape[:2] + (4, -1) + packed.shape[3:])
-
-    w_q, w_kv, w_ckv, w_cq = plane.gather(
-        column_shards([[self_q], [self_k, self_v], [cross_k, cross_v], [cross_q]])
-    )
-    w_out, w_cout = plane.gather(row_shards([self_out, cross_out]))
-    w_gate, w_up = plane.gather(column_shards([[ff_gate], [ff_up]]))
-    (w_down,) = plane.gather(row_shards([ff_down]))
+        return lax.ppermute(array, ("dp", "seq"), pairs)
 
     def share(partial):
         partial = partial.astype(bf16)
-        return partial.astype(f32) + plane.swap_core(partial).astype(f32)
+        return partial.astype(f32) + swap_core(partial).astype(f32)
 
     def share_half(partial):
         partial = partial.astype(bf16).reshape(4, 2, -1, partial.shape[-1])
-        got = plane.swap_core(pick(partial, 1 - core, 1))
+        got = swap_core(pick(partial, 1 - core, 1))
         return pick(partial, core, 1).astype(f32) + got.astype(f32)
 
     def own_half(value):
         return pick(value.reshape(4, 2, -1, value.shape[-1]), core, 1)
 
+    def grad_pack(left, right, lanes):
+        grad = weight_grad(left, right).astype(bf16)
+        return grad.reshape(depth, lanes, 2, 2, -1, grad.shape[-1])
+
     hidden = inputs.astype(f32)
     normed_self = (hidden * inverse_rms(hidden) * gain_self).astype(bf16)
-    queries = project(normed_self, w_q).astype(bf16)
-    kv = project(normed_self, w_kv).astype(bf16)
+    qkv = project(normed_self, w_qkv).astype(bf16)
+    queries, kv = qkv[:, :inner], qkv[:, inner:]
     far_kv = project(encoded, w_ckv).astype(bf16)
     context, self_sums = attention_forward(queries, kv, keep_self, seeds_fore)
     first = hidden + share(project(context, w_out))
@@ -1005,7 +1451,7 @@
     upward = project(normed_ff, w_up)
     middle = gated(gate, upward).astype(bf16)
     third = own_half(second) + share_half(project(middle, w_down))
-    output = plane.deliver((third * own_half(valid)).astype(bf16))
+    output = (third * own_half(valid)).astype(bf16)
 
     top = upstream.astype(f32) * valid
     top_low = top.astype(bf16)
@@ -1013,42 +1459,40 @@
     gate_grad, upward_grad = pullback(project_back(top_low, w_down))
     gate_grad = gate_grad.astype(bf16)
     upward_grad = upward_grad.astype(bf16)
-    g_down = weight_grad(middle, top_low).astype(bf16)
-    g_gate = weight_grad(normed_ff, gate_grad).astype(bf16)
-    g_up = weight_grad(normed_ff, upward_grad).astype(bf16)
-    r_down = plane.scatter([g_down], 1)
-    r_ff = plane.scatter([g_gate, g_up], 2)
     change, gain_ff_terms = rms_back(
         second, gain_ff, share(project_back(gate_grad, w_gate) + project_back(upward_grad, w_up))
     )
+    g_down = grad_pack(middle, top_low, 1)
+    g_gate = grad_pack(normed_ff, gate_grad, 2)
+    g_up = grad_pack(normed_ff, upward_grad, 2)
+    (r_gate, r_up, r_down), (q_gate, q_up, _), (output,), _ = reduce_over_chips(
+        depth, 1, [g_gate, g_up, g_down], [output]
+    )
     second_grad = top + change
     cross_grad = second_grad.astype(bf16)
-    g_cout = weight_grad(cross_context, cross_grad).astype(bf16)
+    g_cout = grad_pack(cross_context, cross_grad, 1)
     cross_up = project_back(cross_grad, w_cout).astype(bf16)
     dqc, dkc, dvc = attention_backward(
         cross_queries, far_kv, cross_context, cross_up, cross_sums, keep_cross
     )
     dkvc = jnp.concatenate([dkc, dvc], axis=1)
-    g_cq = weight_grad(normed_cross, dqc).astype(bf16)
-    g_ckv = weight_grad(encoded, dkvc).astype(bf16)
-    memory_grad = plane.deliver(share_half(project_back(dkvc, w_ckv)).astype(bf16))
+    g_cq = grad_pack(normed_cross, dqc, 2)
+    g_ckv = grad_pack(encoded, dkvc, 2)
+    memory_grad = share_half(project_back(dkvc, w_ckv)).astype(bf16)
     change, gain_cross_terms = rms_back(first, gain_cross, share(project_back(dqc, w_cq)))
     first_grad = second_grad + change
     self_grad = first_grad.astype(bf16)
-    g_out = weight_grad(context, self_grad).astype(bf16)
+    g_out = grad_pack(context, self_grad, 1)
     self_up = project_back(self_grad, w_out).astype(bf16)
     dq, dk, dv, diagonal = attention_backward(
         queries, kv, context, self_up, self_sums, keep_self, seeds_back
     )
-    dkv = jnp.concatenate([dk, dv], axis=1)
-    g_q = weight_grad(normed_self, dq).astype(bf16)
-    g_kv = weight_grad(normed_self, dkv).astype(bf16)
-    r_rows = plane.scatter([g_out, g_cout], 1)
-    r_columns = plane.scatter([g_q, g_kv, g_ckv, g_cq], 2)
+    dqkv = jnp.concatenate([dq, dk, dv], axis=1)
+    g_qkv = grad_pack(normed_self, dqkv, 2)
     change, gain_self_terms = rms_back(
-        own_half(hidden), gain_self, share_half(project_back(dq, w_q) + project_back(dkv, w_kv))
-    )
-    input_grad = plane.deliver((own_half(first_grad) + change).astype(bf16)).astype(f32)
+        own_half(hidden), gain_self, share_half(project_back(dqkv, w_qkv))
+    )
+    input_grad = (own_half(first_grad) + change).astype(bf16)
 
     terms = [
         jnp.sum(own_half(gain_ff_terms), axis=(0, 1)),
@@ -1064,53 +1508,53 @@
     bias_terms = jnp.concatenate(
         [jnp.where(core == 0, bias_terms, 0.0), jnp.where(core == 1, bias_terms, 0.0)], axis=2
     ).reshape(-1)
-    packed = lax.psum(jnp.concatenate(terms + [bias_terms]), ("dp", "seq"))
-    mine = lax.axis_index("dp") * 4 + plane.corner
-    piece = width // (plane.depth * 8)
+    terms = jnp.concatenate(terms + [bias_terms, jnp.zeros((4096 - 3 * width - BUCKETS * HEADS,), f32)])
+    (r_cout, r_cq, r_ckv, r_out, r_qkv), (_, q_cq, q_ckv, _, q_qkv), (memory_grad, input_grad), packed = (
+        reduce_over_chips(
+            depth,
+            2,
+            [g_cout, g_cq, g_ckv, g_out, g_qkv],
+            [memory_grad, input_grad],
+            terms.reshape(32, 128),
+        )
+    )
+    packed = packed.reshape(-1)
+    mine = lax.axis_index("dp") * 4 + spot.corner
+    piece = width // (depth * 8)
     n_ff, n_cross, n_self = (
         lax.dynamic_slice_in_dim(packed, i * width + mine * piece, piece) for i in range(3)
     )
-    bias_grad = packed[3 * width :].reshape(BUCKETS, HEADS)
+    bias_grad = packed[3 * width : 3 * width + BUCKETS * HEADS].reshape(BUCKETS, HEADS)
     bias_grad = lax.dynamic_slice(
-        bias_grad, (lax.axis_index("dp") * rel_bias.shape[0], plane.corner * rel_bias.shape[1]), rel_bias.shape
-    )
-
-    def columns_home(sums):
-        got = plane.swap_core(pick(sums, 1 - core, 1).astype(bf16)).astype(f32)
-        own = pick(sums, core, 1)
-        return jnp.where(core == 0, own, got), jnp.where(core == 0, got, own)
-
-    def merge(even, odd):
-        rows = even.shape[0]
+        bias_grad, (lax.axis_index("dp") * rel_bias.shape[0], spot.corner * rel_bias.shape[1]), rel_bias.shape
+    )
+
+    def merge(own, got):
+        rows = own.shape[0]
+        got = got.astype(f32)
+        even, odd = jnp.where(core == 0, own, got), jnp.where(core == 0, got, own)
         return jnp.stack([even.reshape(rows, 4, -1), odd.reshape(rows, 4, -1)], axis=2).reshape(rows, -1)
 
-    even, odd = columns_home(r_columns)
-    quarter = even.shape[-1] // 2
-    d_q = merge(even[0], odd[0])
-    d_k, d_v = (merge(even[1][:, s], odd[1][:, s]) for s in (slice(0, quarter), slice(quarter, None)))
-    d_ck, d_cv = (merge(even[2][:, s], odd[2][:, s]) for s in (slice(0, quarter), slice(quarter, None)))
-    d_cq = merge(even[3], odd[3])
-    even, odd = columns_home(r_ff)
-    d_gate, d_up = merge(even[0], odd[0]), merge(even[1], odd[1])
+    half = inner // 2
     return (
         output.reshape(layer_input.shape),
-        input_grad.reshape(layer_input.shape),
+        input_grad.astype(f32).reshape(layer_input.shape),
         memory_grad.astype(f32).reshape(memory.shape),
         n_self,
-        d_q,
-        d_k,
-        d_v,
-        r_rows[0, 0],
+        merge(r_qkv[:, :inner], q_qkv[:, :inner]),
+        merge(r_qkv[:, inner : inner + half], q_qkv[:, inner : inner + half]),
+        merge(r_qkv[:, inner + half :], q_qkv[:, inner + half :]),
+        r_out,
         bias_grad,
         n_cross,
-        d_cq,
-        d_ck,
-        d_cv,
-        r_rows[1, 0],
+        merge(r_cq, q_cq),
+        merge(r_ckv[:, :half], q_ckv[:, :half]),
+        merge(r_ckv[:, half:], q_ckv[:, half:]),
+        r_cout,
         n_ff,
-        d_gate,
-        d_up,
-        r_down[0, 0],
+        merge(r_gate, q_gate),
+        merge(r_up, q_up),
+        r_down,
     )
 
 

time: 876 us -> 667 us (0.76)
  Pallas kernels: 69.5 us -> 430 us
  waiting for transfers between devices: 199 us -> 0.02 us
  starting transfers between devices: 174 us -> 2.31 us
  blocking collectives: 114 us -> 0 us
  other arithmetic: 116 us -> 69.1 us
  local copies, waits for them, and re-layouts: 95.3 us -> 63.7 us
    pallas_call x0 -> x3, Pallas kernels: none -> 359 us  [the longest x2 208 us: reduce_over_chips(): pl.pallas_call(functools.partial(reduce_kernel, depth, lanes, len(pieces)...]
    ppermute x85 -> x7, waiting for transfers between devices: 199 us -> 0.02 us  [swap_core(): return lax.ppermute(array, ('dp', 'seq'), pairs)]
    ppermute x85 -> x7, starting transfers between devices: 174 us -> 2.31 us  [swap_core(): return lax.ppermute(array, ('dp', 'seq'), pairs)]
    all_gather x1 -> x0, blocking collectives: 65.6 us -> none  [per_chip(): small = lax.all_gather(small, ('dp', 'seq'), axis=0, tiled=False)]
    psum x1 -> x0, blocking collectives: 48 us -> none  [per_chip(): packed = lax.psum(jnp.concatenate(terms + [bias_terms]), ('dp', 'seq'))]
    unnamed x117 -> x10, other arithmetic: 31.1 us -> 12 us
    convert_element_type x23 -> x7, other arithmetic: 20.8 us -> 4.8 us  [the longest x1 1.65 us: per_chip(): input_grad = (own_half(first_grad) + change).astype(bf16)]
    another operation x42 -> x1, other arithmetic: 12.8 us -> 0.05 us  [per_chip(): jnp.stack([self_out, cross_out]).reshape(2, 4, -1, width)]
  transfers between devices with their start and end apart: 85 -> 7, of which waited for: 29 -> 0; matrix products, arithmetic and copies ran while one was open for 24% -> 9% of each run, Pallas kernels for 2% -> 0%
where the time goes in v2:
time: 667 us; the launch traced here: 660 us
  Pallas kernels  430 us (64%)
  matrix products  91.9 us (14%)
  other arithmetic  69.1 us (10%)
  local copies, waits for them, and re-layouts  63.7 us (10%)
    pallas_call x2, Pallas kernels, reduce_over_chips(): pl.pallas_call(functools.partial(reduce_kernel, depth, lanes, len(pieces)...  208 us
    pallas_call x1, Pallas kernels, front(): pl.pallas_call(functools.partial(front_kernel, depth), in_specs=[hbm] * 9...  151 us
    pallas_call x2, Pallas kernels, attention_backward(): pl.pallas_call(functools.partial(backward_kernel, causal), grid=(heads //...  41.4 us
    dot_general x8, matrix products, project(): return jnp.dot(left, right, preferred_element_type=jnp.float32)  33.1 us
    dot_general x8, matrix products, project_back(): lax.dot_general(grad, weight, (((1,), (1,)), ((), ())), preferred_element...  29.6 us
    pallas_call x2, Pallas kernels, attention_forward(): pl.pallas_call(functools.partial(forward_kernel, causal), grid=(heads //...  29.1 us
    dot_general x8, matrix products, weight_grad(): lax.dot_general(left, right, (((0,), (0,)), ((), ())), preferred_element_...  28.4 us
    unnamed x193, local copies, waits for them, and re-layouts  27.9 us
  transfers between devices with their start and end apart: 7, of which 0 were waited for; matrix products, arithmetic and copies ran while one was open for 9% of the time, Pallas kernels for 0%

profile of v2, /device:TPU:0, one launch (start us, length us, event | category | flops | bytes accessed | tf_op | source)
XLA Modules:
  0.0 659.9 jit_solution(6298028307029926484)
XLA Ops:
  10.9 151.3 %shard_map.340 = (bf16[4,2,128,1024]{3,2,1,0:T(8,128)(2,1)S(1)}, bf16[4,2,128,1024]{3,2,1,0:T(8,128)(2,1)S(1)}, bf16[4,2,64,1024]{3,2,1,0:T(8,128)(2,1)S(1)}, f3...) custom-call(bf16[2,2,128,1024]{3,2,1,0:T(8,128)(2,1)S(1)} %bitcast.2, ...), custom_call_target="tpu_custom_call" | custom-call | bytes 268435456 | tf_op jit(solution)/shard_map/pallas_call | solution.py:1245
  164.9 2.5 copy-done.8
  167.4 1.6 copy-done.9
  191.0 1.6 fusion.66
  195.7 1.6 fusion.69
  197.3 1.6 fusion.70
  200.3 2.1 copy.234.rest_0_
  202.5 3.7 fusion.9
  207.8 2.3 convolution_convert_fusion.9
  213.7 18.6 %shard_map.341 = (bf16[1024,512]{1,0:T(8,128)(2,1)}, f32[2,4,1024]{2,1,0:T(4,128)}) custom-call(bf16[1024,512]{1,0:T(8,128)(2,1)} %get-tuple-element.206.q_ref, bf16[1024,512]{1,0:T(8,128)(2,1)} %get-tuple-element.205.k_ref.v_ref, bf16[1024,512]{1,0:T(8,128)(2,1)} %get-tuple-element.205.k_ref.v_ref, f32[1,1024]{1,0:T(1,128)} %compare_select_fusion.keep_ref, ...), custom_call_target="tpu_custom_call" | custom-call | flops 4294967296 | bytes 4194304 | tf_op jit(solution)/shard_map/pallas_call | solution.py:688
  232.2 3.8 convolution_convert_fusion.8
  236.1 2.4 convert_element_type.310
  239.9 2.7 convolution_convert_fusion.18.k_ref.v_ref
  242.7 5.2 multiply_reduce_fusion.3
  247.9 1.9 copy-done.19
  249.8 2.3 convolution_convert_fusion.15.q_ref
  252.1 10.6 %shard_map.342 = (bf16[1024,512]{1,0:T(8,128)(2,1)}, f32[2,4,1024]{2,1,0:T(4,128)}) custom-call(bf16[1024,512]{1,0:T(8,128)(2,1)} %convolution_convert_fusion.15.q_ref, bf16[512,512]{1,0:T(8,128)(2,1)} %convolution_convert_fusion.18.k_ref.v_ref, bf16[512,512]{1,0:T(8,128)(2,1)} %convolution_convert_fusion.18.k_ref.v_ref, f32[1,512]{1,0:T(1,128)} %compare_select_fusion.1.keep_ref), custom_call_target="tpu_custom_call" | custom-call | flops 4294967296 | bytes 4194304 | tf_op jit(solution)/shard_map/pallas_call | solution.py:688
  262.7 3.9 convolution_convert_fusion.7
  269.9 2.0 fusion.26
  276.1 7.2 %fusion.94 = f32[1024,1408]{1,0:T(8,128)} fusion(bf16[1024,1024]{1,0:T(8,128)(2,1)} %bitcast.339, bf16[1408,1024]{1,0:T(8,128)(2,1)S(1)} %bitcast.300), kind=kOutput, calls=%fused_computation.256 | convolution fusion | flops 2952790016 | bytes 10747904 | tf_op jit(solution)/shard_map/dot_general | solution.py:41
  283.2 3.2 multiply_reduce_fusion.2
  286.9 3.4 fusion.17
  290.3 11.0 %multiply_convert_fusion = (bf16[1024,1408]{1,0:T(8,128)(2,1)}, bf16[1024,1408]{1,0:T(8,128)(2,1)S(1)}, bf16[1024,1408]{1,0:T(8,128)(2,1)}) fusion(f32[1024,1408]{1,0:T(8,128)S(1)} %fusion.17, f32[1024,1408]{1,0:T(8,128)} %fusion.94, bf16[1024,1024]{1,0:T(8,128)(2,1)S(1)} %multiply_convert_fusion.3, bf16[1024,2816]{1,0:T(8,128)(2,1)S(1)} %bitcast.297), kind=kOutput, calls=%fused_computation.9 | convolution fusion | flops 2990276608 | bytes 25165824 | tf_op jit(solution)/shard_map/dot_general | solution.py:37
  301.4 3.4 fusion.15
  304.8 3.7 add_convert_fusion
  308.6 3.6 convolution_convert_fusion.6
  312.9 5.0 convolution_convert_fusion.1
  317.9 4.8 convolution_convert_fusion.2
  325.8 4.4 multiply_multiply_fusion.4
  330.2 4.6 convolution_convert_fusion
  334.8 117.2 %shard_map.343 = (f32[32,1408]{1,0:T(8,128)}, f32[32,1408]{1,0:T(8,128)}, f32[88,1024]{1,0:T(8,128)}, bf16[32,1408]{1,0:T(8,128)(2,1)}, bf16[32,1408]{1,0:T(8,128)(2,1)}, /*index=5*/bf16[2,2,128,1024]{3,2,1,0:T(8,128)(2,1)}) custom-call(bf16[4,2,2,2,32,1408]{5,4,3,2,1,0:T(8,128)(2,1)} %bitcast.333, bf16[4,2,2,2,32,1408]{5,4,3,2,1,0:T(8,128)(2,1)} %bitcast.332, ...), custom_call_target="tpu_custom_call" | custom-call | bytes 268435456 | tf_op jit(solution)/shard_map/pallas_call | solution.py:1309
  454.8 4.4 convolution_convert_fusion.13.do_ref
  459.3 16.3 %shard_map.344 = (bf16[1024,512]{1,0:T(8,128)(2,1)}, bf16[512,256]{1,0:T(8,128)(2,1)}, bf16[512,256]{1,0:T(8,128)(2,1)}) custom-call(bf16[1024,512]{1,0:T(8,128)(2,1)} %convolution_convert_fusion.15.q_ref, bf16[512,512]{1,0:T(8,128)(2,1)} %convolution_convert_fusion.18.k_ref.v_ref, bf16[512,512]{1,0:T(8,128)(2,1)} %convolution_convert_fusion.18.k_ref.v_ref, ...), custom_call_target="tpu_custom_call" | custom-call | flops 10737418240 | bytes 8388608 | tf_op jit(solution)/shard_map/pallas_call | solution.py:742
  475.7 3.9 convolution_convert_fusion.5
  484.2 2.2 convolution_convert_fusion.16
  487.2 1.8 convolution_convert_fusion.17
  489.0 3.7 convolution_convert_fusion.14
  492.7 2.4 convolution_convert_fusion.12
  496.2 3.2 multiply_reduce_fusion
  499.4 5.0 multiply_multiply_fusion.3
  504.4 2.3 convolution_convert_fusion.10.do_ref
  506.7 25.0 %shard_map.345 = (bf16[1024,512]{1,0:T(8,128)(2,1)}, bf16[1024,256]{1,0:T(8,128)(2,1)}, bf16[1024,256]{1,0:T(8,128)(2,1)}, f32[8,4,8,512]{3,2,1,0:T(8,128)}) custom-call(bf16[1024,512]{1,0:T(8,128)(2,1)} %get-tuple-element.206.q_ref, bf16[1024,512]{1,0:T(8,128)(2,1)} %get-tuple-element.205.k_ref.v_ref, bf16[1024,512]{1,0:T(8,128)(2,1)} %get-tuple-element.205.k_ref.v_ref, ...), custom_call_target="tpu_custom_call" | custom-call | flops 10737418240 | bytes 8388608 | tf_op jit(solution)/shard_map/pallas_call | solution.py:742
  536.3 1.9 dynamic-slice_reduce_fusion
  538.6 2.4 convolution_convert_fusion.3
  541.7 2.3 convolution_convert_fusion.11
  544.0 3.7 convolution_convert_fusion.4
  548.6 1.7 fusion.23.refs_6_
  550.2 91.0 %shard_map.346 = (f32[32,1024]{1,0:T(8,128)}, f32[32,512]{1,0:T(8,128)}, f32[32,512]{1,0:T(8,128)}, f32[32,1024]{1,0:T(8,128)}, f32[32,1024]{1,0:T(8,128)}, /*in...) custom-call(bf16[4,1,2,2,32,1024]{5,4,3,2,1,0:T(8,128)(2,1)} %bitcas, ...), custom_call_target="tpu_custom_call" | custom-call | bytes 268435456 | tf_op jit(solution)/shard_map/pallas_call | solution.py:1309
  (396 shorter events, 90.3 us)
Async XLA Ops:
  5.3 3.6 copy-start.68
  10.9 161.2 %copy-start.66 = (s32[1024]{0:T(1024)S(1)}, s32[1024]{0:T(1024)}, u32[]{:S(2)}) copy-start(s32[1024]{0:T(1024)} %param.29) | copy-start | bytes 12292
  171.7 68.2 %copy-start.17 = (bf16[4,2,64,1024]{3,2,1,0:T(8,128)(2,1)}, bf16[4,2,64,1024]{3,2,1,0:T(8,128)(2,1)S(1)}, u32[]{:S(2)}) copy-start(bf16[4,2,64,1024]{3,2,1,0:T(8,128)(2,1)S(1)} %get-tuple-element.85) | copy-start | bytes 3145732
  183.3 59.3 %copy-start.53 = (f32[8,1,128]{2,1,0:T(1,128)}, f32[8,1,128]{2,1,0:T(1,128)S(1)}, u32[]{:S(2)}) copy-start(f32[8,1,128]{2,1,0:T(1,128)S(1)} %get-tuple-element.225) | copy-start | bytes 12292
  213.7 18.6 %copy-start.31 = (bf16[1,4,4,32,1024]{4,3,2,1,0:T(8,128)(2,1)}, bf16[1,4,4,32,1024]{4,3,2,1,0:T(8,128)(2,1)S(1)}, u32[]{:S(2)}) copy-start(bf16[1,4,4,32,1024]{4,3,2,1,0:T(8,128)(2,1)S(1)} %get-tuple-element.204) | copy-start | bytes 3145732
  236.0 6.6 %collective-permute-start = (bf16[1024,1024]{1,0:T(8,128)(2,1)}, bf16[1024,1024]{1,0:T(8,128)(2,1)}, u32[]{:S(2)}, u32[]{:S(2)}) collective-permute-start(bf16[1024,1024]{1,0:T(8,128)(2,1)} %convolution_convert_fusion.8), channel_id=1, source_target_pairs={{0,4},{1,5},{2,6},{3,7},{4,0},{5,1},{6,2},{7,3},{8,12},{9,13},{10,... | collective-permute-start | bytes 6291464 | tf_op jit(solution)/shard_map/ppermute | solution.py:1420
  242.7 7.1 %copy-start.15 = (bf16[4,2,4,32,1024]{4,3,2,1,0:T(8,128)(2,1)S(1)}, bf16[4,2,4,32,1024]{4,3,2,1,0:T(8,128)(2,1)}, u32[]{:S(2)}) copy-start(bf16[4,2,4,32,1024]{4,3,2,1,0:T(8,128)(2,1)} %copy-done.14) | copy-start | bytes 6291460
  252.1 10.6 %copy-start.33 = (bf16[1,4,4,32,1024]{4,3,2,1,0:T(8,128)(2,1)S(1)}, bf16[1,4,4,32,1024]{4,3,2,1,0:T(8,128)(2,1)}, u32[]{:S(2)}) copy-start(bf16[1,4,4,32,1024]{4,3,2,1,0:T(8,128)(2,1)} %get-tuple-element.203) | copy-start | bytes 3145732
  262.7 4.7 copy-start.59
  262.7 4.8 copy-start.58
  262.7 5.0 copy-start.57
  262.7 5.2 copy-start.56
  262.7 5.4 copy-start.55
  266.6 16.6 %collective-permute-start.1 = (bf16[1024,1024]{1,0:T(8,128)(2,1)}, bf16[1024,1024]{1,0:T(8,128)(2,1)}, u32[]{:S(2)}, u32[]{:S(2)}) collective-permute-start(bf16[1024,1024]{1,0:T(8,128)(2,1)} %convolution_convert_fusion.7), channel_id=1, source_target_pairs={{0,4},{1,5},{2,6},{3,7},{4,0},{5,1},{6,2},{7,3},{8,12},{9,13},{10,... | collective-permute-start | bytes 6291464 | tf_op jit(solution)/shard_map/ppermute | solution.py:1420
  267.3 8.8 %copy-start.10 = (bf16[1,4,4,88,1024]{4,3,2,1,0:T(8,128)(2,1)S(1)}, bf16[1,4,4,88,1024]{4,3,2,1,0:T(8,128)(2,1)}, u32[]{:S(2)}) copy-start(bf16[1,4,4,88,1024]{4,3,2,1,0:T(8,128)(2,1)} %copy-done.9) | copy-start | bytes 8650756
  269.9 17.0 %slice-start = ((s8[5767168]{0:T(1024)(128)(4,1)}), s8[4194304]{0:T(1024)(128)(4,1)S(1)}, s32[]{:S(2)}) async-start(s8[5767168]{0:T(1024)(128)(4,1)} %bitcast.294), calls=%async_computation | async-start | bytes 8388608
  276.1 7.2 %copy-start.20 = (f32[1024,1024]{1,0:T(8,128)S(1)}, f32[1024,1024]{1,0:T(8,128)}, u32[]{:S(2)}) copy-start(f32[1024,1024]{1,0:T(8,128)} %copy-done.19) | copy-start | bytes 12582916
  276.1 10.8 %slice-start.1 = ((s8[5767168]{0:T(1024)(128)(4,1)}), s8[1572864]{0:T(1024)(128)(4,1)S(1)}, s32[]{:S(2)}) async-start(s8[5767168]{0:T(1024)(128)(4,1)} %bitcast.294), calls=%async_computation.1 | async-start | bytes 3145728
  301.4 3.4 copy-start.73
  304.8 3.8 copy-start.74
  308.5 15.6 %collective-permute-start.3 = (bf16[1024,1024]{1,0:T(8,128)(2,1)S(1)}, bf16[1024,1024]{1,0:T(8,128)(2,1)S(1)}, u32[]{:S(2)}, u32[]{:S(2)}) collective-permute-start(bf16[1024,1024]{1,0:T(8,128)(2,1)S(1)} %add_convert_fusion), channel_id=1, source_target_pairs={{0,4},{1,5},{2,6},{3,7},{4,0},{5,1},{6,2},{7,3},{8,12},{9,13},{10,... | collective-permute-start | bytes 6291464 | tf_op jit(solution)/shard_map/ppermute | solution.py:1420
  312.4 10.4 %collective-permute-start.2 = (bf16[4,128,1024]{2,1,0:T(8,128)(2,1)S(1)}, bf16[4,128,1024]{2,1,0:T(8,128)(2,1)S(1)}, u32[]{:S(2)}, u32[]{:S(2)}) collective-permute-start(bf16[4,128,1024]{2,1,0:T(8,128)(2,1)S(1)} %dynamic-slice_bitcast_fusion.1), channel_id=1, source_target_pairs={{0,4},{1,5},{2,6},{3,7},{4,0},{5,1},{6,2},{7,3},{8,12},{9,13},{10,... | collective-permute-start | bytes 3145736 | tf_op jit(solution)/shard_map/ppermute | solution.py:1420
  334.8 120.0 %copy-start.34 = (bf16[1,4,4,32,1024]{4,3,2,1,0:T(8,128)(2,1)S(1)}, bf16[1,4,4,32,1024]{4,3,2,1,0:T(8,128)(2,1)}, u32[]{:S(2)}) copy-start(bf16[1,4,4,32,1024]{4,3,2,1,0:T(8,128)(2,1)} %get-tuple-element.203) | copy-start | bytes 3145732
  459.3 16.4 %copy-start.16 = (bf16[4,2,4,32,1024]{4,3,2,1,0:T(8,128)(2,1)S(1)}, bf16[4,2,4,32,1024]{4,3,2,1,0:T(8,128)(2,1)}, u32[]{:S(2)}) copy-start(bf16[4,2,4,32,1024]{4,3,2,1,0:T(8,128)(2,1)} %copy-done.14) | copy-start | bytes 6291460
  475.6 4.1 copy-start.43
  479.5 3.9 copy-start.42
  479.5 16.6 %collective-permute-start.4 = (bf16[1024,1024]{1,0:T(8,128)(2,1)}, bf16[1024,1024]{1,0:T(8,128)(2,1)}, u32[]{:S(2)}, u32[]{:S(2)}) collective-permute-start(bf16[1024,1024]{1,0:T(8,128)(2,1)} %convolution_convert_fusion.5), channel_id=1, source_target_pairs={{0,4},{1,5},{2,6},{3,7},{4,0},{5,1},{6,2},{7,3},{8,12},{9,13},{10,... | collective-permute-start | bytes 6291464 | tf_op jit(solution)/shard_map/ppermute | solution.py:1420
  483.4 3.6 copy-start.24
  484.2 3.0 copy-start.18
  484.2 3.1 copy-start.47
  486.5 8.6 %collective-permute-start.5 = (bf16[4,64,1024]{2,1,0:T(8,128)(2,1)S(1)}, bf16[4,64,1024]{2,1,0:T(8,128)(2,1)S(1)}, u32[]{:S(2)}, u32[]{:S(2)}) collective-permute-start(bf16[4,64,1024]{2,1,0:T(8,128)(2,1)S(1)} %dynamic-slice_bitcast_fusion.2), channel_id=1, source_target_pairs={{0,4},{1,5},{2,6},{3,7},{4,0},{5,1},{6,2},{7,3},{8,12},{9,13},{10,... | collective-permute-start | bytes 1572872 | tf_op jit(solution)/shard_map/ppermute | solution.py:1420
  489.0 3.7 copy-start.21
  489.0 3.7 copy-start.71
  499.4 5.0 copy-start.32
  531.8 3.6 copy-start.67
  533.2 5.1 copy-start.30
  535.1 3.3 copy-start.38
  538.6 3.1 copy-start.26
  538.6 3.1 copy-start.72
  541.1 6.7 %collective-permute-start.6 = (bf16[4,128,1024]{2,1,0:T(8,128)(2,1)S(1)}, bf16[4,128,1024]{2,1,0:T(8,128)(2,1)S(1)}, u32[]{:S(2)}, u32[]{:S(2)}) collective-permute-start(bf16[4,128,1024]{2,1,0:T(8,128)(2,1)S(1)} %dynamic-slice_bitcast_fusion), channel_id=1, source_target_pairs={{0,4},{1,5},{2,6},{3,7},{4,0},{5,1},{6,2},{7,3},{8,12},{9,13},{10,... | collective-permute-start | bytes 3145736 | tf_op jit(solution)/shard_map/ppermute | solution.py:1420
  544.0 3.8 copy-start.22
  544.0 3.8 copy-start.54
  643.8 7.2 %copy-start.28 = (bf16[2,2,128,1024]{3,2,1,0:T(8,128)(2,1)S(1)}, bf16[2,2,128,1024]{3,2,1,0:T(8,128)(2,1)}, u32[]{:S(2)}) copy-start(bf16[2,2,128,1024]{3,2,1,0:T(8,128)(2,1)} %get-tuple-element.100) | copy-start | bytes 3145732
  648.0 4.7 copy-start.36
  650.1 6.3 copy-start.29
  651.0 6.3 copy-start.52
  651.0 7.0 %copy-start.51 = (f32[32,1024]{1,0:T(8,128)S(1)}, f32[32,1024]{1,0:T(8,128)}, u32[]{:S(2)}) copy-start(f32[32,1024]{1,0:T(8,128)} %get-tuple-element.297) | copy-start | bytes 393220
  652.6 6.1 copy-start.39
  (36 other events, 69.1 us)

commit v3 on v2

--- a/solution.py
+++ b/solution.py
@@ -1209,60 +1209,239 @@
     ]
 
 
-def front_kernel(depth, x, t, m, s, p1, p2, p3, p4, p5, wx, wt, wm, ws, w1, w2, w3, w4, w5, *sems):
+def spread_row(vector):
+    tile = pltpu.roll(jnp.broadcast_to(vector, (8, 2 * QB)), 0, 1, stride=1, stride_axis=0)
+    return spread(tile)
+
+
+def attend_block(query, keys, values, keep, bias):
+    scores = nt(query, keys) + keep
+    if bias is not None:
+        scores = scores + bias
+    peak = jnp.max(scores, axis=1, keepdims=True)
+    weights = jnp.exp(scores - peak)
+    total = jnp.sum(weights, axis=1, keepdims=True)
+    return nn(weights.astype(jnp.bfloat16), values) / total, peak + jnp.log(total)
+
+
+def pair_rows(block, kv):
+    both = block[:, 2 * kv * HEAD_DIM : 2 * (kv + 1) * HEAD_DIM]
+    return jnp.concatenate([both[:, :HEAD_DIM], both[:, HEAD_DIM:]], axis=0)
+
+
+def normed(value, gain):
+    return (value * inverse_rms(value) * gain).astype(jnp.bfloat16)
+
+
+def forward_layer_kernel(depth, *refs):
+    (
+        x, t, m, s, p1, p2, p3, p4, p5, codes, holes,
+        wx, wt, wm, ws, w1, w2, w3, w4, w5,
+        a1, qkv, ctx, lse, x1, a2, qc, ckv, ctxc, lsec, x2, a3, gains, keeps, keepc, bent,
+        bias, own, got, own2, got2, *sems
+    ) = refs
+    f32, bf16 = jnp.float32, jnp.bfloat16
     spot = Spot(depth)
     wires = Wires(*sems)
+    blocks = 4
+    kvs = 4
+    inner = 2 * kvs * HEAD_DIM
+
+    def rows(block):
+        return slice(block * QB, (block + 1) * QB)
+
     spot.greet()
-    staggered(
+    tokens = collect_tokens(spot, wires, x, wx)
+    small = gather_small(spot, wires, s, ws)
+    first = gather_columns(spot, wires, p1, w1)
+    memory = collect_tokens(spot, wires, m, wm)
+    second = gather_columns(spot, wires, p2, w2)
+    outs = gather_rows(spot, wires, p3, w3)
+    wide = gather_columns(spot, wires, p4, w4)
+    down = gather_rows(spot, wires, p5, w5)
+    top = collect_tokens(spot, wires, t, wt)
+    over = wires.take(2 * blocks)
+    for program in (tokens, small, first, small, tokens, first):
+        next(program)
+    next(outs)
+    next(second)
+    next(memory)
+    for program in (small, first, tokens, small, first):
+        next(program)
+
+    def line(row):
+        return jnp.concatenate([ws[z, c, 0, row : row + 1, :] for z in range(depth) for c in range(2)], axis=1)
+
+    for row in range(3):
+        gains[row : row + 1, :] = line(row)
+    counts = ws[spot.z, spot.x, 0, 3:4, :]
+    length = jnp.where(spot.y == 0, counts[:, 0:1], counts[:, 1:2])
+    span = jnp.where(spot.y == 0, counts[:, 2:3], counts[:, 3:4])
+    places = lax.broadcasted_iota(jnp.int32, (1, blocks * QB), 1).astype(f32)
+    keeps[...] = jnp.where(places < length, 0.0, NEG)
+    keepc[...] = jnp.where(places[:, : keepc.shape[1]] < span, 0.0, NEG)
+    table = jnp.concatenate(
         [
-            collect_tokens(spot, wires, x, wx),
-            gather_columns(spot, wires, p1, w1),
-            gather_small(spot, wires, s, ws),
-            collect_tokens(spot, wires, m, wm),
-            gather_columns(spot, wires, p2, w2),
-            gather_rows(spot, wires, p3, w3),
-            gather_columns(spot, wires, p4, w4),
-            gather_rows(spot, wires, p5, w5),
-            collect_tokens(spot, wires, t, wt),
-        ]
-    )
+            ws[z, c, 0, 4:8, :] + ws[z, c, 1, 4:8, :] + ws[z, c, 2, 4:8, :] + ws[z, c, 3, 4:8, :]
+            for z in range(depth)
+            for c in range(2)
+        ],
+        axis=0,
+    )
+    table = jnp.where(spot.core == 0, table[:, :64], table[:, 64:]).astype(bf16)
+    vectors = tn(table, codes[...])[:8] + holes[...]
+    bent[...] = vectors[:, 4 * 2 * QB :]
+    for kv in range(kvs):
+        for member in range(2):
+            for offset in range(4):
+                head = 2 * kv + member
+                bias[kv, member * QB : (member + 1) * QB, (3 - offset) * QB : (4 - offset) * QB] = spread_row(
+                    vectors[head : head + 1, offset * 2 * QB : (offset + 1) * 2 * QB]
+                )
+
+    def attend_rows(block, queries, keys, stop, keep, mixed, sums, causal):
+        for kv in range(kvs):
+            lanes = slice(kv * HEAD_DIM, (kv + 1) * HEAD_DIM)
+            upper = slice(inner // 2 + kv * HEAD_DIM, inner // 2 + (kv + 1) * HEAD_DIM)
+            shape = None
+            if causal:
+                shape = bias[kv, :, (3 - block) * QB : (3 - block) * QB + stop]
+            out, level = attend_block(
+                pair_rows(queries[rows(block), :inner], kv),
+                keys[:stop, lanes],
+                keys[:stop, upper],
+                keep[:, :stop],
+                shape,
+            )
+            mixed[rows(block), 2 * kv * HEAD_DIM : 2 * (kv + 1) * HEAD_DIM] = jnp.concatenate(
+                [out[:QB], out[QB:]], axis=1
+            ).astype(bf16)
+            level = jnp.broadcast_to(level, (2 * QB, 128)).T
+            sums[2 * kv : 2 * kv + 1, rows(block)] = level[:1, :QB]
+            sums[2 * kv + 1 : 2 * kv + 2, rows(block)] = level[:1, QB:]
+
+    weight = w1[...].reshape(-1, w1.shape[-1])
+    for block in range(blocks):
+        value = wx[block].reshape(QB, -1).astype(f32)
+        a1[rows(block), :] = normed(value, gains[0:1, :])
+        qkv[rows(block), :] = nn(a1[rows(block), :], weight).astype(bf16)
+        if block == 0:
+            next(outs)
+            next(second)
+            next(wide)
+        if block == 1:
+            next(outs)
+            next(second)
+            next(memory)
+        if block == 2:
+            next(outs)
+            next(second)
+            next(memory)
+            next(wide)
+            next(down)
+        attend_rows(block, qkv, qkv.at[:, inner:], (block + 1) * QB, keeps, ctx, lse, True)
+
+    def pass_on(block, mine, theirs, value, weight, index):
+        mine[rows(block), :] = nn(value[rows(block), :], weight).astype(bf16)
+        wires.send(mine.at[rows(block)], theirs.at[rows(block)], spot.sibling(), over + index + block)
+
+    def joined(block, mine, theirs, index):
+        wires.arrive(theirs.at[rows(block)], spot.sibling(), over + index + block)
+        return mine[rows(block), :].astype(f32) + theirs[rows(block), :].astype(f32)
+
+    weight = w3[0].reshape(-1, w3.shape[-1])
+    for block in range(blocks):
+        pass_on(block, own, got, ctx, weight, 0)
+    next(wide)
+    next(down)
+    next(top)
+    weight = w2[...].reshape(-1, w2.shape[-1])
+    ckv[...] = nn(wm[...].reshape(-1, wm.shape[-1]), weight[:, :inner]).astype(bf16)
+    for block in range(blocks):
+        value = wx[block].reshape(QB, -1).astype(f32) + joined(block, own, got, 0)
+        x1[rows(block), :] = value
+        a2[rows(block), :] = normed(value, gains[1:2, :])
+        qc[rows(block), :] = nn(a2[rows(block), :], weight[:, inner:]).astype(bf16)
+    weight = w3[1].reshape(-1, w3.shape[-1])
+    for block in range(blocks):
+        attend_rows(block, qc, ckv, ckv.shape[0], keepc, ctxc, lsec, False)
+        pass_on(block, own2, got2, ctxc, weight, blocks)
+        if block == 1:
+            next(down)
+            next(top)
+    for block in range(blocks):
+        value = x1[rows(block), :] + joined(block, own2, got2, blocks)
+        x2[rows(block), :] = value
+        a3[rows(block), :] = normed(value, gains[2:3, :])
+    for program in (wide, down, top):
+        next(program)
+    for program in (tokens, small, first, memory, second, outs, wide, down, top):
+        assert next(program, None) is None
     wires.close()
 
 
-def front(depth, x, t, m, small, p1, p2, p3, p4, p5):
-    bf16 = jnp.bfloat16
+def forward_layer(depth, x, t, m, small, p1, p2, p3, p4, p5, codes, holes):
+    bf16, f32 = jnp.bfloat16, jnp.float32
+    shape = jax.ShapeDtypeStruct
 
     def whole_columns(pack):
-        return jax.ShapeDtypeStruct((depth, 2) + pack.shape[1:], bf16)
+        return shape((depth, 2) + pack.shape[1:], bf16)
 
     def whole_rows(pack):
-        return jax.ShapeDtypeStruct((pack.shape[0], depth) + pack.shape[1:], bf16)
+        return shape((pack.shape[0], depth) + pack.shape[1:], bf16)
 
     def whole_tokens(parcel):
-        return jax.ShapeDtypeStruct((4, 2) + parcel.shape[2:], bf16)
-
+        return shape((4, 2) + parcel.shape[2:], bf16)
+
+    width = x.shape[-1]
+    tokens = 8 * x.shape[2]
+    span = 8 * m.shape[2]
+    inner = p3.shape[0] * p3.shape[1] * p3.shape[2] * depth // 2
+    heads = inner // HEAD_DIM
     hbm = pl.BlockSpec(memory_space=pl.ANY)
+    vmem = pl.BlockSpec(memory_space=pltpu.VMEM)
+    outs = [
+        (whole_tokens(x), vmem),
+        (whole_tokens(t), hbm),
+        (whole_tokens(m), vmem),
+        (shape((depth, 2, 4, 8, 128), f32), vmem),
+        (whole_columns(p1), vmem),
+        (whole_columns(p2), vmem),
+        (whole_rows(p3), vmem),
+        (whole_columns(p4), hbm),
+        (whole_rows(p5), hbm),
+        (shape((tokens, width), bf16), vmem),
+        (shape((tokens, 2 * inner), bf16), vmem),
+        (shape((tokens, inner), bf16), vmem),
+        (shape((heads, tokens), f32), vmem),
+        (shape((tokens, width), f32), vmem),
+        (shape((tokens, width), bf16), vmem),
+        (shape((tokens, inner), bf16), vmem),
+        (shape((span, inner), bf16), vmem),
+        (shape((tokens, inner), bf16), vmem),
+        (shape((heads, tokens), f32), vmem),
+        (shape((tokens, width), f32), vmem),
+        (shape((tokens, width), bf16), vmem),
+        (shape((8, width), f32), vmem),
+        (shape((1, tokens), f32), vmem),
+        (shape((1, span), f32), vmem),
+        (shape((heads, 8 * QB), f32), vmem),
+    ]
+    swap = pltpu.VMEM((tokens, width), bf16)
     return pl.pallas_call(
-        functools.partial(front_kernel, depth),
-        in_specs=[hbm] * 9,
-        out_specs=[hbm] * 9,
-        out_shape=[
-            whole_tokens(x),
-            whole_tokens(t),
-            whole_tokens(m),
-            jax.ShapeDtypeStruct((depth, 2, 4, 8, 128), jnp.float32),
-            whole_columns(p1),
-            whole_columns(p2),
-            whole_rows(p3),
-            whole_columns(p4),
-            whole_rows(p5),
-        ],
-        scratch_shapes=wire_scratch(24 + 8 * depth + 22 * depth, 12),
+        functools.partial(forward_layer_kernel, depth),
+        in_specs=[hbm] * 9 + [vmem] * 2,
+        out_specs=[spec for _, spec in outs],
+        out_shape=[kind for kind, _ in outs],
+        scratch_shapes=[pltpu.VMEM((heads // 2, 2 * QB, 4 * QB), f32), swap, swap, swap, swap]
+        + wire_scratch(35 + 30 * depth, 12),
         compiler_params=pltpu.CompilerParams(
-            collective_id=0, has_side_effects=True, vmem_limit_bytes=16 * 2**20
+            collective_id=0, has_side_effects=True, vmem_limit_bytes=60 * 2**20
         ),
-        cost_estimate=pl.CostEstimate(flops=0, bytes_accessed=256 * 2**20, transcendentals=0),
-    )(x, t, m, small, p1, p2, p3, p4, p5)
+        cost_estimate=pl.CostEstimate(
+            flops=16 * 10**9, bytes_accessed=128 * 2**20, transcendentals=10**7
+        ),
+    )(x, t, m, small, p1, p2, p3, p4, p5, codes, holes)
 
 
 def reduce_kernel(depth, lanes, tokens, small, *refs):
@@ -1365,12 +1544,31 @@
         pack = jnp.concatenate([parity_columns(w) for w in weights], axis=2)
         return pack.reshape(2, 4, -1, pack.shape[2])
 
+    heads = jnp.arange(4)
+    spots = (heads // 2) * 64 + 2 * spot.corner + heads % 2
+    placed = jnp.sum(
+        jnp.where(jnp.arange(128)[None, None, :] == spots[None, :, None], rel_bias[:, :, None].astype(f32), 0.0),
+        axis=1,
+    )
+    lengths = jnp.concatenate([target_lengths, memory_lengths]).reshape(1, 4).astype(f32)
     small = jnp.concatenate(
-        [norm_self, norm_cross, norm_ff, rel_bias.reshape(-1)]
-    ).astype(f32)
-    lengths = jnp.concatenate([target_lengths, memory_lengths]).reshape(-1).astype(f32)
-    small = jnp.concatenate([small, lengths, jnp.zeros((1024 - small.size - 4,), f32)]).reshape(8, 128)
-    inputs, upstream, encoded, small, w_qkv, w_cross, w_outs, w_gu, w_down = front(
+        [
+            jnp.stack([norm_self, norm_cross, norm_ff]).astype(f32),
+            jnp.pad(lengths, ((0, 0), (0, 124))),
+            placed,
+        ]
+    )
+    padded = jnp.concatenate([jnp.full((1, QB), -1, jnp.int32), buckets[None, :]], axis=1)
+    vectors = row_pieces(padded)
+    vectors = jnp.concatenate([jnp.roll(vectors[..., ::-1], 1, axis=-1), vectors], axis=1).reshape(1, -1)
+    codes = (vectors == jnp.arange(BUCKETS, dtype=jnp.int32)[:, None]).astype(bf16)
+    holes = jnp.where(vectors < 0, NEG, 0.0).astype(f32)
+    onehot = (buckets[:, None] == jnp.arange(BUCKETS, dtype=jnp.int32)[None, :]).astype(f32)
+    (
+        inputs, upstream, encoded, _, w_qkv, w_cross, w_outs, w_gu, w_down,
+        normed_self, qkv, context, self_sums, first, normed_cross, cross_queries, far_kv, cross_context,
+        cross_sums, second, normed_ff, gains, keep_self, keep_cross, bent,
+    ) = forward_layer(
         depth,
         layer_input.reshape(2, 2, local // 2, width),
         cotangent.reshape(2, 2, local // 2, width),
@@ -1381,6 +1579,8 @@
         jnp.stack([self_out, cross_out]).reshape(2, 4, -1, width),
         column_pack([ff_gate, ff_up]),
         ff_down.reshape(1, 4, -1, width),
+        codes,
+        holes,
     )
     inputs, upstream, encoded = (a.reshape(-1, width) for a in (inputs, upstream, encoded))
     w_qkv, w_cross, w_gu, w_down = (a.reshape(-1, a.shape[-1]) for a in (w_qkv, w_cross, w_gu, w_down))
@@ -1389,29 +1589,13 @@
     w_ckv, w_cq = w_cross[:, :inner], w_cross[:, inner:]
     hidden_width = w_gu.shape[1] // 2
     w_gate, w_up = w_gu[:, :hidden_width], w_gu[:, hidden_width:]
-    small = small.reshape(2 * depth, 4, 1024)
-    gain_self, gain_cross, gain_ff = (
-        small[:, 0, i * shard : (i + 1) * shard].reshape(-1) for i in range(3)
-    )
-    bias = small[:, :, 3 * shard : 3 * shard + 16].reshape(-1, 4, 4, 4)
-    bias = jnp.swapaxes(bias, 1, 2).reshape(BUCKETS, HEADS)
-    bias = pick(bias.reshape(BUCKETS, 4, 2, 2), core, 2).reshape(BUCKETS, -1)
-    lengths = pick(small[:, 0], 2 * spot.z + spot.x)[3 * shard + 16 : 3 * shard + 20]
-    lengths = pick(lengths.reshape(2, 2), spot.y, 1).astype(jnp.int32)
-    length, span = lengths[0], lengths[1]
-
-    onehot = (buckets[:, None] == jnp.arange(BUCKETS, dtype=jnp.int32)[None, :]).astype(f32)
-    table = lax.dot_general(bias, onehot, (((0,), (1,)), ((), ())), precision=HIGH)
-    full = jnp.concatenate([jnp.full((table.shape[0], QB), NEG, f32), table], axis=1)
-    vectors = row_pieces(full)
-    seeds_back = seed_rows(vectors)
-    seeds_fore = seed_rows(jnp.roll(vectors[..., ::-1], 1, axis=-1))
-
+    gain_self, gain_cross, gain_ff = gains[0], gains[1], gains[2]
+    queries, kv = qkv[:, :inner], qkv[:, inner:]
+    self_sums, cross_sums = self_sums.reshape(2, 4, -1), cross_sums.reshape(2, 4, -1)
+    seeds_back = seed_rows(bent.reshape(-1, 4, 2 * QB))
     tokens = inputs.shape[0]
-    positions = jnp.arange(tokens, dtype=jnp.int32)
-    valid = (positions < length).astype(f32)[:, None]
-    keep_self = jnp.where(positions < length, 0.0, NEG).astype(f32)
-    keep_cross = jnp.where(jnp.arange(encoded.shape[0], dtype=jnp.int32) < span, 0.0, NEG).astype(f32)
+    hidden = inputs.astype(f32)
+    valid = (keep_self[0] == 0).astype(f32)[:, None]
 
     def swap_core(array):
         pairs = [
@@ -1435,18 +1619,6 @@
         grad = weight_grad(left, right).astype(bf16)
         return grad.reshape(depth, lanes, 2, 2, -1, grad.shape[-1])
 
-    hidden = inputs.astype(f32)
-    normed_self = (hidden * inverse_rms(hidden) * gain_self).astype(bf16)
-    qkv = project(normed_self, w_qkv).astype(bf16)
-    queries, kv = qkv[:, :inner], qkv[:, inner:]
-    far_kv = project(encoded, w_ckv).astype(bf16)
-    context, self_sums = attention_forward(queries, kv, keep_self, seeds_fore)
-    first = hidden + share(project(context, w_out))
-    normed_cross = (first * inverse_rms(first) * gain_cross).astype(bf16)
-    cross_queries = project(normed_cross, w_cq).astype(bf16)
-    cross_context, cross_sums = attention_forward(cross_queries, far_kv, keep_cross)
-    second = first + share(project(cross_context, w_cout))
-    normed_ff = (second * inverse_rms(second) * gain_ff).astype(bf16)
     gate = project(normed_ff, w_gate)
     upward = project(normed_ff, w_up)
     middle = gated(gate, upward).astype(bf16)

time: 667 us -> 587 us (0.88)
  Pallas kernels: 430 us -> 400 us
  other arithmetic: 69.1 us -> 45.4 us
  matrix products: 91.9 us -> 78 us
  local copies, waits for them, and re-layouts: 63.7 us -> 54 us
    pallas_call x3 -> x1, Pallas kernels: 180 us -> 160 us  [forward_layer(): pl.pallas_call(functools.partial(forward_layer_kernel, depth), in_specs=[...]
    unnamed x193 -> x154, local copies, waits for them, and re-layouts: 27.9 us -> 7.8 us
    dot_general x8 -> x3, matrix products: 33.1 us -> 19.4 us  [project(): return jnp.dot(left, right, preferred_element_type=jnp.float32)]
    unnamed x10 -> x6, other arithmetic: 12 us -> 2.81 us
    pallas_call x2, Pallas kernels: 208 us -> 199 us  [reduce_over_chips(): pl.pallas_call(functools.partial(reduce_kernel, depth, lanes, len(pieces)...]
    reduce_sum x4 -> x3, other arithmetic: 14.1 us -> 5.71 us  [inverse_rms(): return lax.rsqrt(jnp.mean(value * value, axis=-1, keepdims=True) + EPS)]
  transfers between devices with their start and end apart: 7 -> 5, of which waited for: 0 -> 0; matrix products, arithmetic and copies ran while one was open for 9% -> 12% of each run, Pallas kernels for 0% -> 0%
where the time goes in v3:
time: 587 us; the launch traced here: 582 us
  Pallas kernels  400 us (68%)
  matrix products  78 us (13%)
  local copies, waits for them, and re-layouts  54 us (9%)
  other arithmetic  45.4 us (8%)
    pallas_call x2, Pallas kernels, reduce_over_chips(): pl.pallas_call(functools.partial(reduce_kernel, depth, lanes, len(pieces)...  199 us
    pallas_call x1, Pallas kernels, forward_layer(): pl.pallas_call(functools.partial(forward_layer_kernel, depth), in_specs=[...  160 us
    pallas_call x2, Pallas kernels, attention_backward(): pl.pallas_call(functools.partial(backward_kernel, causal), grid=(heads //...  40.8 us
    dot_general x8, matrix products, weight_grad(): lax.dot_general(left, right, (((0,), (0,)), ((), ())), preferred_element_...  31.6 us
    dot_general x8, matrix products, project_back(): lax.dot_general(grad, weight, (((1,), (1,)), ((), ())), preferred_element...  26.6 us
    dot_general x3, matrix products, project(): return jnp.dot(left, right, preferred_element_type=jnp.float32)  19.4 us
  transfers between devices with their start and end apart: 5, of which 0 were waited for; matrix products, arithmetic and copies ran while one was open for 12% of the time, Pallas kernels for 0%

profile of v3, /device:TPU:0, one launch (start us, length us, event | category | flops | bytes accessed | tf_op | source)
XLA Modules:
  0.0 582.1 jit_solution(6907050687609593230)
XLA Ops:
  6.1 1.2 reshape.527
  14.5 1.2 pad_maximum_fusion.refs_7_
  18.3 159.8 %shard_map.340 = (bf16[4,2,128,1024]{3,2,1,0:T(8,128)(2,1)}, bf16[4,2,128,1024]{3,2,1,0:T(8,128)(2,1)}, bf16[4,2,64,1024]{3,2,1,0:T(8,128)(2,1)}, f32[4,2,4,8,12...) custom-call(bf16[2,2,128,1024]{3,2,1,0:T(8,128)(2,1)} %bitcast.308, ...), custom_call_target="tpu_custom_call" | custom-call | flops 16000000000 | bytes 134217728 | tf_op jit(solution)/shard_map/pallas_call | solution.py:1431
  179.6 2.3 multiply_convert_fusion.2
  182.0 3.5 fusion.60
  185.5 3.4 fusion.12
  188.9 10.6 %multiply_convert_fusion = (bf16[1024,1408]{1,0:T(8,128)(2,1)}, bf16[1024,1408]{1,0:T(8,128)(2,1)}, bf16[1024,1408]{1,0:T(8,128)(2,1)}) fusion(f32[1024,1408]{1,0:T(8,128)S(1)} %fusion.12, f32[1024,1408]{1,0:T(8,128)S(1)} %fusion.60, bf16[1024,1024]{1,0:T(8,128)(2,1)S(1)} %copy-done.56, bf16[1024,2816]{1,0:T(8,128)(2,1)S(1)} %bitcast.316), kind=kOutput, calls=%fused_computation.9 | convolution fusion | flops 2990276608 | bytes 25165824 | tf_op jit(solution)/shard_map/dot_general | solution.py:37
  199.5 5.4 convolution_convert_fusion.6
  206.7 6.7 %fusion.10 = f32[1024,1024]{1,0:T(8,128)S(1)} fusion(bf16[1024,1408]{1,0:T(8,128)(2,1)} %get-tuple-element.217, bf16[1024,2816]{1,0:T(8,128)(2,1)} %bitcast.312), kind=kOutput, calls=%fused_computation.31 | convolution fusion | flops 2952790016 | bytes 9961472 | tf_op jit(solution)/shard_map/dot_general | solution.py:41
  213.5 3.9 add_convert_fusion
  220.5 1.5 fusion.57
  222.0 3.1 fusion.55
  225.1 1.5 fusion.21
  228.3 1.5 maximum_bitcast_fusion.4
  229.8 1.4 maximum_bitcast_fusion.5
  231.9 7.5 %convolution_convert_fusion.1 = bf16[1024,1408]{1,0:T(8,128)(2,1)} fusion(bf16[1024,1024]{1,0:T(8,128)(2,1)} %get-tuple-element.90, bf16[1024,1408]{1,0:T(8,128)(2,1)} %get-tuple-element.218), kind=kOutput, calls=%fused_computation.29 | convolution fusion | flops 2954231808 | bytes 7864320 | tf_op jit(solution)/shard_map/dot_general | solution.py:47
  240.8 1.5 copy.190
  242.3 1.5 stack.86
  244.7 1.4 reshape.541.lse_ref
  247.1 1.4 reshape.548.lse_ref
  248.5 2.2 stack.87.rest_0_
  250.7 3.1 fusion.56
  253.8 6.8 %convolution_convert_fusion.2 = bf16[1024,1408]{1,0:T(8,128)(2,1)} fusion(bf16[1024,1024]{1,0:T(8,128)(2,1)S(1)} %copy-done.57, bf16[1024,1408]{1,0:T(8,128)(2,1)} %get-tuple-element.217), kind=kOutput, calls=%fused_computation.30 | convolution fusion | flops 2954231808 | bytes 7864320 | tf_op jit(solution)/shard_map/dot_general | solution.py:47
  260.7 1.4 fusion.20.refs_3_
  262.1 3.0 multiply_reduce_fusion.3
  265.1 5.6 multiply_multiply_fusion.4
  270.8 5.0 convolution_convert_fusion
  275.8 108.2 %shard_map.341 = (f32[32,1408]{1,0:T(8,128)}, f32[32,1408]{1,0:T(8,128)}, f32[88,1024]{1,0:T(8,128)}, bf16[32,1408]{1,0:T(8,128)(2,1)}, bf16[32,1408]{1,0:T(8,128)(2,1)}, /*index=5*/bf16[2,2,128,1024]{3,2,1,0:T(8,128)(2,1)}) custom-call(bf16[4,2,2,2,32,1408]{5,4,3,2,1,0:T(8,128)(2,1)} %bitcast.255, bf16[4,2,2,2,32,1408]{5,4,3,2,1,0:T(8,128)(2,1)} %bitcast.254, ...), custom_call_target="tpu_custom_call" | custom-call | bytes 268435456 | tf_op jit(solution)/shard_map/pallas_call | solution.py:1488
  385.8 1.2 reshape.573
  389.0 4.4 convolution_convert_fusion.10.do_ref
  393.4 15.8 %shard_map.342 = (bf16[1024,512]{1,0:T(8,128)(2,1)}, bf16[512,256]{1,0:T(8,128)(2,1)}, bf16[512,256]{1,0:T(8,128)(2,1)}) custom-call(bf16[1024,512]{1,0:T(8,128)(2,1)} %get-tuple-element.100.q_ref, bf16[512,512]{1,0:T(8,128)(2,1)} %get-tuple-element.101.k_ref.v_ref, bf16[512,512]{1,0:T(8,128)(2,1)} %get-tuple-element.101.k_ref.v_ref, ...), custom_call_target="tpu_custom_call" | custom-call | flops 10737418240 | bytes 8388608 | tf_op jit(solution)/shard_map/pallas_call | solution.py:742
  409.3 2.6 convolution_convert_fusion.5
  414.4 1.8 convolution_convert_fusion.13
  416.2 2.3 convolution_convert_fusion.9
  419.0 2.3 convolution_convert_fusion.11
  422.3 1.2 multiply_reduce_fusion.1
  423.6 3.1 multiply_multiply_fusion.3
  426.7 2.3 convolution_convert_fusion.7.do_ref
  429.1 25.0 %shard_map.343 = (bf16[1024,512]{1,0:T(8,128)(2,1)}, bf16[1024,256]{1,0:T(8,128)(2,1)}, bf16[1024,256]{1,0:T(8,128)(2,1)}, f32[8,4,8,512]{3,2,1,0:T(8,128)}) custom-call(bf16[1024,512]{1,0:T(8,128)(2,1)} %get-tuple-element.227.q_ref, bf16[1024,512]{1,0:T(8,128)(2,1)} %get-tuple-element.226.k_ref.v_ref, bf16[1024,512]{1,0:T(8,128)(2,1)} %get-tuple-element.226.k_ref.v_ref, ...), custom_call_target="tpu_custom_call" | custom-call | flops 10737418240 | bytes 8388608 | tf_op jit(solution)/shard_map/pallas_call | solution.py:742
  454.1 1.4 copy.195
  458.6 1.9 dynamic-slice_reduce_fusion
  460.9 2.4 convolution_convert_fusion.3
  463.5 2.2 convolution_convert_fusion.8
  465.8 3.8 convolution_convert_fusion.4
  470.5 1.7 fusion.18.refs_6_
  472.3 91.2 %shard_map.344 = (f32[32,1024]{1,0:T(8,128)}, f32[32,512]{1,0:T(8,128)}, f32[32,512]{1,0:T(8,128)}, f32[32,1024]{1,0:T(8,128)}, f32[32,1024]{1,0:T(8,128)}, /*in...) custom-call(bf16[4,1,2,2,32,1024]{5,4,3,2,1,0:T(8,128)(2,1)} %bitcas, ...), custom_call_target="tpu_custom_call" | custom-call | bytes 268435456 | tf_op jit(solution)/shard_map/pallas_call | solution.py:1488
  573.3 1.6 bitcast_convert_fusion
  577.4 1.3 fusion.58
  (313 shorter events, 54.3 us)
Async XLA Ops:
  0.7 6.8 %copy-start.27 = (bf16[128,512]{1,0:T(8,128)(2,1)S(1)}, bf16[128,512]{1,0:T(8,128)(2,1)}, u32[]{:S(2)}) copy-start(bf16[128,512]{1,0:T(8,128)(2,1)} %param.32) | copy-start | bytes 393220
  0.7 7.4 %copy-start.28 = (bf16[128,512]{1,0:T(8,128)(2,1)S(1)}, bf16[128,512]{1,0:T(8,128)(2,1)}, u32[]{:S(2)}) copy-start(bf16[128,512]{1,0:T(8,128)(2,1)} %param.33) | copy-start | bytes 393220
  1.4 7.2 %copy-start.29 = (bf16[128,512]{1,0:T(8,128)(2,1)S(1)}, bf16[128,512]{1,0:T(8,128)(2,1)}, u32[]{:S(2)}) copy-start(bf16[128,512]{1,0:T(8,128)(2,1)} %param.38) | copy-start | bytes 393220
  5.9 3.3 copy-start.30
  6.1 3.6 copy-start.15
  11.6 4.2 copy-start.24
  12.4 4.2 copy-start.45
  12.4 4.2 copy-start.46
  12.4 4.2 copy-start.47
  178.2 3.8 copy-start.48
  179.6 5.8 slice-start
  182.0 3.5 slice-start.1
  182.0 3.5 copy-start.56
  204.9 8.5 %copy-start.8 = (bf16[1024,1024]{1,0:T(8,128)(2,1)}, bf16[1024,1024]{1,0:T(8,128)(2,1)S(1)}, u32[]{:S(2)}) copy-start(bf16[1024,1024]{1,0:T(8,128)(2,1)S(1)} %convolution_convert_fusion.6) | copy-start | bytes 6291460
  205.0 8.5 %slice-start.2 = ((s8[5767168]{0:T(1024)(128)(4,1)}), s8[4194304]{0:T(1024)(128)(4,1)S(1)}, s32[]{:S(2)}) async-start(s8[5767168]{0:T(1024)(128)(4,1)} %bitcast.317), calls=%async_computation.2 | async-start | bytes 8388608
  206.0 54.7 %collective-permute-start = (bf16[4,128,1024]{2,1,0:T(8,128)(2,1)}, bf16[4,128,1024]{2,1,0:T(8,128)(2,1)S(1)}, u32[]{:S(2)}, u32[]{:S(2)}) collective-permute-start(bf16[4,128,1024]{2,1,0:T(8,128)(2,1)} %dynamic-slice_bitcast_fusion.1), channel_id=1, source_target_pairs={{0,4},{1,5},{2,6},{3,7},{4,0},{5,1},{6,2},{7,3},{8,12},{9,13},{10,... | collective-permute-start | bytes 3145736 | tf_op jit(solution)/shard_map/ppermute | solution.py:1604
  206.7 6.8 %slice-start.3 = ((s8[5767168]{0:T(1024)(128)(4,1)}), s8[1572864]{0:T(1024)(128)(4,1)S(1)}, s32[]{:S(2)}) async-start(s8[5767168]{0:T(1024)(128)(4,1)} %bitcast.317), calls=%async_computation.3 | async-start | bytes 3145728
  206.7 6.8 %copy-start.59 = (bf16[1024,1408]{1,0:T(8,128)(2,1)S(1)}, bf16[1024,1408]{1,0:T(8,128)(2,1)}, u32[]{:S(2)}) copy-start(bf16[1024,1408]{1,0:T(8,128)(2,1)} %get-tuple-element.218) | copy-start | bytes 8650756
  213.5 4.5 copy-start.23
  217.4 44.6 %collective-permute-start.1 = (bf16[1024,1024]{1,0:T(8,128)(2,1)S(1)}, bf16[1024,1024]{1,0:T(8,128)(2,1)}, u32[]{:S(2)}, u32[]{:S(2)}) collective-permute-start(bf16[1024,1024]{1,0:T(8,128)(2,1)S(1)} %add_convert_fusion), channel_id=1, source_target_pairs={{0,4},{1,5},{2,6},{3,7},{4,0},{5,1},{6,2},{7,3},{8,12},{9,13},{10,... | collective-permute-start | bytes 6291464 | tf_op jit(solution)/shard_map/ppermute | solution.py:1604
  231.9 7.5 %copy-start.35 = (f32[1,1024]{1,0:T(1,128)S(1)}, f32[1,1024]{1,0:T(1,128)}, u32[]{:S(2)}) copy-start(f32[1,1024]{1,0:T(1,128)} %copy-done.34) | copy-start | bytes 12292
  231.9 11.9 %copy-start.44 = (f32[1,512]{1,0:T(1,128)S(1)}, f32[1,512]{1,0:T(1,128)}, u32[]{:S(2)}) copy-start(f32[1,512]{1,0:T(1,128)} %get-tuple-element.104) | copy-start | bytes 6148
  231.9 14.1 %copy-start.41 = (f32[1,1024]{1,0:T(1,128)S(1)}, f32[1,1024]{1,0:T(1,128)}, u32[]{:S(2)}) copy-start(f32[1,1024]{1,0:T(1,128)} %get-tuple-element.92) | copy-start | bytes 12292
  253.8 6.8 %copy-start = (f32[1024,1024]{1,0:T(8,128)S(1)}, f32[1024,1024]{1,0:T(8,128)}, u32[]{:S(2)}) copy-start(f32[1024,1024]{1,0:T(8,128)} %get-tuple-element.95) | copy-start | bytes 12582916
  253.8 6.8 %copy-start.9 = (bf16[1024,1024]{1,0:T(8,128)(2,1)S(1)}, bf16[1024,1024]{1,0:T(8,128)(2,1)}, u32[]{:S(2)}) copy-start(bf16[1024,1024]{1,0:T(8,128)(2,1)} %copy-done.8) | copy-start | bytes 6291460
  265.1 5.7 copy-start.60
  385.4 3.6 copy-start.14
  393.4 15.9 %copy-start.50 = (bf16[4,2,4,32,1024]{4,3,2,1,0:T(8,128)(2,1)S(1)}, bf16[4,2,4,32,1024]{4,3,2,1,0:T(8,128)(2,1)}, u32[]{:S(2)}) copy-start(bf16[4,2,4,32,1024]{4,3,2,1,0:T(8,128)(2,1)} %get-tuple-element.111) | copy-start | bytes 6291460
  411.9 10.5 %collective-permute-start.2 = (bf16[1024,1024]{1,0:T(8,128)(2,1)S(1)}, bf16[1024,1024]{1,0:T(8,128)(2,1)S(1)}, u32[]{:S(2)}, u32[]{:S(2)}) collective-permute-start(bf16[1024,1024]{1,0:T(8,128)(2,1)S(1)} %convolution_convert_fusion.5), channel_id=1, source_target_pairs={{0,4},{1,5},{2,6},{3,7},{4,0},{5,1},{6,2},{7,3},{8,12},{9,13},{10,... | collective-permute-start | bytes 6291464 | tf_op jit(solution)/shard_map/ppermute | solution.py:1604
  412.9 3.3 copy-start.52
  412.9 3.3 copy-start.55
  412.9 8.4 %collective-permute-start.3 = (bf16[4,64,1024]{2,1,0:T(8,128)(2,1)S(1)}, bf16[4,64,1024]{2,1,0:T(8,128)(2,1)S(1)}, u32[]{:S(2)}, u32[]{:S(2)}) collective-permute-start(bf16[4,64,1024]{2,1,0:T(8,128)(2,1)S(1)} %dynamic-slice_bitcast_fusion.2), channel_id=1, source_target_pairs={{0,4},{1,5},{2,6},{3,7},{4,0},{5,1},{6,2},{7,3},{8,12},{9,13},{10,... | collective-permute-start | bytes 1572872 | tf_op jit(solution)/shard_map/ppermute | solution.py:1604
  419.0 3.3 copy-start.2
  419.0 3.3 copy-start.37
  423.6 3.2 copy-start.13
  454.1 3.6 copy-start.43
  455.5 5.1 copy-start.12
  457.4 3.3 copy-start.19
  463.4 6.2 %collective-permute-start.4 = (bf16[4,128,1024]{2,1,0:T(8,128)(2,1)S(1)}, bf16[4,128,1024]{2,1,0:T(8,128)(2,1)S(1)}, u32[]{:S(2)}, u32[]{:S(2)}) collective-permute-start(bf16[4,128,1024]{2,1,0:T(8,128)(2,1)S(1)} %dynamic-slice_bitcast_fusion), channel_id=1, source_target_pairs={{0,4},{1,5},{2,6},{3,7},{4,0},{5,1},{6,2},{7,3},{8,12},{9,13},{10,... | collective-permute-start | bytes 3145736 | tf_op jit(solution)/shard_map/ppermute | solution.py:1604
  465.8 3.8 copy-start.7
  465.8 3.8 copy-start.36
  465.8 3.8 copy-start.40
  566.1 7.2 %copy-start.10 = (bf16[2,2,128,1024]{3,2,1,0:T(8,128)(2,1)S(1)}, bf16[2,2,128,1024]{3,2,1,0:T(8,128)(2,1)}, u32[]{:S(2)}) copy-start(bf16[2,2,128,1024]{3,2,1,0:T(8,128)(2,1)} %get-tuple-element.122) | copy-start | bytes 3145732
  570.2 4.7 copy-start.17
  572.3 6.3 %copy-start.11 = (bf16[2,2,128,1024]{3,2,1,0:T(8,128)(2,1)S(1)}, bf16[2,2,128,1024]{3,2,1,0:T(8,128)(2,1)}, u32[]{:S(2)}) copy-start(bf16[2,2,128,1024]{3,2,1,0:T(8,128)(2,1)} %get-tuple-element.96) | copy-start | bytes 3145732
  573.3 6.3 %copy-start.32 = (f32[32,1024]{1,0:T(8,128)S(1)}, f32[32,1024]{1,0:T(8,128)}, u32[]{:S(2)}) copy-start(f32[32,1024]{1,0:T(8,128)} %get-tuple-element.293) | copy-start | bytes 393220
  573.3 7.0 %copy-start.31 = (f32[32,1024]{1,0:T(8,128)S(1)}, f32[32,1024]{1,0:T(8,128)}, u32[]{:S(2)}) copy-start(f32[32,1024]{1,0:T(8,128)} %get-tuple-element.299) | copy-start | bytes 393220
  574.9 6.1 %copy-start.20 = (f32[88,1024]{1,0:T(8,128)S(1)}, f32[88,1024]{1,0:T(8,128)}, u32[]{:S(2)}) copy-start(f32[88,1024]{1,0:T(8,128)} %get-tuple-element.303) | copy-start | bytes 1081348
  (22 other events, 51.9 us)

commit v4 on v3

--- a/solution.py
+++ b/solution.py
@@ -565,203 +565,8 @@
     return lax.dot_general(left, right, (((1,), (0,)), ((), ())), preferred_element_type=jnp.float32)
 
 
-def forward_kernel(causal, q_ref, k_ref, v_ref, keep_ref, *rest):
-    if causal:
-        seed_ref, o_ref, lse_ref, bias = rest
-    else:
-        o_ref, lse_ref = rest
-    span = k_ref.shape[0]
-    for kv in range(2):
-        lanes = slice(kv * HEAD_DIM, (kv + 1) * HEAD_DIM)
-        keys = k_ref[:, lanes]
-        values = v_ref[:, lanes]
-        if causal:
-            for member in range(2):
-                for offset in range(4):
-                    bias[member * QB : (member + 1) * QB, (3 - offset) * QB : (4 - offset) * QB] = spread(
-                        seed_ref[2 * kv + member, offset]
-                    )
-        for block in range(q_ref.shape[0] // QB):
-            stop = (block + 1) * QB if causal else span
-            rows = slice(block * QB, (block + 1) * QB)
-            both = q_ref[rows, 2 * kv * HEAD_DIM : 2 * (kv + 1) * HEAD_DIM]
-            query = jnp.concatenate([both[:, :HEAD_DIM], both[:, HEAD_DIM:]], axis=0)
-            scores = nt(query, keys[:stop]) + keep_ref[:, :stop]
-            if causal:
-                scores = scores + bias[:, (3 - block) * QB : (3 - block) * QB + stop]
-            peak = jnp.max(scores, axis=1, keepdims=True)
-            weights = jnp.exp(scores - peak)
-            total = jnp.sum(weights, axis=1, keepdims=True)
-            mixed = nn(weights.astype(jnp.bfloat16), values[:stop]) / total
-            o_ref[rows, 2 * kv * HEAD_DIM : 2 * (kv + 1) * HEAD_DIM] = jnp.concatenate(
-                [mixed[:QB], mixed[QB:]], axis=1
-            ).astype(jnp.bfloat16)
-            sums = jnp.broadcast_to(peak + jnp.log(total), (2 * QB, 128)).T
-            lse_ref[2 * kv : 2 * kv + 1, rows] = sums[:1, :QB]
-            lse_ref[2 * kv + 1 : 2 * kv + 2, rows] = sums[:1, QB:]
-
-
-def backward_kernel(causal, q_ref, k_ref, v_ref, o_ref, do_ref, lse_ref, keep_ref, *rest):
-    if causal:
-        seed_ref, dq_ref, dk_ref, dv_ref, diag_ref, bias, sums, dk_sum, dv_sum = rest
-    else:
-        dq_ref, dk_ref, dv_ref, dk_sum, dv_sum = rest
-    span = k_ref.shape[0]
-    blocks = q_ref.shape[0] // QB
-    for kv in range(2):
-        lanes = slice(kv * HEAD_DIM, (kv + 1) * HEAD_DIM)
-        dk_sum[...] = jnp.zeros_like(dk_sum)
-        dv_sum[...] = jnp.zeros_like(dv_sum)
-        if causal:
-            for member in range(2):
-                for offset in range(4):
-                    bias[offset, :, member * QB : (member + 1) * QB] = spread(
-                        seed_ref[2 * kv + member, offset]
-                    )
-            sums[...] = jnp.zeros_like(sums)
-        for block in range(blocks):
-            rows = slice(block * QB, (block + 1) * QB)
-            both = slice(2 * kv * HEAD_DIM, 2 * (kv + 1) * HEAD_DIM)
-            pair = q_ref[rows, both]
-            query = jnp.concatenate([pair[:, :HEAD_DIM], pair[:, HEAD_DIM:]], axis=0)
-            upstream = do_ref[rows, both]
-            grads = jnp.concatenate([upstream[:, :HEAD_DIM], upstream[:, HEAD_DIM:]], axis=0)
-            inner = (upstream.astype(jnp.float32) * o_ref[rows, both].astype(jnp.float32)).T
-            delta = jnp.concatenate(
-                [
-                    jnp.sum(inner[:HEAD_DIM], axis=0, keepdims=True),
-                    jnp.sum(inner[HEAD_DIM:], axis=0, keepdims=True),
-                ],
-                axis=1,
-            )
-            level = jnp.concatenate(
-                [lse_ref[2 * kv : 2 * kv + 1, rows], lse_ref[2 * kv + 1 : 2 * kv + 2, rows]], axis=1
-            )
-            dq = jnp.zeros((2 * QB, HEAD_DIM), jnp.float32)
-            for part in range(block + 1 if causal else span // QB):
-                columns = slice(part * QB, (part + 1) * QB)
-                keys = k_ref[columns, lanes]
-                values = v_ref[columns, lanes]
-                scores = nt(keys, query) + keep_ref[columns]
-                if causal:
-                    scores = scores + bias[block - part]
-                probs = jnp.exp(scores - level)
-                dscores = probs * (nt(values, grads) - delta)
-                if causal:
-                    sums[block - part] += dscores
-                dscores = dscores.astype(jnp.bfloat16)
-                dv_sum[columns] += nn(probs.astype(jnp.bfloat16), grads)
-                dk_sum[columns] += nn(dscores, query)
-                dq += tn(dscores, keys)
-            dq_ref[rows, both] = jnp.concatenate([dq[:QB], dq[QB:]], axis=1).astype(jnp.bfloat16)
-        dk_ref[:, lanes] = dk_sum[...].astype(jnp.bfloat16)
-        dv_ref[:, lanes] = dv_sum[...].astype(jnp.bfloat16)
-        if causal:
-            for member in range(2):
-                for offset in range(4):
-                    diag_ref[2 * kv + member, offset] = fold(
-                        sums[offset, :, member * QB : (member + 1) * QB]
-                    )
-
-
-PARAMS = pltpu.CompilerParams(vmem_limit_bytes=56 * 2**20)
-
-
-def attention_forward(queries, kv, keep, seeds=None):
-    tokens, width = queries.shape
-    span = kv.shape[0]
-    heads = width // HEAD_DIM
-    causal = seeds is not None
-    in_specs = [
-        pl.BlockSpec((tokens, 256), lambda i: (0, i)),
-        pl.BlockSpec((span, 128), lambda i: (0, i)),
-        pl.BlockSpec((span, 128), lambda i: (0, i + 2)),
-        pl.BlockSpec((1, span), lambda i: (0, 0)),
-    ]
-    operands = [queries, kv, kv, keep.reshape(1, span)]
-    scratch = []
-    if causal:
-        in_specs.append(pl.BlockSpec((4, 4, 8, 512), lambda i: (i, 0, 0, 0)))
-        operands.append(seeds)
-        scratch.append(pltpu.VMEM((2 * QB, 4 * QB), jnp.float32))
-    work = heads * tokens * span // (2 if causal else 1)
-    context, sums = pl.pallas_call(
-        functools.partial(forward_kernel, causal),
-        grid=(heads // 4,),
-        in_specs=in_specs,
-        out_specs=[
-            pl.BlockSpec((tokens, 256), lambda i: (0, i)),
-            pl.BlockSpec((None, 4, tokens), lambda i: (i, 0, 0)),
-        ],
-        out_shape=[
-            jax.ShapeDtypeStruct((tokens, width), jnp.bfloat16),
-            jax.ShapeDtypeStruct((heads // 4, 4, tokens), jnp.float32),
-        ],
-        scratch_shapes=scratch,
-        compiler_params=PARAMS,
-        cost_estimate=pl.CostEstimate(
-            flops=work * 4 * 4 * HEAD_DIM, bytes_accessed=4 * 2**20, transcendentals=work
-        ),
-    )(*operands)
-    return context, sums
-
-
-def attention_backward(queries, kv, context, grads, sums, keep, seeds=None):
-    tokens, width = queries.shape
-    span = kv.shape[0]
-    heads = width // HEAD_DIM
-    causal = seeds is not None
-    wide = pl.BlockSpec((tokens, 256), lambda i: (0, i))
-    narrow = pl.BlockSpec((span, 128), lambda i: (0, i))
-    in_specs = [
-        wide,
-        narrow,
-        pl.BlockSpec((span, 128), lambda i: (0, i + 2)),
-        wide,
-        wide,
-        pl.BlockSpec((None, 4, tokens), lambda i: (i, 0, 0)),
-        pl.BlockSpec((span, 1), lambda i: (0, 0)),
-    ]
-    operands = [queries, kv, kv, context, grads, sums, keep.reshape(span, 1)]
-    out_specs = [wide, narrow, narrow]
-    out_shape = [
-        jax.ShapeDtypeStruct((tokens, width), jnp.bfloat16),
-        jax.ShapeDtypeStruct((span, width // 2), jnp.bfloat16),
-        jax.ShapeDtypeStruct((span, width // 2), jnp.bfloat16),
-    ]
-    scratch = []
-    if causal:
-        quad = pl.BlockSpec((4, 4, 8, 512), lambda i: (i, 0, 0, 0))
-        in_specs.append(quad)
-        operands.append(seeds)
-        out_specs.append(quad)
-        out_shape.append(jax.ShapeDtypeStruct((heads, 4, 8, 512), jnp.float32))
-        scratch = [pltpu.VMEM((4, QB, 2 * QB), jnp.float32), pltpu.VMEM((4, QB, 2 * QB), jnp.float32)]
-    scratch += [pltpu.VMEM((span, HEAD_DIM), jnp.float32), pltpu.VMEM((span, HEAD_DIM), jnp.float32)]
-    work = heads * tokens * span // (2 if causal else 1)
-    return pl.pallas_call(
-        functools.partial(backward_kernel, causal),
-        grid=(heads // 4,),
-        in_specs=in_specs,
-        out_specs=out_specs,
-        out_shape=out_shape,
-        scratch_shapes=scratch,
-        compiler_params=PARAMS,
-        cost_estimate=pl.CostEstimate(
-            flops=work * 10 * 4 * HEAD_DIM, bytes_accessed=8 * 2**20, transcendentals=work
-        ),
-    )(*operands)
-
-
 def inverse_rms(value):
     return lax.rsqrt(jnp.mean(value * value, axis=-1, keepdims=True) + EPS)
-
-
-def rms_back(value, gain, upstream):
-    inverse = inverse_rms(value)
-    scaled = upstream * gain
-    mean = jnp.mean(value * scaled, axis=-1, keepdims=True)
-    return inverse * scaled - value * (inverse * inverse * inverse) * mean, upstream * value * inverse
 
 
 def pick(array, index, axis=0):
@@ -1187,18 +992,6 @@
         result = result + work[6 + step]
     total[...] = result
     yield
-
-
-def staggered(programs):
-    live = list(enumerate(programs))
-    step = 0
-    while live:
-        rest = []
-        for start, program in reversed(live):
-            if step < start or next(program, False) is not False:
-                rest.append((start, program))
-        live = rest[::-1]
-        step += 1
 
 
 def wire_scratch(number, moves):
@@ -1301,15 +1094,18 @@
 
     def attend_rows(block, queries, keys, stop, keep, mixed, sums, causal):
         for kv in range(kvs):
-            lanes = slice(kv * HEAD_DIM, (kv + 1) * HEAD_DIM)
-            upper = slice(inner // 2 + kv * HEAD_DIM, inner // 2 + (kv + 1) * HEAD_DIM)
+            base = 2 * kv * HEAD_DIM
+            query = queries[rows(block), base : base + 2 * HEAD_DIM]
             shape = None
             if causal:
+                base = 4 * kv * HEAD_DIM
+                query = queries[rows(block), base : base + 2 * HEAD_DIM]
+                base += 2 * HEAD_DIM
                 shape = bias[kv, :, (3 - block) * QB : (3 - block) * QB + stop]
             out, level = attend_block(
-                pair_rows(queries[rows(block), :inner], kv),
-                keys[:stop, lanes],
-                keys[:stop, upper],
+                pair_rows(query, 0),
+                keys[:stop, base : base + HEAD_DIM],
+                keys[:stop, base + HEAD_DIM : base + 2 * HEAD_DIM],
                 keep[:, :stop],
                 shape,
             )
@@ -1339,7 +1135,7 @@
             next(memory)
             next(wide)
             next(down)
-        attend_rows(block, qkv, qkv.at[:, inner:], (block + 1) * QB, keeps, ctx, lse, True)
+        attend_rows(block, qkv, qkv, (block + 1) * QB, keeps, ctx, lse, True)
 
     def pass_on(block, mine, theirs, value, weight, index):
         mine[rows(block), :] = nn(value[rows(block), :], weight).astype(bf16)
@@ -1444,68 +1240,488 @@
     )(x, t, m, small, p1, p2, p3, p4, p5, codes, holes)
 
 
-def reduce_kernel(depth, lanes, tokens, small, *refs):
+def parts_of(width, pieces):
+    step = -(-width // (128 * pieces)) * 128
+    return [(start, min(step, width - start)) for start in range(0, width, step)]
+
+
+class Reduction:
+    def __init__(self, spot, wires, grads, buffers, total, got, pieces):
+        self.programs = []
+        for (start, size), scratch in zip(pieces, buffers):
+            lanes = pl.ds(start, size)
+            self.programs.append(
+                scatter_sums(
+                    spot,
+                    wires,
+                    grads.at[:, :, :, :, :, lanes],
+                    scratch,
+                    total.at[:, lanes],
+                    None if got is None else got.at[:, lanes],
+                )
+            )
+
+
+def pipeline(programs, ahead=2, stages=5):
+    count = len(programs)
+    for turn in range(count + stages):
+        if turn == 0:
+            for program in programs[:ahead]:
+                next(program)
+            yield
+        for stage in range(stages - 1, 0, -1):
+            index = turn - (stage - 1)
+            if 0 <= index < count:
+                next(programs[index])
+        if turn + ahead < count:
+            next(programs[turn + ahead])
+        yield
+
+
+def backward_tile(keys, values, query, grads, keep, bias, level, delta):
+    scores = nt(keys, query) + keep
+    if bias is not None:
+        scores = scores + bias
+    probs = jnp.exp(scores - level)
+    return probs, probs * (nt(values, grads) - delta)
+
+
+def row_sums(upstream, mixed):
+    inner = (upstream.astype(jnp.float32) * mixed.astype(jnp.float32)).T
+    return jnp.concatenate(
+        [
+            jnp.sum(inner[:HEAD_DIM], axis=0, keepdims=True),
+            jnp.sum(inner[HEAD_DIM:], axis=0, keepdims=True),
+        ],
+        axis=1,
+    )
+
+
+def cross_backward_kernel(depth, *refs):
+    (
+        g_down, g_gate, g_up, x2, x1, u, top, qc, ckv, ctxc, lsec, keep, a2, mem, w2, w3, ctx, gains,
+        r_down, r_gate, r_up, q_gate, q_up, half, do_s, o_cout, o_cq, o_ckv, o_out, o_mem, terms,
+        *rest
+    ) = refs
+    take = lambda n: [rest.pop(0) for _ in range(n)]
+    stage, e2, eb, do_c, dqc, dkv, dk_sum, dv_sum, got, own_c, got_c, own_m, got_m, grad = take(14)
+    buffers = [[take(9) for _ in range(2)] for _ in range(3)]
+    f32, bf16 = jnp.float32, jnp.bfloat16
     spot = Spot(depth)
-    refs = list(refs)
-    take = lambda n: [refs.pop(0) for _ in range(n)]
-    grads = take(len(lanes))
-    pieces = take(tokens)
-    terms = take(1 if small else 0)
-    totals = take(len(lanes))
-    gots = [take(1)[0] if count == 2 else None for count in lanes]
-    homes = take(tokens)
-    sums = take(1 if small else 0)
-    buffers = [take(9) for _ in lanes]
-    work = take(1 if small else 0)
-    wires = Wires(*refs)
+    wires = Wires(*rest)
+    blocks = kvs = 4
+    inner = 2 * kvs * HEAD_DIM
+
+    def rows(block):
+        return slice(block * QB, (block + 1) * QB)
+
     spot.greet()
-    programs = [deliver_tokens(spot, wires, *pair) for pair in zip(pieces, homes)]
-    if small:
-        programs.append(total_small(spot, wires, terms[0], work[0], sums[0]))
-    programs += [
-        scatter_sums(spot, wires, grad, scratch, total, got)
-        for grad, scratch, total, got in zip(grads, buffers, totals, gots)
-    ]
-    staggered(programs)
+    over = wires.take(2 * blocks + 4)
+    for block in range(blocks):
+        wires.send(u.at[rows(block)], got.at[rows(block)], spot.sibling(), over + block)
+    programs = []
+    for grads, scratch, total, other in (
+        (g_down, buffers[0], r_down, None),
+        (g_gate, buffers[1], r_gate, q_gate),
+        (g_up, buffers[2], r_up, q_up),
+    ):
+        programs += Reduction(
+            spot, wires, grads, scratch, total, other, parts_of(grads.shape[-1], 2)
+        ).programs
+    links = pipeline(programs)
+    next(links)
+
+    loads = {}
+
+    def fetch(source, block, slot):
+        loads[slot] = wires.move(source.at[rows(block)], stage.at[slot])
+
+    def norm_back(block, slot, gain, upstream):
+        loads[slot].wait()
+        value = stage[slot]
+        inverse = inverse_rms(value)
+        scaled = upstream * gain
+        mean = jnp.mean(value * scaled, axis=-1, keepdims=True)
+        change = inverse * scaled - value * (inverse * inverse * inverse) * mean
+        return change, jnp.sum(upstream * value * inverse, axis=0, keepdims=True)
+
+    fetch(x2, 0, 0)
+    gain_terms = jnp.zeros((1, e2.shape[1]), f32)
+    for block in range(blocks):
+        if block + 1 < blocks:
+            fetch(x2, block + 1, (block + 1) % 2)
+        else:
+            fetch(x1, 0, 0)
+        wires.arrive(got.at[rows(block)], spot.sibling(), over + block)
+        change, term = norm_back(
+            block, block % 2, gains[2:3, :], u[rows(block), :].astype(f32) + got[rows(block), :].astype(f32)
+        )
+        gain_terms = gain_terms + term
+        value = top[rows(block), :].astype(f32) + change
+        e2[rows(block), :] = value
+        eb[rows(block), :] = value.astype(bf16)
+        do_c[rows(block), :] = nt(value.astype(bf16), w3[1].reshape(inner, -1)).astype(bf16)
+    terms[0:1, :] = 0.5 * gain_terms
+    next(links)
+
+    span = ckv.shape[0]
+    for kv in range(kvs):
+        both = slice(2 * kv * HEAD_DIM, 2 * (kv + 1) * HEAD_DIM)
+        base = 2 * kv * HEAD_DIM
+        dk_sum[...] = jnp.zeros_like(dk_sum)
+        dv_sum[...] = jnp.zeros_like(dv_sum)
+        for block in range(blocks):
+            query = pair_rows(qc[rows(block), :], kv)
+            grads = pair_rows(do_c[rows(block), :], kv)
+            delta = row_sums(do_c[rows(block), both], ctxc[rows(block), both])
+            level = jnp.concatenate(
+                [lsec[2 * kv : 2 * kv + 1, rows(block)], lsec[2 * kv + 1 : 2 * kv + 2, rows(block)]], axis=1
+            )
+            dq = jnp.zeros((2 * QB, HEAD_DIM), f32)
+            for part in range(span // QB):
+                keys = ckv[rows(part), base : base + HEAD_DIM]
+                values = ckv[rows(part), base + HEAD_DIM : base + 2 * HEAD_DIM]
+                probs, dscores = backward_tile(keys, values, query, grads, keep[rows(part)], None, level, delta)
+                dscores = dscores.astype(bf16)
+                dv_sum[rows(part)] += nn(probs.astype(bf16), grads)
+                dk_sum[rows(part)] += nn(dscores, query)
+                dq += tn(dscores, keys)
+            dqc[rows(block), both] = jnp.concatenate([dq[:QB], dq[QB:]], axis=1).astype(bf16)
+        dkv[:, base : base + HEAD_DIM] = dk_sum[...].astype(bf16)
+        dkv[:, base + HEAD_DIM : base + 2 * HEAD_DIM] = dv_sum[...].astype(bf16)
+        if kv % 2 == 1:
+            next(links)
+
+    writes = {}
+
+    def put(slot, value, target):
+        if slot in writes:
+            writes[slot].wait()
+        view = grad.at[slot, pl.ds(0, value.shape[0]), pl.ds(0, value.shape[1])]
+        view[...] = value.astype(bf16)
+        writes[slot] = wires.move(view, target)
+
+    weight = w2[...].reshape(-1, w2.shape[-1])
+    for block in range(blocks):
+        own_c[rows(block), :] = nt(dqc[rows(block), :], weight[:, inner:]).astype(bf16)
+        wires.send(own_c.at[rows(block)], got_c.at[rows(block)], spot.sibling(), over + blocks + block)
+    own_m[...] = nt(dkv[...], weight[:, :inner]).astype(bf16).reshape(own_m.shape)
+    wires.send(own_m.at[:, 1 - spot.core], got_m, spot.sibling(), over + 2 * blocks)
+    slot = 0
+    for block in range(blocks):
+        put(slot, tn(a2[:, rows(block)], dqc[...]), o_cq.at[rows(block)])
+        slot = 1 - slot
+    next(links)
+    for block in range(blocks):
+        put(slot, tn(mem[:, rows(block)], dkv[...]), o_ckv.at[rows(block)])
+        slot = 1 - slot
+    for block in range(inner // QB):
+        put(slot, tn(ctxc[:, rows(block)], eb[...]), o_cout.at[rows(block)])
+        slot = 1 - slot
+    next(links)
+
+    gain_terms = jnp.zeros((1, e2.shape[1]), f32)
+    for block in range(blocks):
+        if block + 1 < blocks:
+            fetch(x1, block + 1, (block + 1) % 2)
+        wires.arrive(got_c.at[rows(block)], spot.sibling(), over + blocks + block)
+        change, term = norm_back(
+            block,
+            block % 2,
+            gains[1:2, :],
+            own_c[rows(block), :].astype(f32) + got_c[rows(block), :].astype(f32),
+        )
+        gain_terms = gain_terms + term
+        value = e2[rows(block), :] + change
+        e2[rows(block), :] = value
+        half[block] = e2[pl.ds(pl.multiple_of(block * QB + spot.core * (QB // 2), QB // 2), QB // 2), :]
+        eb[rows(block), :] = value.astype(bf16)
+        do_s[rows(block), :] = nt(value.astype(bf16), w3[0].reshape(inner, -1)).astype(bf16)
+    terms[1:2, :] = 0.5 * gain_terms
+    next(links)
+    for block in range(inner // QB):
+        put(slot, tn(ctx[:, rows(block)], eb[...]), o_out.at[rows(block)])
+        slot = 1 - slot
+    wires.arrive(got_m, spot.sibling(), over + 2 * blocks)
+    o_mem[...] = (own_m[:, spot.core].astype(f32) + got_m[...].astype(f32)).astype(bf16)
+    for _ in links:
+        pass
+    for copy in writes.values():
+        copy.wait()
     wires.close()
 
 
-def reduce_over_chips(depth, identity, grads, pieces=(), terms=None):
-    lanes = tuple(g.shape[1] for g in grads)
+def cross_part(depth, g_down, g_gate, g_up, x2, x1, u, top, qc, ckv, ctxc, lsec, keep, a2, mem, w2, w3, ctx, gains):
+    bf16, f32 = jnp.bfloat16, jnp.float32
+    shape = jax.ShapeDtypeStruct
     hbm = pl.BlockSpec(memory_space=pl.ANY)
     vmem = pl.BlockSpec(memory_space=pltpu.VMEM)
-    extra = 0 if terms is None else 1
-    out_shape = [jax.ShapeDtypeStruct(g.shape[4:], jnp.float32) for g in grads]
-    out_shape += [jax.ShapeDtypeStruct(g.shape[4:], jnp.bfloat16) for g in grads if g.shape[1] == 2]
-    out_shape += [jax.ShapeDtypeStruct((2, 2) + p.shape[1:], p.dtype) for p in pieces]
-    out_shape += [jax.ShapeDtypeStruct((32, 128), jnp.float32)] * extra
-    out_specs = [vmem] * (len(grads) + sum(n == 2 for n in lanes)) + [hbm] * len(pieces) + [vmem] * extra
-    scratch = []
-    for grad in grads:
-        scratch += scatter_buffers(depth, grad.shape[1], *grad.shape[4:])
-    scratch += [pltpu.VMEM((6 + depth, 32, 128), jnp.float32)] * extra
-    number = len(grads) * (4 + depth) + 4 * len(pieces) + extra * (3 + depth)
-    results = pl.pallas_call(
-        functools.partial(reduce_kernel, depth, lanes, len(pieces), extra == 1),
-        in_specs=[hbm] * (len(grads) + len(pieces)) + [vmem] * extra,
-        out_specs=out_specs,
-        out_shape=out_shape,
-        scratch_shapes=scratch + wire_scratch(number, 2 * len(grads) + len(pieces) + 1),
+    tokens, width = x2.shape
+    span, inner = ckv.shape
+    own = tokens // 8
+    outs = [
+        (shape(g_down.shape[4:], f32), vmem),
+        (shape(g_gate.shape[4:], f32), vmem),
+        (shape(g_up.shape[4:], f32), vmem),
+        (shape(g_gate.shape[4:], bf16), vmem),
+        (shape(g_up.shape[4:], bf16), vmem),
+        (shape((4, own, width), f32), vmem),
+        (shape((tokens, inner), bf16), vmem),
+        (shape((inner, width), bf16), hbm),
+        (shape((width, inner), bf16), hbm),
+        (shape((width, inner), bf16), hbm),
+        (shape((inner, width), bf16), hbm),
+        (shape((4, span // 8, width), bf16), vmem),
+        (shape((8, width), f32), vmem),
+    ]
+    scratch = [
+        pltpu.VMEM((2, QB, width), f32),
+        pltpu.VMEM((tokens, width), f32),
+        pltpu.VMEM((tokens, width), bf16),
+        pltpu.VMEM((tokens, inner), bf16),
+        pltpu.VMEM((tokens, inner), bf16),
+        pltpu.VMEM((span, inner), bf16),
+        pltpu.VMEM((span, HEAD_DIM), f32),
+        pltpu.VMEM((span, HEAD_DIM), f32),
+        pltpu.VMEM((tokens, width), bf16),
+        pltpu.VMEM((tokens, width), bf16),
+        pltpu.VMEM((tokens, width), bf16),
+        pltpu.VMEM((4, 2, span // 8, width), bf16),
+        pltpu.VMEM((4, span // 8, width), bf16),
+        pltpu.VMEM((2, QB, width), bf16),
+    ]
+    number = 12
+    for grads in (g_down, g_gate, g_up):
+        for _, size in parts_of(grads.shape[-1], 2):
+            scratch += scatter_buffers(depth, grads.shape[1], grads.shape[4], size)
+            number += 4 + depth
+    return pl.pallas_call(
+        functools.partial(cross_backward_kernel, depth),
+        in_specs=[hbm] * 5 + [vmem] * 13,
+        out_specs=[spec for _, spec in outs],
+        out_shape=[kind for kind, _ in outs],
+        scratch_shapes=scratch + wire_scratch(number, 48),
         compiler_params=pltpu.CompilerParams(
-            collective_id=identity, has_side_effects=True, vmem_limit_bytes=56 * 2**20
+            collective_id=1, has_side_effects=True, vmem_limit_bytes=60 * 2**20
         ),
-        cost_estimate=pl.CostEstimate(flops=0, bytes_accessed=256 * 2**20, transcendentals=0),
-    )(*grads, *pieces, *(() if terms is None else (terms,)))
-    results = list(results)
-    totals = [results.pop(0) for _ in grads]
-    gots = [results.pop(0) if n == 2 else None for n in lanes]
-    homes = [results.pop(0) for _ in pieces]
-    return totals, gots, homes, results[0] if extra else None
-
-
-def parity_columns(weight):
-    rows, columns = weight.shape
-    return jnp.moveaxis(weight.reshape(rows, 4, 2, columns // 8), 2, 0).reshape(2, rows, columns // 2)
+        cost_estimate=pl.CostEstimate(
+            flops=16 * 10**9, bytes_accessed=128 * 2**20, transcendentals=10**7
+        ),
+    )(g_down, g_gate, g_up, x2, x1, u, top, qc, ckv, ctxc, lsec, keep, a2, mem, w2, w3, ctx, gains)
+
+
+def self_backward_kernel(depth, *refs):
+    (
+        g_cout, g_cq, g_ckv, g_out, t_out, t_mem, do_s, qkv, ctx, lse, keep, bent, a1, x, gains, half, w1,
+        terms, codes,
+        r_cout, r_cq, r_ckv, r_out, r_qkv, q_cq, q_ckv, q_qkv, h_out, h_mem, h_in, packed,
+        *rest
+    ) = refs
+    take = lambda n: [rest.pop(0) for _ in range(n)]
+    bias, sums, dk_sum, dv_sum, dqkv, grad, mine, theirs, pieces, line, small, work = take(12)
+    buffers = [take(9) for _ in range(8)]
+    f32, bf16 = jnp.float32, jnp.bfloat16
+    spot = Spot(depth)
+    wires = Wires(*rest)
+    blocks = kvs = 4
+    inner = 2 * kvs * HEAD_DIM
+
+    def rows(block):
+        return slice(block * QB, (block + 1) * QB)
+
+    spot.greet()
+    over = wires.take(blocks)
+    homes = [deliver_tokens(spot, wires, t_out, h_out), deliver_tokens(spot, wires, t_mem, h_mem)]
+    programs = [
+        scatter_sums(spot, wires, g_cout, buffers[0], r_cout, None),
+        scatter_sums(spot, wires, g_out, buffers[1], r_out, None),
+        scatter_sums(spot, wires, g_cq, buffers[2], r_cq, q_cq),
+        scatter_sums(spot, wires, g_ckv, buffers[3], r_ckv, q_ckv),
+    ]
+    for kv in range(kvs):
+        lanes = pl.ds(kv * QB, QB)
+        programs.append(
+            scatter_sums(spot, wires, grad.at[kv], buffers[4 + kv], r_qkv.at[:, lanes], q_qkv.at[:, lanes])
+        )
+    early = pipeline(programs[:4], ahead=2)
+    late = programs[4:]
+    next(early)
+    for program in homes:
+        next(program)
+    for kv in range(kvs):
+        base = kv * 4 * HEAD_DIM
+        both = slice(2 * kv * HEAD_DIM, 2 * (kv + 1) * HEAD_DIM)
+        dk_sum[...] = jnp.zeros_like(dk_sum)
+        dv_sum[...] = jnp.zeros_like(dv_sum)
+        sums[...] = jnp.zeros_like(sums)
+        for member in range(2):
+            for offset in range(4):
+                head = 2 * kv + member
+                bias[offset, :, member * QB : (member + 1) * QB] = spread_row(
+                    bent[head : head + 1, offset * 2 * QB : (offset + 1) * 2 * QB]
+                )
+        for block in range(blocks):
+            query = pair_rows(qkv[rows(block), base : base + 2 * HEAD_DIM], 0)
+            grads = pair_rows(do_s[rows(block), :], kv)
+            delta = row_sums(do_s[rows(block), both], ctx[rows(block), both])
+            level = jnp.concatenate(
+                [lse[2 * kv : 2 * kv + 1, rows(block)], lse[2 * kv + 1 : 2 * kv + 2, rows(block)]], axis=1
+            )
+            dq = jnp.zeros((2 * QB, HEAD_DIM), f32)
+            for part in range(block + 1):
+                keys = qkv[rows(part), base + 2 * HEAD_DIM : base + 3 * HEAD_DIM]
+                values = qkv[rows(part), base + 3 * HEAD_DIM : base + 4 * HEAD_DIM]
+                probs, dscores = backward_tile(
+                    keys, values, query, grads, keep[rows(part)], bias[block - part], level, delta
+                )
+                sums[block - part] += dscores
+                dscores = dscores.astype(bf16)
+                dv_sum[rows(part)] += nn(probs.astype(bf16), grads)
+                dk_sum[rows(part)] += nn(dscores, query)
+                dq += tn(dscores, keys)
+            dqkv[rows(block), base : base + 2 * HEAD_DIM] = jnp.concatenate(
+                [dq[:QB], dq[QB:]], axis=1
+            ).astype(bf16)
+            if block == 2:
+                next(early, None)
+        dqkv[:, base + 2 * HEAD_DIM : base + 3 * HEAD_DIM] = dk_sum[...].astype(bf16)
+        dqkv[:, base + 3 * HEAD_DIM : base + 4 * HEAD_DIM] = dv_sum[...].astype(bf16)
+        for member in range(2):
+            for offset in range(4):
+                tile = fold(sums[offset, :, member * QB : (member + 1) * QB])
+                row = tile[0:1]
+                for r in range(1, 8):
+                    row = row + pltpu.roll(tile[r : r + 1], 2 * QB - r, 1)
+                head = 2 * kv + member
+                line[head : head + 1, (offset + 1) * QB : (offset + 2) * QB] = row[:, :QB]
+                if offset > 0:
+                    line[head : head + 1, offset * QB : (offset + 1) * QB] += row[:, QB:]
+        chunk = dqkv[:, base : base + 4 * HEAD_DIM]
+        for block in range(blocks):
+            grad[kv, block] = tn(a1[:, rows(block)], chunk).astype(bf16).reshape(grad.shape[2:])
+        next(late[kv])
+        for earlier in range(kv):
+            next(late[earlier])
+        next(early, None)
+        if kv == 1:
+            for program in homes:
+                next(program)
+    weight = w1[...].reshape(-1, w1.shape[-1])
+    size = QB // 2
+
+    def half_rows(block, core):
+        return pl.ds(pl.multiple_of(block * QB + core * size, size), size)
+
+    for block in range(blocks):
+        mine[block] = nt(dqkv[half_rows(block, 1 - spot.core), :], weight).astype(bf16)
+        wires.send(mine.at[block], theirs.at[block], spot.sibling(), over + block)
+    for program in late:
+        next(program, None)
+    gain_terms = jnp.zeros((1, x.shape[-1]), f32)
+    for block in range(blocks):
+        upstream = nt(dqkv[half_rows(block, spot.core), :], weight).astype(bf16).astype(f32)
+        wires.arrive(theirs.at[block], spot.sibling(), over + block)
+        upstream = upstream + theirs[block].astype(f32)
+        value = x[block, spot.core].astype(f32)
+        inverse = inverse_rms(value)
+        scaled = upstream * gains[0:1, :]
+        mean = jnp.mean(value * scaled, axis=-1, keepdims=True)
+        change = inverse * scaled - value * (inverse * inverse * inverse) * mean
+        gain_terms = gain_terms + jnp.sum(upstream * value * inverse, axis=0, keepdims=True)
+        pieces[block] = (half[block] + change).astype(bf16)
+    homing = deliver_tokens(spot, wires, pieces, h_in)
+    next(homing)
+    shares = nt_exact(line[:, QB:], codes[...])
+    small[...] = jnp.zeros_like(small)
+    for r in range(8):
+        lanes = slice(r * 128, (r + 1) * 128)
+        small[r : r + 1, :] = terms[0:1, lanes]
+        small[8 + r : 9 + r, :] = terms[1:2, lanes]
+        small[16 + r : 17 + r, :] = gain_terms[:, lanes]
+    zero = jnp.zeros_like(shares)
+    small[24:32, :BUCKETS] = jnp.where(spot.core == 0, shares, zero)
+    small[24:32, BUCKETS : 2 * BUCKETS] = jnp.where(spot.core == 1, shares, zero)
+    summing = total_small(spot, wires, small, work, packed)
+    next(summing)
+    for _ in range(4):
+        next(summing, None)
+        for program in late:
+            next(program, None)
+    for program in late + homes + [homing, summing]:
+        for _ in program:
+            pass
+    for _ in early:
+        pass
+    wires.close()
+
+
+def nt_exact(left, right):
+    return lax.dot_general(
+        left, right, (((1,), (1,)), ((), ())), precision=HIGH, preferred_element_type=jnp.float32
+    )
+
+
+def self_part(depth, *operands):
+    bf16, f32 = jnp.bfloat16, jnp.float32
+    shape = jax.ShapeDtypeStruct
+    hbm = pl.BlockSpec(memory_space=pl.ANY)
+    vmem = pl.BlockSpec(memory_space=pltpu.VMEM)
+    g_cout, g_cq, g_ckv, g_out, t_out, t_mem, do_s, qkv = operands[:8]
+    tokens, inner = do_s.shape
+    width = g_cout.shape[-1]
+    rows = g_cout.shape[4]
+    own = tokens // 8
+    outs = [
+        (shape((rows, width), f32), vmem),
+        (shape((rows, inner), f32), vmem),
+        (shape((rows, inner), f32), vmem),
+        (shape((rows, width), f32), vmem),
+        (shape((rows, 2 * inner), f32), vmem),
+        (shape((rows, inner), bf16), vmem),
+        (shape((rows, inner), bf16), vmem),
+        (shape((rows, 2 * inner), bf16), vmem),
+        (shape((2, 2) + t_out.shape[1:], bf16), hbm),
+        (shape((2, 2) + t_mem.shape[1:], bf16), hbm),
+        (shape((2, 2, own, width), bf16), hbm),
+        (shape((32, 128), f32), vmem),
+    ]
+    scratch = [
+        pltpu.VMEM((4, QB, 2 * QB), f32),
+        pltpu.VMEM((4, QB, 2 * QB), f32),
+        pltpu.VMEM((tokens, HEAD_DIM), f32),
+        pltpu.VMEM((tokens, HEAD_DIM), f32),
+        pltpu.VMEM((tokens, 2 * inner), bf16),
+        pltpu.VMEM((4, depth, 2, 2, 2, rows, QB), bf16),
+        pltpu.VMEM((4, own, width), bf16),
+        pltpu.VMEM((4, own, width), bf16),
+        pltpu.VMEM((4, own, width), bf16),
+        pltpu.VMEM((8, 5 * QB), f32),
+        pltpu.VMEM((32, 128), f32),
+        pltpu.VMEM((6 + depth, 32, 128), f32),
+    ]
+    scratch += scatter_buffers(depth, 1, rows, width) + scatter_buffers(depth, 1, rows, width)
+    scratch += scatter_buffers(depth, 2, rows, inner) + scatter_buffers(depth, 2, rows, inner)
+    for _ in range(4):
+        scratch += scatter_buffers(depth, 2, rows, QB)
+    return pl.pallas_call(
+        functools.partial(self_backward_kernel, depth),
+        in_specs=[hbm] * 6 + [vmem] * 13,
+        out_specs=[spec for _, spec in outs],
+        out_shape=[kind for kind, _ in outs],
+        scratch_shapes=scratch + wire_scratch(4 + 12 + 3 + depth + 8 * (4 + depth), 24),
+        compiler_params=pltpu.CompilerParams(
+            collective_id=2, has_side_effects=True, vmem_limit_bytes=60 * 2**20
+        ),
+        cost_estimate=pl.CostEstimate(
+            flops=16 * 10**9, bytes_accessed=128 * 2**20, transcendentals=10**7
+        ),
+    )(*operands)
+
+
+def parity_columns(weights):
+    rows = weights[0].shape[0]
+    pack = jnp.concatenate([w.reshape(rows, 4, 2, -1) for w in weights], axis=3)
+    return jnp.moveaxis(pack, 2, 0).reshape(2, rows, -1)
 
 
 def per_chip(
@@ -1540,8 +1756,8 @@
     near = memory.shape[2]
     shard = norm_self.shape[0]
 
-    def column_pack(weights):
-        pack = jnp.concatenate([parity_columns(w) for w in weights], axis=2)
+    def column_pack(*groups):
+        pack = jnp.concatenate([parity_columns(weights) for weights in groups], axis=2)
         return pack.reshape(2, 4, -1, pack.shape[2])
 
     heads = jnp.arange(4)
@@ -1575,26 +1791,17 @@
         memory.reshape(2, 2, near // 2, width),
         small,
         column_pack([self_q, self_k, self_v]),
-        column_pack([cross_k, cross_v, cross_q]),
+        column_pack([cross_k, cross_v], [cross_q]),
         jnp.stack([self_out, cross_out]).reshape(2, 4, -1, width),
-        column_pack([ff_gate, ff_up]),
+        column_pack([ff_gate], [ff_up]),
         ff_down.reshape(1, 4, -1, width),
         codes,
         holes,
     )
-    inputs, upstream, encoded = (a.reshape(-1, width) for a in (inputs, upstream, encoded))
-    w_qkv, w_cross, w_gu, w_down = (a.reshape(-1, a.shape[-1]) for a in (w_qkv, w_cross, w_gu, w_down))
-    w_out, w_cout = w_outs[0].reshape(-1, width), w_outs[1].reshape(-1, width)
-    inner = self_q.shape[1] // 2
-    w_ckv, w_cq = w_cross[:, :inner], w_cross[:, inner:]
+    upstream, encoded = upstream.reshape(-1, width), encoded.reshape(-1, width)
+    w_gu, w_down = w_gu.reshape(-1, w_gu.shape[-1]), w_down.reshape(-1, width)
     hidden_width = w_gu.shape[1] // 2
     w_gate, w_up = w_gu[:, :hidden_width], w_gu[:, hidden_width:]
-    gain_self, gain_cross, gain_ff = gains[0], gains[1], gains[2]
-    queries, kv = qkv[:, :inner], qkv[:, inner:]
-    self_sums, cross_sums = self_sums.reshape(2, 4, -1), cross_sums.reshape(2, 4, -1)
-    seeds_back = seed_rows(bent.reshape(-1, 4, 2 * QB))
-    tokens = inputs.shape[0]
-    hidden = inputs.astype(f32)
     valid = (keep_self[0] == 0).astype(f32)[:, None]
 
     def swap_core(array):
@@ -1602,10 +1809,6 @@
             (place * 4 + corner, (place ^ 1) * 4 + corner) for place in range(2 * depth) for corner in range(4)
         ]
         return lax.ppermute(array, ("dp", "seq"), pairs)
-
-    def share(partial):
-        partial = partial.astype(bf16)
-        return partial.astype(f32) + swap_core(partial).astype(f32)
 
     def share_half(partial):
         partial = partial.astype(bf16).reshape(4, 2, -1, partial.shape[-1])
@@ -1631,101 +1834,69 @@
     gate_grad, upward_grad = pullback(project_back(top_low, w_down))
     gate_grad = gate_grad.astype(bf16)
     upward_grad = upward_grad.astype(bf16)
-    change, gain_ff_terms = rms_back(
-        second, gain_ff, share(project_back(gate_grad, w_gate) + project_back(upward_grad, w_up))
-    )
+    changed = (project_back(gate_grad, w_gate) + project_back(upward_grad, w_up)).astype(bf16)
     g_down = grad_pack(middle, top_low, 1)
     g_gate = grad_pack(normed_ff, gate_grad, 2)
     g_up = grad_pack(normed_ff, upward_grad, 2)
-    (r_gate, r_up, r_down), (q_gate, q_up, _), (output,), _ = reduce_over_chips(
-        depth, 1, [g_gate, g_up, g_down], [output]
-    )
-    second_grad = top + change
-    cross_grad = second_grad.astype(bf16)
-    g_cout = grad_pack(cross_context, cross_grad, 1)
-    cross_up = project_back(cross_grad, w_cout).astype(bf16)
-    dqc, dkc, dvc = attention_backward(
-        cross_queries, far_kv, cross_context, cross_up, cross_sums, keep_cross
-    )
-    dkvc = jnp.concatenate([dkc, dvc], axis=1)
-    g_cq = grad_pack(normed_cross, dqc, 2)
-    g_ckv = grad_pack(encoded, dkvc, 2)
-    memory_grad = share_half(project_back(dkvc, w_ckv)).astype(bf16)
-    change, gain_cross_terms = rms_back(first, gain_cross, share(project_back(dqc, w_cq)))
-    first_grad = second_grad + change
-    self_grad = first_grad.astype(bf16)
-    g_out = grad_pack(context, self_grad, 1)
-    self_up = project_back(self_grad, w_out).astype(bf16)
-    dq, dk, dv, diagonal = attention_backward(
-        queries, kv, context, self_up, self_sums, keep_self, seeds_back
-    )
-    dqkv = jnp.concatenate([dq, dk, dv], axis=1)
-    g_qkv = grad_pack(normed_self, dqkv, 2)
-    change, gain_self_terms = rms_back(
-        own_half(hidden), gain_self, share_half(project_back(dqkv, w_qkv))
-    )
-    input_grad = (own_half(first_grad) + change).astype(bf16)
-
-    terms = [
-        jnp.sum(own_half(gain_ff_terms), axis=(0, 1)),
-        jnp.sum(own_half(gain_cross_terms), axis=(0, 1)),
-        jnp.sum(gain_self_terms, axis=(0, 1)),
-    ]
-    diagonal = sum(jnp.roll(diagonal[:, :, r], -r, axis=-1) for r in range(8))
-    blocks = jnp.zeros((diagonal.shape[0], 5, QB), f32)
-    blocks = blocks.at[:, 1:].add(diagonal[:, :, :QB]).at[:, :4].add(diagonal[:, :, QB:])
-    distances = blocks[:, 1:].reshape(-1, tokens)
-    bias_terms = lax.dot_general(onehot, distances, (((0,), (1,)), ((), ())), precision=HIGH)
-    bias_terms = bias_terms.reshape(BUCKETS, 4, 1, 2)
-    bias_terms = jnp.concatenate(
-        [jnp.where(core == 0, bias_terms, 0.0), jnp.where(core == 1, bias_terms, 0.0)], axis=2
-    ).reshape(-1)
-    terms = jnp.concatenate(terms + [bias_terms, jnp.zeros((4096 - 3 * width - BUCKETS * HEADS,), f32)])
-    (r_cout, r_cq, r_ckv, r_out, r_qkv), (_, q_cq, q_ckv, _, q_qkv), (memory_grad, input_grad), packed = (
-        reduce_over_chips(
-            depth,
-            2,
-            [g_cout, g_cq, g_ckv, g_out, g_qkv],
-            [memory_grad, input_grad],
-            terms.reshape(32, 128),
-        )
-    )
-    packed = packed.reshape(-1)
+    (
+        r_down, r_gate, r_up, q_gate, q_up, half, self_up, g_cout, g_cq, g_ckv, g_out, memory_grad, terms,
+    ) = cross_part(
+        depth, g_down, g_gate, g_up, second, first, changed, top_low, cross_queries, far_kv, cross_context,
+        cross_sums, keep_cross.reshape(-1, 1), normed_cross, encoded, w_cross, w_outs, context, gains,
+    )
+
+    def pack(grad, lanes):
+        return grad.reshape(depth, lanes, 2, 2, -1, grad.shape[-1])
+
+    (
+        r_cout, r_cq, r_ckv, r_out, r_qkv, q_cq, q_ckv, q_qkv, output, memory_grad, input_grad, packed,
+    ) = self_part(
+        depth, pack(g_cout, 1), pack(g_cq, 2), pack(g_ckv, 2), pack(g_out, 1), output, memory_grad, self_up,
+        qkv, context, self_sums, keep_self.reshape(-1, 1), bent, normed_self, inputs, gains, half, w_qkv,
+        terms, onehot.T,
+    )
+    bias_grad = packed[24:, :64].reshape(4, 2, 2, BUCKETS)
+    bias_grad = jnp.transpose(bias_grad, (3, 0, 2, 1)).reshape(BUCKETS, HEADS)
+    packed = packed[:24].reshape(3, width)
     mine = lax.axis_index("dp") * 4 + spot.corner
     piece = width // (depth * 8)
-    n_ff, n_cross, n_self = (
-        lax.dynamic_slice_in_dim(packed, i * width + mine * piece, piece) for i in range(3)
-    )
-    bias_grad = packed[3 * width : 3 * width + BUCKETS * HEADS].reshape(BUCKETS, HEADS)
+    n_ff, n_cross, n_self = (lax.dynamic_slice_in_dim(packed[i], mine * piece, piece) for i in range(3))
     bias_grad = lax.dynamic_slice(
         bias_grad, (lax.axis_index("dp") * rel_bias.shape[0], spot.corner * rel_bias.shape[1]), rel_bias.shape
     )
 
-    def merge(own, got):
+    def merge(own, got, *sizes):
         rows = own.shape[0]
         got = got.astype(f32)
         even, odd = jnp.where(core == 0, own, got), jnp.where(core == 0, got, own)
-        return jnp.stack([even.reshape(rows, 4, -1), odd.reshape(rows, 4, -1)], axis=2).reshape(rows, -1)
-
-    half = inner // 2
+        both = jnp.stack([even.reshape(rows, 4, -1), odd.reshape(rows, 4, -1)], axis=2)
+        results, start = [], 0
+        for size in sizes or both.shape[3:]:
+            results.append(both[..., start : start + size].reshape(rows, -1))
+            start += size
+        return results
+
+    d_q, d_k, d_v = merge(r_qkv, q_qkv, 2 * HEAD_DIM, HEAD_DIM, HEAD_DIM)
+    d_ck, d_cv = merge(r_ckv, q_ckv, HEAD_DIM, HEAD_DIM)
+    (d_cq,), (d_gate,), (d_up,) = merge(r_cq, q_cq), merge(r_gate, q_gate), merge(r_up, q_up)
     return (
         output.reshape(layer_input.shape),
         input_grad.astype(f32).reshape(layer_input.shape),
         memory_grad.astype(f32).reshape(memory.shape),
         n_self,
-        merge(r_qkv[:, :inner], q_qkv[:, :inner]),
-        merge(r_qkv[:, inner : inner + half], q_qkv[:, inner : inner + half]),
-        merge(r_qkv[:, inner + half :], q_qkv[:, inner + half :]),
+        d_q,
+        d_k,
+        d_v,
         r_out,
         bias_grad,
         n_cross,
-        merge(r_cq, q_cq),
-        merge(r_ckv[:, :half], q_ckv[:, :half]),
-        merge(r_ckv[:, half:], q_ckv[:, half:]),
+        d_cq,
+        d_ck,
+        d_cv,
         r_cout,
         n_ff,
-        merge(r_gate, q_gate),
-        merge(r_up, q_up),
+        d_gate,
+        d_up,
         r_down,
     )
 

time: 587 us -> 497 us (0.85)
  Pallas kernels: 400 us -> 370 us
  other arithmetic: 45.4 us -> 19.9 us
  matrix products: 78 us -> 62.5 us
  local copies, waits for them, and re-layouts: 54 us -> 39.6 us
    pallas_call x4 -> x2, Pallas kernels: 240 us -> 210 us  [the longest x1 114 us: self_part(): pl.pallas_call(functools.partial(self_backward_kernel, depth), in_specs=[...]
    dot_general x8 -> x3, matrix products: 31.6 us -> 17.8 us  [weight_grad(): lax.dot_general(left, right, (((0,), (0,)), ((), ())), preferred_element_...]
    slice x27 -> x9, local copies, waits for them, and re-layouts: 12.5 us -> 1.58 us  [the longest x8 0.8 us: merge(): results.append(both[..., start:start + size].reshape(rows, -1))]
    mul x3 -> x0, other arithmetic: 9.38 us -> none  [the longest x2 8.79 us: rms_back(): upstream * value * inverse]
    reduce_sum x6 -> x0, other arithmetic: 8.67 us -> none  [the longest x3 5.71 us: inverse_rms(): return lax.rsqrt(jnp.mean(value * value, axis=-1, keepdims=True) + EPS)]
    unnamed x154 -> x75, local copies, waits for them, and re-layouts: 7.8 us -> 14 us
    reshape x18 -> x17, local copies, waits for them, and re-layouts: 13.4 us -> 10.8 us  [the longest x8 7.04 us: merge(): results.append(both[..., start:start + size].reshape(rows, -1))]
    dot_general x8 -> x3, matrix products: 26.6 us -> 26.5 us  [project_back(): lax.dot_general(grad, weight, (((1,), (1,)), ((), ())), preferred_element...]
  transfers between devices with their start and end apart: 5 -> 1, of which waited for: 0 -> 0; matrix products, arithmetic and copies ran while one was open for 12% -> 9% of each run, Pallas kernels for 0% -> 19%
where the time goes in v4:
time: 497 us; the launch traced here: 494 us
  Pallas kernels  370 us (74%)
  matrix products  62.5 us (13%)
  local copies, waits for them, and re-layouts  39.6 us (8%)
  other arithmetic  19.9 us (4%)
    pallas_call x1, Pallas kernels, forward_layer(): pl.pallas_call(functools.partial(forward_layer_kernel, depth), in_specs=[...  160 us
    pallas_call x1, Pallas kernels, self_part(): pl.pallas_call(functools.partial(self_backward_kernel, depth), in_specs=[...  114 us
    pallas_call x1, Pallas kernels, cross_part(): pl.pallas_call(functools.partial(cross_backward_kernel, depth), in_specs=...  95.8 us
    dot_general x3, matrix products, project_back(): lax.dot_general(grad, weight, (((1,), (1,)), ((), ())), preferred_element...  26.5 us
    dot_general x3, matrix products, project(): return jnp.dot(left, right, preferred_element_type=jnp.float32)  18.2 us
    dot_general x3, matrix products, weight_grad(): lax.dot_general(left, right, (((0,), (0,)), ((), ())), preferred_element_...  17.8 us
    unnamed x75, local copies, waits for them, and re-layouts  14 us
  transfers between devices with their start and end apart: 1, of which 0 were waited for; matrix products, arithmetic and copies ran while one was open for 9% of the time, Pallas kernels for 19%

profile of v4, /device:TPU:0, one launch (start us, length us, event | category | flops | bytes accessed | tf_op | source)
XLA Modules:
  0.0 493.9 jit_solution(6648336744980827028)
XLA Ops:
  0.7 0.8 pad_reduce_fusion
  2.1 0.7 fusion.20.refs_9_
  4.8 1.0 copy.95
  5.8 1.0 copy.96
  7.2 1.1 reshape.324
  10.4 0.8 copy.102
  11.7 1.1 reshape.319
  12.9 1.0 copy.90
  14.2 1.0 copy.91
  15.9 1.2 reshape_reshape.3.refs_4_
  18.6 1.2 pad_maximum_fusion.refs_7_
  20.4 2.1 pad_maximum_fusion.1
  22.5 160.3 %shard_map.340 = (bf16[4,2,128,1024]{3,2,1,0:T(8,128)(2,1)}, bf16[4,2,128,1024]{3,2,1,0:T(8,128)(2,1)}, bf16[4,2,64,1024]{3,2,1,0:T(8,128)(2,1)}, f32[4,2,4,8,12...) custom-call(bf16[2,2,128,1024]{3,2,1,0:T(8,128)(2,1)} %bitcast.144, ...), custom_call_target="tpu_custom_call" | custom-call | flops 16000000000 | bytes 134217728 | tf_op jit(solution)/shard_map/pallas_call | solution.py:1227
  182.8 8.5 %fusion.10 = f32[1024,1408]{1,0:T(8,128)} fusion(bf16[1024,1024]{1,0:T(8,128)(2,1)} %get-tuple-element.67, bf16[1024,2816]{1,0:T(8,128)(2,1)} %bitcast.148), kind=kOutput, calls=%fused_computation.21 | convolution fusion | flops 2952790016 | bytes 10747904 | tf_op jit(solution)/shard_map/dot_general | solution.py:37
  191.3 5.2 %fusion.14 = f32[1024,1408]{1,0:T(8,128)} fusion(bf16[1024,1024]{1,0:T(8,128)(2,1)S(1)} %copy-done.23, bf16[1024,2816]{1,0:T(8,128)(2,1)S(1)} %bitcast.151), kind=kOutput, calls=%fused_computation.25 | convolution fusion | flops 2952790016 | bytes 10747904 | tf_op jit(solution)/shard_map/dot_general | solution.py:37
  196.9 1.4 copy-done.21
  198.2 11.7 %multiply_convert_fusion = (bf16[1024,1408]{1,0:T(8,128)(2,1)}, bf16[1024,1408]{1,0:T(8,128)(2,1)}, bf16[1024,1408]{1,0:T(8,128)(2,1)S(1)}) fusion(f32[1024,1408]{1,0:T(8,128)} %fusion.14, f32[1024,1408]{1,0:T(8,128)} %fusion.10, bf16[1024,1024]{1,0:T(8,128)(2,1)S(1)} %bitcast.118, bf16[1408,1024]{1,0:T(8,128)(2,1)S(1)} %bitcast.152), kind=kOutput, calls=%fused_computation.9 | convolution fusion | flops 2990276608 | bytes 25165824 | tf_op jit(solution)/shard_map/dot_general | solution.py:41
  210.0 1.6 copy-done.27
  211.6 4.6 convolution_convert_fusion.3
  216.2 2.3 dynamic-slice_bitcast_fusion
  219.0 8.3 %fusion.8 = f32[1024,1024]{1,0:T(8,128)} fusion(bf16[1024,1408]{1,0:T(8,128)(2,1)} %get-tuple-element.170, bf16[1024,2816]{1,0:T(8,128)(2,1)} %bitcast.149), kind=kOutput, calls=%fused_computation.19 | convolution fusion | flops 2952790016 | bytes 9961472 | tf_op jit(solution)/shard_map/dot_general | solution.py:41
  227.3 5.0 %convolution_convert_fusion = bf16[1024,1408]{1,0:T(8,128)(2,1)} fusion(bf16[1024,1024]{1,0:T(8,128)(2,1)S(1)} %copy-done.24, bf16[1024,1408]{1,0:T(8,128)(2,1)S(1)} %copy-done.26), kind=kOutput, calls=%fused_computation.16 | convolution fusion | flops 2954231808 | bytes 7864320 | tf_op jit(solution)/shard_map/dot_general | solution.py:47
  232.3 7.7 %convolution_convert_fusion.1 = bf16[1024,1408]{1,0:T(8,128)(2,1)} fusion(bf16[1024,1024]{1,0:T(8,128)(2,1)} %get-tuple-element.67, bf16[1024,1408]{1,0:T(8,128)(2,1)} %get-tuple-element.171), kind=kOutput, calls=%fused_computation.17 | convolution fusion | flops 2954231808 | bytes 7864320 | tf_op jit(solution)/shard_map/dot_general | solution.py:47
  240.1 6.5 %add_convert_fusion.refs_5_ = bf16[1024,1024]{1,0:T(8,128)(2,1)} fusion(f32[1024,1024]{1,0:T(8,128)S(1)} %copy-done.22, bf16[1024,1408]{1,0:T(8,128)(2,1)S(1)} %copy-done.25, bf16[1024,2816]{1,0:T(8,128)(2,1)} %bitcast.150), kind=kOutput, calls=%fused_computation.14 | convolution fusion | flops 2954887168 | bytes 12058624 | tf_op jit(solution)/shard_map/dot_general | solution.py:41
  247.0 1.4 copy-done.28
  248.4 5.0 %convolution_convert_fusion.2 = bf16[1408,1024]{1,0:T(8,128)(2,1)} fusion(bf16[1024,1408]{1,0:T(8,128)(2,1)S(1)} %copy-done.28, bf16[1024,1024]{1,0:T(8,128)(2,1)S(1)} %fusion.7.refs_6_), kind=kOutput, calls=%fused_computation.18 | convolution fusion | flops 2954231808 | bytes 7864320 | tf_op jit(solution)/shard_map/dot_general | solution.py:47
  253.4 0.9 copy.103.refs_11_
  254.2 95.8 %shard_map.341 = (f32[88,1024]{1,0:T(8,128)}, f32[32,1408]{1,0:T(8,128)}, f32[32,1408]{1,0:T(8,128)}, bf16[32,1408]{1,0:T(8,128)(2,1)}, bf16[32,1408]{1,0:T(8,12...) custom-call(bf16[4,1,2,2,88,1024]{5,4,3,2,1,0:T(8,128)(2,1)} %bitcas, ...), custom_call_target="tpu_custom_call" | custom-call | flops 16000000000 | bytes 134217728 | tf_op jit(solution)/shard_map/pallas_call | solution.py:1498
  350.0 1.0 convert_select_fusion.1
  351.8 1.2 reshape.356
  353.0 1.7 convert_select_fusion.3
  354.9 1.1 stack_reshape.37
  356.4 1.2 reshape.355
  357.6 1.0 copy.106.refs_10_
  359.3 2.9 fusion.17.refs_4_
  362.2 113.7 %shard_map.342 = (f32[32,1024]{1,0:T(8,128)}, f32[32,512]{1,0:T(8,128)}, f32[32,512]{1,0:T(8,128)}, f32[32,1024]{1,0:T(8,128)}, f32[32,1024]{1,0:T(8,128)}, /*in...) custom-call(bf16[4,1,2,2,32,1024]{5,4,3,2,1,0:T(8,128)(2,1)} %bitcas, ...), custom_call_target="tpu_custom_call" | custom-call | flops 16000000000 | bytes 134217728 | tf_op jit(solution)/shard_map/pallas_call | solution.py:1706
  476.0 1.0 convert_select_fusion.4
  477.3 0.8 slice.71
  478.7 0.9 convert_select_fusion.6
  480.0 0.8 reshape.353
  480.9 0.8 reshape.354
  481.9 0.8 reshape.352
  482.8 0.8 reshape.348
  483.7 0.8 reshape.349
  484.6 0.8 reshape.347
  485.3 1.6 bitcast_convert_fusion
  486.9 1.1 bitcast_convert_fusion.1
  490.6 1.0 copy.132
  (132 shorter events, 18.5 us)
Async XLA Ops:
  0.7 7.9 %copy-start.5 = (bf16[128,2816]{1,0:T(8,128)(2,1)S(1)}, bf16[128,2816]{1,0:T(8,128)(2,1)}, u32[]{:S(2)}) copy-start(bf16[128,2816]{1,0:T(8,128)(2,1)} %param.38) | copy-start | bytes 2162692
  8.3 1.7 copy-start.6
  15.2 4.6 copy-start.17
  15.2 4.6 copy-start.18
  15.2 4.6 copy-start.19
  15.2 5.2 %copy-start.9 = (bf16[128,1024]{1,0:T(8,128)(2,1)S(1)}, bf16[128,1024]{1,0:T(8,128)(2,1)}, u32[]{:S(2)}) copy-start(bf16[128,1024]{1,0:T(8,128)(2,1)} %param.36) | copy-start | bytes 786436
  182.8 8.5 %copy-start.20 = (bf16[4,2,4,32,2816]{4,3,2,1,0:T(8,128)(2,1)S(1)}, bf16[4,2,4,32,2816]{4,3,2,1,0:T(8,128)(2,1)}, u32[]{:S(2)}) copy-start(bf16[4,2,4,32,2816]{4,3,2,1,0:T(8,128)(2,1)} %get-tuple-element.68) | copy-start | bytes 17301508
  182.8 8.5 %copy-start.23 = (bf16[1024,1024]{1,0:T(8,128)(2,1)S(1)}, bf16[1024,1024]{1,0:T(8,128)(2,1)}, u32[]{:S(2)}) copy-start(bf16[1024,1024]{1,0:T(8,128)(2,1)} %get-tuple-element.67) | copy-start | bytes 6291460
  191.2 5.2 %copy-start.14 = (f32[1,1024]{1,0:T(1,128)S(1)}, f32[1,1024]{1,0:T(1,128)}, u32[]{:S(2)}) copy-start(f32[1,1024]{1,0:T(1,128)} %get-tuple-element.70) | copy-start | bytes 12292
  191.2 5.2 %copy-start = (bf16[4,2,128,1024]{3,2,1,0:T(8,128)(2,1)S(1)}, bf16[4,2,128,1024]{3,2,1,0:T(8,128)(2,1)}, u32[]{:S(2)}) copy-start(bf16[4,2,128,1024]{3,2,1,0:T(8,128)(2,1)} %get-tuple-element.69) | copy-start | bytes 6291460
  196.4 1.8 copy-start.21
  210.0 1.6 copy-start.27
  218.4 140.8 %collective-permute-start = (bf16[4,128,1024]{2,1,0:T(8,128)(2,1)}, bf16[4,128,1024]{2,1,0:T(8,128)(2,1)S(1)}, u32[]{:S(2)}, u32[]{:S(2)}) collective-permute-start(bf16[4,128,1024]{2,1,0:T(8,128)(2,1)} %dynamic-slice_bitcast_fusion), channel_id=1, source_target_pairs={{0,4},{1,5},{2,6},{3,7},{4,0},{5,1},{6,2},{7,3},{8,12},{9,13},{10,... | collective-permute-start | bytes 3145736 | tf_op jit(solution)/shard_map/ppermute | solution.py:1811
  219.0 8.3 %copy-start.24 = (bf16[1024,1024]{1,0:T(8,128)(2,1)S(1)}, bf16[1024,1024]{1,0:T(8,128)(2,1)}, u32[]{:S(2)}) copy-start(bf16[1024,1024]{1,0:T(8,128)(2,1)} %get-tuple-element.67) | copy-start | bytes 6291460
  219.0 8.3 %copy-start.26 = (bf16[1024,1408]{1,0:T(8,128)(2,1)S(1)}, bf16[1024,1408]{1,0:T(8,128)(2,1)}, u32[]{:S(2)}) copy-start(bf16[1024,1408]{1,0:T(8,128)(2,1)} %get-tuple-element.170) | copy-start | bytes 8650756
  232.3 7.7 %copy-start.22 = (f32[1024,1024]{1,0:T(8,128)S(1)}, f32[1024,1024]{1,0:T(8,128)}, u32[]{:S(2)}) copy-start(f32[1024,1024]{1,0:T(8,128)} %fusion.8) | copy-start | bytes 12582916
  232.3 7.7 %copy-start.25 = (bf16[1024,1408]{1,0:T(8,128)(2,1)S(1)}, bf16[1024,1408]{1,0:T(8,128)(2,1)}, u32[]{:S(2)}) copy-start(bf16[1024,1408]{1,0:T(8,128)(2,1)} %get-tuple-element.171) | copy-start | bytes 8650756
  246.5 1.8 copy-start.28
  248.4 5.0 %copy-start.2 = (bf16[1024,1024]{1,0:T(8,128)(2,1)}, bf16[1024,1024]{1,0:T(8,128)(2,1)S(1)}, u32[]{:S(2)}) copy-start(bf16[1024,1024]{1,0:T(8,128)(2,1)S(1)} %fusion.7.refs_6_) | copy-start | bytes 6291460
  248.4 5.0 %copy-start.16 = (f32[1,512]{1,0:T(1,128)S(1)}, f32[1,512]{1,0:T(1,128)}, u32[]{:S(2)}) copy-start(f32[1,512]{1,0:T(1,128)} %get-tuple-element.78) | copy-start | bytes 6148
  351.5 7.1 %copy-start.15 = (s32[1024]{0:T(1024)S(1)}, s32[1024]{0:T(1024)}, u32[]{:S(2)}) copy-start(s32[1024]{0:T(1024)} %param.25) | copy-start | bytes 12292
  351.5 7.7 %copy-start.1 = (bf16[1024,1024]{1,0:T(8,128)(2,1)S(1)}, bf16[1024,1024]{1,0:T(8,128)(2,1)}, u32[]{:S(2)}) copy-start(bf16[1024,1024]{1,0:T(8,128)(2,1)} %convolution_convert_fusion.3) | copy-start | bytes 6291460
  475.9 5.7 %copy-start.12 = (f32[32,512]{1,0:T(8,128)S(1)}, f32[32,512]{1,0:T(8,128)}, u32[]{:S(2)}) copy-start(f32[32,512]{1,0:T(8,128)} %get-tuple-element.106) | copy-start | bytes 196612
  475.9 5.7 %copy-start.13 = (bf16[32,512]{1,0:T(8,128)(2,1)S(1)}, bf16[32,512]{1,0:T(8,128)(2,1)}, u32[]{:S(2)}) copy-start(bf16[32,512]{1,0:T(8,128)(2,1)} %get-tuple-element.107) | copy-start | bytes 98308
  477.1 8.2 %copy-start.3 = (bf16[2,2,128,1024]{3,2,1,0:T(8,128)(2,1)S(1)}, bf16[2,2,128,1024]{3,2,1,0:T(8,128)(2,1)}, u32[]{:S(2)}) copy-start(bf16[2,2,128,1024]{3,2,1,0:T(8,128)(2,1)} %get-tuple-element.100) | copy-start | bytes 3145732
  481.7 5.2 %copy-start.7 = (bf16[2,2,64,1024]{3,2,1,0:T(8,128)(2,1)S(1)}, bf16[2,2,64,1024]{3,2,1,0:T(8,128)(2,1)}, u32[]{:S(2)}) copy-start(bf16[2,2,64,1024]{3,2,1,0:T(8,128)(2,1)} %get-tuple-element.101) | copy-start | bytes 1572868
  483.5 7.0 %copy-start.4 = (bf16[2,2,128,1024]{3,2,1,0:T(8,128)(2,1)S(1)}, bf16[2,2,128,1024]{3,2,1,0:T(8,128)(2,1)}, u32[]{:S(2)}) copy-start(bf16[2,2,128,1024]{3,2,1,0:T(8,128)(2,1)} %get-tuple-element.99) | copy-start | bytes 3145732
  485.3 6.2 %copy-start.11 = (f32[32,1024]{1,0:T(8,128)S(1)}, f32[32,1024]{1,0:T(8,128)}, u32[]{:S(2)}) copy-start(f32[32,1024]{1,0:T(8,128)} %get-tuple-element.219) | copy-start | bytes 393220
  485.3 6.9 %copy-start.10 = (f32[32,1024]{1,0:T(8,128)S(1)}, f32[32,1024]{1,0:T(8,128)}, u32[]{:S(2)}) copy-start(f32[32,1024]{1,0:T(8,128)} %get-tuple-element.225) | copy-start | bytes 393220
  486.9 6.0 %copy-start.8 = (f32[88,1024]{1,0:T(8,128)S(1)}, f32[88,1024]{1,0:T(8,128)}, u32[]{:S(2)}) copy-start(f32[88,1024]{1,0:T(8,128)} %get-tuple-element.229) | copy-start | bytes 1081348

commit v5 on v4

--- a/solution.py
+++ b/solution.py
@@ -14,6 +14,8 @@
 TGT = 1024
 MEM = 512
 QB = 256
+GELU_SCALE = 0.7978845608
+GELU_CUBE = 0.044715
 
 
 EPS = 1e-06
@@ -888,11 +890,61 @@
     yield
 
 
-def add_into(target, other, places):
-    for place in places:
-        target[place] = (
-            target[place].astype(jnp.float32) + other[place].astype(jnp.float32)
-        ).astype(jnp.bfloat16)
+def reach_columns(spot, wires, pack, near):
+    depth, me = spot.depth, spot.corner
+    ahead = wires.take(2 * depth)
+    own = wires.move(pack.at[spot.core, me], near.at[spot.z, spot.core])
+    for step in range(depth):
+        for flip in range(2):
+            if step or flip:
+                wires.send(
+                    pack.at[spot.core ^ flip, me],
+                    near.at[spot.z, spot.core],
+                    spot.at((spot.z + step) % depth, spot.core ^ flip),
+                    ahead + 2 * step + flip,
+                )
+    yield
+    own.wait()
+    for step in range(depth):
+        z = (spot.z - step + depth) % depth
+        for flip in range(2):
+            if step or flip:
+                wires.arrive(near.at[z, spot.core ^ flip], spot.sibling(), ahead + 2 * step + flip)
+    yield
+
+
+def reach_rows(spot, wires, pack, near):
+    depth, me = spot.depth, spot.corner
+    ahead = wires.take(depth)
+    own = wires.move(pack.at[0, me], near.at[spot.z])
+    for step in range(1, depth):
+        wires.send(pack.at[0, me], near.at[spot.z], spot.at((spot.z + step) % depth), ahead + step)
+    yield
+    own.wait()
+    for step in range(1, depth):
+        z = (spot.z - step + depth) % depth
+        wires.arrive(near.at[z], spot.sibling(), ahead + step)
+    yield
+
+
+def share_plane(spot, wires, near, whole, parts):
+    me = spot.corner
+    flat = wires.take(4)
+    own = wires.move(near, whole(me))
+    wires.send(near, whole(me), spot.beside(), flat)
+    wires.send(near, whole(me), spot.below(), flat + 1)
+    yield
+    wires.arrive(whole(me ^ 1), spot.sibling(), flat)
+    piece = parts(whole(me ^ 1), 0)
+    wires.send(piece, piece, spot.below(), flat + 2)
+    wires.arrive(whole(me ^ 2), spot.sibling(), flat + 1)
+    piece = parts(whole(me ^ 2), 1)
+    wires.send(piece, piece, spot.beside(), flat + 3)
+    yield
+    own.wait()
+    wires.arrive(parts(whole(me ^ 3), 0), spot.sibling(), flat + 2)
+    wires.arrive(parts(whole(me ^ 3), 1), spot.sibling(), flat + 3)
+    yield
 
 
 def scatter_buffers(depth, lanes, rows, width):
@@ -910,26 +962,39 @@
     ]
 
 
-def scatter_sums(spot, wires, grads, buffers, total, got):
+def scatter_sums(spot, wires, grads, buffers, total, got, resident=False):
     depth, half = spot.depth, spot.depth // 2
     lanes = grads.shape[1]
-    low, high, low_in, high_in, low_last, high_last, column, column_in, passing = buffers
+    places = [(z, a, s) for z in range(half) for a in range(lanes) for s in range(2)]
+    if resident:
+        low_in, high_in, low_last, high_last, column, column_in, passing = buffers
+        low, high = low_in, high_in
+    else:
+        low, high, low_in, high_in, low_last, high_last, column, column_in, passing = buffers
     first = wires.take(4)
     away = wires.take(depth)
-    mine = [
-        wires.move(grads.at[pl.ds(0, half), :, :, spot.x], low),
-        wires.move(grads.at[pl.ds(half, half), :, spot.y], high),
-    ]
+    mine = []
+    if not resident:
+        mine = [
+            wires.move(grads.at[pl.ds(0, half), :, :, spot.x], low),
+            wires.move(grads.at[pl.ds(half, half), :, spot.y], high),
+        ]
     wires.send(grads.at[pl.ds(0, half), :, :, 1 - spot.x], low_in, spot.beside(), first)
     wires.send(grads.at[pl.ds(half, half), :, 1 - spot.y], high_in, spot.below(), first + 1)
     yield
     for copy in mine:
         copy.wait()
+
+    def join(target, other, index):
+        target[index] = (target[index].astype(jnp.float32) + other.astype(jnp.float32)).astype(jnp.bfloat16)
+
     wires.arrive(low_in, spot.beside(), first)
-    add_into(low, low_in, [(z, a, s) for z in range(half) for a in range(lanes) for s in range(2)])
+    for z, a, s in places:
+        join(low, grads[z, a, s, spot.x] if resident else low_in[z, a, s], (z, a, s))
     wires.send(low.at[:, :, 1 - spot.y], low_last, spot.below(), first + 2)
     wires.arrive(high_in, spot.below(), first + 1)
-    add_into(high, high_in, [(z, a, s) for z in range(half) for a in range(lanes) for s in range(2)])
+    for z, a, s in places:
+        join(high, grads[half + z, a, spot.y, s] if resident else high_in[z, a, s], (z, a, s))
     wires.send(high.at[:, :, 1 - spot.x], high_last, spot.beside(), first + 3)
     yield
     wires.arrive(low_last, spot.below(), first + 2)
@@ -1028,11 +1093,17 @@
 
 def forward_layer_kernel(depth, *refs):
     (
-        x, t, m, s, p1, p2, p3, p4, p5, codes, holes,
-        wx, wt, wm, ws, w1, w2, w3, w4, w5,
-        a1, qkv, ctx, lse, x1, a2, qc, ckv, ctxc, lsec, x2, a3, gains, keeps, keepc, bent,
-        bias, own, got, own2, got2, *sems
+        x, t, m, s, p1, p2, p3, p4, p5, p6, p7, codes, holes,
+        o_wx, wt, o_wm, ws, o_w1, o_w2, o_w3, w4, w5,
+        o_a1, o_qkv, o_ctx, lse, o_x1, o_a2, o_qc, o_ckv, o_ctxc, lsec, o_x2, o_a3, gains, keeps, keepc, bent,
+        down_s, down_c, n6, n7,
+        bias, own, got, own2, got2, wx, wm, w1, w2, w3, a1, qkv, ctx, x1, a2, qc, ckv, ctxc, x2, a3, *sems
     ) = refs
+    leaving = []
+
+    def leave(*pairs):
+        leaving.extend(wires.move(source, target) for source, target in pairs)
+
     f32, bf16 = jnp.float32, jnp.bfloat16
     spot = Spot(depth)
     wires = Wires(*sems)
@@ -1053,14 +1124,15 @@
     wide = gather_columns(spot, wires, p4, w4)
     down = gather_rows(spot, wires, p5, w5)
     top = collect_tokens(spot, wires, t, wt)
+    wide_next = reach_columns(spot, wires, p6, n6)
+    down_next = reach_rows(spot, wires, p7, n7)
     over = wires.take(2 * blocks)
-    for program in (tokens, small, first, small, tokens, first):
-        next(program)
-    next(outs)
-    next(second)
-    next(memory)
-    for program in (small, first, tokens, small, first):
-        next(program)
+
+    def advance(*programs):
+        for program in programs:
+            next(program)
+
+    advance(small, first, small, tokens, small, small)
 
     def line(row):
         return jnp.concatenate([ws[z, c, 0, row : row + 1, :] for z in range(depth) for c in range(2)], axis=1)
@@ -1073,6 +1145,9 @@
     places = lax.broadcasted_iota(jnp.int32, (1, blocks * QB), 1).astype(f32)
     keeps[...] = jnp.where(places < length, 0.0, NEG)
     keepc[...] = jnp.where(places[:, : keepc.shape[1]] < span, 0.0, NEG)
+    places = lax.broadcasted_iota(jnp.int32, (blocks * QB, 1), 0).astype(f32)
+    down_s[...] = jnp.where(places < length, 0.0, NEG)
+    down_c[...] = jnp.where(places[: down_c.shape[0]] < span, 0.0, NEG)
     table = jnp.concatenate(
         [
             ws[z, c, 0, 4:8, :] + ws[z, c, 1, 4:8, :] + ws[z, c, 2, 4:8, :] + ws[z, c, 3, 4:8, :]
@@ -1091,6 +1166,12 @@
                 bias[kv, member * QB : (member + 1) * QB, (3 - offset) * QB : (4 - offset) * QB] = spread_row(
                     vectors[head : head + 1, offset * 2 * QB : (offset + 1) * 2 * QB]
                 )
+
+    advance(first, outs, second, tokens, tokens)
+    for block in range(blocks):
+        a1[rows(block), :] = normed(wx[block].reshape(QB, -1).astype(f32), gains[0:1, :])
+    advance(first, memory, first)
+    leave((wx, o_wx), (w1, o_w1), (a1, o_a1))
 
     def attend_rows(block, queries, keys, stop, keep, mixed, sums, causal):
         for kv in range(kvs):
@@ -1118,24 +1199,13 @@
 
     weight = w1[...].reshape(-1, w1.shape[-1])
     for block in range(blocks):
-        value = wx[block].reshape(QB, -1).astype(f32)
-        a1[rows(block), :] = normed(value, gains[0:1, :])
         qkv[rows(block), :] = nn(a1[rows(block), :], weight).astype(bf16)
-        if block == 0:
-            next(outs)
-            next(second)
-            next(wide)
+        attend_rows(block, qkv, qkv, (block + 1) * QB, keeps, ctx, lse, True)
         if block == 1:
-            next(outs)
-            next(second)
-            next(memory)
+            advance(outs, wide, down, second, memory)
         if block == 2:
-            next(outs)
-            next(second)
-            next(memory)
-            next(wide)
-            next(down)
-        attend_rows(block, qkv, qkv, (block + 1) * QB, keeps, ctx, lse, True)
+            advance(outs)
+    advance(outs, second, wide, down, wide_next, down_next)
 
     def pass_on(block, mine, theirs, value, weight, index):
         mine[rows(block), :] = nn(value[rows(block), :], weight).astype(bf16)
@@ -1148,9 +1218,8 @@
     weight = w3[0].reshape(-1, w3.shape[-1])
     for block in range(blocks):
         pass_on(block, own, got, ctx, weight, 0)
-    next(wide)
-    next(down)
-    next(top)
+    advance(memory, second, wide, down, top)
+    leave((wm, o_wm), (w2, o_w2), (w3, o_w3), (qkv, o_qkv), (ctx, o_ctx))
     weight = w2[...].reshape(-1, w2.shape[-1])
     ckv[...] = nn(wm[...].reshape(-1, wm.shape[-1]), weight[:, :inner]).astype(bf16)
     for block in range(blocks):
@@ -1158,25 +1227,33 @@
         x1[rows(block), :] = value
         a2[rows(block), :] = normed(value, gains[1:2, :])
         qc[rows(block), :] = nn(a2[rows(block), :], weight[:, inner:]).astype(bf16)
+    leave((x1, o_x1), (a2, o_a2), (qc, o_qc), (ckv, o_ckv))
     weight = w3[1].reshape(-1, w3.shape[-1])
     for block in range(blocks):
         attend_rows(block, qc, ckv, ckv.shape[0], keepc, ctxc, lsec, False)
         pass_on(block, own2, got2, ctxc, weight, blocks)
-        if block == 1:
-            next(down)
-            next(top)
+        if block == 0:
+            advance(wide, down)
+        if block == 2:
+            advance(top)
     for block in range(blocks):
         value = x1[rows(block), :] + joined(block, own2, got2, blocks)
         x2[rows(block), :] = value
         a3[rows(block), :] = normed(value, gains[2:3, :])
-    for program in (wide, down, top):
-        next(program)
-    for program in (tokens, small, first, memory, second, outs, wide, down, top):
+        leave(
+            (x2.at[rows(block)], o_x2.at[rows(block)]),
+            (a3.at[rows(block)], o_a3.at[rows(block)]),
+            (ctxc.at[rows(block)], o_ctxc.at[rows(block)]),
+        )
+    advance(wide_next, down_next, top)
+    for program in (tokens, small, first, memory, second, outs, wide, down, top, wide_next, down_next):
         assert next(program, None) is None
+    for copy in leaving:
+        copy.wait()
     wires.close()
 
 
-def forward_layer(depth, x, t, m, small, p1, p2, p3, p4, p5, codes, holes):
+def forward_layer(depth, x, t, m, small, p1, p2, p3, p4, p5, p6, p7, codes, holes):
     bf16, f32 = jnp.bfloat16, jnp.float32
     shape = jax.ShapeDtypeStruct
 
@@ -1197,69 +1274,52 @@
     hbm = pl.BlockSpec(memory_space=pl.ANY)
     vmem = pl.BlockSpec(memory_space=pltpu.VMEM)
     outs = [
-        (whole_tokens(x), vmem),
+        (whole_tokens(x), hbm),
         (whole_tokens(t), hbm),
-        (whole_tokens(m), vmem),
+        (whole_tokens(m), hbm),
         (shape((depth, 2, 4, 8, 128), f32), vmem),
-        (whole_columns(p1), vmem),
-        (whole_columns(p2), vmem),
-        (whole_rows(p3), vmem),
+        (whole_columns(p1), hbm),
+        (whole_columns(p2), hbm),
+        (whole_rows(p3), hbm),
         (whole_columns(p4), hbm),
         (whole_rows(p5), hbm),
-        (shape((tokens, width), bf16), vmem),
-        (shape((tokens, 2 * inner), bf16), vmem),
-        (shape((tokens, inner), bf16), vmem),
+        (shape((tokens, width), bf16), hbm),
+        (shape((tokens, 2 * inner), bf16), hbm),
+        (shape((tokens, inner), bf16), hbm),
         (shape((heads, tokens), f32), vmem),
-        (shape((tokens, width), f32), vmem),
-        (shape((tokens, width), bf16), vmem),
-        (shape((tokens, inner), bf16), vmem),
-        (shape((span, inner), bf16), vmem),
-        (shape((tokens, inner), bf16), vmem),
+        (shape((tokens, width), f32), hbm),
+        (shape((tokens, width), bf16), hbm),
+        (shape((tokens, inner), bf16), hbm),
+        (shape((span, inner), bf16), hbm),
+        (shape((tokens, inner), bf16), hbm),
         (shape((heads, tokens), f32), vmem),
-        (shape((tokens, width), f32), vmem),
-        (shape((tokens, width), bf16), vmem),
+        (shape((tokens, width), f32), hbm),
+        (shape((tokens, width), bf16), hbm),
         (shape((8, width), f32), vmem),
         (shape((1, tokens), f32), vmem),
         (shape((1, span), f32), vmem),
         (shape((heads, 8 * QB), f32), vmem),
+        (shape((tokens, 1), f32), vmem),
+        (shape((span, 1), f32), vmem),
+        (shape((depth, 2) + p6.shape[2:], bf16), hbm),
+        (shape((depth,) + p7.shape[2:], bf16), hbm),
     ]
     swap = pltpu.VMEM((tokens, width), bf16)
     return pl.pallas_call(
         functools.partial(forward_layer_kernel, depth),
-        in_specs=[hbm] * 9 + [vmem] * 2,
+        in_specs=[hbm] * 11 + [vmem] * 2,
         out_specs=[spec for _, spec in outs],
         out_shape=[kind for kind, _ in outs],
         scratch_shapes=[pltpu.VMEM((heads // 2, 2 * QB, 4 * QB), f32), swap, swap, swap, swap]
-        + wire_scratch(35 + 30 * depth, 12),
+        + [pltpu.VMEM(outs[i][0].shape, outs[i][0].dtype) for i in (0, 2, 4, 5, 6, 9, 10, 11, 13, 14, 15, 16, 17, 19, 20)]
+        + wire_scratch(35 + 33 * depth, 40),
         compiler_params=pltpu.CompilerParams(
             collective_id=0, has_side_effects=True, vmem_limit_bytes=60 * 2**20
         ),
         cost_estimate=pl.CostEstimate(
             flops=16 * 10**9, bytes_accessed=128 * 2**20, transcendentals=10**7
         ),
-    )(x, t, m, small, p1, p2, p3, p4, p5, codes, holes)
-
-
-def parts_of(width, pieces):
-    step = -(-width // (128 * pieces)) * 128
-    return [(start, min(step, width - start)) for start in range(0, width, step)]
-
-
-class Reduction:
-    def __init__(self, spot, wires, grads, buffers, total, got, pieces):
-        self.programs = []
-        for (start, size), scratch in zip(pieces, buffers):
-            lanes = pl.ds(start, size)
-            self.programs.append(
-                scatter_sums(
-                    spot,
-                    wires,
-                    grads.at[:, :, :, :, :, lanes],
-                    scratch,
-                    total.at[:, lanes],
-                    None if got is None else got.at[:, lanes],
-                )
-            )
+    )(x, t, m, small, p1, p2, p3, p4, p5, p6, p7, codes, holes)
 
 
 def pipeline(programs, ahead=2, stages=5):
@@ -1298,14 +1358,18 @@
 
 
 def cross_backward_kernel(depth, *refs):
+    g_down, g_gate, g_up, x2, x1, t_out, *far = refs[:16]
     (
-        g_down, g_gate, g_up, x2, x1, u, top, qc, ckv, ctxc, lsec, keep, a2, mem, w2, w3, ctx, gains,
-        r_down, r_gate, r_up, q_gate, q_up, half, do_s, o_cout, o_cq, o_ckv, o_out, o_mem, terms,
+        lsec, keep, gains,
+        r_down, r_gate, r_up, q_gate, q_up, o_cout, o_cq, o_ckv, half, do_s, g_out, o_mem, terms, h_out,
         *rest
-    ) = refs
+    ) = refs[16:]
     take = lambda n: [rest.pop(0) for _ in range(n)]
-    stage, e2, eb, do_c, dqc, dkv, dk_sum, dv_sum, got, own_c, got_c, own_m, got_m, grad = take(14)
-    buffers = [[take(9) for _ in range(2)] for _ in range(3)]
+    near = take(10)
+    u, top, qc, ckv, ctxc, a2, mem, w2, w3, ctx = near
+    g_cout, g_cq, g_ckv = take(3)
+    stage, e2, eb, do_c, dqc, dkv, dk_sum, dv_sum, got, own_c, got_c, own_m, got_m = take(13)
+    buffers = [take(9) for _ in range(3)]
     f32, bf16 = jnp.float32, jnp.bfloat16
     spot = Spot(depth)
     wires = Wires(*rest)
@@ -1315,21 +1379,20 @@
     def rows(block):
         return slice(block * QB, (block + 1) * QB)
 
+    coming = [wires.move(source, target) for source, target in zip(far, near)]
     spot.greet()
     over = wires.take(2 * blocks + 4)
     for block in range(blocks):
-        wires.send(u.at[rows(block)], got.at[rows(block)], spot.sibling(), over + block)
-    programs = []
-    for grads, scratch, total, other in (
-        (g_down, buffers[0], r_down, None),
-        (g_gate, buffers[1], r_gate, q_gate),
-        (g_up, buffers[2], r_up, q_up),
-    ):
-        programs += Reduction(
-            spot, wires, grads, scratch, total, other, parts_of(grads.shape[-1], 2)
-        ).programs
+        wires.send(far[0].at[rows(block)], got.at[rows(block)], spot.sibling(), over + block)
+    home = deliver_tokens(spot, wires, t_out, h_out)
+    programs = [
+        scatter_sums(spot, wires, g_down, buffers[0], r_down, None),
+        scatter_sums(spot, wires, g_gate, buffers[1], r_gate, q_gate),
+        scatter_sums(spot, wires, g_up, buffers[2], r_up, q_up),
+    ]
     links = pipeline(programs)
     next(links)
+    next(home)
 
     loads = {}
 
@@ -1346,6 +1409,8 @@
         return change, jnp.sum(upstream * value * inverse, axis=0, keepdims=True)
 
     fetch(x2, 0, 0)
+    for copy in coming:
+        copy.wait()
     gain_terms = jnp.zeros((1, e2.shape[1]), f32)
     for block in range(blocks):
         if block + 1 < blocks:
@@ -1389,17 +1454,10 @@
             dqc[rows(block), both] = jnp.concatenate([dq[:QB], dq[QB:]], axis=1).astype(bf16)
         dkv[:, base : base + HEAD_DIM] = dk_sum[...].astype(bf16)
         dkv[:, base + HEAD_DIM : base + 2 * HEAD_DIM] = dv_sum[...].astype(bf16)
-        if kv % 2 == 1:
+        if kv:
             next(links)
-
-    writes = {}
-
-    def put(slot, value, target):
-        if slot in writes:
-            writes[slot].wait()
-        view = grad.at[slot, pl.ds(0, value.shape[0]), pl.ds(0, value.shape[1])]
-        view[...] = value.astype(bf16)
-        writes[slot] = wires.move(view, target)
+        if kv == 3:
+            next(home)
 
     weight = w2[...].reshape(-1, w2.shape[-1])
     for block in range(blocks):
@@ -1407,19 +1465,17 @@
         wires.send(own_c.at[rows(block)], got_c.at[rows(block)], spot.sibling(), over + blocks + block)
     own_m[...] = nt(dkv[...], weight[:, :inner]).astype(bf16).reshape(own_m.shape)
     wires.send(own_m.at[:, 1 - spot.core], got_m, spot.sibling(), over + 2 * blocks)
-    slot = 0
     for block in range(blocks):
-        put(slot, tn(a2[:, rows(block)], dqc[...]), o_cq.at[rows(block)])
-        slot = 1 - slot
+        g_cq[block] = tn(a2[:, rows(block)], dqc[...]).reshape(g_cq.shape[1:]).astype(bf16)
     next(links)
     for block in range(blocks):
-        put(slot, tn(mem[:, rows(block)], dkv[...]), o_ckv.at[rows(block)])
-        slot = 1 - slot
-    for block in range(inner // QB):
-        put(slot, tn(ctxc[:, rows(block)], eb[...]), o_cout.at[rows(block)])
-        slot = 1 - slot
+        g_ckv[block] = tn(mem[:, rows(block)], dkv[...]).reshape(g_ckv.shape[1:]).astype(bf16)
     next(links)
-
+    for block in range(2):
+        g_cout[2 * block : 2 * block + 2] = (
+            tn(ctxc[:, rows(block)], eb[...]).reshape((2,) + g_cout.shape[1:]).astype(bf16)
+        )
+    leaving = [wires.move(*pair) for pair in ((g_cq, o_cq), (g_ckv, o_ckv), (g_cout, o_cout))]
     gain_terms = jnp.zeros((1, e2.shape[1]), f32)
     for block in range(blocks):
         if block + 1 < blocks:
@@ -1440,41 +1496,49 @@
     terms[1:2, :] = 0.5 * gain_terms
     next(links)
     for block in range(inner // QB):
-        put(slot, tn(ctx[:, rows(block)], eb[...]), o_out.at[rows(block)])
-        slot = 1 - slot
+        g_out[rows(block), :] = tn(ctx[:, rows(block)], eb[...]).astype(bf16)
     wires.arrive(got_m, spot.sibling(), over + 2 * blocks)
     o_mem[...] = (own_m[:, spot.core].astype(f32) + got_m[...].astype(f32)).astype(bf16)
     for _ in links:
         pass
-    for copy in writes.values():
+    for program in [home]:
+        for _ in program:
+            pass
+    for copy in leaving:
         copy.wait()
     wires.close()
 
 
-def cross_part(depth, g_down, g_gate, g_up, x2, x1, u, top, qc, ckv, ctxc, lsec, keep, a2, mem, w2, w3, ctx, gains):
+def cross_part(depth, *operands):
     bf16, f32 = jnp.bfloat16, jnp.float32
     shape = jax.ShapeDtypeStruct
     hbm = pl.BlockSpec(memory_space=pl.ANY)
     vmem = pl.BlockSpec(memory_space=pltpu.VMEM)
+    g_down, g_gate, g_up, x2, _, t_out, _, _, _, ckv = operands[:10]
+    far = operands[6:16]
     tokens, width = x2.shape
     span, inner = ckv.shape
     own = tokens // 8
+    rows = g_gate.shape[4]
     outs = [
         (shape(g_down.shape[4:], f32), vmem),
         (shape(g_gate.shape[4:], f32), vmem),
         (shape(g_up.shape[4:], f32), vmem),
         (shape(g_gate.shape[4:], bf16), vmem),
         (shape(g_up.shape[4:], bf16), vmem),
+        (shape((depth, 1, 2, 2, rows, width), bf16), hbm),
+        (shape((depth, 2, 2, 2, rows, inner), bf16), hbm),
+        (shape((depth, 2, 2, 2, rows, inner), bf16), hbm),
         (shape((4, own, width), f32), vmem),
         (shape((tokens, inner), bf16), vmem),
-        (shape((inner, width), bf16), hbm),
-        (shape((width, inner), bf16), hbm),
-        (shape((width, inner), bf16), hbm),
-        (shape((inner, width), bf16), hbm),
+        (shape((inner, width), bf16), vmem),
         (shape((4, span // 8, width), bf16), vmem),
         (shape((8, width), f32), vmem),
+        (shape((2, 2) + t_out.shape[1:], bf16), hbm),
     ]
-    scratch = [
+    scratch = [pltpu.VMEM(array.shape, bf16) for array in far]
+    scratch += [pltpu.VMEM(outs[i][0].shape, bf16) for i in (5, 6, 7)]
+    scratch += [
         pltpu.VMEM((2, QB, width), f32),
         pltpu.VMEM((tokens, width), f32),
         pltpu.VMEM((tokens, width), bf16),
@@ -1488,16 +1552,13 @@
         pltpu.VMEM((tokens, width), bf16),
         pltpu.VMEM((4, 2, span // 8, width), bf16),
         pltpu.VMEM((4, span // 8, width), bf16),
-        pltpu.VMEM((2, QB, width), bf16),
     ]
-    number = 12
     for grads in (g_down, g_gate, g_up):
-        for _, size in parts_of(grads.shape[-1], 2):
-            scratch += scatter_buffers(depth, grads.shape[1], grads.shape[4], size)
-            number += 4 + depth
+        scratch += scatter_buffers(depth, grads.shape[1], *grads.shape[4:])
+    number = 16 + 3 * (4 + depth)
     return pl.pallas_call(
         functools.partial(cross_backward_kernel, depth),
-        in_specs=[hbm] * 5 + [vmem] * 13,
+        in_specs=[hbm] * 16 + [vmem] * 3,
         out_specs=[spec for _, spec in outs],
         out_shape=[kind for kind, _ in outs],
         scratch_shapes=scratch + wire_scratch(number, 48),
@@ -1507,19 +1568,22 @@
         cost_estimate=pl.CostEstimate(
             flops=16 * 10**9, bytes_accessed=128 * 2**20, transcendentals=10**7
         ),
-    )(g_down, g_gate, g_up, x2, x1, u, top, qc, ckv, ctxc, lsec, keep, a2, mem, w2, w3, ctx, gains)
+    )(*operands)
 
 
 def self_backward_kernel(depth, *refs):
     (
-        g_cout, g_cq, g_ckv, g_out, t_out, t_mem, do_s, qkv, ctx, lse, keep, bent, a1, x, gains, half, w1,
+        g_cout, g_cq, g_ckv, g_out, t_mem, f_do, f_qkv, f_ctx, f_a1, f_x, f_half, f_w1, lse, keep, bent, gains,
         terms, codes,
-        r_cout, r_cq, r_ckv, r_out, r_qkv, q_cq, q_ckv, q_qkv, h_out, h_mem, h_in, packed,
+        r_cout, r_cq, r_ckv, r_out, r_qkv, q_cq, q_ckv, q_qkv, h_mem, h_in, packed,
         *rest
     ) = refs
     take = lambda n: [rest.pop(0) for _ in range(n)]
     bias, sums, dk_sum, dv_sum, dqkv, grad, mine, theirs, pieces, line, small, work = take(12)
-    buffers = [take(9) for _ in range(8)]
+    near = take(7)
+    do_s, qkv, ctx, a1, x, half, w1 = near
+    buffers = [take(9) for _ in range(4)]
+    resident = [take(7) for _ in range(4)]
     f32, bf16 = jnp.float32, jnp.bfloat16
     spot = Spot(depth)
     wires = Wires(*rest)
@@ -1529,25 +1593,32 @@
     def rows(block):
         return slice(block * QB, (block + 1) * QB)
 
+    far = (f_do, f_qkv, f_ctx, f_a1, f_x, f_half, f_w1)
+    coming = [wires.move(source, target) for source, target in zip(far, near)]
     spot.greet()
     over = wires.take(blocks)
-    homes = [deliver_tokens(spot, wires, t_out, h_out), deliver_tokens(spot, wires, t_mem, h_mem)]
-    programs = [
-        scatter_sums(spot, wires, g_cout, buffers[0], r_cout, None),
-        scatter_sums(spot, wires, g_out, buffers[1], r_out, None),
-        scatter_sums(spot, wires, g_cq, buffers[2], r_cq, q_cq),
-        scatter_sums(spot, wires, g_ckv, buffers[3], r_ckv, q_ckv),
-    ]
+    homes = [deliver_tokens(spot, wires, t_mem, h_mem)]
+    early = pipeline(
+        [
+            scatter_sums(spot, wires, g_cout, buffers[0], r_cout, None),
+            scatter_sums(spot, wires, g_cq, buffers[1], r_cq, q_cq),
+            scatter_sums(spot, wires, g_ckv, buffers[2], r_ckv, q_ckv),
+            scatter_sums(spot, wires, g_out, buffers[3], r_out, None),
+        ]
+    )
+    late = []
     for kv in range(kvs):
         lanes = pl.ds(kv * QB, QB)
-        programs.append(
-            scatter_sums(spot, wires, grad.at[kv], buffers[4 + kv], r_qkv.at[:, lanes], q_qkv.at[:, lanes])
-        )
-    early = pipeline(programs[:4], ahead=2)
-    late = programs[4:]
+        late.append(
+            scatter_sums(
+                spot, wires, grad.at[kv], resident[kv], r_qkv.at[:, lanes], q_qkv.at[:, lanes], True
+            )
+        )
     next(early)
     for program in homes:
         next(program)
+    for copy in coming:
+        copy.wait()
     for kv in range(kvs):
         base = kv * 4 * HEAD_DIM
         both = slice(2 * kv * HEAD_DIM, 2 * (kv + 1) * HEAD_DIM)
@@ -1582,8 +1653,11 @@
             dqkv[rows(block), base : base + 2 * HEAD_DIM] = jnp.concatenate(
                 [dq[:QB], dq[QB:]], axis=1
             ).astype(bf16)
-            if block == 2:
+            if block % 2 or kv == 0 and block:
                 next(early, None)
+            for earlier in range(kv):
+                if block == 2:
+                    next(late[earlier], None)
         dqkv[:, base + 2 * HEAD_DIM : base + 3 * HEAD_DIM] = dk_sum[...].astype(bf16)
         dqkv[:, base + 3 * HEAD_DIM : base + 4 * HEAD_DIM] = dv_sum[...].astype(bf16)
         for member in range(2):
@@ -1600,9 +1674,6 @@
         for block in range(blocks):
             grad[kv, block] = tn(a1[:, rows(block)], chunk).astype(bf16).reshape(grad.shape[2:])
         next(late[kv])
-        for earlier in range(kv):
-            next(late[earlier])
-        next(early, None)
         if kv == 1:
             for program in homes:
                 next(program)
@@ -1666,10 +1737,10 @@
     shape = jax.ShapeDtypeStruct
     hbm = pl.BlockSpec(memory_space=pl.ANY)
     vmem = pl.BlockSpec(memory_space=pltpu.VMEM)
-    g_cout, g_cq, g_ckv, g_out, t_out, t_mem, do_s, qkv = operands[:8]
+    _, g_cq, _, g_out, t_mem, do_s = operands[:6]
     tokens, inner = do_s.shape
-    width = g_cout.shape[-1]
-    rows = g_cout.shape[4]
+    width = g_out.shape[-1]
+    rows = g_out.shape[4]
     own = tokens // 8
     outs = [
         (shape((rows, width), f32), vmem),
@@ -1680,7 +1751,6 @@
         (shape((rows, inner), bf16), vmem),
         (shape((rows, inner), bf16), vmem),
         (shape((rows, 2 * inner), bf16), vmem),
-        (shape((2, 2) + t_out.shape[1:], bf16), hbm),
         (shape((2, 2) + t_mem.shape[1:], bf16), hbm),
         (shape((2, 2, own, width), bf16), hbm),
         (shape((32, 128), f32), vmem),
@@ -1699,21 +1769,271 @@
         pltpu.VMEM((32, 128), f32),
         pltpu.VMEM((6 + depth, 32, 128), f32),
     ]
-    scratch += scatter_buffers(depth, 1, rows, width) + scatter_buffers(depth, 1, rows, width)
-    scratch += scatter_buffers(depth, 2, rows, inner) + scatter_buffers(depth, 2, rows, inner)
+    scratch += [pltpu.VMEM(array.shape, array.dtype) for array in operands[5:12]]
+    for lanes, size in ((1, width), (2, inner), (2, inner), (1, width)):
+        scratch += scatter_buffers(depth, lanes, rows, size)
     for _ in range(4):
-        scratch += scatter_buffers(depth, 2, rows, QB)
+        scratch += scatter_buffers(depth, 2, rows, QB)[2:]
     return pl.pallas_call(
         functools.partial(self_backward_kernel, depth),
-        in_specs=[hbm] * 6 + [vmem] * 13,
+        in_specs=[hbm] * 12 + [vmem] * 6,
         out_specs=[spec for _, spec in outs],
         out_shape=[kind for kind, _ in outs],
-        scratch_shapes=scratch + wire_scratch(4 + 12 + 3 + depth + 8 * (4 + depth), 24),
+        scratch_shapes=scratch + wire_scratch(4 + 8 + 3 + depth + 8 * (4 + depth), 20),
         compiler_params=pltpu.CompilerParams(
             collective_id=2, has_side_effects=True, vmem_limit_bytes=60 * 2**20
         ),
         cost_estimate=pl.CostEstimate(
             flops=16 * 10**9, bytes_accessed=128 * 2**20, transcendentals=10**7
+        ),
+    )(*operands)
+
+
+def feed_forward_kernel(depth, tiles, *refs):
+    (
+        a3_far, wt_far, valid, x2, gu0_far, d0_far, gu1p, d1p, gu2p, d2p,
+        o_top, o_u, pieces, g_gate2, g_up2, g_down2,
+        r_gate0, r_up0, r_down0, r_gate1, r_up1, r_down1, q_gate0, q_up0, q_gate1, q_up1,
+        *rest
+    ) = refs
+    take = lambda n: [rest.pop(0) for _ in range(n)]
+    gu1, d1, gu2, d2, mid, dgate, dup, g0, g1, g2, g3, g4, g5, mine, theirs, second = take(16)
+    a3, wt, gu0, d0, low_top, u = take(6)
+    buffers = [take(7) for _ in range(6)]
+    f32, bf16 = jnp.float32, jnp.bfloat16
+    spot = Spot(depth)
+    wires = Wires(*rest)
+    blocks = 4
+    starts = [sum(tiles[:i]) for i in range(3)]
+    coming = [
+        wires.move(source, target)
+        for source, target in ((wt_far, wt), (a3_far, a3), (gu0_far, gu0), (d0_far, d0))
+    ]
+
+    def rows(block):
+        return slice(block * QB, (block + 1) * QB)
+
+    spot.greet()
+    over = wires.take(blocks)
+    middle = d1.shape[-1] // 2
+    wide1 = share_plane(
+        spot, wires, gu1p, lambda corner: gu1.at[:, :, corner], lambda view, side: view.at[:, side]
+    )
+    down1 = share_plane(
+        spot,
+        wires,
+        d1p,
+        lambda corner: d1.at[0, :, corner],
+        lambda view, side: view.at[:, :, pl.ds(side * middle, middle)],
+    )
+    wide2 = gather_columns(spot, wires, gu2p, gu2)
+    down2 = gather_rows(spot, wires, d2p, d2)
+    sums = [
+        scatter_sums(spot, wires, grads, scratch, total, got, True)
+        for grads, scratch, total, got in (
+            (g0, buffers[0], r_gate0, q_gate0),
+            (g1, buffers[1], r_up0, q_up0),
+            (g2, buffers[2], r_down0, None),
+            (g3, buffers[3], r_gate1, q_gate1),
+            (g4, buffers[4], r_up1, q_up1),
+            (g5, buffers[5], r_down1, None),
+        )
+    ]
+
+    def advance(*programs):
+        for program in programs:
+            next(program, None)
+
+    advance(wide1, down1, wide2, down2)
+    halves = [
+        wires.move(
+            x2.at[pl.ds(pl.multiple_of(block * QB + spot.core * (QB // 2), QB // 2), QB // 2)], second.at[block]
+        )
+        for block in range(blocks)
+    ]
+    for copy in coming:
+        copy.wait()
+    for block in range(blocks):
+        value = wt[block].reshape(QB, -1).astype(f32) * valid[rows(block)]
+        low_top[rows(block), :] = value.astype(bf16)
+    coming = [wires.move(low_top, o_top)]
+    wides = [gu0, gu1, gu2]
+    downs = [d0, d1, d2]
+
+    def wide_weight(tile, part):
+        both = wides[tile]
+        lanes = pl.ds(part * tiles[tile], tiles[tile])
+        return both[:, :, :, :, lanes].reshape(-1, tiles[tile])
+
+    def down_weight(tile):
+        weight = downs[tile][0]
+        if weight.shape[2] % 16:
+            return weight.astype(f32).reshape(tiles[tile], -1).astype(bf16)
+        return weight.reshape(tiles[tile], -1)
+
+    def hidden(tile, block):
+        lanes = slice(starts[tile], starts[tile] + tiles[tile])
+        left = a3[rows(block), :]
+        gate = nn(left, wide_weight(tile, 0))
+        upward = nn(left, wide_weight(tile, 1))
+        back = nt(low_top[rows(block), :], down_weight(tile))
+        bend = jnp.tanh(GELU_SCALE * (gate + GELU_CUBE * gate * gate * gate))
+        share = 0.5 * (1.0 + bend)
+        active = gate * share
+        slope = share + 0.5 * gate * (1.0 - bend * bend) * (
+            GELU_SCALE * (1.0 + 3.0 * GELU_CUBE * gate * gate)
+        )
+        mid[rows(block), lanes] = (active * upward).astype(bf16)
+        dgate[rows(block), lanes] = (back * upward * slope).astype(bf16)
+        dup[rows(block), lanes] = (back * active).astype(bf16)
+
+    def wide_grads(tile, source, target):
+        lanes = slice(starts[tile], starts[tile] + tiles[tile])
+        right = source[:, lanes]
+        for block in range(blocks):
+            target[block] = tn(a3[:, rows(block)], right).reshape(target.shape[1:]).astype(bf16)
+
+    def down_grads(tile, target):
+        lanes = slice(starts[tile], starts[tile] + tiles[tile])
+        target[...] = tn(mid[:, lanes], low_top[...]).reshape(target.shape).astype(bf16)
+
+    hidden(0, 0)
+    hidden(0, 1)
+    hidden(0, 2)
+    hidden(0, 3)
+    wide_grads(0, dgate, g0)
+    advance(sums[0])
+    wide_grads(0, dup, g1)
+    advance(wide1, down1, wide2, down2)
+    down_grads(0, g2)
+    advance(wide1, down1, sums[1])
+    for block in range(blocks):
+        hidden(1, block)
+        if block == 1:
+            advance(sums[0], wide2, down2, sums[2])
+    advance(sums[1])
+    wide_grads(1, dgate, g3)
+    advance(sums[0], wide2, down2, sums[3])
+    wide_grads(1, dup, g4)
+    advance(sums[2], sums[1])
+    down_grads(1, g5)
+    advance(sums[0], sums[4])
+    for block in range(blocks):
+        hidden(2, block)
+        if block == 1:
+            advance(sums[3], sums[2], sums[5])
+        if block == 3:
+            advance(sums[1], sums[0])
+    wide_grads(2, dgate, g_gate2)
+    wide_grads(2, dup, g_up2)
+    advance(sums[4], sums[3], sums[2])
+    down_grads(2, g_down2)
+
+    def half_rows(block, core):
+        return pl.ds(pl.multiple_of(block * QB + core * (QB // 2), QB // 2), QB // 2)
+
+    def contribution(block, core):
+        total = None
+        for tile in range(3):
+            lanes = slice(starts[tile], starts[tile] + tiles[tile])
+            term = nn(mid[half_rows(block, core), lanes], down_weight(tile))
+            total = term if total is None else total + term
+        return total.astype(bf16)
+
+    for block in range(blocks):
+        mine[block] = contribution(block, 1 - spot.core)
+        wires.send(mine.at[block], theirs.at[block], spot.sibling(), over + block)
+    for block in range(blocks):
+        total = None
+        for tile in range(3):
+            lanes = slice(starts[tile], starts[tile] + tiles[tile])
+            term = nt(dgate[rows(block), lanes], wide_weight(tile, 0))
+            term = term + nt(dup[rows(block), lanes], wide_weight(tile, 1))
+            total = term if total is None else total + term
+        u[rows(block), :] = total.astype(bf16)
+        coming.append(wires.move(u.at[rows(block)], o_u.at[rows(block)]))
+        if block == 1:
+            advance(sums[5], sums[4], sums[3])
+    advance(sums[5], sums[4])
+    for block in range(blocks):
+        value = contribution(block, spot.core).astype(f32)
+        wires.arrive(theirs.at[block], spot.sibling(), over + block)
+        value = value + theirs[block].astype(f32)
+        halves[block].wait()
+        pieces[block] = ((second[block] + value) * valid[half_rows(block, spot.core), :]).astype(bf16)
+    for program in sums + [wide1, down1, wide2, down2]:
+        for _ in program:
+            pass
+    for copy in coming:
+        copy.wait()
+    wires.close()
+
+
+def feed_forward(depth, tiles, *operands):
+    bf16, f32 = jnp.bfloat16, jnp.float32
+    shape = jax.ShapeDtypeStruct
+    hbm = pl.BlockSpec(memory_space=pl.ANY)
+    vmem = pl.BlockSpec(memory_space=pltpu.VMEM)
+    a3, _, _, _, gu0, d0, gu1p, d1p, gu2p, d2p = operands
+    tokens, width = a3.shape
+    hidden_width = sum(tiles)
+    rows = [d1p.shape[1], d1p.shape[1], d2p.shape[2]]
+    own = tokens // 8
+    wide = gu2p.shape[2]
+
+    def wide_grad(tile):
+        return (depth, 2, 2, 2, wide, tiles[tile])
+
+    def down_grad(tile):
+        return (depth, 1, 2, 2, rows[tile], width)
+
+    outs = [
+        (shape((tokens, width), bf16), hbm),
+        (shape((tokens, width), bf16), hbm),
+        (shape((4, own, width), bf16), vmem),
+        (shape(wide_grad(2), bf16), vmem),
+        (shape(wide_grad(2), bf16), vmem),
+        (shape(down_grad(2), bf16), vmem),
+    ]
+    for tile in range(2):
+        outs += [(shape((wide, tiles[tile]), f32), vmem)] * 2 + [(shape((rows[tile], width), f32), vmem)]
+    for tile in range(2):
+        outs += [(shape((wide, tiles[tile]), bf16), vmem)] * 2
+    scratch = [
+        pltpu.VMEM(gu0.shape, bf16),
+        pltpu.VMEM(d0.shape, bf16),
+        pltpu.VMEM((depth, 2) + gu2p.shape[1:], bf16),
+        pltpu.VMEM((1, depth) + d2p.shape[1:], bf16),
+    ]
+    scratch += [pltpu.VMEM((tokens, hidden_width), bf16)] * 3
+    for tile in range(2):
+        scratch += [pltpu.VMEM(wide_grad(tile), bf16)] * 2 + [pltpu.VMEM(down_grad(tile), bf16)]
+    scratch += [
+        pltpu.VMEM((4, own, width), bf16),
+        pltpu.VMEM((4, own, width), bf16),
+        pltpu.VMEM((4, own, width), f32),
+        pltpu.VMEM((tokens, width), bf16),
+        pltpu.VMEM((4, 2, own, width), bf16),
+        pltpu.VMEM(gu0.shape, bf16),
+        pltpu.VMEM(d0.shape, bf16),
+        pltpu.VMEM((tokens, width), bf16),
+        pltpu.VMEM((tokens, width), bf16),
+    ]
+    for tile in range(2):
+        for _ in range(2):
+            scratch += scatter_buffers(depth, 2, wide, tiles[tile])[2:]
+        scratch += scatter_buffers(depth, 1, rows[tile], width)[2:]
+    return pl.pallas_call(
+        functools.partial(feed_forward_kernel, depth, tiles),
+        in_specs=[hbm, hbm, vmem] + [hbm] * 7,
+        out_specs=[spec for _, spec in outs],
+        out_shape=[kind for kind, _ in outs],
+        scratch_shapes=scratch + wire_scratch(4 + 22 * depth + 6 * (4 + depth), 24),
+        compiler_params=pltpu.CompilerParams(
+            collective_id=3, has_side_effects=True, vmem_limit_bytes=60 * 2**20
+        ),
+        cost_estimate=pl.CostEstimate(
+            flops=27 * 10**9, bytes_accessed=64 * 2**20, transcendentals=10**7
         ),
     )(*operands)
 
@@ -1760,6 +2080,20 @@
         pack = jnp.concatenate([parity_columns(weights) for weights in groups], axis=2)
         return pack.reshape(2, 4, -1, pack.shape[2])
 
+    cuts = [(0, 32), (32, 64), (64, ff_down.shape[0] // 4)]
+    tiles = tuple(16 * (stop - start) for start, stop in cuts)
+    down_packs = [ff_down.reshape(4, -1, width)[None, :, start:stop] for start, stop in cuts]
+
+    def wide_pack(weights, start, stop):
+        sides = [
+            jnp.moveaxis(w.reshape(-1, 4, 2, 4, w.shape[1] // 32)[..., start:stop], 2, 0).reshape(
+                2, 4, -1, 16 * (stop - start)
+            )
+            for w in weights
+        ]
+        return jnp.concatenate(sides, axis=3)
+
+    wide_packs = [wide_pack([ff_gate, ff_up], start, stop) for start, stop in cuts]
     heads = jnp.arange(4)
     spots = (heads // 2) * 64 + 2 * spot.corner + heads % 2
     placed = jnp.sum(
@@ -1783,7 +2117,7 @@
     (
         inputs, upstream, encoded, _, w_qkv, w_cross, w_outs, w_gu, w_down,
         normed_self, qkv, context, self_sums, first, normed_cross, cross_queries, far_kv, cross_context,
-        cross_sums, second, normed_ff, gains, keep_self, keep_cross, bent,
+        cross_sums, second, normed_ff, gains, _, _, bent, keep_self, keep_cross, near_wide, near_down,
     ) = forward_layer(
         depth,
         layer_input.reshape(2, 2, local // 2, width),
@@ -1793,67 +2127,33 @@
         column_pack([self_q, self_k, self_v]),
         column_pack([cross_k, cross_v], [cross_q]),
         jnp.stack([self_out, cross_out]).reshape(2, 4, -1, width),
-        column_pack([ff_gate], [ff_up]),
-        ff_down.reshape(1, 4, -1, width),
+        wide_packs[0],
+        down_packs[0],
+        wide_packs[1],
+        down_packs[1],
         codes,
         holes,
     )
-    upstream, encoded = upstream.reshape(-1, width), encoded.reshape(-1, width)
-    w_gu, w_down = w_gu.reshape(-1, w_gu.shape[-1]), w_down.reshape(-1, width)
-    hidden_width = w_gu.shape[1] // 2
-    w_gate, w_up = w_gu[:, :hidden_width], w_gu[:, hidden_width:]
-    valid = (keep_self[0] == 0).astype(f32)[:, None]
-
-    def swap_core(array):
-        pairs = [
-            (place * 4 + corner, (place ^ 1) * 4 + corner) for place in range(2 * depth) for corner in range(4)
-        ]
-        return lax.ppermute(array, ("dp", "seq"), pairs)
-
-    def share_half(partial):
-        partial = partial.astype(bf16).reshape(4, 2, -1, partial.shape[-1])
-        got = swap_core(pick(partial, 1 - core, 1))
-        return pick(partial, core, 1).astype(f32) + got.astype(f32)
-
-    def own_half(value):
-        return pick(value.reshape(4, 2, -1, value.shape[-1]), core, 1)
-
-    def grad_pack(left, right, lanes):
-        grad = weight_grad(left, right).astype(bf16)
-        return grad.reshape(depth, lanes, 2, 2, -1, grad.shape[-1])
-
-    gate = project(normed_ff, w_gate)
-    upward = project(normed_ff, w_up)
-    middle = gated(gate, upward).astype(bf16)
-    third = own_half(second) + share_half(project(middle, w_down))
-    output = (third * own_half(valid)).astype(bf16)
-
-    top = upstream.astype(f32) * valid
-    top_low = top.astype(bf16)
-    _, pullback = jax.vjp(gated, gate, upward)
-    gate_grad, upward_grad = pullback(project_back(top_low, w_down))
-    gate_grad = gate_grad.astype(bf16)
-    upward_grad = upward_grad.astype(bf16)
-    changed = (project_back(gate_grad, w_gate) + project_back(upward_grad, w_up)).astype(bf16)
-    g_down = grad_pack(middle, top_low, 1)
-    g_gate = grad_pack(normed_ff, gate_grad, 2)
-    g_up = grad_pack(normed_ff, upward_grad, 2)
+    encoded = encoded.reshape(-1, width)
+    valid = (keep_self == 0).astype(f32)
     (
-        r_down, r_gate, r_up, q_gate, q_up, half, self_up, g_cout, g_cq, g_ckv, g_out, memory_grad, terms,
+        top_low, changed, output, g_gate, g_up, g_down,
+        r_gate0, r_up0, r_down0, r_gate1, r_up1, r_down1, q_gate0, q_up0, q_gate1, q_up1,
+    ) = feed_forward(
+        depth, tiles, normed_ff, upstream, valid, second, w_gu, w_down,
+        near_wide, near_down, wide_packs[2], down_packs[2],
+    )
+
+    (
+        r_down2, r_gate2, r_up2, q_gate2, q_up2, g_cout, g_cq, g_ckv, half, self_up, g_out, memory_grad, terms,
+        output,
     ) = cross_part(
-        depth, g_down, g_gate, g_up, second, first, changed, top_low, cross_queries, far_kv, cross_context,
-        cross_sums, keep_cross.reshape(-1, 1), normed_cross, encoded, w_cross, w_outs, context, gains,
-    )
-
-    def pack(grad, lanes):
-        return grad.reshape(depth, lanes, 2, 2, -1, grad.shape[-1])
-
-    (
-        r_cout, r_cq, r_ckv, r_out, r_qkv, q_cq, q_ckv, q_qkv, output, memory_grad, input_grad, packed,
-    ) = self_part(
-        depth, pack(g_cout, 1), pack(g_cq, 2), pack(g_ckv, 2), pack(g_out, 1), output, memory_grad, self_up,
-        qkv, context, self_sums, keep_self.reshape(-1, 1), bent, normed_self, inputs, gains, half, w_qkv,
-        terms, onehot.T,
+        depth, g_down, g_gate, g_up, second, first, output, changed, top_low, cross_queries, far_kv, cross_context,
+        normed_cross, encoded, w_cross, w_outs, context, cross_sums, keep_cross, gains,
+    )
+    r_cout, r_cq, r_ckv, r_out, r_qkv, q_cq, q_ckv, q_qkv, memory_grad, input_grad, packed = self_part(
+        depth, g_cout, g_cq, g_ckv, g_out.reshape(depth, 1, 2, 2, -1, width), memory_grad, self_up, qkv, context,
+        normed_self, inputs, half, w_qkv, self_sums, keep_self, bent, gains, terms, onehot.T,
     )
     bias_grad = packed[24:, :64].reshape(4, 2, 2, BUCKETS)
     bias_grad = jnp.transpose(bias_grad, (3, 0, 2, 1)).reshape(BUCKETS, HEADS)
@@ -1878,7 +2178,23 @@
 
     d_q, d_k, d_v = merge(r_qkv, q_qkv, 2 * HEAD_DIM, HEAD_DIM, HEAD_DIM)
     d_ck, d_cv = merge(r_ckv, q_ckv, HEAD_DIM, HEAD_DIM)
-    (d_cq,), (d_gate,), (d_up,) = merge(r_cq, q_cq), merge(r_gate, q_gate), merge(r_up, q_up)
+    (d_cq,) = merge(r_cq, q_cq)
+
+    def join(owns, gots):
+        sides = []
+        for own, got in zip(owns, gots):
+            got = got.astype(f32)
+            sides.append(
+                jnp.stack([jnp.where(core == 0, own, got), jnp.where(core == 0, got, own)]).reshape(
+                    2, own.shape[0], 4, 4, -1
+                )
+            )
+        whole = jnp.concatenate(sides, axis=4)
+        return jnp.transpose(whole, (1, 2, 0, 3, 4)).reshape(whole.shape[1], -1)
+
+    d_gate = join((r_gate0, r_gate1, r_gate2), (q_gate0, q_gate1, q_gate2))
+    d_up = join((r_up0, r_up1, r_up2), (q_up0, q_up1, q_up2))
+    r_down = jnp.concatenate([r_down0, r_down1, r_down2], axis=0)
     return (
         output.reshape(layer_input.shape),
         input_grad.astype(f32).reshape(layer_input.shape),

time: 497 us -> 444 us (0.89)
  matrix products: 62.5 us -> 0 us
  Pallas kernels: 370 us -> 381 us
    pallas_call x0 -> x1, Pallas kernels: none -> 109 us  [feed_forward(): pl.pallas_call(functools.partial(feed_forward_kernel, depth, tiles), in_s...]
    dot_general x9 -> x0, matrix products: 62.5 us -> none  [the longest x3 26.5 us: project_back(): lax.dot_general(grad, weight, (((1,), (1,)), ((), ())), preferred_element...]
    pallas_call x1, Pallas kernels: 160 us -> 120 us  [forward_layer(): pl.pallas_call(functools.partial(forward_layer_kernel, depth), in_specs=[...]
    pallas_call x1, Pallas kernels: 95.8 us -> 57 us  [cross_part(): pl.pallas_call(functools.partial(cross_backward_kernel, depth), in_specs=...]
    pallas_call x1, Pallas kernels: 114 us -> 95.2 us  [self_part(): pl.pallas_call(functools.partial(self_backward_kernel, depth), in_specs=[...]
    reshape x1 -> x10, local copies, waits for them, and re-layouts: 0.86 us -> 10.5 us  [the longest x8 8.06 us: wide_pack(): jnp.moveaxis(w.reshape(-1, 4, 2, 4, w.shape[1] // 32)[..., start:stop], 2...]
    unnamed x75 -> x84, local copies, waits for them, and re-layouts: 14 us -> 10.3 us
  transfers between devices with their start and end apart: 1 -> 0, of which waited for: 0 -> 0; matrix products, arithmetic and copies ran while one was open for 9% -> 0% of each run, Pallas kernels for 19% -> 0%
where the time goes in v5:
time: 444 us; the launch traced here: 439 us
  Pallas kernels  381 us (86%)
  local copies, waits for them, and re-layouts  40.5 us (9%)
  other arithmetic  16.3 us (4%)
    pallas_call x1, Pallas kernels, forward_layer(): pl.pallas_call(functools.partial(forward_layer_kernel, depth), in_specs=[...  120 us
    pallas_call x1, Pallas kernels, feed_forward(): pl.pallas_call(functools.partial(feed_forward_kernel, depth, tiles), in_s...  109 us
    pallas_call x1, Pallas kernels, self_part(): pl.pallas_call(functools.partial(self_backward_kernel, depth), in_specs=[...  95.2 us
    pallas_call x1, Pallas kernels, cross_part(): pl.pallas_call(functools.partial(cross_backward_kernel, depth), in_specs=...  57 us
    unnamed x84, local copies, waits for them, and re-layouts  10.3 us

profile of v5, /device:TPU:0, one launch (start us, length us, event | category | flops | bytes accessed | tf_op | source)
XLA Modules:
  0.0 439.4 jit_solution(12140411581603602673)
XLA Ops:
  0.7 0.7 pad_reduce_fusion
  2.0 0.8 fusion.refs_11_
  3.4 1.5 copy.104
  5.0 0.9 copy.105
  5.9 1.0 reshape.295
  6.9 1.5 copy.106
  8.4 0.9 copy.107
  9.3 1.0 reshape.297
  10.3 0.9 copy.108
  11.3 1.0 reshape.299
  12.3 1.2 copy.109
  13.5 1.0 reshape.300
  14.5 1.1 pad_maximum_fusion.2
  15.9 0.7 fusion.8
  17.2 0.8 slice_bitcast_fusion
  18.1 1.1 copy.100
  19.1 1.0 copy.101
  20.9 2.1 pad_maximum_fusion
  23.6 1.0 copy.96
  25.3 1.2 reshape_reshape.3.refs_4_
  26.4 119.6 %shard_map.340 = (bf16[4,2,128,1024]{3,2,1,0:T(8,128)(2,1)}, bf16[4,2,128,1024]{3,2,1,0:T(8,128)(2,1)}, bf16[4,2,64,1024]{3,2,1,0:T(8,128)(2,1)}, f32[4,2,4,8,12...) custom-call(bf16[2,2,128,1024]{3,2,1,0:T(8,128)(2,1)} %bitcast.106, ...), custom_call_target="tpu_custom_call" | custom-call | flops 16000000000 | bytes 134217728 | tf_op jit(solution)/shard_map/pallas_call | solution.py:1308
  146.1 1.9 compare_convert_fusion.refs_2_
  148.0 0.9 copy.127
  148.9 1.1 reshape.325
  150.1 0.9 copy.128
  151.0 1.1 reshape.326
  152.1 0.8 pad_maximum_fusion.4.refs_8_
  152.9 0.7 slice_bitcast_fusion.6.refs_9_
  153.6 108.9 %shard_map.341 = (bf16[1024,1024]{1,0:T(8,128)(2,1)}, bf16[1024,1024]{1,0:T(8,128)(2,1)}, bf16[4,128,1024]{2,1,0:T(8,128)(2,1)}, bf16[4,2,2,2,32,384]{5,4,3,2,1,...) custom-call(bf16[1024,1024]{1,0:T(8,128)(2,1)} %get-tuple-element.85, ...), custom_call_target="tpu_custom_call" | custom-call | flops 27000000512 | bytes 67108864 | tf_op jit(solution)/shard_map/pallas_call | solution.py:2026
  262.6 57.0 %shard_map.342 = (f32[24,1024]{1,0:T(8,128)}, f32[32,384]{1,0:T(8,128)}, f32[32,384]{1,0:T(8,128)}, bf16[32,384]{1,0:T(8,128)(2,1)}, bf16[32,384]{1,0:T(8,128)(2...) custom-call(bf16[4,1,2,2,24,1024]{5,4,3,2,1,0:T(8,128)(2,1)} %get-tu, ...), custom_call_target="tpu_custom_call" | custom-call | flops 16000000000 | bytes 134217728 | tf_op jit(solution)/shard_map/pallas_call | solution.py:1559
  319.6 1.9 pad_maximum_fusion.5
  323.9 1.2 reshape.320
  327.4 1.2 reshape.319
  328.6 0.7 fusion.1.refs_17_
  329.3 95.2 %shard_map.343 = (f32[32,1024]{1,0:T(8,128)}, f32[32,512]{1,0:T(8,128)}, f32[32,512]{1,0:T(8,128)}, f32[32,1024]{1,0:T(8,128)}, f32[32,1024]{1,0:T(8,128)}, /*in...) custom-call(bf16[4,1,2,2,32,1024]{5,4,3,2,1,0:T(8,128)(2,1)} %get-tu, ...), custom_call_target="tpu_custom_call" | custom-call | flops 16000000000 | bytes 134217728 | tf_op jit(solution)/shard_map/pallas_call | solution.py:1777
  424.6 0.9 convert_select_fusion.10
  425.8 0.8 reshape.317
  426.7 0.8 reshape.318
  427.8 0.8 reshape.316
  429.0 0.8 reshape.312
  429.9 0.8 reshape.313
  430.9 0.8 reshape.311
  431.6 1.6 bitcast_convert_fusion
  433.2 1.1 bitcast_convert_fusion.1
  434.5 0.7 copy.126
  436.9 1.0 copy.140
  437.9 0.7 copy.141
  438.5 0.7 copy.142
  (152 shorter events, 11.9 us)
Async XLA Ops:
  12.3 3.5 copy-start.30
  12.3 3.6 copy-start.31
  12.3 3.6 copy-start.32
  12.3 3.6 copy-start.33
  14.5 2.7 copy-start.2
  15.7 4.9 %copy-start.4 = (bf16[128,1024]{1,0:T(8,128)(2,1)S(1)}, bf16[128,1024]{1,0:T(8,128)(2,1)}, u32[]{:S(2)}) copy-start(bf16[128,1024]{1,0:T(8,128)(2,1)} %param.33) | copy-start | bytes 786436
  18.1 2.8 copy-start.6
  20.4 2.6 copy-start.5
  20.9 2.3 copy-start.7
  262.5 57.1 %copy-start.11 = (f32[32,1024]{1,0:T(8,128)S(1)}, f32[32,1024]{1,0:T(8,128)}, u32[]{:S(2)}) copy-start(f32[32,1024]{1,0:T(8,128)} %get-tuple-element.149) | copy-start | bytes 393220
  262.5 57.1 %copy-start.12 = (f32[32,1024]{1,0:T(8,128)S(1)}, f32[32,1024]{1,0:T(8,128)}, u32[]{:S(2)}) copy-start(f32[32,1024]{1,0:T(8,128)} %get-tuple-element.150) | copy-start | bytes 393220
  262.6 58.9 %copy-start.16 = (f32[32,512]{1,0:T(8,128)S(1)}, f32[32,512]{1,0:T(8,128)}, u32[]{:S(2)}) copy-start(f32[32,512]{1,0:T(8,128)} %get-tuple-element.143) | copy-start | bytes 196612
  262.6 58.9 %copy-start.24 = (bf16[32,512]{1,0:T(8,128)(2,1)S(1)}, bf16[32,512]{1,0:T(8,128)(2,1)}, u32[]{:S(2)}) copy-start(bf16[32,512]{1,0:T(8,128)(2,1)} %get-tuple-element.144) | copy-start | bytes 98308
  262.6 59.3 %copy-start.15 = (f32[32,512]{1,0:T(8,128)S(1)}, f32[32,512]{1,0:T(8,128)}, u32[]{:S(2)}) copy-start(f32[32,512]{1,0:T(8,128)} %get-tuple-element.145) | copy-start | bytes 196612
  262.6 59.3 %copy-start.23 = (bf16[32,512]{1,0:T(8,128)(2,1)S(1)}, bf16[32,512]{1,0:T(8,128)(2,1)}, u32[]{:S(2)}) copy-start(bf16[32,512]{1,0:T(8,128)(2,1)} %get-tuple-element.146) | copy-start | bytes 98308
  319.6 2.7 copy-start.20
  319.6 2.7 copy-start.27
  322.7 2.4 copy-start.14
  322.7 2.4 copy-start.22
  323.1 2.4 copy-start.13
  323.1 2.4 copy-start.21
  323.7 2.2 copy-start.19
  323.7 2.2 copy-start.26
  326.7 2.0 copy-start.28
  424.5 3.0 copy-start.17
  424.5 3.0 copy-start.25
  424.6 4.0 copy-start.10
  424.6 4.0 copy-start.18
  427.7 4.0 copy-start
  429.9 3.3 copy-start.3
  431.6 2.7 copy-start.29
  431.6 5.3 %copy-start.1 = (bf16[2,2,128,1024]{3,2,1,0:T(8,128)(2,1)S(1)}, bf16[2,2,128,1024]{3,2,1,0:T(8,128)(2,1)}, u32[]{:S(2)}) copy-start(bf16[2,2,128,1024]{3,2,1,0:T(8,128)(2,1)} %get-tuple-element.111) | copy-start | bytes 3145732
  433.2 4.7 %copy-start.9 = (f32[32,1024]{1,0:T(8,128)S(1)}, f32[32,1024]{1,0:T(8,128)}, u32[]{:S(2)}) copy-start(f32[32,1024]{1,0:T(8,128)} %get-tuple-element.268) | copy-start | bytes 393220
  433.2 5.3 %copy-start.8 = (f32[32,1024]{1,0:T(8,128)S(1)}, f32[32,1024]{1,0:T(8,128)}, u32[]{:S(2)}) copy-start(f32[32,1024]{1,0:T(8,128)} %get-tuple-element.274) | copy-start | bytes 393220

commit v6 on v5

--- a/solution.py
+++ b/solution.py
@@ -1091,15 +1091,43 @@
     return (value * inverse_rms(value) * gain).astype(jnp.bfloat16)
 
 
-def forward_layer_kernel(depth, *refs):
+def pack_heads(pack, weights, start):
+    size = sum(w.shape[1] for w in weights) // 8
+    for place in range(8):
+        units = [w.shape[1] // 8 for w in weights]
+        pieces = [w[:, place * u : (place + 1) * u] for w, u in zip(weights, units)]
+        piece = pieces[0] if len(pieces) == 1 else jnp.concatenate(pieces, axis=1)
+        lanes = slice(start + place // 2 * size, start + (place // 2 + 1) * size)
+        pack[place % 2, :, :, lanes] = piece.reshape(4, -1, size)
+
+
+def pack_hidden(pack, weights, first, last):
+    size = 16 * (last - first)
+    for order, weight in enumerate(weights):
+        unit = weight.shape[1] // 8
+        quarter = unit // 4
+        for side in range(2):
+            pieces = [
+                weight[:, place * unit + q * quarter + first : place * unit + q * quarter + last]
+                for place in range(side, 8, 2)
+                for q in range(4)
+            ]
+            row = jnp.concatenate(pieces, axis=1)
+            pack[side, :, :, order * size : (order + 1) * size] = row.reshape(4, -1, size).astype(pack.dtype)
+
+
+def forward_layer_kernel(depth, cuts, *refs):
     (
-        x, t, m, s, p1, p2, p3, p4, p5, p6, p7, codes, holes,
+        x, t, m, s, p3, p5, p7, codes, holes, sq, sk, sv, ck, cv, cq, wg, wu,
         o_wx, wt, o_wm, ws, o_w1, o_w2, o_w3, w4, w5,
         o_a1, o_qkv, o_ctx, lse, o_x1, o_a2, o_qc, o_ckv, o_ctxc, lsec, o_x2, o_a3, gains, keeps, keepc, bent,
-        down_s, down_c, n6, n7,
-        bias, own, got, own2, got2, wx, wm, w1, w2, w3, a1, qkv, ctx, x1, a2, qc, ckv, ctxc, x2, a3, *sems
+        down_s, down_c, n6, n7, p8,
+        p1, p2, p4, p6, bias, own, got, own2, got2, wx, wm, w1, w2, w3, a1, qkv, ctx, x1, a2, qc, ckv, ctxc, x2, a3, *sems
     ) = refs
     leaving = []
+    pack_heads(p1, [sq, sk, sv], 0)
+    pack_heads(p2, [ck, cv], 0)
+    pack_heads(p2, [cq], ck.shape[1])
 
     def leave(*pairs):
         leaving.extend(wires.move(source, target) for source, target in pairs)
@@ -1132,7 +1160,11 @@
         for program in programs:
             next(program)
 
-    advance(small, first, small, tokens, small, small)
+    advance(small, first, small, tokens)
+    pack_hidden(p4, [wg[...], wu[...]], 0, cuts[0])
+    pack_hidden(p6, [wg[...], wu[...]], cuts[0], cuts[1])
+    pack_hidden(p8, [wg[...], wu[...]], cuts[1], cuts[2])
+    advance(small, small)
 
     def line(row):
         return jnp.concatenate([ws[z, c, 0, row : row + 1, :] for z in range(depth) for c in range(2)], axis=1)
@@ -1165,7 +1197,7 @@
                 head = 2 * kv + member
                 bias[kv, member * QB : (member + 1) * QB, (3 - offset) * QB : (4 - offset) * QB] = spread_row(
                     vectors[head : head + 1, offset * 2 * QB : (offset + 1) * 2 * QB]
-                )
+                ).astype(bf16)
 
     advance(first, outs, second, tokens, tokens)
     for block in range(blocks):
@@ -1253,7 +1285,7 @@
     wires.close()
 
 
-def forward_layer(depth, x, t, m, small, p1, p2, p3, p4, p5, p6, p7, codes, holes):
+def forward_layer(depth, cuts, x, t, m, small, p3, p5, p7, codes, holes, *weights):
     bf16, f32 = jnp.bfloat16, jnp.float32
     shape = jax.ShapeDtypeStruct
 
@@ -1266,6 +1298,11 @@
     def whole_tokens(parcel):
         return shape((4, 2) + parcel.shape[2:], bf16)
 
+    rows = p3.shape[2]
+    p1 = p2 = shape((2, 4, rows, weights[0].shape[1]), bf16)
+    p4, p6, p8 = (
+        shape((2, 4, rows, 32 * (stop - start)), bf16) for start, stop in zip((0,) + cuts[:2], cuts)
+    )
     width = x.shape[-1]
     tokens = 8 * x.shape[2]
     span = 8 * m.shape[2]
@@ -1303,14 +1340,17 @@
         (shape((span, 1), f32), vmem),
         (shape((depth, 2) + p6.shape[2:], bf16), hbm),
         (shape((depth,) + p7.shape[2:], bf16), hbm),
+        (p8, vmem),
     ]
+    packs = [pltpu.VMEM(pack.shape, bf16) for pack in (p1, p2, p4, p6)]
     swap = pltpu.VMEM((tokens, width), bf16)
     return pl.pallas_call(
-        functools.partial(forward_layer_kernel, depth),
-        in_specs=[hbm] * 11 + [vmem] * 2,
+        functools.partial(forward_layer_kernel, depth, cuts),
+        in_specs=[hbm] * 7 + [vmem] * 10,
         out_specs=[spec for _, spec in outs],
         out_shape=[kind for kind, _ in outs],
-        scratch_shapes=[pltpu.VMEM((heads // 2, 2 * QB, 4 * QB), f32), swap, swap, swap, swap]
+        scratch_shapes=packs
+        + [pltpu.VMEM((heads // 2, 2 * QB, 4 * QB), bf16), swap, swap, swap, swap]
         + [pltpu.VMEM(outs[i][0].shape, outs[i][0].dtype) for i in (0, 2, 4, 5, 6, 9, 10, 11, 13, 14, 15, 16, 17, 19, 20)]
         + wire_scratch(35 + 33 * depth, 40),
         compiler_params=pltpu.CompilerParams(
@@ -1319,7 +1359,7 @@
         cost_estimate=pl.CostEstimate(
             flops=16 * 10**9, bytes_accessed=128 * 2**20, transcendentals=10**7
         ),
-    )(x, t, m, small, p1, p2, p3, p4, p5, p6, p7, codes, holes)
+    )(x, t, m, small, p3, p5, p7, codes, holes, *weights)
 
 
 def pipeline(programs, ahead=2, stages=5):
@@ -1358,18 +1398,18 @@
 
 
 def cross_backward_kernel(depth, *refs):
-    g_down, g_gate, g_up, x2, x1, t_out, *far = refs[:16]
+    g_early, g_down, g_gate, g_up, x2, x1, t_out, *far = refs[:17]
     (
         lsec, keep, gains,
-        r_down, r_gate, r_up, q_gate, q_up, o_cout, o_cq, o_ckv, half, do_s, g_out, o_mem, terms, h_out,
+        r_early, r_down, r_gate, r_up, q_gate, q_up, o_cout, o_cq, o_ckv, half, do_s, g_out, o_mem, terms, h_out,
         *rest
-    ) = refs[16:]
+    ) = refs[17:]
     take = lambda n: [rest.pop(0) for _ in range(n)]
     near = take(10)
     u, top, qc, ckv, ctxc, a2, mem, w2, w3, ctx = near
     g_cout, g_cq, g_ckv = take(3)
     stage, e2, eb, do_c, dqc, dkv, dk_sum, dv_sum, got, own_c, got_c, own_m, got_m = take(13)
-    buffers = [take(9) for _ in range(3)]
+    buffers = [take(9) for _ in range(4)]
     f32, bf16 = jnp.float32, jnp.bfloat16
     spot = Spot(depth)
     wires = Wires(*rest)
@@ -1389,6 +1429,7 @@
         scatter_sums(spot, wires, g_down, buffers[0], r_down, None),
         scatter_sums(spot, wires, g_gate, buffers[1], r_gate, q_gate),
         scatter_sums(spot, wires, g_up, buffers[2], r_up, q_up),
+        scatter_sums(spot, wires, g_early, buffers[3], r_early, None),
     ]
     links = pipeline(programs)
     next(links)
@@ -1514,13 +1555,14 @@
     shape = jax.ShapeDtypeStruct
     hbm = pl.BlockSpec(memory_space=pl.ANY)
     vmem = pl.BlockSpec(memory_space=pltpu.VMEM)
-    g_down, g_gate, g_up, x2, _, t_out, _, _, _, ckv = operands[:10]
-    far = operands[6:16]
+    g_early, g_down, g_gate, g_up, x2, _, t_out, _, _, _, ckv = operands[:11]
+    far = operands[7:17]
     tokens, width = x2.shape
     span, inner = ckv.shape
     own = tokens // 8
     rows = g_gate.shape[4]
     outs = [
+        (shape(g_early.shape[4:], f32), vmem),
         (shape(g_down.shape[4:], f32), vmem),
         (shape(g_gate.shape[4:], f32), vmem),
         (shape(g_up.shape[4:], f32), vmem),
@@ -1537,7 +1579,7 @@
         (shape((2, 2) + t_out.shape[1:], bf16), hbm),
     ]
     scratch = [pltpu.VMEM(array.shape, bf16) for array in far]
-    scratch += [pltpu.VMEM(outs[i][0].shape, bf16) for i in (5, 6, 7)]
+    scratch += [pltpu.VMEM(outs[i][0].shape, bf16) for i in (6, 7, 8)]
     scratch += [
         pltpu.VMEM((2, QB, width), f32),
         pltpu.VMEM((tokens, width), f32),
@@ -1553,12 +1595,12 @@
         pltpu.VMEM((4, 2, span // 8, width), bf16),
         pltpu.VMEM((4, span // 8, width), bf16),
     ]
-    for grads in (g_down, g_gate, g_up):
+    for grads in (g_down, g_gate, g_up, g_early):
         scratch += scatter_buffers(depth, grads.shape[1], *grads.shape[4:])
-    number = 16 + 3 * (4 + depth)
+    number = 16 + 4 * (4 + depth)
     return pl.pallas_call(
         functools.partial(cross_backward_kernel, depth),
-        in_specs=[hbm] * 16 + [vmem] * 3,
+        in_specs=[hbm] * 17 + [vmem] * 3,
         out_specs=[spec for _, spec in outs],
         out_shape=[kind for kind, _ in outs],
         scratch_shapes=scratch + wire_scratch(number, 48),
@@ -1571,17 +1613,51 @@
     )(*operands)
 
 
+def sides(core, own, got):
+    got = got.astype(jnp.float32)
+    return jnp.where(core == 0, own, got), jnp.where(core == 0, got, own)
+
+
+def spread_hidden(core, owns, gots):
+    pairs = [sides(core, own[...], got[...]) for own, got in zip(owns, gots)]
+    sizes = [own.shape[1] // 16 for own in owns]
+    return jnp.concatenate(
+        [
+            pair[place % 2][:, (place // 2 * 4 + q) * size : (place // 2 * 4 + q + 1) * size]
+            for place in range(8)
+            for q in range(4)
+            for pair, size in zip(pairs, sizes)
+        ],
+        axis=1,
+    )
+
+
+def spread_heads(core, own, got, targets, units):
+    even, odd = sides(core, own[...], got[...])
+    step = even.shape[1] // 4
+    for group in range(4):
+        start = group * step
+        for target, unit in zip(targets, units):
+            lanes = slice(start, start + unit)
+            target[:, 2 * group * unit : 2 * (group + 1) * unit] = jnp.concatenate(
+                [even[:, lanes], odd[:, lanes]], axis=1
+            )
+            start += unit
+
+
 def self_backward_kernel(depth, *refs):
     (
         g_cout, g_cq, g_ckv, g_out, t_mem, f_do, f_qkv, f_ctx, f_a1, f_x, f_half, f_w1, lse, keep, bent, gains,
         terms, codes,
-        r_cout, r_cq, r_ckv, r_out, r_qkv, q_cq, q_ckv, q_qkv, h_mem, h_in, packed,
+        rg0, rg1, rg2, ru0, ru1, ru2, qg0, qg1, qg2, qu0, qu1, qu2, rd0, rd1, rd2,
+        r_cout, r_out, h_mem, h_in, packed, d_q, d_k, d_v, d_cq, d_ck, d_cv, d_gate, d_up, d_down,
         *rest
     ) = refs
     take = lambda n: [rest.pop(0) for _ in range(n)]
     bias, sums, dk_sum, dv_sum, dqkv, grad, mine, theirs, pieces, line, small, work = take(12)
     near = take(7)
     do_s, qkv, ctx, a1, x, half, w1 = near
+    r_cq, r_ckv, r_qkv, q_cq, q_ckv, q_qkv = take(6)
     buffers = [take(9) for _ in range(4)]
     resident = [take(7) for _ in range(4)]
     f32, bf16 = jnp.float32, jnp.bfloat16
@@ -1617,6 +1693,12 @@
     next(early)
     for program in homes:
         next(program)
+    d_gate[...] = spread_hidden(spot.core, (rg0, rg1, rg2), (qg0, qg1, qg2))
+    d_up[...] = spread_hidden(spot.core, (ru0, ru1, ru2), (qu0, qu1, qu2))
+    low = 0
+    for piece in (rd0, rd1, rd2):
+        d_down[low : low + piece.shape[0], :] = piece[...]
+        low += piece.shape[0]
     for copy in coming:
         copy.wait()
     for kv in range(kvs):
@@ -1723,6 +1805,9 @@
             pass
     for _ in early:
         pass
+    spread_heads(spot.core, r_qkv, q_qkv, (d_q, d_k, d_v), (2 * HEAD_DIM, HEAD_DIM, HEAD_DIM))
+    spread_heads(spot.core, r_ckv, q_ckv, (d_ck, d_cv), (HEAD_DIM, HEAD_DIM))
+    spread_heads(spot.core, r_cq, q_cq, (d_cq,), (2 * HEAD_DIM,))
     wires.close()
 
 
@@ -1742,19 +1827,17 @@
     width = g_out.shape[-1]
     rows = g_out.shape[4]
     own = tokens // 8
+    hidden = 2 * sum(tile.shape[1] for tile in operands[18:21])
     outs = [
         (shape((rows, width), f32), vmem),
-        (shape((rows, inner), f32), vmem),
-        (shape((rows, inner), f32), vmem),
         (shape((rows, width), f32), vmem),
-        (shape((rows, 2 * inner), f32), vmem),
-        (shape((rows, inner), bf16), vmem),
-        (shape((rows, inner), bf16), vmem),
-        (shape((rows, 2 * inner), bf16), vmem),
         (shape((2, 2) + t_mem.shape[1:], bf16), hbm),
         (shape((2, 2, own, width), bf16), hbm),
         (shape((32, 128), f32), vmem),
     ]
+    for size in (2 * inner, inner, inner, 2 * inner, inner, inner, hidden, hidden):
+        outs.append((shape((rows, size), f32), vmem))
+    outs.append((shape((sum(piece.shape[0] for piece in operands[-3:]), width), f32), vmem))
     scratch = [
         pltpu.VMEM((4, QB, 2 * QB), f32),
         pltpu.VMEM((4, QB, 2 * QB), f32),
@@ -1770,13 +1853,15 @@
         pltpu.VMEM((6 + depth, 32, 128), f32),
     ]
     scratch += [pltpu.VMEM(array.shape, array.dtype) for array in operands[5:12]]
+    for kind in (f32, bf16):
+        scratch += [pltpu.VMEM((rows, size), kind) for size in (inner, inner, 2 * inner)]
     for lanes, size in ((1, width), (2, inner), (2, inner), (1, width)):
         scratch += scatter_buffers(depth, lanes, rows, size)
     for _ in range(4):
         scratch += scatter_buffers(depth, 2, rows, QB)[2:]
     return pl.pallas_call(
         functools.partial(self_backward_kernel, depth),
-        in_specs=[hbm] * 12 + [vmem] * 6,
+        in_specs=[hbm] * 12 + [vmem] * 21,
         out_specs=[spec for _, spec in outs],
         out_shape=[kind for kind, _ in outs],
         scratch_shapes=scratch + wire_scratch(4 + 8 + 3 + depth + 8 * (4 + depth), 20),
@@ -1792,14 +1877,14 @@
 def feed_forward_kernel(depth, tiles, *refs):
     (
         a3_far, wt_far, valid, x2, gu0_far, d0_far, gu1p, d1p, gu2p, d2p,
-        o_top, o_u, pieces, g_gate2, g_up2, g_down2,
-        r_gate0, r_up0, r_down0, r_gate1, r_up1, r_down1, q_gate0, q_up0, q_gate1, q_up1,
+        o_top, o_u, pieces, g_gate2, g_up2, g_down2, g5,
+        r_gate0, r_up0, r_down0, r_gate1, r_up1, q_gate0, q_up0, q_gate1, q_up1,
         *rest
     ) = refs
     take = lambda n: [rest.pop(0) for _ in range(n)]
-    gu1, d1, gu2, d2, mid, dgate, dup, g0, g1, g2, g3, g4, g5, mine, theirs, second = take(16)
+    gu1, d1, gu2, d2, mid, dgate, dup, g0, g1, g2, g3, g4, mine, theirs, second = take(15)
     a3, wt, gu0, d0, low_top, u = take(6)
-    buffers = [take(7) for _ in range(6)]
+    buffers = [take(7) for _ in range(5)]
     f32, bf16 = jnp.float32, jnp.bfloat16
     spot = Spot(depth)
     wires = Wires(*rest)
@@ -1836,7 +1921,6 @@
             (g2, buffers[2], r_down0, None),
             (g3, buffers[3], r_gate1, q_gate1),
             (g4, buffers[4], r_up1, q_up1),
-            (g5, buffers[5], r_down1, None),
         )
     ]
 
@@ -1921,7 +2005,7 @@
     for block in range(blocks):
         hidden(2, block)
         if block == 1:
-            advance(sums[3], sums[2], sums[5])
+            advance(sums[3], sums[2])
         if block == 3:
             advance(sums[1], sums[0])
     wide_grads(2, dgate, g_gate2)
@@ -1953,8 +2037,8 @@
         u[rows(block), :] = total.astype(bf16)
         coming.append(wires.move(u.at[rows(block)], o_u.at[rows(block)]))
         if block == 1:
-            advance(sums[5], sums[4], sums[3])
-    advance(sums[5], sums[4])
+            advance(sums[4], sums[3])
+    advance(sums[4])
     for block in range(blocks):
         value = contribution(block, spot.core).astype(f32)
         wires.arrive(theirs.at[block], spot.sibling(), over + block)
@@ -1994,9 +2078,12 @@
         (shape(wide_grad(2), bf16), vmem),
         (shape(wide_grad(2), bf16), vmem),
         (shape(down_grad(2), bf16), vmem),
+        (shape(down_grad(1), bf16), vmem),
     ]
     for tile in range(2):
-        outs += [(shape((wide, tiles[tile]), f32), vmem)] * 2 + [(shape((rows[tile], width), f32), vmem)]
+        outs += [(shape((wide, tiles[tile]), f32), vmem)] * 2
+        if tile == 0:
+            outs.append((shape((rows[tile], width), f32), vmem))
     for tile in range(2):
         outs += [(shape((wide, tiles[tile]), bf16), vmem)] * 2
     scratch = [
@@ -2007,7 +2094,9 @@
     ]
     scratch += [pltpu.VMEM((tokens, hidden_width), bf16)] * 3
     for tile in range(2):
-        scratch += [pltpu.VMEM(wide_grad(tile), bf16)] * 2 + [pltpu.VMEM(down_grad(tile), bf16)]
+        scratch += [pltpu.VMEM(wide_grad(tile), bf16)] * 2
+        if tile == 0:
+            scratch.append(pltpu.VMEM(down_grad(tile), bf16))
     scratch += [
         pltpu.VMEM((4, own, width), bf16),
         pltpu.VMEM((4, own, width), bf16),
@@ -2022,7 +2111,8 @@
     for tile in range(2):
         for _ in range(2):
             scratch += scatter_buffers(depth, 2, wide, tiles[tile])[2:]
-        scratch += scatter_buffers(depth, 1, rows[tile], width)[2:]
+        if tile == 0:
+            scratch += scatter_buffers(depth, 1, rows[tile], width)[2:]
     return pl.pallas_call(
         functools.partial(feed_forward_kernel, depth, tiles),
         in_specs=[hbm, hbm, vmem] + [hbm] * 7,
@@ -2036,12 +2126,6 @@
             flops=27 * 10**9, bytes_accessed=64 * 2**20, transcendentals=10**7
         ),
     )(*operands)
-
-
-def parity_columns(weights):
-    rows = weights[0].shape[0]
-    pack = jnp.concatenate([w.reshape(rows, 4, 2, -1) for w in weights], axis=3)
-    return jnp.moveaxis(pack, 2, 0).reshape(2, rows, -1)
 
 
 def per_chip(
@@ -2076,24 +2160,10 @@
     near = memory.shape[2]
     shard = norm_self.shape[0]
 
-    def column_pack(*groups):
-        pack = jnp.concatenate([parity_columns(weights) for weights in groups], axis=2)
-        return pack.reshape(2, 4, -1, pack.shape[2])
-
     cuts = [(0, 32), (32, 64), (64, ff_down.shape[0] // 4)]
     tiles = tuple(16 * (stop - start) for start, stop in cuts)
     down_packs = [ff_down.reshape(4, -1, width)[None, :, start:stop] for start, stop in cuts]
 
-    def wide_pack(weights, start, stop):
-        sides = [
-            jnp.moveaxis(w.reshape(-1, 4, 2, 4, w.shape[1] // 32)[..., start:stop], 2, 0).reshape(
-                2, 4, -1, 16 * (stop - start)
-            )
-            for w in weights
-        ]
-        return jnp.concatenate(sides, axis=3)
-
-    wide_packs = [wide_pack([ff_gate, ff_up], start, stop) for start, stop in cuts]
     heads = jnp.arange(4)
     spots = (heads // 2) * 64 + 2 * spot.corner + heads % 2
     placed = jnp.sum(
@@ -2117,43 +2187,52 @@
     (
         inputs, upstream, encoded, _, w_qkv, w_cross, w_outs, w_gu, w_down,
         normed_self, qkv, context, self_sums, first, normed_cross, cross_queries, far_kv, cross_context,
-        cross_sums, second, normed_ff, gains, _, _, bent, keep_self, keep_cross, near_wide, near_down,
+        cross_sums, second, normed_ff, gains, _, _, bent, keep_self, keep_cross, near_wide, near_down, wide_pack,
     ) = forward_layer(
         depth,
+        tuple(stop for _, stop in cuts),
         layer_input.reshape(2, 2, local // 2, width),
         cotangent.reshape(2, 2, local // 2, width),
         memory.reshape(2, 2, near // 2, width),
         small,
-        column_pack([self_q, self_k, self_v]),
-        column_pack([cross_k, cross_v], [cross_q]),
         jnp.stack([self_out, cross_out]).reshape(2, 4, -1, width),
-        wide_packs[0],
         down_packs[0],
-        wide_packs[1],
         down_packs[1],
         codes,
         holes,
+        self_q,
+        self_k,
+        self_v,
+        cross_k,
+        cross_v,
+        cross_q,
+        ff_gate,
+        ff_up,
     )
     encoded = encoded.reshape(-1, width)
     valid = (keep_self == 0).astype(f32)
     (
-        top_low, changed, output, g_gate, g_up, g_down,
-        r_gate0, r_up0, r_down0, r_gate1, r_up1, r_down1, q_gate0, q_up0, q_gate1, q_up1,
+        top_low, changed, output, g_gate, g_up, g_down, g_early,
+        r_gate0, r_up0, r_down0, r_gate1, r_up1, q_gate0, q_up0, q_gate1, q_up1,
     ) = feed_forward(
         depth, tiles, normed_ff, upstream, valid, second, w_gu, w_down,
-        near_wide, near_down, wide_packs[2], down_packs[2],
+        near_wide, near_down, wide_pack, down_packs[2],
     )
 
     (
-        r_down2, r_gate2, r_up2, q_gate2, q_up2, g_cout, g_cq, g_ckv, half, self_up, g_out, memory_grad, terms,
+        r_down1, r_down2, r_gate2, r_up2, q_gate2, q_up2, g_cout, g_cq, g_ckv, half, self_up, g_out, memory_grad, terms,
         output,
     ) = cross_part(
-        depth, g_down, g_gate, g_up, second, first, output, changed, top_low, cross_queries, far_kv, cross_context,
+        depth, g_early, g_down, g_gate, g_up, second, first, output, changed, top_low, cross_queries, far_kv, cross_context,
         normed_cross, encoded, w_cross, w_outs, context, cross_sums, keep_cross, gains,
     )
-    r_cout, r_cq, r_ckv, r_out, r_qkv, q_cq, q_ckv, q_qkv, memory_grad, input_grad, packed = self_part(
+    (
+        r_cout, r_out, memory_grad, input_grad, packed, d_q, d_k, d_v, d_cq, d_ck, d_cv, d_gate, d_up, d_down,
+    ) = self_part(
         depth, g_cout, g_cq, g_ckv, g_out.reshape(depth, 1, 2, 2, -1, width), memory_grad, self_up, qkv, context,
         normed_self, inputs, half, w_qkv, self_sums, keep_self, bent, gains, terms, onehot.T,
+        r_gate0, r_gate1, r_gate2, r_up0, r_up1, r_up2, q_gate0, q_gate1, q_gate2, q_up0, q_up1, q_up2,
+        r_down0, r_down1, r_down2,
     )
     bias_grad = packed[24:, :64].reshape(4, 2, 2, BUCKETS)
     bias_grad = jnp.transpose(bias_grad, (3, 0, 2, 1)).reshape(BUCKETS, HEADS)
@@ -2165,36 +2244,6 @@
         bias_grad, (lax.axis_index("dp") * rel_bias.shape[0], spot.corner * rel_bias.shape[1]), rel_bias.shape
     )
 
-    def merge(own, got, *sizes):
-        rows = own.shape[0]
-        got = got.astype(f32)
-        even, odd = jnp.where(core == 0, own, got), jnp.where(core == 0, got, own)
-        both = jnp.stack([even.reshape(rows, 4, -1), odd.reshape(rows, 4, -1)], axis=2)
-        results, start = [], 0
-        for size in sizes or both.shape[3:]:
-            results.append(both[..., start : start + size].reshape(rows, -1))
-            start += size
-        return results
-
-    d_q, d_k, d_v = merge(r_qkv, q_qkv, 2 * HEAD_DIM, HEAD_DIM, HEAD_DIM)
-    d_ck, d_cv = merge(r_ckv, q_ckv, HEAD_DIM, HEAD_DIM)
-    (d_cq,) = merge(r_cq, q_cq)
-
-    def join(owns, gots):
-        sides = []
-        for own, got in zip(owns, gots):
-            got = got.astype(f32)
-            sides.append(
-                jnp.stack([jnp.where(core == 0, own, got), jnp.where(core == 0, got, own)]).reshape(
-                    2, own.shape[0], 4, 4, -1
-                )
-            )
-        whole = jnp.concatenate(sides, axis=4)
-        return jnp.transpose(whole, (1, 2, 0, 3, 4)).reshape(whole.shape[1], -1)
-
-    d_gate = join((r_gate0, r_gate1, r_gate2), (q_gate0, q_gate1, q_gate2))
-    d_up = join((r_up0, r_up1, r_up2), (q_up0, q_up1, q_up2))
-    r_down = jnp.concatenate([r_down0, r_down1, r_down2], axis=0)
     return (
         output.reshape(layer_input.shape),
         input_grad.astype(f32).reshape(layer_input.shape),
@@ -2213,7 +2262,7 @@
         n_ff,
         d_gate,
         d_up,
-        r_down,
+        d_down,
     )
 
 

time: 444 us -> 418 us (0.941)
  local copies, waits for them, and re-layouts: 40.5 us -> 16.2 us
    reshape x22 -> x0, local copies, waits for them, and re-layouts: 16.1 us -> none  [the longest x8 8.06 us: wide_pack(): jnp.moveaxis(w.reshape(-1, 4, 2, 4, w.shape[1] // 32)[..., start:stop], 2...]
    pallas_call x1, Pallas kernels: 57 us -> 62.9 us  [cross_part(): pl.pallas_call(functools.partial(cross_backward_kernel, depth), in_specs=...]
    concatenate x4 -> x0, other arithmetic: 5.83 us -> none  [the longest x1 2.06 us: column_pack(): jnp.concatenate([parity_columns(weights) for weights in groups], axis=2)]
    transpose x11 -> x0, local copies, waits for them, and re-layouts: 4.58 us -> none  [the longest x8 4.12 us: wide_pack(): jnp.moveaxis(w.reshape(-1, 4, 2, 4, w.shape[1] // 32)[..., start:stop], 2...]
    unnamed x84 -> x47, local copies, waits for them, and re-layouts: 10.3 us -> 10.1 us
where the time goes in v6:
time: 418 us; the launch traced here: 413 us
  Pallas kernels  384 us (92%)
  local copies, waits for them, and re-layouts  16.2 us (4%)
  other arithmetic  12.3 us (3%)
    pallas_call x1, Pallas kernels, forward_layer(): pl.pallas_call(functools.partial(forward_layer_kernel, depth, cuts), in_s...  118 us
    pallas_call x1, Pallas kernels, feed_forward(): pl.pallas_call(functools.partial(feed_forward_kernel, depth, tiles), in_s...  105 us
    pallas_call x1, Pallas kernels, self_part(): pl.pallas_call(functools.partial(self_backward_kernel, depth), in_specs=[...  97.2 us
    pallas_call x1, Pallas kernels, cross_part(): pl.pallas_call(functools.partial(cross_backward_kernel, depth), in_specs=...  62.9 us
    unnamed x47, local copies, waits for them, and re-layouts  10.1 us

profile of v6, /device:TPU:0, one launch (start us, length us, event | category | flops | bytes accessed | tf_op | source)
XLA Modules:
  0.0 413.1 jit_solution(12132404240804154882)
XLA Ops:
  0.7 0.7 pad_reduce_fusion
  1.4 0.1 pad_add_fusion
  1.5 0.4 reverse.2
  1.8 0.1 slice.72
  1.9 0.1 fusion.2
  2.0 0.8 fusion.refs_7_
  2.7 0.1 select_bitcast_fusion
  2.8 0.6 copy.54
  3.4 0.1 iota_compare_fusion.4
  3.5 0.7 convert_element_type.38
  4.2 0.1 select_reduce_fusion
  4.3 0.7 maximum_convert_fusion
  5.0 0.7 fusion.8
  5.7 0.6 fusion.3.refs_3_
  6.3 1.9 slice_bitcast_fusion
  8.2 1.9 pad_maximum_fusion.refs_4_
  10.1 118.2 %shard_map.340 = (bf16[4,2,128,1024]{3,2,1,0:T(8,128)(2,1)}, bf16[4,2,128,1024]{3,2,1,0:T(8,128)(2,1)}, bf16[4,2,64,1024]{3,2,1,0:T(8,128)(2,1)}, f32[4,2,4,8,12...) custom-call(bf16[2,2,128,1024]{3,2,1,0:T(8,128)(2,1)} %bitcast.68, ...), custom_call_target="tpu_custom_call" | custom-call | flops 16000000000 | bytes 134217728 | tf_op jit(solution)/shard_map/pallas_call | solution.py:1347
  128.3 1.9 compare_convert_fusion.refs_2_
  130.2 1.6 slice_bitcast_fusion.2.refs_9_
  131.8 105.3 %shard_map.341 = (bf16[1024,1024]{1,0:T(8,128)(2,1)}, bf16[1024,1024]{1,0:T(8,128)(2,1)}, bf16[4,128,1024]{2,1,0:T(8,128)(2,1)}, bf16[4,2,2,2,32,384]{5,4,3,2,1,...) custom-call(bf16[1024,1024]{1,0:T(8,128)(2,1)} %get-tuple-element.90, ...), custom_call_target="tpu_custom_call" | custom-call | flops 27000000512 | bytes 67108864 | tf_op jit(solution)/shard_map/pallas_call | solution.py:2116
  237.1 0.0 copy-start.13
  237.1 62.9 %shard_map.342 = (f32[32,1024]{1,0:T(8,128)}, f32[24,1024]{1,0:T(8,128)}, f32[32,384]{1,0:T(8,128)}, f32[32,384]{1,0:T(8,128)}, bf16[32,384]{1,0:T(8,128)(2,1)},...) custom-call(bf16[4,1,2,2,32,1024]{5,4,3,2,1,0:T(8,128)(2,1)} %get-tu, ...), custom_call_target="tpu_custom_call" | custom-call | flops 16000000000 | bytes 134217728 | tf_op jit(solution)/shard_map/pallas_call | solution.py:1601
  300.0 0.0 copy-done.13
  300.0 0.7 fusion.1.refs_17_
  300.7 97.2 %shard_map.343 = (f32[32,1024]{1,0:T(8,128)}, f32[32,1024]{1,0:T(8,128)}, bf16[2,2,64,1024]{3,2,1,0:T(8,128)(2,1)}, bf16[2,2,128,1024]{3,2,1,0:T(8,128)(2,1)}, f...) custom-call(bf16[4,1,2,2,32,1024]{5,4,3,2,1,0:T(8,128)(2,1)} %get-tu, ...), custom_call_target="tpu_custom_call" | custom-call | flops 16000000000 | bytes 134217728 | tf_op jit(solution)/shard_map/pallas_call | solution.py:1862
  397.9 2.9 bitcast_convert_fusion
  400.9 1.1 bitcast_convert_fusion.1
  402.0 0.1 reshape.190
  402.1 0.1 dynamic_slice.13
  402.2 0.7 copy.52
  402.8 0.6 dynamic_slice.12
  403.4 0.6 dynamic_slice.14
  404.0 0.6 dynamic_slice.15
  404.6 1.0 copy.67
  405.6 0.0 copy-done.8
  405.6 0.7 copy.68
  406.2 0.0 copy-done.12
  406.2 0.6 copy.69
  406.8 0.6 copy.70
  407.5 0.7 copy.71
  408.1 0.7 copy.72
  408.8 0.6 copy.73
  409.4 0.0 copy-done.9
  409.4 0.6 copy.74
  410.1 0.7 copy.75
  410.7 0.7 copy.76
  411.5 0.7 copy.77
  412.2 0.7 copy.78
  (33 shorter events, 0.1 us)
Async XLA Ops:
  237.1 63.0 %copy-start.13 = (s32[1024]{0:T(1024)S(1)}, s32[1024]{0:T(1024)}, u32[]{:S(2)}) copy-start(s32[1024]{0:T(1024)} %param.25) | copy-start | bytes 12292
  397.9 2.9 copy-start.1
  397.9 4.1 copy-start.14
  397.9 6.6 %copy-start = (bf16[2,2,128,1024]{3,2,1,0:T(8,128)(2,1)S(1)}, bf16[2,2,128,1024]{3,2,1,0:T(8,128)(2,1)}, u32[]{:S(2)}) copy-start(bf16[2,2,128,1024]{3,2,1,0:T(8,128)(2,1)} %get-tuple-element.118) | copy-start | bytes 3145732
  400.8 4.7 %copy-start.8 = (f32[32,1024]{1,0:T(8,128)S(1)}, f32[32,1024]{1,0:T(8,128)}, u32[]{:S(2)}) copy-start(f32[32,1024]{1,0:T(8,128)} %get-tuple-element.245) | copy-start | bytes 393220
  400.8 5.4 %copy-start.12 = (f32[32,512]{1,0:T(8,128)S(1)}, f32[32,512]{1,0:T(8,128)}, u32[]{:S(2)}) copy-start(f32[32,512]{1,0:T(8,128)} %get-tuple-element.246) | copy-start | bytes 196612
  400.9 6.0 %copy-start.11 = (f32[32,512]{1,0:T(8,128)S(1)}, f32[32,512]{1,0:T(8,128)}, u32[]{:S(2)}) copy-start(f32[32,512]{1,0:T(8,128)} %get-tuple-element.247) | copy-start | bytes 196612
  400.9 6.6 %copy-start.7 = (f32[32,1024]{1,0:T(8,128)S(1)}, f32[32,1024]{1,0:T(8,128)}, u32[]{:S(2)}) copy-start(f32[32,1024]{1,0:T(8,128)} %get-tuple-element.248) | copy-start | bytes 393220
  400.9 7.3 %copy-start.6 = (f32[32,1024]{1,0:T(8,128)S(1)}, f32[32,1024]{1,0:T(8,128)}, u32[]{:S(2)}) copy-start(f32[32,1024]{1,0:T(8,128)} %get-tuple-element.251) | copy-start | bytes 393220
  400.9 7.9 %copy-start.10 = (f32[32,512]{1,0:T(8,128)S(1)}, f32[32,512]{1,0:T(8,128)}, u32[]{:S(2)}) copy-start(f32[32,512]{1,0:T(8,128)} %get-tuple-element.252) | copy-start | bytes 196612
  402.0 7.5 %copy-start.9 = (f32[32,512]{1,0:T(8,128)S(1)}, f32[32,512]{1,0:T(8,128)}, u32[]{:S(2)}) copy-start(f32[32,512]{1,0:T(8,128)} %get-tuple-element.253) | copy-start | bytes 196612
  402.0 8.1 %copy-start.5 = (f32[32,1024]{1,0:T(8,128)S(1)}, f32[32,1024]{1,0:T(8,128)}, u32[]{:S(2)}) copy-start(f32[32,1024]{1,0:T(8,128)} %get-tuple-element.254) | copy-start | bytes 393220
  402.0 8.7 %copy-start.4 = (f32[32,2816]{1,0:T(8,128)S(1)}, f32[32,2816]{1,0:T(8,128)}, u32[]{:S(2)}) copy-start(f32[32,2816]{1,0:T(8,128)} %get-tuple-element.256) | copy-start | bytes 1081348
  404.6 6.9 %copy-start.3 = (f32[32,2816]{1,0:T(8,128)S(1)}, f32[32,2816]{1,0:T(8,128)}, u32[]{:S(2)}) copy-start(f32[32,2816]{1,0:T(8,128)} %get-tuple-element.257) | copy-start | bytes 1081348
  404.6 7.6 %copy-start.2 = (f32[88,1024]{1,0:T(8,128)S(1)}, f32[88,1024]{1,0:T(8,128)}, u32[]{:S(2)}) copy-start(f32[88,1024]{1,0:T(8,128)} %get-tuple-element.258) | copy-start | bytes 1081348

commit v7 on v6

--- a/solution.py
+++ b/solution.py
@@ -1649,15 +1649,13 @@
     (
         g_cout, g_cq, g_ckv, g_out, t_mem, f_do, f_qkv, f_ctx, f_a1, f_x, f_half, f_w1, lse, keep, bent, gains,
         terms, codes,
-        rg0, rg1, rg2, ru0, ru1, ru2, qg0, qg1, qg2, qu0, qu1, qu2, rd0, rd1, rd2,
-        r_cout, r_out, h_mem, h_in, packed, d_q, d_k, d_v, d_cq, d_ck, d_cv, d_gate, d_up, d_down,
+        r_cout, r_out, h_mem, h_in, packed, r_cq, r_ckv, r_qkv, q_cq, q_ckv, q_qkv,
         *rest
     ) = refs
     take = lambda n: [rest.pop(0) for _ in range(n)]
     bias, sums, dk_sum, dv_sum, dqkv, grad, mine, theirs, pieces, line, small, work = take(12)
     near = take(7)
     do_s, qkv, ctx, a1, x, half, w1 = near
-    r_cq, r_ckv, r_qkv, q_cq, q_ckv, q_qkv = take(6)
     buffers = [take(9) for _ in range(4)]
     resident = [take(7) for _ in range(4)]
     f32, bf16 = jnp.float32, jnp.bfloat16
@@ -1693,12 +1691,6 @@
     next(early)
     for program in homes:
         next(program)
-    d_gate[...] = spread_hidden(spot.core, (rg0, rg1, rg2), (qg0, qg1, qg2))
-    d_up[...] = spread_hidden(spot.core, (ru0, ru1, ru2), (qu0, qu1, qu2))
-    low = 0
-    for piece in (rd0, rd1, rd2):
-        d_down[low : low + piece.shape[0], :] = piece[...]
-        low += piece.shape[0]
     for copy in coming:
         copy.wait()
     for kv in range(kvs):
@@ -1805,9 +1797,6 @@
             pass
     for _ in early:
         pass
-    spread_heads(spot.core, r_qkv, q_qkv, (d_q, d_k, d_v), (2 * HEAD_DIM, HEAD_DIM, HEAD_DIM))
-    spread_heads(spot.core, r_ckv, q_ckv, (d_ck, d_cv), (HEAD_DIM, HEAD_DIM))
-    spread_heads(spot.core, r_cq, q_cq, (d_cq,), (2 * HEAD_DIM,))
     wires.close()
 
 
@@ -1827,7 +1816,6 @@
     width = g_out.shape[-1]
     rows = g_out.shape[4]
     own = tokens // 8
-    hidden = 2 * sum(tile.shape[1] for tile in operands[18:21])
     outs = [
         (shape((rows, width), f32), vmem),
         (shape((rows, width), f32), vmem),
@@ -1835,9 +1823,8 @@
         (shape((2, 2, own, width), bf16), hbm),
         (shape((32, 128), f32), vmem),
     ]
-    for size in (2 * inner, inner, inner, 2 * inner, inner, inner, hidden, hidden):
-        outs.append((shape((rows, size), f32), vmem))
-    outs.append((shape((sum(piece.shape[0] for piece in operands[-3:]), width), f32), vmem))
+    for kind in (f32, bf16):
+        outs += [(shape((rows, size), kind), vmem) for size in (inner, inner, 2 * inner)]
     scratch = [
         pltpu.VMEM((4, QB, 2 * QB), f32),
         pltpu.VMEM((4, QB, 2 * QB), f32),
@@ -1853,15 +1840,13 @@
         pltpu.VMEM((6 + depth, 32, 128), f32),
     ]
     scratch += [pltpu.VMEM(array.shape, array.dtype) for array in operands[5:12]]
-    for kind in (f32, bf16):
-        scratch += [pltpu.VMEM((rows, size), kind) for size in (inner, inner, 2 * inner)]
     for lanes, size in ((1, width), (2, inner), (2, inner), (1, width)):
         scratch += scatter_buffers(depth, lanes, rows, size)
     for _ in range(4):
         scratch += scatter_buffers(depth, 2, rows, QB)[2:]
     return pl.pallas_call(
         functools.partial(self_backward_kernel, depth),
-        in_specs=[hbm] * 12 + [vmem] * 21,
+        in_specs=[hbm] * 12 + [vmem] * 6,
         out_specs=[spec for _, spec in outs],
         out_shape=[kind for kind, _ in outs],
         scratch_shapes=scratch + wire_scratch(4 + 8 + 3 + depth + 8 * (4 + depth), 20),
@@ -1874,9 +1859,64 @@
     )(*operands)
 
 
+def finish_kernel(
+    t_in, t_mem, t_out, packed, c_out, c_cout, r_cq, r_ckv, r_qkv, q_cq, q_ckv, q_qkv,
+    rg0, rg1, rg2, ru0, ru1, ru2, qg0, qg1, qg2, qu0, qu1, qu2, rd0, rd1, rd2,
+    d_in, d_mem, d_out, n_self, n_cross, n_ff, d_self, d_cross, d_q, d_k, d_v, d_cq, d_ck, d_cv, d_gate, d_up,
+    d_down,
+):
+    core = lax.axis_index("dp") % 2
+    d_in[...] = t_in[...].astype(jnp.float32)
+    d_mem[...] = t_mem[...].astype(jnp.float32)
+    d_out[...] = t_out[...]
+    mine = lax.axis_index("dp") * 4 + lax.axis_index("seq")
+    size = n_self.shape[1]
+    per = 128 // size
+    for index, target in ((2, n_self), (1, n_cross), (0, n_ff)):
+        line = packed[pl.ds(8 * index + mine // per, 1), :]
+        value = line[:, :size]
+        for place in range(1, per):
+            value = jnp.where(mine % per == place, line[:, place * size : (place + 1) * size], value)
+        target[...] = value
+    d_self[...] = c_out[...]
+    d_cross[...] = c_cout[...]
+    d_gate[...] = spread_hidden(core, (rg0, rg1, rg2), (qg0, qg1, qg2))
+    d_up[...] = spread_hidden(core, (ru0, ru1, ru2), (qu0, qu1, qu2))
+    low = 0
+    for piece in (rd0, rd1, rd2):
+        d_down[low : low + piece.shape[0], :] = piece[...]
+        low += piece.shape[0]
+    spread_heads(core, r_qkv, q_qkv, (d_q, d_k, d_v), (2 * HEAD_DIM, HEAD_DIM, HEAD_DIM))
+    spread_heads(core, r_ckv, q_ckv, (d_ck, d_cv), (HEAD_DIM, HEAD_DIM))
+    spread_heads(core, r_cq, q_cq, (d_cq,), (2 * HEAD_DIM,))
+
+
+def finish(piece, *operands):
+    f32 = jnp.float32
+    shape = jax.ShapeDtypeStruct
+    t_in, t_mem, t_out = operands[:3]
+    rows, width = operands[4].shape
+    inner = operands[6].shape[1]
+    hidden = 2 * sum(tile.shape[1] for tile in operands[12:15])
+    outs = [shape(t_in.shape, f32), shape(t_mem.shape, f32), shape(t_out.shape, t_out.dtype)]
+    outs += [shape((1, piece), f32)] * 3 + [shape((rows, width), f32)] * 2
+    for size in (2 * inner, inner, inner, 2 * inner, inner, inner, hidden, hidden):
+        outs.append(shape((rows, size), f32))
+    outs.append(shape((sum(down.shape[0] for down in operands[-3:]), width), f32))
+    vmem = pl.BlockSpec(memory_space=pltpu.VMEM)
+    return pl.pallas_call(
+        finish_kernel,
+        in_specs=[vmem] * len(operands),
+        out_specs=[vmem] * len(outs),
+        out_shape=outs,
+        compiler_params=pltpu.CompilerParams(vmem_limit_bytes=60 * 2**20),
+        cost_estimate=pl.CostEstimate(flops=0, bytes_accessed=16 * 2**20, transcendentals=0),
+    )(*operands)
+
+
 def feed_forward_kernel(depth, tiles, *refs):
     (
-        a3_far, wt_far, valid, x2, gu0_far, d0_far, gu1p, d1p, gu2p, d2p,
+        a3_far, wt_far, keep, x2, gu0_far, d0_far, gu1p, d1p, gu2p, d2p,
         o_top, o_u, pieces, g_gate2, g_up2, g_down2, g5,
         r_gate0, r_up0, r_down0, r_gate1, r_up1, q_gate0, q_up0, q_gate1, q_up1,
         *rest
@@ -1938,7 +1978,7 @@
     for copy in coming:
         copy.wait()
     for block in range(blocks):
-        value = wt[block].reshape(QB, -1).astype(f32) * valid[rows(block)]
+        value = wt[block].reshape(QB, -1).astype(f32) * (keep[rows(block)] == 0.0).astype(f32)
         low_top[rows(block), :] = value.astype(bf16)
     coming = [wires.move(low_top, o_top)]
     wides = [gu0, gu1, gu2]
@@ -2044,7 +2084,8 @@
         wires.arrive(theirs.at[block], spot.sibling(), over + block)
         value = value + theirs[block].astype(f32)
         halves[block].wait()
-        pieces[block] = ((second[block] + value) * valid[half_rows(block, spot.core), :]).astype(bf16)
+        kept = (keep[half_rows(block, spot.core), :] == 0.0).astype(f32)
+        pieces[block] = ((second[block] + value) * kept).astype(bf16)
     for program in sums + [wide1, down1, wide2, down2]:
         for _ in program:
             pass
@@ -2210,12 +2251,11 @@
         ff_up,
     )
     encoded = encoded.reshape(-1, width)
-    valid = (keep_self == 0).astype(f32)
     (
         top_low, changed, output, g_gate, g_up, g_down, g_early,
         r_gate0, r_up0, r_down0, r_gate1, r_up1, q_gate0, q_up0, q_gate1, q_up1,
     ) = feed_forward(
-        depth, tiles, normed_ff, upstream, valid, second, w_gu, w_down,
+        depth, tiles, normed_ff, upstream, keep_self, second, w_gu, w_down,
         near_wide, near_down, wide_pack, down_packs[2],
     )
 
@@ -2226,40 +2266,41 @@
         depth, g_early, g_down, g_gate, g_up, second, first, output, changed, top_low, cross_queries, far_kv, cross_context,
         normed_cross, encoded, w_cross, w_outs, context, cross_sums, keep_cross, gains,
     )
-    (
-        r_cout, r_out, memory_grad, input_grad, packed, d_q, d_k, d_v, d_cq, d_ck, d_cv, d_gate, d_up, d_down,
-    ) = self_part(
+    r_cout, r_out, memory_grad, input_grad, packed, r_cq, r_ckv, r_qkv, q_cq, q_ckv, q_qkv = self_part(
         depth, g_cout, g_cq, g_ckv, g_out.reshape(depth, 1, 2, 2, -1, width), memory_grad, self_up, qkv, context,
         normed_self, inputs, half, w_qkv, self_sums, keep_self, bent, gains, terms, onehot.T,
+    )
+    (
+        input_grad, memory_grad, output, n_self, n_cross, n_ff, r_out, r_cout, d_q, d_k, d_v, d_cq, d_ck, d_cv,
+        d_gate, d_up, d_down,
+    ) = finish(
+        width // (depth * 8),
+        input_grad, memory_grad, output, packed, r_out, r_cout, r_cq, r_ckv, r_qkv, q_cq, q_ckv, q_qkv,
         r_gate0, r_gate1, r_gate2, r_up0, r_up1, r_up2, q_gate0, q_gate1, q_gate2, q_up0, q_up1, q_up2,
         r_down0, r_down1, r_down2,
     )
     bias_grad = packed[24:, :64].reshape(4, 2, 2, BUCKETS)
     bias_grad = jnp.transpose(bias_grad, (3, 0, 2, 1)).reshape(BUCKETS, HEADS)
-    packed = packed[:24].reshape(3, width)
-    mine = lax.axis_index("dp") * 4 + spot.corner
-    piece = width // (depth * 8)
-    n_ff, n_cross, n_self = (lax.dynamic_slice_in_dim(packed[i], mine * piece, piece) for i in range(3))
     bias_grad = lax.dynamic_slice(
         bias_grad, (lax.axis_index("dp") * rel_bias.shape[0], spot.corner * rel_bias.shape[1]), rel_bias.shape
     )
 
     return (
         output.reshape(layer_input.shape),
-        input_grad.astype(f32).reshape(layer_input.shape),
-        memory_grad.astype(f32).reshape(memory.shape),
-        n_self,
+        input_grad.reshape(layer_input.shape),
+        memory_grad.reshape(memory.shape),
+        n_self.reshape(-1),
         d_q,
         d_k,
         d_v,
         r_out,
         bias_grad,
-        n_cross,
+        n_cross.reshape(-1),
         d_cq,
         d_ck,
         d_cv,
         r_cout,
-        n_ff,
+        n_ff.reshape(-1),
         d_gate,
         d_up,
         d_down,

time: 418 us -> 407 us (0.974)
  local copies, waits for them, and re-layouts: 16.2 us -> 6.78 us
  other arithmetic: 12.3 us -> 6.41 us
  Pallas kernels: 384 us -> 389 us
    unnamed x47 -> x7, local copies, waits for them, and re-layouts: 10.1 us -> 1.74 us
    pallas_call x0 -> x1, Pallas kernels: none -> 5.6 us  [finish(): pl.pallas_call(finish_kernel, in_specs=[vmem] * len(operands), out_specs=...]
where the time goes in v7:
time: 407 us; the launch traced here: 403 us
  Pallas kernels  389 us (96%)
  local copies, waits for them, and re-layouts  6.78 us (2%)
  other arithmetic  6.41 us (2%)
    pallas_call x1, Pallas kernels, forward_layer(): pl.pallas_call(functools.partial(forward_layer_kernel, depth, cuts), in_s...  118 us
    pallas_call x1, Pallas kernels, feed_forward(): pl.pallas_call(functools.partial(feed_forward_kernel, depth, tiles), in_s...  105 us
    pallas_call x1, Pallas kernels, self_part(): pl.pallas_call(functools.partial(self_backward_kernel, depth), in_specs=[...  96.9 us
    pallas_call x1, Pallas kernels, cross_part(): pl.pallas_call(functools.partial(cross_backward_kernel, depth), in_specs=...  63 us

profile of v7, /device:TPU:0, one launch (start us, length us, event | category | flops | bytes accessed | tf_op | source)
XLA Modules:
  0.0 403.0 jit_solution(4865767680322570786)
XLA Ops:
  0.7 0.7 pad_reduce_fusion
  1.4 0.1 pad_add_fusion
  1.5 0.4 reverse.2
  1.8 0.1 slice.50
  1.9 0.1 fusion.2
  2.0 0.8 fusion.refs_7_
  2.7 0.1 select_bitcast_fusion
  2.8 0.6 copy.54
  3.4 1.9 slice_bitcast_fusion
  5.3 0.1 iota_compare_fusion.4
  5.4 0.7 convert_element_type.33
  6.1 0.1 select_reduce_fusion
  6.1 0.7 maximum_convert_fusion
  6.8 0.7 fusion.8
  7.6 0.6 fusion.3.refs_3_
  8.2 1.9 pad_maximum_fusion.refs_4_
  10.1 118.2 %shard_map.340 = (bf16[4,2,128,1024]{3,2,1,0:T(8,128)(2,1)}, bf16[4,2,128,1024]{3,2,1,0:T(8,128)(2,1)}, bf16[4,2,64,1024]{3,2,1,0:T(8,128)(2,1)}, f32[4,2,4,8,12...) custom-call(bf16[2,2,128,1024]{3,2,1,0:T(8,128)(2,1)} %bitcast.55, ...), custom_call_target="tpu_custom_call" | custom-call | flops 16000000000 | bytes 134217728 | tf_op jit(solution)/shard_map/pallas_call | solution.py:1347
  128.2 1.6 slice_bitcast_fusion.2.refs_9_
  129.9 105.2 %shard_map.341 = (bf16[1024,1024]{1,0:T(8,128)(2,1)}, bf16[1024,1024]{1,0:T(8,128)(2,1)}, bf16[4,128,1024]{2,1,0:T(8,128)(2,1)}, bf16[4,2,2,2,32,384]{5,4,3,2,1,...) custom-call(bf16[1024,1024]{1,0:T(8,128)(2,1)} %get-tuple-element.10, ...), custom_call_target="tpu_custom_call" | custom-call | flops 27000000512 | bytes 67108864 | tf_op jit(solution)/shard_map/pallas_call | solution.py:2157
  235.1 0.0 copy-start
  235.1 63.0 %shard_map.342 = (f32[32,1024]{1,0:T(8,128)}, f32[24,1024]{1,0:T(8,128)}, f32[32,384]{1,0:T(8,128)}, f32[32,384]{1,0:T(8,128)}, bf16[32,384]{1,0:T(8,128)(2,1)},...) custom-call(bf16[4,1,2,2,32,1024]{5,4,3,2,1,0:T(8,128)(2,1)} %get-tu, ...), custom_call_target="tpu_custom_call" | custom-call | flops 16000000000 | bytes 134217728 | tf_op jit(solution)/shard_map/pallas_call | solution.py:1601
  298.1 0.0 copy-done
  298.1 0.7 fusion.1.refs_17_
  298.8 96.9 %shard_map.343 = (f32[32,1024]{1,0:T(8,128)}, f32[32,1024]{1,0:T(8,128)}, bf16[2,2,64,1024]{3,2,1,0:T(8,128)(2,1)}, bf16[2,2,128,1024]{3,2,1,0:T(8,128)(2,1)}, f...) custom-call(bf16[4,1,2,2,32,1024]{5,4,3,2,1,0:T(8,128)(2,1)} %get-tu, ...), custom_call_target="tpu_custom_call" | custom-call | flops 16000000000 | bytes 134217728 | tf_op jit(solution)/shard_map/pallas_call | solution.py:1847
  395.7 5.6 %shard_map.344 = (f32[2,2,128,1024]{3,2,1,0:T(8,128)}, f32[2,2,64,1024]{3,2,1,0:T(8,128)}, bf16[2,2,128,1024]{3,2,1,0:T(8,128)(2,1)}, f32[1,32]{1,0:T(1,128)}, f...) custom-call(bf16[2,2,128,1024]{3,2,1,0:T(8,128)(2,1)} %get-tuple-ele, ...), custom_call_target="tpu_custom_call" | custom-call | bytes 16777216 | tf_op jit(solution)/shard_map/pallas_call | solution.py:1907
  401.3 0.7 slice.40
  402.0 0.1 reshape.185
  402.1 0.1 dynamic_slice.3
  402.2 0.7 copy.52
  (6 shorter events, 0.0 us)
Async XLA Ops:
  235.1 63.0 %copy-start = (s32[1024]{0:T(1024)S(1)}, s32[1024]{0:T(1024)}, u32[]{:S(2)}) copy-start(s32[1024]{0:T(1024)} %param.25) | copy-start | bytes 12292

commit v8 on v7

--- a/solution.py
+++ b/solution.py
@@ -1118,13 +1118,18 @@
 
 def forward_layer_kernel(depth, cuts, *refs):
     (
-        x, t, m, s, p3, p5, p7, codes, holes, sq, sk, sv, ck, cv, cq, wg, wu,
+        x, t, m, s, codes, holes, sq, sk, sv, ck, cv, cq, wg, wu, so, co, wd,
         o_wx, wt, o_wm, ws, o_w1, o_w2, o_w3, w4, w5,
         o_a1, o_qkv, o_ctx, lse, o_x1, o_a2, o_qc, o_ckv, o_ctxc, lsec, o_x2, o_a3, gains, keeps, keepc, bent,
-        down_s, down_c, n6, n7, p8,
-        p1, p2, p4, p6, bias, own, got, own2, got2, wx, wm, w1, w2, w3, a1, qkv, ctx, x1, a2, qc, ckv, ctxc, x2, a3, *sems
+        down_s, down_c, n6, n7, p8, p9,
+        p1, p2, p4, p6, p3, p5, p7, bias, own, got, got2, wx, wm, w1, w2, w3, a1, qkv, ctx, x1, a2, qc, ckv, ctxc, x2, a3, *sems
     ) = refs
     leaving = []
+    p3[0] = so[...].reshape(p3.shape[1:])
+    p3[1] = co[...].reshape(p3.shape[1:])
+    p5[0] = wd[:, : cuts[0]]
+    p7[0] = wd[:, cuts[0] : cuts[1]]
+    p9[0] = wd[:, cuts[1] : cuts[2]]
     pack_heads(p1, [sq, sk, sv], 0)
     pack_heads(p2, [ck, cv], 0)
     pack_heads(p2, [cq], ck.shape[1])
@@ -1239,9 +1244,16 @@
             advance(outs)
     advance(outs, second, wide, down, wide_next, down_next)
 
+    sent = {}
+
     def pass_on(block, mine, theirs, value, weight, index):
+        if block in sent:
+            sent[block].wait_send()
+            wires.open = [copy for copy in wires.open if copy is not sent[block]]
         mine[rows(block), :] = nn(value[rows(block), :], weight).astype(bf16)
-        wires.send(mine.at[rows(block)], theirs.at[rows(block)], spot.sibling(), over + index + block)
+        sent[block] = wires.send(
+            mine.at[rows(block)], theirs.at[rows(block)], spot.sibling(), over + index + block
+        )
 
     def joined(block, mine, theirs, index):
         wires.arrive(theirs.at[rows(block)], spot.sibling(), over + index + block)
@@ -1263,13 +1275,13 @@
     weight = w3[1].reshape(-1, w3.shape[-1])
     for block in range(blocks):
         attend_rows(block, qc, ckv, ckv.shape[0], keepc, ctxc, lsec, False)
-        pass_on(block, own2, got2, ctxc, weight, blocks)
+        pass_on(block, own, got2, ctxc, weight, blocks)
         if block == 0:
             advance(wide, down)
         if block == 2:
             advance(top)
     for block in range(blocks):
-        value = x1[rows(block), :] + joined(block, own2, got2, blocks)
+        value = x1[rows(block), :] + joined(block, own, got2, blocks)
         x2[rows(block), :] = value
         a3[rows(block), :] = normed(value, gains[2:3, :])
         leave(
@@ -1285,7 +1297,7 @@
     wires.close()
 
 
-def forward_layer(depth, cuts, x, t, m, small, p3, p5, p7, codes, holes, *weights):
+def forward_layer(depth, cuts, x, t, m, small, codes, holes, *weights):
     bf16, f32 = jnp.bfloat16, jnp.float32
     shape = jax.ShapeDtypeStruct
 
@@ -1298,7 +1310,11 @@
     def whole_tokens(parcel):
         return shape((4, 2) + parcel.shape[2:], bf16)
 
-    rows = p3.shape[2]
+    rows = weights[0].shape[0] // 4
+    p3 = shape((2, 4) + (rows, weights[8].shape[1]), bf16)
+    p5, p7, p9 = (
+        shape((1, 4, stop - start, weights[10].shape[2]), bf16) for start, stop in zip((0,) + cuts[:2], cuts)
+    )
     p1 = p2 = shape((2, 4, rows, weights[0].shape[1]), bf16)
     p4, p6, p8 = (
         shape((2, 4, rows, 32 * (stop - start)), bf16) for start, stop in zip((0,) + cuts[:2], cuts)
@@ -1341,16 +1357,17 @@
         (shape((depth, 2) + p6.shape[2:], bf16), hbm),
         (shape((depth,) + p7.shape[2:], bf16), hbm),
         (p8, vmem),
+        (p9, vmem),
     ]
-    packs = [pltpu.VMEM(pack.shape, bf16) for pack in (p1, p2, p4, p6)]
+    packs = [pltpu.VMEM(pack.shape, bf16) for pack in (p1, p2, p4, p6, p3, p5, p7)]
     swap = pltpu.VMEM((tokens, width), bf16)
     return pl.pallas_call(
         functools.partial(forward_layer_kernel, depth, cuts),
-        in_specs=[hbm] * 7 + [vmem] * 10,
+        in_specs=[hbm] * 4 + [vmem] * 13,
         out_specs=[spec for _, spec in outs],
         out_shape=[kind for kind, _ in outs],
         scratch_shapes=packs
-        + [pltpu.VMEM((heads // 2, 2 * QB, 4 * QB), bf16), swap, swap, swap, swap]
+        + [pltpu.VMEM((heads // 2, 2 * QB, 4 * QB), bf16), swap, swap, swap]
         + [pltpu.VMEM(outs[i][0].shape, outs[i][0].dtype) for i in (0, 2, 4, 5, 6, 9, 10, 11, 13, 14, 15, 16, 17, 19, 20)]
         + wire_scratch(35 + 33 * depth, 40),
         compiler_params=pltpu.CompilerParams(
@@ -1359,7 +1376,7 @@
         cost_estimate=pl.CostEstimate(
             flops=16 * 10**9, bytes_accessed=128 * 2**20, transcendentals=10**7
         ),
-    )(x, t, m, small, p3, p5, p7, codes, holes, *weights)
+    )(x, t, m, small, codes, holes, *weights)
 
 
 def pipeline(programs, ahead=2, stages=5):
@@ -2203,7 +2220,6 @@
 
     cuts = [(0, 32), (32, 64), (64, ff_down.shape[0] // 4)]
     tiles = tuple(16 * (stop - start) for start, stop in cuts)
-    down_packs = [ff_down.reshape(4, -1, width)[None, :, start:stop] for start, stop in cuts]
 
     heads = jnp.arange(4)
     spots = (heads // 2) * 64 + 2 * spot.corner + heads % 2
@@ -2228,7 +2244,7 @@
     (
         inputs, upstream, encoded, _, w_qkv, w_cross, w_outs, w_gu, w_down,
         normed_self, qkv, context, self_sums, first, normed_cross, cross_queries, far_kv, cross_context,
-        cross_sums, second, normed_ff, gains, _, _, bent, keep_self, keep_cross, near_wide, near_down, wide_pack,
+        cross_sums, second, normed_ff, gains, _, _, bent, keep_self, keep_cross, near_wide, near_down, wide_pack, down_pack,
     ) = forward_layer(
         depth,
         tuple(stop for _, stop in cuts),
@@ -2236,9 +2252,6 @@
         cotangent.reshape(2, 2, local // 2, width),
         memory.reshape(2, 2, near // 2, width),
         small,
-        jnp.stack([self_out, cross_out]).reshape(2, 4, -1, width),
-        down_packs[0],
-        down_packs[1],
         codes,
         holes,
         self_q,
@@ -2249,6 +2262,9 @@
         cross_q,
         ff_gate,
         ff_up,
+        self_out,
+        cross_out,
+        ff_down.reshape(4, -1, width),
     )
     encoded = encoded.reshape(-1, width)
     (
@@ -2256,7 +2272,7 @@
         r_gate0, r_up0, r_down0, r_gate1, r_up1, q_gate0, q_up0, q_gate1, q_up1,
     ) = feed_forward(
         depth, tiles, normed_ff, upstream, keep_self, second, w_gu, w_down,
-        near_wide, near_down, wide_pack, down_packs[2],
+        near_wide, near_down, wide_pack, down_pack,
     )
 
     (

time: 407 us -> 402 us (0.988)
  no operation moved by 1% of the time
where the time goes in v8:
time: 402 us; the launch traced here: 397 us
  Pallas kernels  389 us (97%)
  other arithmetic  4.54 us (1%)
    pallas_call x1, Pallas kernels, forward_layer(): pl.pallas_call(functools.partial(forward_layer_kernel, depth, cuts), in_s...  118 us
    pallas_call x1, Pallas kernels, feed_forward(): pl.pallas_call(functools.partial(feed_forward_kernel, depth, tiles), in_s...  105 us
    pallas_call x1, Pallas kernels, self_part(): pl.pallas_call(functools.partial(self_backward_kernel, depth), in_specs=[...  96.1 us
    pallas_call x1, Pallas kernels, cross_part(): pl.pallas_call(functools.partial(cross_backward_kernel, depth), in_specs=...  63.8 us

profile of v8, /device:TPU:0, one launch (start us, length us, event | category | flops | bytes accessed | tf_op | source)
XLA Modules:
  0.0 397.5 jit_solution(16883485478794564806)
XLA Ops:
  0.7 0.7 pad_reduce_fusion
  1.4 0.1 pad_add_fusion
  1.5 0.4 reverse.2
  1.8 0.1 slice.32
  1.9 0.1 fusion.2
  2.0 0.8 fusion.refs_4_
  2.7 0.1 select_bitcast_fusion
  2.8 0.6 copy.54
  3.4 0.1 iota_compare_fusion.4
  3.5 0.7 convert_element_type.33
  4.2 0.1 select_reduce_fusion
  4.3 0.7 maximum_convert_fusion
  5.0 0.7 fusion.8
  5.7 0.6 fusion.3.refs_3_
  6.3 118.3 %shard_map.340 = (bf16[4,2,128,1024]{3,2,1,0:T(8,128)(2,1)}, bf16[4,2,128,1024]{3,2,1,0:T(8,128)(2,1)}, bf16[4,2,64,1024]{3,2,1,0:T(8,128)(2,1)}, f32[4,2,4,8,12...) custom-call(bf16[2,2,128,1024]{3,2,1,0:T(8,128)(2,1)} %bitcast.43, ...), custom_call_target="tpu_custom_call" | custom-call | flops 16000000000 | bytes 134217728 | tf_op jit(solution)/shard_map/pallas_call | solution.py:1364
  124.7 104.8 %shard_map.341 = (bf16[1024,1024]{1,0:T(8,128)(2,1)}, bf16[1024,1024]{1,0:T(8,128)(2,1)}, bf16[4,128,1024]{2,1,0:T(8,128)(2,1)}, bf16[4,2,2,2,32,384]{5,4,3,2,1,...) custom-call(bf16[1024,1024]{1,0:T(8,128)(2,1)} %get-tuple-element.10, ...), custom_call_target="tpu_custom_call" | custom-call | flops 27000000512 | bytes 67108864 | tf_op jit(solution)/shard_map/pallas_call | solution.py:2174
  229.5 0.0 copy-start
  229.5 63.8 %shard_map.342 = (f32[32,1024]{1,0:T(8,128)}, f32[24,1024]{1,0:T(8,128)}, f32[32,384]{1,0:T(8,128)}, f32[32,384]{1,0:T(8,128)}, bf16[32,384]{1,0:T(8,128)(2,1)},...) custom-call(bf16[4,1,2,2,32,1024]{5,4,3,2,1,0:T(8,128)(2,1)} %get-tu, ...), custom_call_target="tpu_custom_call" | custom-call | flops 16000000000 | bytes 134217728 | tf_op jit(solution)/shard_map/pallas_call | solution.py:1618
  293.4 0.0 copy-done
  293.4 0.7 fusion.1.refs_17_
  294.1 96.1 %shard_map.343 = (f32[32,1024]{1,0:T(8,128)}, f32[32,1024]{1,0:T(8,128)}, bf16[2,2,64,1024]{3,2,1,0:T(8,128)(2,1)}, bf16[2,2,128,1024]{3,2,1,0:T(8,128)(2,1)}, f...) custom-call(bf16[4,1,2,2,32,1024]{5,4,3,2,1,0:T(8,128)(2,1)} %get-tu, ...), custom_call_target="tpu_custom_call" | custom-call | flops 16000000000 | bytes 134217728 | tf_op jit(solution)/shard_map/pallas_call | solution.py:1864
  390.2 5.6 %shard_map.344 = (f32[2,2,128,1024]{3,2,1,0:T(8,128)}, f32[2,2,64,1024]{3,2,1,0:T(8,128)}, bf16[2,2,128,1024]{3,2,1,0:T(8,128)(2,1)}, f32[1,32]{1,0:T(1,128)}, f...) custom-call(bf16[2,2,128,1024]{3,2,1,0:T(8,128)(2,1)} %get-tuple-ele, ...), custom_call_target="tpu_custom_call" | custom-call | bytes 16777216 | tf_op jit(solution)/shard_map/pallas_call | solution.py:1924
  395.8 0.7 slice.28
  396.5 0.1 reshape.178
  396.6 0.1 dynamic_slice.3
  396.6 0.7 copy.52
  (6 shorter events, 0.0 us)
Async XLA Ops:
  229.5 63.9 %copy-start = (s32[1024]{0:T(1024)S(1)}, s32[1024]{0:T(1024)}, u32[]{:S(2)}) copy-start(s32[1024]{0:T(1024)} %param.25) | copy-start | bytes 12292
